TPU v7x, 256 devices: a whole 4x4x8 slice. The times are simulated.
256 devices in a mesh: space: 32 (over y, z_lo, core), harm: 8 (over z_hi, x).
Axes of the slice: x: 4, y: 4, z: 8 (z_hi: 2, z_lo: 4; z = z_hi * 4 + z_lo), core: 2. Of those that a mesh axis runs over, the one named last changes fastest.
Arguments:
- coeffs: bfloat16 [120, 32, 256, 256], P('harm', 'space'), may hold values from -6 to 6
- synthesis: bfloat16 [256, 120], replicated, may hold values from -0.5 to 0.5
- projection: bfloat16 [120, 256], replicated, may hold values from -0.375 to 0.375
- turn_projection: bfloat16 [3, 120, 256], replicated, may hold values from -0.375 to 0.375
- damping: float32 [120], replicated, may hold values from 0.2 to 2
Outputs:
- rate: bfloat16 [120, 32, 256, 256], P('harm', 'space')
- velocity: float32 [3, 32, 256, 256], P(None, 'space', 'harm')
All inputs are finite; a program needn't handle non-finite values.
Results may differ from a plain program's by a relative error of at most 0.0042.
Values may be sent and summed in bfloat16 or wider, within the bound.
No kernel may reach another device: no remote copies, remote signals or barrier semaphores. Data moves between devices by JAX's collectives and lax.ppermute only.
A program may use at most 128 MiB of HBM per device.

v0:
```python
import functools
import math

import jax
import jax.numpy as jnp
import ml_dtypes
import numpy as np
from jax import lax
from jax.experimental import pallas as pl
from jax.experimental.pallas import tpu as pltpu
from jax.sharding import PartitionSpec as P

activity = -3.0
swim_speed = 1.0
transl_diff = 0.25
shape_factor = 0.9
golden_angle = math.pi * (3.0 - math.sqrt(5.0))

NX, NY, NZ = 256, 256, 32
COEFS, QUAD = 120, 256
SPACES, GROUPS = 32, 8
OWN = COEFS // GROUPS
PAD = 16
ROWS = NY // GROUPS
CELLS = ROWS * NX
HALF = NX // 2
ALL_PAD = GROUPS * PAD
LANES = 128
BLOCKS = 12
bf16, f32 = jnp.bfloat16, jnp.float32
VMEM = pl.BlockSpec(memory_space=pltpu.VMEM)
SMEM = pl.BlockSpec(memory_space=pltpu.SMEM)
PARAMS = pltpu.CompilerParams(vmem_limit_bytes=56 * 1024 * 1024)


def split_table(table):
    high = table.astype(ml_dtypes.bfloat16)
    low = (table - high.astype(np.float64)).astype(ml_dtypes.bfloat16)
    return (high, low)


def signed_wave(length):
    index = np.arange(length)
    signed = np.where(index < length // 2, index, index - length)
    return 2.0 * math.pi / length * np.where(index == length // 2, 0, signed)


def sphere_directions():
    position = np.arange(QUAD, dtype=np.float64)
    height = 1.0 - (2.0 * position + 1.0) / QUAD
    radius = np.sqrt(1.0 - height * height)
    turning = position * golden_angle
    return np.stack([radius * np.cos(turning), radius * np.sin(turning), height])


def tables():
    x = np.arange(NX)[None, :]
    k = np.arange(HALF)[:, None]
    angle = 2.0 * math.pi * (k * x % NX) / NX
    cos_x, sin_x = np.cos(angle), np.sin(angle)
    sign = (-1.0) ** x[0]
    minus = -sin_x
    minus[0] = sign
    forward_x = np.concatenate([cos_x, minus])
    scale = 1.0 / (NX * NY * NZ)
    weight = np.where(k == 0, 1.0, 2.0) * scale
    wave = 2.0 * math.pi / NX * k
    real_x = weight * cos_x
    imag_x = -weight * sin_x
    imag_x[0] = sign * scale
    slope_real = -weight * wave * sin_x
    slope_imag = -weight * wave * cos_x
    back_x = np.concatenate([real_x, imag_x, slope_real, slope_imag], axis=1)
    back_x = np.concatenate([back_x, back_x])

    z = np.arange(NZ)
    angle = 2.0 * math.pi * (z[:, None] * z[None, :] % NZ) / NZ
    both_z = np.concatenate([np.cos(angle), np.sin(angle)])
    forward_z = np.tile(both_z, (1, GROUPS))

    y = np.arange(HALF)[:, None]
    ky = np.arange(NY)[None, :]
    angle = 2.0 * math.pi * (y * ky % NY) / NY
    forward_y = np.block([[np.cos(angle), -np.sin(angle)], [np.sin(angle), np.cos(angle)]])

    ky = np.arange(NY)[:, None]
    angle = 2.0 * math.pi * (ky * np.arange(NY)[None, :] % NY) / NY
    cos_y = np.cos(angle).reshape(NY, GROUPS, 1, ROWS)
    sin_y = np.sin(angle).reshape(NY, GROUPS, 1, ROWS)
    from_real = np.concatenate([cos_y, sin_y], axis=2).reshape(NY, 2 * NY)
    from_imag = np.concatenate([-sin_y, cos_y], axis=2).reshape(NY, 2 * NY)
    back_y = np.concatenate([from_real, from_imag])
    return forward_x, forward_z, forward_y, both_z, back_y, back_x


def halves(value):
    high = value.astype(bf16)
    return high, (value - high.astype(f32)).astype(bf16)


def dot(a, b):
    return jnp.dot(a, b, preferred_element_type=f32)


def regroup_kernel(group_ref, coef_ref, *refs):
    outs, stages = refs[:GROUPS], refs[GROUPS:]
    group = group_ref[0]
    for stage in stages:
        stage[pl.ds(OWN * ROWS, ROWS), :] = jnp.zeros((ROWS, LANES), f32)
    for j in range(GROUPS):
        first = pl.multiple_of((group ^ j) * ROWS, ROWS)
        rows = coef_ref[:, pl.ds(first, ROWS), :].astype(f32)
        rows = rows.reshape(OWN * ROWS, NX)
        for side, stage in enumerate(stages):
            stage[pl.ds(0, OWN * ROWS), :] = rows[:, side * LANES : (side + 1) * LANES]
            for r in range(ROWS):
                lane = r * NX + side * LANES
                outs[j][:, lane : lane + LANES] = stage[pl.ds(r, PAD, stride=ROWS), :].astype(bf16)


def stress_kernel(table_ref, coef_ref, high_ref, low_ref, out_ref, stress_high, stress_low):
    step = 32

    def rows(i, carry):
        first = pl.multiple_of(i * step, step)
        sums = [jnp.zeros((step, NX), f32)] * 5
        for c in range(OWN):
            value = coef_ref[c, pl.ds(first, step), :].astype(f32)
            sums = [s + table_ref[r, c] * value for r, s in enumerate(sums)]
        for r in range(5):
            high, low = halves(sums[r])
            stress_high[r, pl.ds(first, step), :] = high
            stress_low[r, pl.ds(first, step), :] = low
        return carry

    lax.fori_loop(0, NY // step, rows, 0)

    def across(a, b):
        return lax.dot_general(a, b, (((1,), (1,)), ((), ())), preferred_element_type=f32)

    for r in range(5):
        high, low = high_ref[...], low_ref[...]
        result = (
            across(high, stress_high[r]) + across(low, stress_high[r]) + across(high, stress_low[r])
        ).astype(bf16)
        for half in range(2):
            for part in range(2):
                lane = (2 * r + part) * HALF
                out_ref[half * HALF : (half + 1) * HALF, lane : lane + HALF] = result[
                    part * HALF : (part + 1) * HALF, half * HALF : (half + 1) * HALF
                ]


def solve_kernel(
    wave_ref, half_ref, ky_ref, kz_ref, recv_ref,
    fz_high, fz_low, fy_high, fy_low, bz, by_high, by_low, out_ref,
):
    recv = recv_ref[...]
    by_z = dot(fz_high[...], recv) + dot(fz_low[...], recv)
    lines = []
    for r in range(5):
        lane = 2 * r * HALF
        cos_re, cos_im = by_z[:NZ, lane : lane + HALF], by_z[:NZ, lane + HALF : lane + 2 * HALF]
        sin_re, sin_im = by_z[NZ:, lane : lane + HALF], by_z[NZ:, lane + HALF : lane + 2 * HALF]
        lines.append(jnp.concatenate([cos_re + sin_im, cos_im - sin_re], axis=1))
    high, low = halves(jnp.concatenate(lines))
    spec = dot(high, fy_high[...]) + dot(low, fy_high[...]) + dot(high, fy_low[...])
    lane = lax.broadcasted_iota(jnp.int32, (NZ, NY), 1)
    flip = jnp.where((lane % 2) * half_ref[0] == 1, -1.0, 1.0)
    real = [spec[r * NZ : (r + 1) * NZ, :NY] * flip for r in range(5)]
    imag = [spec[r * NZ : (r + 1) * NZ, NY:] * flip for r in range(5)]
    kx = jnp.full((NZ, NY), wave_ref[0], f32)
    ky = jnp.broadcast_to(ky_ref[...], (NZ, NY))
    kz = jnp.broadcast_to(kz_ref[...], (NZ, NY))
    square = kx * kx + ky * ky + kz * kz
    inverse = jnp.where(square > 0, 1.0 / jnp.where(square > 0, square, 1.0), 0.0)

    def force(part):
        xx, yy, xy, xz, yz = part
        return (
            kx * xx + ky * xy + kz * xz,
            kx * xy + ky * yy + kz * yz,
            kx * xz + ky * yz,
        )

    def solve(f):
        along = (kx * f[0] + ky * f[1] + kz * f[2]) * inverse
        return [(f[i] - k * along) * inverse for i, k in enumerate((kx, ky, kz))]

    flow_re = solve([-f for f in force(imag)])
    flow_im = solve(force(real))
    fields = list(zip(flow_re, flow_im))
    fields += [(-ky * flow_im[i], ky * flow_re[i]) for i in range(3)]
    fields += [(-kz * flow_im[i], kz * flow_re[i]) for i in range(2)]
    back = []
    for re, im in fields:
        high, low = halves(jnp.concatenate([re, im], axis=1))
        both = dot(bz[...], jnp.concatenate([high, low, high]))
        back.append(
            jnp.concatenate(
                [both[:NZ, :NY] - both[NZ:, NY:], both[:NZ, NY:] + both[NZ:, :NY]], axis=1
            )
        )
    high, low = halves(jnp.concatenate(back))
    done = dot(high, by_high[...]) + dot(low, by_high[...]) + dot(high, by_low[...])
    for h in range(GROUPS):
        lane = 2 * ROWS * h
        pieces = [done[f * NZ : (f + 1) * NZ, lane : lane + 2 * ROWS] for f in range(8)]
        out_ref[h * NZ : (h + 1) * NZ, :] = jnp.concatenate(pieces, axis=1).astype(bf16)


def fields_kernel(recv_ref, high_ref, low_ref, out_ref):
    flat = recv_ref[...].astype(f32).T.astype(bf16)
    both = dot(flat, high_ref[...]) + dot(flat, low_ref[...])

    def field(f, lane):
        row = 2 * ROWS * f
        return (
            both[row : row + ROWS, lane : lane + NX]
            + both[row + ROWS : row + 2 * ROWS, lane + NX : lane + 2 * NX]
        )

    for i in range(3):
        out_ref[i] = field(i, 0)
        out_ref[3 + i] = field(i, 2 * NX)
    for i in range(5):
        out_ref[6 + i] = field(3 + i, 0)


def weights_kernel(dir_ref, synth_ref, proj_ref, turn_ref, out_ref):
    synth = synth_ref[...]
    p = [dir_ref[j : j + 1, :] for j in range(3)]
    proj = proj_ref[...].astype(f32)
    turn = [turn_ref[k].astype(f32) for k in range(3)]
    radial = turn[0] * p[0] + turn[1] * p[1] + turn[2] * p[2]
    same = 0.5 * (shape_factor + 1.0)
    swap = 0.5 * (shape_factor - 1.0)

    def plain(i, j):
        return turn[i] * p[j] - radial * (p[i] * p[j])

    def strain(i, j):
        return same * plain(i, j) + swap * plain(j, i)

    left = [-0.5 * swim_speed * proj * p[j] for j in range(3)] + [-0.5 * proj]
    trace = strain(2, 2)
    left += [strain(0, 0) - trace, strain(1, 0), strain(2, 0)]
    left += [strain(0, 1), strain(1, 1) - trace, strain(2, 1)]
    left += [strain(0, 2), strain(1, 2)]
    for n, value in enumerate(left):
        high, low = halves(value)
        out_ref[:, n * ALL_PAD : (n + 1) * ALL_PAD] = (dot(high, synth) + dot(low, synth)).astype(bf16)


def assemble_kernel(group_ref, *refs):
    out_ref = refs[GROUPS]
    group = group_ref[0]
    for j in range(GROUPS):
        out_ref[pl.ds(pl.multiple_of((group ^ j) * PAD, PAD), PAD), :] = refs[j][...]


def rate_kernel(
    center_ref, zlow_ref, zhigh_ref, ylow_ref, yhigh_ref, flow_ref, weight_ref, damp_ref,
    out_ref, padded, operand, local_terms, *stages,
):
    chunk = 16
    padded[:, :NX] = ylow_ref[...]
    padded[:, NX : NX + CELLS] = center_ref[...]
    padded[:, NX + CELLS :] = yhigh_ref[...]

    def row(r, carry, part):
        y = part * chunk + r
        here = pl.multiple_of(y * NX, NX)
        flow = [flow_ref[f, pl.ds(y, 1), :] for f in range(11)]
        for g in range(GROUPS):
            rows = slice(g * PAD, (g + 1) * PAD)
            value = padded[rows, pl.ds(here + NX, NX)].astype(f32)
            y_low = padded[rows, pl.ds(here, NX)].astype(f32)
            y_high = padded[rows, pl.ds(here + 2 * NX, NX)].astype(f32)
            z_low = zlow_ref[rows, pl.ds(here, NX)].astype(f32)
            z_high = zhigh_ref[rows, pl.ds(here, NX)].astype(f32)
            x_low = pltpu.roll(value, 1, 1)
            x_high = pltpu.roll(value, NX - 1, 1)
            diffs = (x_high - x_low, y_high - y_low, z_high - z_low)
            drift = flow[0] * diffs[0] + flow[1] * diffs[1] + flow[2] * diffs[2]
            lap = x_high + x_low + y_high + y_low + z_high + z_low - 6.0 * value
            local_terms[rows, :] = transl_diff * lap - damp_ref[rows, :] * value
            terms = list(diffs) + [drift] + [flow[3 + n] * value for n in range(8)]
            for n, term in enumerate(terms):
                operand[n * ALL_PAD + g * PAD : n * ALL_PAD + (g + 1) * PAD, :] = term.astype(bf16)
        result = dot(weight_ref[...], operand[...]) + local_terms[...]
        for side, stage in enumerate(stages):
            stage[pl.ds(r, ALL_PAD, stride=chunk), :] = result[:, side * LANES : (side + 1) * LANES]
        return carry

    for part in range(ROWS // chunk):
        lax.fori_loop(0, chunk, functools.partial(row, part=part), 0)
        for g in range(GROUPS):
            for c in range(OWN):
                first = (g * PAD + c) * chunk
                for side, stage in enumerate(stages):
                    out_ref[
                        g, c, part * chunk : (part + 1) * chunk, side * LANES : (side + 1) * LANES
                    ] = stage[first : first + chunk, :].astype(bf16)


def call(kernel, out_shape, ins, scratch=(), scalars=0, flops=0, byte_count=0):
    return pl.pallas_call(
        kernel,
        out_shape=out_shape,
        in_specs=[SMEM] * scalars + [VMEM] * (len(ins) - scalars),
        out_specs=jax.tree.map(lambda _: VMEM, out_shape),
        scratch_shapes=list(scratch),
        compiler_params=PARAMS,
        cost_estimate=pl.CostEstimate(flops=flops, bytes_accessed=byte_count, transcendentals=0),
    )(*ins)


def shape(*dims, dtype=bf16):
    return jax.ShapeDtypeStruct(dims, dtype)


def pad_groups(value, axis):
    parts = value.reshape(*value.shape[:axis], GROUPS, OWN, *value.shape[axis + 1 :])
    widths = [(0, 0)] * parts.ndim
    widths[axis + 1] = (0, PAD - OWN)
    parts = jnp.pad(parts, widths)
    return parts.reshape(*value.shape[:axis], ALL_PAD, *value.shape[axis + 1 :])


def stress_table(synthesis, directions, group):
    dir_x, dir_y, dir_z = directions
    third = 1.0 / 3.0
    moments = np.stack(
        [
            dir_x * dir_x - third,
            dir_y * dir_y - third,
            dir_z * dir_z - third,
            dir_x * dir_y,
            dir_x * dir_z,
            dir_y * dir_z,
        ]
    ).astype(np.float32)
    own = lax.dynamic_slice_in_dim(synthesis, group * OWN, OWN, 1).astype(f32)
    table = jnp.dot(moments, own, precision=lax.Precision.HIGHEST)
    table = (table * (activity / math.sqrt(QUAD))).astype(bf16).astype(f32)
    return jnp.concatenate([table[0:2] - table[2:3], table[3:6]])


def local(coeffs, synthesis, projection, turn_projection, damping):
    group = lax.axis_index("harm")
    plane = lax.axis_index("space")
    everyone = ("harm", "space")
    position = group * SPACES + plane
    forward_x, forward_z, forward_y, back_z, back_y, back_x = tables()
    directions = sphere_directions()
    own = coeffs.reshape(OWN, NY, NX)
    group_arg = group.astype(jnp.int32).reshape(1)

    chunks = call(
        regroup_kernel, [shape(PAD, CELLS)] * GROUPS, [group_arg, own],
        [pltpu.VMEM((PAD * ROWS, LANES), f32)] * 2, 1, 0, 4 << 20,
    )
    arrived = [chunks[0]]
    for j in range(1, GROUPS):
        arrived.append(lax.ppermute(chunks[j], "harm", [(i, i ^ j) for i in range(GROUPS)]))

    table = stress_table(synthesis, directions, group)
    high, low = split_table(forward_x)
    sent = call(
        stress_kernel, shape(NX, 10 * HALF), [table, own, high, low],
        [pltpu.VMEM((5, NY, NX), bf16)] * 2, 1, 1 << 30, 3 << 20,
    )
    columns = lax.all_to_all(sent, everyone, 0, 0, tiled=True)

    wave = (position % HALF).astype(f32) * (2.0 * math.pi / NX)
    half = (position // HALF).astype(jnp.int32)
    bz_high, bz_low = split_table(back_z)
    sent = call(
        solve_kernel, shape(NX, 16 * ROWS),
        [
            wave.reshape(1), half.reshape(1),
            signed_wave(NY).astype(np.float32)[None, :], signed_wave(NZ).astype(np.float32)[:, None],
            columns, *split_table(forward_z), *split_table(forward_y),
            np.concatenate([bz_high, bz_high, bz_low], axis=1), *split_table(back_y),
        ],
        (), 2, 1 << 30, 3 << 20,
    )
    mixed = lax.all_to_all(sent, everyone, 0, 0, tiled=True)
    flow = call(fields_kernel, shape(11, ROWS, NX, dtype=f32), [mixed, *split_table(back_x)], (), 0, 1 << 29, 2 << 20)

    weights = call(
        weights_kernel, shape(ALL_PAD, BLOCKS * ALL_PAD),
        [
            directions.astype(np.float32), pad_groups(synthesis, 1),
            pad_groups(projection, 0), pad_groups(turn_projection, 1),
        ],
        (), 0, 1 << 28, 1 << 20,
    )
    center = call(assemble_kernel, shape(ALL_PAD, CELLS), [group_arg, *arrived], (), 1, 0, 4 << 20)
    up = [(i, (i + 1) % SPACES) for i in range(SPACES)]
    z_low = lax.ppermute(center, "space", up)
    z_high = lax.ppermute(center, "space", [(b, a) for a, b in up])
    up = [(i, (i + 1) % GROUPS) for i in range(GROUPS)]
    y_low = lax.ppermute(center[:, -NX:], "harm", up)
    y_high = lax.ppermute(center[:, :NX], "harm", [(b, a) for a, b in up])

    rates = call(
        rate_kernel, shape(GROUPS, OWN, ROWS, NX),
        [center, z_low, z_high, y_low, y_high, flow, weights, pad_groups(damping, 0)[:, None]],
        [
            pltpu.VMEM((ALL_PAD, CELLS + 2 * NX), bf16),
            pltpu.VMEM((BLOCKS * ALL_PAD, NX), bf16),
            pltpu.VMEM((ALL_PAD, NX), f32),
            pltpu.VMEM((ALL_PAD * 16, LANES), f32),
            pltpu.VMEM((ALL_PAD * 16, LANES), f32),
        ],
        0, 7 << 30, 9 << 20,
    )
    back = lax.all_to_all(rates, "harm", 0, 0, tiled=True)
    rate = jnp.moveaxis(back, 0, 1).reshape(OWN, 1, NY, NX)
    return (rate, flow[0:3].reshape(3, 1, ROWS, NX))


def solution(mesh):
    in_specs = (P("harm", "space", None, None), P(), P(), P(), P())
    out_specs = (P("harm", "space", None, None), P(None, "space", "harm", None))
    return jax.shard_map(local, mesh=mesh, in_specs=in_specs, out_specs=out_specs, check_vma=False)
```

profile of v0, /device:TPU:62, one launch (start us, length us, event | category | flops | bytes accessed | tf_op | source)
XLA Modules:
  0.0 250.9 jit_solution(12462493830004938928)
XLA Ops:
  0.7 6.0 %shard_map.203 = (bf16[16,8192]{1,0:T(8,128)(2,1)}, bf16[16,8192]{1,0:T(8,128)(2,1)}, bf16[16,8192]{1,0:T(8,128)(2,1)}, bf16[16,8192]{1,0:T(8,128)(2,1)}, bf16[1...) custom-call(s32[1]{0:T(128)} %bitcast.group_ref, ...), custom_call_target="tpu_custom_call" | custom-call | bytes 4194304 | tf_op jit(solution)/shard_map/pallas_call | solution.py:308
  6.6 0.8 collective-permute-start
  7.4 1.1 collective-permute-start.1
  8.6 2.8 %collective-permute-start.2 = (bf16[16,8192]{1,0:T(8,128)(2,1)}, bf16[16,8192]{1,0:T(8,128)(2,1)S(1)}, u32[]{:S(2)}, u32[]{:S(2)}) collective-permute-start(bf16[16,8192]{1,0:T(8,128)(2,1)} %get-tuple-element.13), channel_id=1, source_target_pairs={{0,3},{1,2},{2,1},{3,0},{4,7},{5,6},{6,5},{7,4},{8,11},{9,10},{10,... | collective-permute-start | bytes 786440 | tf_op jit(solution)/shard_map/ppermute | solution.py:366
  11.3 6.3 %collective-permute-start.3 = (bf16[16,8192]{1,0:T(8,128)(2,1)}, bf16[16,8192]{1,0:T(8,128)(2,1)S(1)}, u32[]{:S(2)}, u32[]{:S(2)}) collective-permute-start(bf16[16,8192]{1,0:T(8,128)(2,1)} %get-tuple-element.14), channel_id=1, source_target_pairs={{0,4},{1,5},{2,6},{3,7},{4,0},{5,1},{6,2},{7,3},{8,12},{9,13},{10,... | collective-permute-start | bytes 786440 | tf_op jit(solution)/shard_map/ppermute | solution.py:366
  17.6 0.1 fusion.2
  17.8 6.8 %collective-permute-start.5 = (bf16[16,8192]{1,0:T(8,128)(2,1)}, bf16[16,8192]{1,0:T(8,128)(2,1)S(1)}, u32[]{:S(2)}, u32[]{:S(2)}) collective-permute-start(bf16[16,8192]{1,0:T(8,128)(2,1)} %get-tuple-element.16), channel_id=1, source_target_pairs={{0,6},{1,7},{2,4},{3,5},{4,2},{5,3},{6,0},{7,1},{8,14},{9,15},{10,... | collective-permute-start | bytes 786440 | tf_op jit(solution)/shard_map/ppermute | solution.py:366
  24.6 4.4 %collective-permute-start.6 = (bf16[16,8192]{1,0:T(8,128)(2,1)}, bf16[16,8192]{1,0:T(8,128)(2,1)S(1)}, u32[]{:S(2)}, u32[]{:S(2)}) collective-permute-start(bf16[16,8192]{1,0:T(8,128)(2,1)} %get-tuple-element.17), channel_id=1, source_target_pairs={{0,7},{1,6},{2,5},{3,4},{4,3},{5,2},{6,1},{7,0},{8,15},{9,14},{10,... | collective-permute-start | bytes 786440 | tf_op jit(solution)/shard_map/ppermute | solution.py:366
  29.0 5.6 %collective-permute-done.3.refs_4_ = bf16[16,8192]{1,0:T(8,128)(2,1)S(1)} collective-permute-done((bf16[16,8192]{1,0:T(8,128)(2,1)}, bf16[16,8192]{1,0:T(8,128)(2,1)S(1)}, u32[]{:S(2)}, u32[]{:S(2)}) %collective-permute-start.3) | collective-permute-done | bytes 262176 | tf_op jit(solution)/shard_map/ppermute | solution.py:366
  34.6 13.8 %collective-permute-done.4.refs_5_ = bf16[16,8192]{1,0:T(8,128)(2,1)S(1)} collective-permute-done((bf16[16,8192]{1,0:T(8,128)(2,1)}, bf16[16,8192]{1,0:T(8,128)(2,1)S(1)}, u32[]{:S(2)}, u32[]{:S(2)}) %collective-permute-start.4) | collective-permute-done | bytes 262176 | tf_op jit(solution)/shard_map/ppermute | solution.py:366
  48.4 10.2 %collective-permute-done.5.refs_6_ = bf16[16,8192]{1,0:T(8,128)(2,1)S(1)} collective-permute-done((bf16[16,8192]{1,0:T(8,128)(2,1)}, bf16[16,8192]{1,0:T(8,128)(2,1)S(1)}, u32[]{:S(2)}, u32[]{:S(2)}) %collective-permute-start.5) | collective-permute-done | bytes 262176 | tf_op jit(solution)/shard_map/ppermute | solution.py:366
  58.6 4.1 %collective-permute-done.6.refs_7_ = bf16[16,8192]{1,0:T(8,128)(2,1)S(1)} collective-permute-done((bf16[16,8192]{1,0:T(8,128)(2,1)}, bf16[16,8192]{1,0:T(8,128)(2,1)S(1)}, u32[]{:S(2)}, u32[]{:S(2)}) %collective-permute-start.6) | collective-permute-done | bytes 262176 | tf_op jit(solution)/shard_map/ppermute | solution.py:366
  62.8 0.6 copy-done.6
  63.5 3.0 %shard_map.204.center_ref = bf16[128,8192]{1,0:T(8,128)(2,1)} custom-call(s32[1]{0:T(128)} %bitcast.group_ref, bf16[16,8192]{1,0:T(8,128)(2,1)} %get-tuple-element.10.refs_0_, bf16[16,8192]{1,0:T(8,128)(2,1)} %copy-done, bf16[16,8192]{1,0:T(8,128)(2,1)} %copy-done.1, bf16[16,8192]{1,0:T(8,128)(2,1)} %copy-done.2, bf16[16,8192]{1,0:T(8,128)(2,1)} %copy-done.3, ...), custom_call_target="tpu_custom_call" | custom-call | bytes 4194304 | tf_op jit(solution)/shard_map/pallas_call | solution.py:308
  66.4 1.7 collective-permute-start.8
  68.2 0.6 pad_maximum_fusion.table_ref
  68.8 4.8 %shard_map.205 = bf16[256,1280]{1,0:T(8,128)(2,1)} custom-call(f32[5,15]{1,0:T(8,128)} %pad_maximum_fusion.table_ref, bf16[15,256,256]{2,1,0:T(8,128)(2,1)} %bitcast.32, bf16[256,256]{1,0:T(8,128)(2,1)} %constant.81.clone.high_ref, bf16[256,256]{1,0:T(8,128)(2,1)} %constant.82.clone.low_ref), custom_call_target="tpu_custom_call" | custom-call | flops 1073741824 | bytes 3145728 | tf_op jit(solution)/shard_map/pallas_call | solution.py:308
  73.6 0.5 broadcast.12
  74.1 2.1 reduce
  76.2 1.0 reshape.60
  77.1 16.1 %all-to-all-start = ((bf16[256,2,640]{2,1,0:T(2,128)(2,1)}), bf16[256,2,640]{2,1,0:T(2,128)(2,1)S(1)}, u32[]{:S(2)}, u32[]{:S(2)}) async-start(bf16[256,2,640]{2,1,0:T(2,128)(2,1)} %reshape.60), calls=%async_computation | async-start | bytes 1310720 | tf_op jit(solution)/shard_map/all_to_all | solution.py:374
  93.3 41.6 %all-to-all-done = bf16[256,2,640]{2,1,0:T(2,128)(2,1)S(1)} async-done(((bf16[256,2,640]{2,1,0:T(2,128)(2,1)}), bf16[256,2,640]{2,1,0:T(2,128)(2,1)S(1)}, u32[]{:S(2)}, u32[]{:S(2)}) %all-to-all-start) | async-done | bytes 655392 | tf_op jit(solution)/shard_map/all_to_all | solution.py:374
  134.9 0.5 reshape.61
  135.5 0.9 copy.48
  136.4 4.1 %shard_map.206 = bf16[256,512]{1,0:T(8,128)(2,1)} custom-call(f32[1]{0:T(128)} %bitcast.2.wave_ref, s32[1]{0:T(128)} %bitcast.3.half_ref, f32[1,256]{1,0:T(1,128)} %constant.83.clone.ky_ref, f32[32,1]{1,0:T(8,128)} %constant.84.clone.kz_ref, bf16[256,1280]{1,0:T(8,128)(2,1)} %bitcast.35, bf16[64,256]{1,0:T(8,128)(2,1)} %constant.85.clone.fz_high, ...), custom_call_target="tpu_custom_call" | custom-call | flops 1073741824 | bytes 3145728 | tf_op jit(solution)/shard_map/pallas_call | solution.py:308
  140.4 1.6 reduce.1
  142.1 0.8 reshape.62
  142.9 11.3 %all-to-all-start.1 = ((bf16[256,2,256]{2,1,0:T(2,128)(2,1)}), bf16[256,2,256]{2,1,0:T(2,128)(2,1)S(1)}, u32[]{:S(2)}, u32[]{:S(2)}) async-start(bf16[256,2,256]{2,1,0:T(2,128)(2,1)} %reshape.62), calls=%async_computation.1 | async-start | bytes 524288 | tf_op jit(solution)/shard_map/all_to_all | solution.py:389
  154.2 0.1 reshape.55
  154.3 0.7 pad.18
  155.0 0.7 copy.39.synth_ref
  155.8 0.6 pad.17
  156.4 0.1 reshape.57
  156.5 0.7 broadcast_in_dim_reshape.4.damp_ref
  157.2 0.9 fusion.5
  158.1 0.9 collective-permute-start.10
  159.0 7.2 %collective-permute-start.9 = (bf16[128,256]{1,0:T(8,128)(2,1)S(1)}, bf16[128,256]{1,0:T(8,128)(2,1)S(1)}, u32[]{:S(2)}, u32[]{:S(2)}) collective-permute-start(bf16[128,256]{1,0:T(8,128)(2,1)S(1)} %get-tuple-element.27), channel_id=1, source_target_pairs={{0,1},{1,2},{2,3},{3,4},{4,5},{5,6},{6,7},{7,0},{8,9},{9,10},{10,1... | collective-permute-start | bytes 196616 | tf_op jit(solution)/shard_map/ppermute | solution.py:405
  166.2 2.5 shard_map.208.weight_ref
  168.7 0.2 reshape.63
  169.0 0.7 copy.49
  169.7 2.8 %shard_map.207.flow_ref = f32[11,32,256]{2,1,0:T(8,128)} custom-call(bf16[256,512]{1,0:T(8,128)(2,1)} %bitcast.36, bf16[256,1024]{1,0:T(8,128)(2,1)} %constant.92.clone.high_ref, bf16[256,1024]{1,0:T(8,128)(2,1)} %constant.93.clone.low_ref), custom_call_target="tpu_custom_call" | custom-call | flops 536870912 | bytes 2097152 | tf_op jit(solution)/shard_map/pallas_call | solution.py:308
  172.5 0.6 copy-done.12
  173.1 0.0 copy-done.13
  173.1 19.0 %shard_map.209 = bf16[8,15,32,256]{3,2,1,0:T(8,128)(2,1)} custom-call(bf16[128,8192]{1,0:T(8,128)(2,1)} %shard_map.204.center_ref, bf16[128,8192]{1,0:T(8,128)(2,1)} %collective-permute-done.7.zlow_ref, bf16[128,8192]{1,0:T(8,128)(2,1)} %collective-permute-done.8.zhigh_ref, bf16[128,256]{1,0:T(8,128)(2,1)} %copy-done.13, bf16[128,256]{1,0:T(8,128)(2,1)} %copy-done.12, ...), custom_call_target="tpu_custom_call" | custom-call | flops 7516192768 | bytes 9437184 | tf_op jit(solution)/shard_map/pallas_call | solution.py:308
  192.1 9.5 %all-to-all-start.2 = ((bf16[8,15,32,256]{3,2,1,0:T(8,128)(2,1)}), bf16[8,15,32,256]{3,2,1,0:T(8,128)(2,1)S(1)}, u32[]{:S(2)}, u32[]{:S(2)}) async-start(bf16[8,15,32,256]{3,2,1,0:T(8,128)(2,1)} %shard_map.209), calls=%async_computation.2 | async-start | bytes 3932160 | tf_op jit(solution)/shard_map/all_to_all | solution.py:420
  201.6 1.5 slice_bitcast_fusion
  203.2 46.3 %all-to-all-done.2 = bf16[8,15,32,256]{3,2,1,0:T(8,128)(2,1)S(1)} async-done(((bf16[8,15,32,256]{3,2,1,0:T(8,128)(2,1)}), bf16[8,15,32,256]{3,2,1,0:T(8,128)(2,1)S(1)}, u32[]{:S(2)}, u32[]{:S(2)}) %all-to-all-start.2) | async-done | bytes 1966112 | tf_op jit(solution)/shard_map/all_to_all | solution.py:420
  249.4 1.5 copy.41
  (42 shorter events, 0.2 us)
Async XLA Ops:
  0.6 17.0 %copy-start.10 = (f32[6,256]{1,0:T(8,128)S(1)}, f32[6,256]{1,0:T(8,128)}, u32[]{:S(2)}) copy-start(f32[6,256]{1,0:T(8,128)} %constant.80.clone) | copy-start | bytes 18436
  0.6 17.0 %copy-start.8 = (bf16[256,120]{0,1:T(8,128)(2,1)S(1)}, bf16[256,120]{0,1:T(8,128)(2,1)}, u32[]{:S(2)}) copy-start(bf16[256,120]{0,1:T(8,128)(2,1)} %param.21) | copy-start | bytes 184324
  6.6 11.1 %collective-permute-start = (bf16[16,8192]{1,0:T(8,128)(2,1)}, bf16[16,8192]{1,0:T(8,128)(2,1)S(1)}, u32[]{:S(2)}, u32[]{:S(2)}) collective-permute-start(bf16[16,8192]{1,0:T(8,128)(2,1)} %get-tuple-element.11), channel_id=1, source_target_pairs={{0,1},{1,0},{2,3},{3,2},{4,5},{5,4},{6,7},{7,6},{8,9},{9,8},{10,11... | collective-permute-start | bytes 786440 | tf_op jit(solution)/shard_map/ppermute | solution.py:366
  7.4 17.1 %collective-permute-start.1 = (bf16[16,8192]{1,0:T(8,128)(2,1)}, bf16[16,8192]{1,0:T(8,128)(2,1)S(1)}, u32[]{:S(2)}, u32[]{:S(2)}) collective-permute-start(bf16[16,8192]{1,0:T(8,128)(2,1)} %get-tuple-element.12), channel_id=1, source_target_pairs={{0,2},{1,3},{2,0},{3,1},{4,6},{5,7},{6,4},{7,5},{8,10},{9,11},{10,... | collective-permute-start | bytes 786440 | tf_op jit(solution)/shard_map/ppermute | solution.py:366
  8.6 20.5 %collective-permute-start.2 = (bf16[16,8192]{1,0:T(8,128)(2,1)}, bf16[16,8192]{1,0:T(8,128)(2,1)S(1)}, u32[]{:S(2)}, u32[]{:S(2)}) collective-permute-start(bf16[16,8192]{1,0:T(8,128)(2,1)} %get-tuple-element.13), channel_id=1, source_target_pairs={{0,3},{1,2},{2,1},{3,0},{4,7},{5,6},{6,5},{7,4},{8,11},{9,10},{10,... | collective-permute-start | bytes 786440 | tf_op jit(solution)/shard_map/ppermute | solution.py:366
  11.3 23.3 %collective-permute-start.3 = (bf16[16,8192]{1,0:T(8,128)(2,1)}, bf16[16,8192]{1,0:T(8,128)(2,1)S(1)}, u32[]{:S(2)}, u32[]{:S(2)}) collective-permute-start(bf16[16,8192]{1,0:T(8,128)(2,1)} %get-tuple-element.14), channel_id=1, source_target_pairs={{0,4},{1,5},{2,6},{3,7},{4,0},{5,1},{6,2},{7,3},{8,12},{9,13},{10,... | collective-permute-start | bytes 786440 | tf_op jit(solution)/shard_map/ppermute | solution.py:366
  17.6 30.8 %collective-permute-start.4 = (bf16[16,8192]{1,0:T(8,128)(2,1)}, bf16[16,8192]{1,0:T(8,128)(2,1)S(1)}, u32[]{:S(2)}, u32[]{:S(2)}) collective-permute-start(bf16[16,8192]{1,0:T(8,128)(2,1)} %get-tuple-element.15), channel_id=1, source_target_pairs={{0,5},{1,4},{2,7},{3,6},{4,1},{5,0},{6,3},{7,2},{8,13},{9,12},{10,... | collective-permute-start | bytes 786440 | tf_op jit(solution)/shard_map/ppermute | solution.py:366
  17.7 45.0 %copy-start = (bf16[16,8192]{1,0:T(8,128)(2,1)}, bf16[16,8192]{1,0:T(8,128)(2,1)S(1)}, u32[]{:S(2)}) copy-start(bf16[16,8192]{1,0:T(8,128)(2,1)S(1)} %collective-permute-done.refs_1_) | copy-start | bytes 786436
  17.8 40.9 %collective-permute-start.5 = (bf16[16,8192]{1,0:T(8,128)(2,1)}, bf16[16,8192]{1,0:T(8,128)(2,1)S(1)}, u32[]{:S(2)}, u32[]{:S(2)}) collective-permute-start(bf16[16,8192]{1,0:T(8,128)(2,1)} %get-tuple-element.16), channel_id=1, source_target_pairs={{0,6},{1,7},{2,4},{3,5},{4,2},{5,3},{6,0},{7,1},{8,14},{9,15},{10,... | collective-permute-start | bytes 786440 | tf_op jit(solution)/shard_map/ppermute | solution.py:366
  24.6 38.2 %copy-start.1 = (bf16[16,8192]{1,0:T(8,128)(2,1)}, bf16[16,8192]{1,0:T(8,128)(2,1)S(1)}, u32[]{:S(2)}) copy-start(bf16[16,8192]{1,0:T(8,128)(2,1)S(1)} %collective-permute-done.1.refs_2_) | copy-start | bytes 786436
  24.6 38.2 %collective-permute-start.6 = (bf16[16,8192]{1,0:T(8,128)(2,1)}, bf16[16,8192]{1,0:T(8,128)(2,1)S(1)}, u32[]{:S(2)}, u32[]{:S(2)}) collective-permute-start(bf16[16,8192]{1,0:T(8,128)(2,1)} %get-tuple-element.17), channel_id=1, source_target_pairs={{0,7},{1,6},{2,5},{3,4},{4,3},{5,2},{6,1},{7,0},{8,15},{9,14},{10,... | collective-permute-start | bytes 786440 | tf_op jit(solution)/shard_map/ppermute | solution.py:366
  29.0 33.8 %copy-start.2 = (bf16[16,8192]{1,0:T(8,128)(2,1)}, bf16[16,8192]{1,0:T(8,128)(2,1)S(1)}, u32[]{:S(2)}) copy-start(bf16[16,8192]{1,0:T(8,128)(2,1)S(1)} %collective-permute-done.2.refs_3_) | copy-start | bytes 786436
  34.6 28.2 %copy-start.3 = (bf16[16,8192]{1,0:T(8,128)(2,1)}, bf16[16,8192]{1,0:T(8,128)(2,1)S(1)}, u32[]{:S(2)}) copy-start(bf16[16,8192]{1,0:T(8,128)(2,1)S(1)} %collective-permute-done.3.refs_4_) | copy-start | bytes 786436
  48.4 14.4 %copy-start.4 = (bf16[16,8192]{1,0:T(8,128)(2,1)}, bf16[16,8192]{1,0:T(8,128)(2,1)S(1)}, u32[]{:S(2)}) copy-start(bf16[16,8192]{1,0:T(8,128)(2,1)S(1)} %collective-permute-done.4.refs_5_) | copy-start | bytes 786436
  58.6 4.2 %copy-start.5 = (bf16[16,8192]{1,0:T(8,128)(2,1)}, bf16[16,8192]{1,0:T(8,128)(2,1)S(1)}, u32[]{:S(2)}) copy-start(bf16[16,8192]{1,0:T(8,128)(2,1)S(1)} %collective-permute-done.5.refs_6_) | copy-start | bytes 786436
  62.8 0.7 copy-start.6
  66.4 106.1 %collective-permute-start.7 = (bf16[128,8192]{1,0:T(8,128)(2,1)}, bf16[128,8192]{1,0:T(8,128)(2,1)}, u32[]{:S(2)}, u32[]{:S(2)}) collective-permute-start(bf16[128,8192]{1,0:T(8,128)(2,1)} %shard_map.204.center_ref), channel_id=1, source_target_pairs={{0,8},{8,16},{16,24},{24,32},{32,40},{40,48},{48,56},{56,64},{64,7... | collective-permute-start | bytes 6291464 | tf_op jit(solution)/shard_map/ppermute | solution.py:402
  66.4 106.1 %collective-permute-start.8 = (bf16[128,8192]{1,0:T(8,128)(2,1)}, bf16[128,8192]{1,0:T(8,128)(2,1)}, u32[]{:S(2)}, u32[]{:S(2)}) collective-permute-start(bf16[128,8192]{1,0:T(8,128)(2,1)} %shard_map.204.center_ref), channel_id=1, source_target_pairs={{8,0},{16,8},{24,16},{32,24},{40,32},{48,40},{56,48},{64,56},{72,6... | collective-permute-start | bytes 6291464 | tf_op jit(solution)/shard_map/ppermute | solution.py:403
  77.1 57.8 %all-to-all-start = ((bf16[256,2,640]{2,1,0:T(2,128)(2,1)}), bf16[256,2,640]{2,1,0:T(2,128)(2,1)S(1)}, u32[]{:S(2)}, u32[]{:S(2)}) async-start(bf16[256,2,640]{2,1,0:T(2,128)(2,1)} %reshape.60), calls=%async_computation | async-start | bytes 1310720 | tf_op jit(solution)/shard_map/all_to_all | solution.py:374
  136.4 17.9 %copy-start.7 = (bf16[3,120,256]{2,1,0:T(8,128)(2,1)S(1)}, bf16[3,120,256]{2,1,0:T(8,128)(2,1)}, u32[]{:S(2)}) copy-start(bf16[3,120,256]{2,1,0:T(8,128)(2,1)} %param.23) | copy-start | bytes 552964
  140.4 15.3 %copy-start.9 = (bf16[120,256]{1,0:T(8,128)(2,1)S(1)}, bf16[120,256]{1,0:T(8,128)(2,1)}, u32[]{:S(2)}) copy-start(bf16[120,256]{1,0:T(8,128)(2,1)} %param.22) | copy-start | bytes 184324
  140.4 16.0 %copy-start.11 = (f32[120]{0:T(128)S(1)}, f32[120]{0:T(128)}, u32[]{:S(2)}) copy-start(f32[120]{0:T(128)} %param.24) | copy-start | bytes 1444
  142.9 25.9 %all-to-all-start.1 = ((bf16[256,2,256]{2,1,0:T(2,128)(2,1)}), bf16[256,2,256]{2,1,0:T(2,128)(2,1)S(1)}, u32[]{:S(2)}, u32[]{:S(2)}) async-start(bf16[256,2,256]{2,1,0:T(2,128)(2,1)} %reshape.62), calls=%async_computation.1 | async-start | bytes 524288 | tf_op jit(solution)/shard_map/all_to_all | solution.py:389
  158.1 14.4 %collective-permute-start.10 = (bf16[128,256]{1,0:T(8,128)(2,1)S(1)}, bf16[128,256]{1,0:T(8,128)(2,1)S(1)}, u32[]{:S(2)}, u32[]{:S(2)}) collective-permute-start(bf16[128,256]{1,0:T(8,128)(2,1)S(1)} %get-tuple-element.26), channel_id=1, source_target_pairs={{1,0},{2,1},{3,2},{4,3},{5,4},{6,5},{7,6},{0,7},{9,8},{10,9},{11,1... | collective-permute-start | bytes 196616 | tf_op jit(solution)/shard_map/ppermute | solution.py:406
  159.0 13.4 %collective-permute-start.9 = (bf16[128,256]{1,0:T(8,128)(2,1)S(1)}, bf16[128,256]{1,0:T(8,128)(2,1)S(1)}, u32[]{:S(2)}, u32[]{:S(2)}) collective-permute-start(bf16[128,256]{1,0:T(8,128)(2,1)S(1)} %get-tuple-element.27), channel_id=1, source_target_pairs={{0,1},{1,2},{2,3},{3,4},{4,5},{5,6},{6,7},{7,0},{8,9},{9,10},{10,1... | collective-permute-start | bytes 196616 | tf_op jit(solution)/shard_map/ppermute | solution.py:405
  172.5 0.6 copy-start.12
  172.5 0.6 copy-start.13
  192.1 57.3 %all-to-all-start.2 = ((bf16[8,15,32,256]{3,2,1,0:T(8,128)(2,1)}), bf16[8,15,32,256]{3,2,1,0:T(8,128)(2,1)S(1)}, u32[]{:S(2)}, u32[]{:S(2)}) async-start(bf16[8,15,32,256]{3,2,1,0:T(8,128)(2,1)} %shard_map.209), calls=%async_computation.2 | async-start | bytes 3932160 | tf_op jit(solution)/shard_map/all_to_all | solution.py:420
where the time goes:
time: 252 us; the launch traced here: 251 us
  waiting for transfers between devices  122 us (48%)
  starting transfers between devices  69 us (27%)
  Pallas kernels  42 us (17%)
  local copies, waits for them, and re-layouts  12.9 us (5%)
  other arithmetic  4.31 us (2%)
    all_to_all x1, waiting for transfers between devices, local(): back = lax.all_to_all(rates, 'harm', 0, 0, tiled=True)  46.3 us
    pallas_call x7, Pallas kernels, call(): pl.pallas_call(kernel, out_shape=out_shape, in_specs=[SMEM] * scalars + [...  42 us
    all_to_all x1, waiting for transfers between devices, local(): columns = lax.all_to_all(sent, everyone, 0, 0, tiled=True)  41.6 us
    ppermute x7, waiting for transfers between devices, local(): lax.ppermute(chunks[j], 'harm', [(i, i ^ j) for i in range(GROUPS)])  33.7 us
    ppermute x7, starting transfers between devices, local(): lax.ppermute(chunks[j], 'harm', [(i, i ^ j) for i in range(GROUPS)])  22.2 us
    all_to_all x1, starting transfers between devices, local(): columns = lax.all_to_all(sent, everyone, 0, 0, tiled=True)  16.1 us
    all_to_all x1, starting transfers between devices, local(): mixed = lax.all_to_all(sent, everyone, 0, 0, tiled=True)  11.3 us
    all_to_all x1, starting transfers between devices, local(): back = lax.all_to_all(rates, 'harm', 0, 0, tiled=True)  9.5 us
  transfers between devices with their start and end apart: 14, of which 6 were waited for; matrix products, arithmetic and copies ran while one was open for 6% of the time, Pallas kernels for 6%

commit v1 on v0

--- a/solution.py
+++ b/solution.py
@@ -26,6 +26,10 @@
 HALF = NX // 2
 ALL_PAD = GROUPS * PAD
 LANES = 128
+RUN = 8
+FLIP = GROUPS // 2
+PARTS = 2
+CHUNK = ROWS // PARTS
 BLOCKS = 12
 bf16, f32 = jnp.bfloat16, jnp.float32
 VMEM = pl.BlockSpec(memory_space=pltpu.VMEM)
@@ -102,13 +106,13 @@
     return jnp.dot(a, b, preferred_element_type=f32)
 
 
-def regroup_kernel(group_ref, coef_ref, *refs):
+def regroup_kernel(block_ref, coef_ref, *refs):
     outs, stages = refs[:GROUPS], refs[GROUPS:]
-    group = group_ref[0]
+    block = block_ref[0]
     for stage in stages:
         stage[pl.ds(OWN * ROWS, ROWS), :] = jnp.zeros((ROWS, LANES), f32)
     for j in range(GROUPS):
-        first = pl.multiple_of((group ^ j) * ROWS, ROWS)
+        first = pl.multiple_of((block ^ j) * ROWS, ROWS)
         rows = coef_ref[:, pl.ds(first, ROWS), :].astype(f32)
         rows = rows.reshape(OWN * ROWS, NX)
         for side, stage in enumerate(stages):
@@ -203,10 +207,16 @@
         )
     high, low = halves(jnp.concatenate(back))
     done = dot(high, by_high[...]) + dot(low, by_high[...]) + dot(high, by_low[...])
+    blocks = []
     for h in range(GROUPS):
         lane = 2 * ROWS * h
         pieces = [done[f * NZ : (f + 1) * NZ, lane : lane + 2 * ROWS] for f in range(8)]
-        out_ref[h * NZ : (h + 1) * NZ, :] = jnp.concatenate(pieces, axis=1).astype(bf16)
+        blocks.append(jnp.concatenate(pieces, axis=1))
+    plane = lax.broadcasted_iota(jnp.int32, blocks[0].shape, 0)
+    flipped = (plane // RUN) % 2 == 1
+    for h in range(GROUPS):
+        value = jnp.where(flipped, blocks[h ^ FLIP], blocks[h])
+        out_ref[h * NZ : (h + 1) * NZ, :] = value.astype(bf16)
 
 
 def fields_kernel(recv_ref, high_ref, low_ref, out_ref):
@@ -260,18 +270,19 @@
 
 
 def rate_kernel(
-    center_ref, zlow_ref, zhigh_ref, ylow_ref, yhigh_ref, flow_ref, weight_ref, damp_ref,
-    out_ref, padded, operand, local_terms, *stages,
+    group_ref, center_ref, zlow_ref, zhigh_ref, ylow_ref, yhigh_ref, flow_ref, weight_ref, damp_ref,
+    *refs,
 ):
-    chunk = 16
+    outs, (padded, operands, locals_, *stages) = refs[:GROUPS], refs[GROUPS:]
+    group = group_ref[0]
+    cells = CHUNK * NX
     padded[:, :NX] = ylow_ref[...]
-    padded[:, NX : NX + CELLS] = center_ref[...]
-    padded[:, NX + CELLS :] = yhigh_ref[...]
-
-    def row(r, carry, part):
-        y = part * chunk + r
-        here = pl.multiple_of(y * NX, NX)
-        flow = [flow_ref[f, pl.ds(y, 1), :] for f in range(11)]
+    padded[:, NX : NX + cells] = center_ref[...]
+    padded[:, NX + cells :] = yhigh_ref[...]
+
+    def build(r, operand, local_terms):
+        here = pl.multiple_of(r * NX, NX)
+        flow = [flow_ref[f, pl.ds(r, 1), :] for f in range(11)]
         for g in range(GROUPS):
             rows = slice(g * PAD, (g + 1) * PAD)
             value = padded[rows, pl.ds(here + NX, NX)].astype(f32)
@@ -288,27 +299,42 @@
             terms = list(diffs) + [drift] + [flow[3 + n] * value for n in range(8)]
             for n, term in enumerate(terms):
                 operand[n * ALL_PAD + g * PAD : n * ALL_PAD + (g + 1) * PAD, :] = term.astype(bf16)
-        result = dot(weight_ref[...], operand[...]) + local_terms[...]
-        for side, stage in enumerate(stages):
-            stage[pl.ds(r, ALL_PAD, stride=chunk), :] = result[:, side * LANES : (side + 1) * LANES]
+
+    def rows(i, carry):
+        for n in range(2):
+            build(2 * i + n, operands.at[n], locals_.at[n])
+        for n in range(2):
+            result = dot(weight_ref[...], operands[n]) + locals_[n]
+            for side, stage in enumerate(stages):
+                stage[pl.ds(2 * i + n, ALL_PAD, stride=CHUNK), :] = result[
+                    :, side * LANES : (side + 1) * LANES
+                ]
         return carry
 
-    for part in range(ROWS // chunk):
-        lax.fori_loop(0, chunk, functools.partial(row, part=part), 0)
-        for g in range(GROUPS):
-            for c in range(OWN):
-                first = (g * PAD + c) * chunk
-                for side, stage in enumerate(stages):
-                    out_ref[
-                        g, c, part * chunk : (part + 1) * chunk, side * LANES : (side + 1) * LANES
-                    ] = stage[first : first + chunk, :].astype(bf16)
-
-
-def call(kernel, out_shape, ins, scratch=(), scalars=0, flops=0, byte_count=0):
+    lax.fori_loop(0, CHUNK // 2, rows, 0)
+    for j in range(GROUPS):
+        for c in range(OWN):
+            first = pl.multiple_of(((group ^ j) * PAD + c) * CHUNK, CHUNK)
+            for side, stage in enumerate(stages):
+                outs[j][c, :, side * LANES : (side + 1) * LANES] = stage[
+                    pl.ds(first, CHUNK), :
+                ].astype(bf16)
+
+
+def place_kernel(block_ref, *refs):
+    out_ref = refs[-1]
+    for part in range(PARTS):
+        for j in range(GROUPS):
+            first = pl.multiple_of((block_ref[0] ^ j) * ROWS + part * CHUNK, CHUNK)
+            out_ref[:, pl.ds(first, CHUNK), :] = refs[part * GROUPS + j][...]
+
+
+def call(kernel, out_shape, ins, scratch=(), scalars=0, flops=0, byte_count=0, specs=None):
     return pl.pallas_call(
         kernel,
         out_shape=out_shape,
-        in_specs=[SMEM] * scalars + [VMEM] * (len(ins) - scalars),
+        grid=(1,) if specs else (),
+        in_specs=specs or [SMEM] * scalars + [VMEM] * (len(ins) - scalars),
         out_specs=jax.tree.map(lambda _: VMEM, out_shape),
         scratch_shapes=list(scratch),
         compiler_params=PARAMS,
@@ -347,23 +373,31 @@
     return jnp.concatenate([table[0:2] - table[2:3], table[3:6]])
 
 
+def odd(plane):
+    return (plane // RUN) % 2
+
+
+def pairs(target):
+    found = []
+    for plane in range(SPACES):
+        for group in range(GROUPS):
+            to_plane, to_block = target(plane, group ^ (FLIP * odd(plane)))
+            to_group = to_block ^ (FLIP * odd(to_plane))
+            found.append((plane * GROUPS + group, to_plane * GROUPS + to_group))
+    return found
+
+
 def local(coeffs, synthesis, projection, turn_projection, damping):
     group = lax.axis_index("harm")
     plane = lax.axis_index("space")
+    both = ("space", "harm")
     everyone = ("harm", "space")
     position = group * SPACES + plane
     forward_x, forward_z, forward_y, back_z, back_y, back_x = tables()
     directions = sphere_directions()
     own = coeffs.reshape(OWN, NY, NX)
     group_arg = group.astype(jnp.int32).reshape(1)
-
-    chunks = call(
-        regroup_kernel, [shape(PAD, CELLS)] * GROUPS, [group_arg, own],
-        [pltpu.VMEM((PAD * ROWS, LANES), f32)] * 2, 1, 0, 4 << 20,
-    )
-    arrived = [chunks[0]]
-    for j in range(1, GROUPS):
-        arrived.append(lax.ppermute(chunks[j], "harm", [(i, i ^ j) for i in range(GROUPS)]))
+    block_arg = group_arg ^ (FLIP * odd(plane)).astype(jnp.int32)
 
     table = stress_table(synthesis, directions, group)
     high, low = split_table(forward_x)
@@ -372,6 +406,15 @@
         [pltpu.VMEM((5, NY, NX), bf16)] * 2, 1, 1 << 30, 3 << 20,
     )
     columns = lax.all_to_all(sent, everyone, 0, 0, tiled=True)
+
+    later, _ = lax.optimization_barrier((own, sent))
+    chunks = call(
+        regroup_kernel, [shape(PAD, CELLS)] * GROUPS, [block_arg, later],
+        [pltpu.VMEM((PAD * ROWS, LANES), f32)] * 2, 1, 0, 4 << 20,
+    )
+    arrived = [chunks[0]]
+    for j in range(1, GROUPS):
+        arrived.append(lax.ppermute(chunks[j], "harm", [(i, i ^ j) for i in range(GROUPS)]))
 
     wave = (position % HALF).astype(f32) * (2.0 * math.pi / NX)
     half = (position // HALF).astype(jnp.int32)
@@ -387,7 +430,12 @@
         (), 2, 1 << 30, 3 << 20,
     )
     mixed = lax.all_to_all(sent, everyone, 0, 0, tiled=True)
-    flow = call(fields_kernel, shape(11, ROWS, NX, dtype=f32), [mixed, *split_table(back_x)], (), 0, 1 << 29, 2 << 20)
+    arrived, _ = lax.optimization_barrier((arrived, sent))
+    center = call(assemble_kernel, shape(ALL_PAD, CELLS), [group_arg, *arrived], (), 1, 0, 4 << 20)
+    z_low = lax.ppermute(center, both, pairs(lambda s, b: ((s + 1) % SPACES, b)))
+    z_high = lax.ppermute(center, both, pairs(lambda s, b: ((s - 1) % SPACES, b)))
+    y_low = lax.ppermute(center[:, -NX:], both, pairs(lambda s, b: (s, (b + 1) % GROUPS)))
+    y_high = lax.ppermute(center[:, :NX], both, pairs(lambda s, b: (s, (b - 1) % GROUPS)))
 
     weights = call(
         weights_kernel, shape(ALL_PAD, BLOCKS * ALL_PAD),
@@ -397,29 +445,43 @@
         ],
         (), 0, 1 << 28, 1 << 20,
     )
-    center = call(assemble_kernel, shape(ALL_PAD, CELLS), [group_arg, *arrived], (), 1, 0, 4 << 20)
-    up = [(i, (i + 1) % SPACES) for i in range(SPACES)]
-    z_low = lax.ppermute(center, "space", up)
-    z_high = lax.ppermute(center, "space", [(b, a) for a, b in up])
-    up = [(i, (i + 1) % GROUPS) for i in range(GROUPS)]
-    y_low = lax.ppermute(center[:, -NX:], "harm", up)
-    y_high = lax.ppermute(center[:, :NX], "harm", [(b, a) for a, b in up])
-
-    rates = call(
-        rate_kernel, shape(GROUPS, OWN, ROWS, NX),
-        [center, z_low, z_high, y_low, y_high, flow, weights, pad_groups(damping, 0)[:, None]],
-        [
-            pltpu.VMEM((ALL_PAD, CELLS + 2 * NX), bf16),
-            pltpu.VMEM((BLOCKS * ALL_PAD, NX), bf16),
-            pltpu.VMEM((ALL_PAD, NX), f32),
-            pltpu.VMEM((ALL_PAD * 16, LANES), f32),
-            pltpu.VMEM((ALL_PAD * 16, LANES), f32),
-        ],
-        0, 7 << 30, 9 << 20,
-    )
-    back = lax.all_to_all(rates, "harm", 0, 0, tiled=True)
-    rate = jnp.moveaxis(back, 0, 1).reshape(OWN, 1, NY, NX)
-    return (rate, flow[0:3].reshape(3, 1, ROWS, NX))
+    flow = call(fields_kernel, shape(11, ROWS, NX, dtype=f32), [mixed, *split_table(back_x)], (), 0, 1 << 29, 2 << 20)
+    damp = pad_groups(damping, 0)[:, None]
+    returned, parts = [], []
+    for part in range(PARTS):
+        here = pl.BlockSpec((ALL_PAD, CHUNK * NX), lambda i, part=part: (0, part))
+        first, last = part * CHUNK, (part + 1) * CHUNK
+
+        def edge(row):
+            return pl.BlockSpec((ALL_PAD, NX), lambda i: (0, row))
+
+        low = (y_low, VMEM) if first == 0 else (center, edge(first - 1))
+        high = (y_high, VMEM) if last == ROWS else (center, edge(last))
+        rates = call(
+            rate_kernel, [shape(OWN, CHUNK, NX)] * GROUPS,
+            [group_arg, center, z_low, z_high, low[0], high[0], flow, weights, damp],
+            [
+                pltpu.VMEM((ALL_PAD, (CHUNK + 2) * NX), bf16),
+                pltpu.VMEM((2, BLOCKS * ALL_PAD, NX), bf16),
+                pltpu.VMEM((2, ALL_PAD, NX), f32),
+                pltpu.VMEM((ALL_PAD * CHUNK, LANES), f32),
+                pltpu.VMEM((ALL_PAD * CHUNK, LANES), f32),
+            ],
+            1, 7 << 29, 9 << 19,
+            [
+                SMEM, here, here, here, low[1], high[1],
+                pl.BlockSpec((11, CHUNK, NX), lambda i, part=part: (0, part, 0)), VMEM, VMEM,
+            ],
+        )
+        parts.append(rates[0])
+        returned.append(rates[0])
+        for j in range(1, GROUPS):
+            returned.append(lax.ppermute(rates[j], "harm", [(i, i ^ j) for i in range(GROUPS)]))
+    swap = pairs(lambda s, b: (s, b ^ (FLIP * odd(s))))
+    late, _ = lax.optimization_barrier((flow[0:3], parts))
+    velocity = lax.ppermute(late, both, swap)
+    rate = call(place_kernel, shape(OWN, NY, NX), [block_arg, *returned], (), 1, 0, 4 << 20)
+    return (rate.reshape(OWN, 1, NY, NX), velocity.reshape(3, 1, ROWS, NX))
 
 
 def solution(mesh):

time: 252 us -> 227 us (0.901)
  waiting for transfers between devices: 122 us -> 62.1 us
  starting transfers between devices: 69 us -> 101 us
    all_to_all x1 -> x0, waiting for transfers between devices: 46.3 us -> none  [local(): back = lax.all_to_all(rates, 'harm', 0, 0, tiled=True)]
    ppermute x4 -> x19, starting transfers between devices: 9.87 us -> 52.2 us  [the longest x14 39.8 us: local(): lax.ppermute(rates[j], 'harm', [(i, i ^ j) for i in range(GROUPS)])]
    all_to_all x1, waiting for transfers between devices: 41.6 us -> 0.01 us  [local(): columns = lax.all_to_all(sent, everyone, 0, 0, tiled=True)]
    ppermute x4 -> x19, waiting for transfers between devices: 0.01 us -> 17.7 us  [the longest x14 11.3 us: local(): lax.ppermute(rates[j], 'harm', [(i, i ^ j) for i in range(GROUPS)])]
    all_to_all x1, waiting for transfers between devices: 0.01 us -> 13.2 us  [local(): mixed = lax.all_to_all(sent, everyone, 0, 0, tiled=True)]
    all_to_all x1 -> x0, starting transfers between devices: 9.5 us -> none  [local(): back = lax.all_to_all(rates, 'harm', 0, 0, tiled=True)]
    pallas_call x7 -> x9, Pallas kernels: 42 us -> 43.4 us  [call(): pl.pallas_call(kernel, out_shape=out_shape, grid=(1,) if specs else (), i...]
    unnamed x35 -> x69, local copies, waits for them, and re-layouts: 7 us -> 7.52 us
  transfers between devices with their start and end apart: 14 -> 28, of which waited for: 6 -> 13; matrix products, arithmetic and copies ran while one was open for 6% -> 4% of each run, Pallas kernels for 6% -> 14%
where the time goes in v1:
time: 227 us; the launch traced here: 225 us
  starting transfers between devices  101 us (44%)
  waiting for transfers between devices  62.1 us (27%)
  Pallas kernels  43.4 us (19%)
  local copies, waits for them, and re-layouts  12.9 us (6%)
  other arithmetic  3.56 us (2%)
    pallas_call x9, Pallas kernels, call(): pl.pallas_call(kernel, out_shape=out_shape, grid=(1,) if specs else (), i...  43.4 us
    ppermute x14, starting transfers between devices, local(): lax.ppermute(rates[j], 'harm', [(i, i ^ j) for i in range(GROUPS)])  39.8 us
    ppermute x7, waiting for transfers between devices, local(): lax.ppermute(chunks[j], 'harm', [(i, i ^ j) for i in range(GROUPS)])  31.3 us
    ppermute x7, starting transfers between devices, local(): lax.ppermute(chunks[j], 'harm', [(i, i ^ j) for i in range(GROUPS)])  22.1 us
    all_to_all x1, starting transfers between devices, local(): columns = lax.all_to_all(sent, everyone, 0, 0, tiled=True)  14.2 us
    all_to_all x1, waiting for transfers between devices, local(): mixed = lax.all_to_all(sent, everyone, 0, 0, tiled=True)  13.2 us
    all_to_all x1, starting transfers between devices, local(): mixed = lax.all_to_all(sent, everyone, 0, 0, tiled=True)  12.4 us
    ppermute x14, waiting for transfers between devices, local(): lax.ppermute(rates[j], 'harm', [(i, i ^ j) for i in range(GROUPS)])  11.3 us
  transfers between devices with their start and end apart: 28, of which 13 were waited for; matrix products, arithmetic and copies ran while one was open for 4% of the time, Pallas kernels for 14%

profile of v1, /device:TPU:62, one launch (start us, length us, event | category | flops | bytes accessed | tf_op | source)
XLA Modules:
  0.0 224.7 jit_solution(13775926257569483524)
XLA Ops:
  0.6 0.8 fusion.2
  2.1 4.8 %shard_map.203 = bf16[256,1280]{1,0:T(8,128)(2,1)} custom-call(f32[5,15]{1,0:T(8,128)} %pad_maximum_fusion.table_ref, bf16[15,256,256]{2,1,0:T(8,128)(2,1)} %bitcast.29, bf16[256,256]{1,0:T(8,128)(2,1)} %constant.102.clone.high_ref, bf16[256,256]{1,0:T(8,128)(2,1)} %constant.103.clone.low_ref), custom_call_target="tpu_custom_call" | custom-call | flops 1073741824 | bytes 3145728 | tf_op jit(solution)/shard_map/pallas_call | solution.py:333
  7.5 2.2 reduce
  9.7 1.0 reshape.60
  10.7 14.2 %all-to-all-start = ((bf16[256,2,640]{2,1,0:T(2,128)(2,1)}), bf16[256,2,640]{2,1,0:T(2,128)(2,1)S(1)}, u32[]{:S(2)}, u32[]{:S(2)}) async-start(bf16[256,2,640]{2,1,0:T(2,128)(2,1)} %reshape.60), calls=%async_computation | async-start | bytes 1310720 | tf_op jit(solution)/shard_map/all_to_all | solution.py:408
  24.9 6.0 %shard_map.204 = (bf16[16,8192]{1,0:T(8,128)(2,1)}, bf16[16,8192]{1,0:T(8,128)(2,1)}, bf16[16,8192]{1,0:T(8,128)(2,1)}, bf16[16,8192]{1,0:T(8,128)(2,1)}, bf16[1...) custom-call(s32[1]{0:T(128)S(6)} %xor.7.block_ref, ...), custom_call_target="tpu_custom_call" | custom-call | bytes 4194304 | tf_op jit(solution)/shard_map/pallas_call | solution.py:333
  30.9 0.8 collective-permute-start
  31.7 1.1 collective-permute-start.1
  32.9 2.7 %collective-permute-start.2 = (bf16[16,8192]{1,0:T(8,128)(2,1)}, bf16[16,8192]{1,0:T(8,128)(2,1)S(1)}, u32[]{:S(2)}, u32[]{:S(2)}) collective-permute-start(bf16[16,8192]{1,0:T(8,128)(2,1)} %get-tuple-element.40), channel_id=1, source_target_pairs={{0,3},{1,2},{2,1},{3,0},{4,7},{5,6},{6,5},{7,4},{8,11},{9,10},{10,... | collective-permute-start | bytes 786440 | tf_op jit(solution)/shard_map/ppermute | solution.py:417
  35.6 5.5 %collective-permute-start.3 = (bf16[16,8192]{1,0:T(8,128)(2,1)}, bf16[16,8192]{1,0:T(8,128)(2,1)S(1)}, u32[]{:S(2)}, u32[]{:S(2)}) collective-permute-start(bf16[16,8192]{1,0:T(8,128)(2,1)} %get-tuple-element.41), channel_id=1, source_target_pairs={{0,4},{1,5},{2,6},{3,7},{4,0},{5,1},{6,2},{7,3},{8,12},{9,13},{10,... | collective-permute-start | bytes 786440 | tf_op jit(solution)/shard_map/ppermute | solution.py:417
  41.1 1.7 collective-permute-done.refs_1_
  42.8 5.5 %collective-permute-start.5 = (bf16[16,8192]{1,0:T(8,128)(2,1)}, bf16[16,8192]{1,0:T(8,128)(2,1)S(1)}, u32[]{:S(2)}, u32[]{:S(2)}) collective-permute-start(bf16[16,8192]{1,0:T(8,128)(2,1)} %get-tuple-element.43), channel_id=1, source_target_pairs={{0,6},{1,7},{2,4},{3,5},{4,2},{5,3},{6,0},{7,1},{8,14},{9,15},{10,... | collective-permute-start | bytes 786440 | tf_op jit(solution)/shard_map/ppermute | solution.py:417
  48.5 6.3 %collective-permute-start.6 = (bf16[16,8192]{1,0:T(8,128)(2,1)}, bf16[16,8192]{1,0:T(8,128)(2,1)}, u32[]{:S(2)}, u32[]{:S(2)}) collective-permute-start(bf16[16,8192]{1,0:T(8,128)(2,1)} %get-tuple-element.44), channel_id=1, source_target_pairs={{0,7},{1,6},{2,5},{3,4},{4,3},{5,2},{6,1},{7,0},{8,15},{9,14},{10,... | collective-permute-start | bytes 786440 | tf_op jit(solution)/shard_map/ppermute | solution.py:417
  55.3 0.9 copy.50
  56.2 4.0 %shard_map.205 = bf16[256,512]{1,0:T(8,128)(2,1)} custom-call(f32[1]{0:T(128)} %bitcast.5.wave_ref, s32[1]{0:T(128)} %bitcast.6.half_ref, f32[1,256]{1,0:T(1,128)} %constant.104.clone.ky_ref, f32[32,1]{1,0:T(8,128)} %constant.105.clone.kz_ref, bf16[256,1280]{1,0:T(8,128)(2,1)} %bitcast.33, bf16[64,256]{1,0:T(8,128)(2,1)} %constant.106.clone.fz_high, ...), custom_call_target="tpu_custom_call" | custom-call | flops 1073741824 | bytes 3145728 | tf_op jit(solution)/shard_map/pallas_call | solution.py:333
  60.3 6.8 %collective-permute-done.3.refs_4_ = bf16[16,8192]{1,0:T(8,128)(2,1)S(1)} collective-permute-done((bf16[16,8192]{1,0:T(8,128)(2,1)}, bf16[16,8192]{1,0:T(8,128)(2,1)S(1)}, u32[]{:S(2)}, u32[]{:S(2)}) %collective-permute-start.3) | collective-permute-done | bytes 262176 | tf_op jit(solution)/shard_map/ppermute | solution.py:417
  67.1 11.0 %collective-permute-done.4.refs_5_ = bf16[16,8192]{1,0:T(8,128)(2,1)S(1)} collective-permute-done((bf16[16,8192]{1,0:T(8,128)(2,1)}, bf16[16,8192]{1,0:T(8,128)(2,1)S(1)}, u32[]{:S(2)}, u32[]{:S(2)}) %collective-permute-start.4) | collective-permute-done | bytes 262176 | tf_op jit(solution)/shard_map/ppermute | solution.py:417
  78.1 7.1 %collective-permute-done.5.refs_6_ = bf16[16,8192]{1,0:T(8,128)(2,1)S(1)} collective-permute-done((bf16[16,8192]{1,0:T(8,128)(2,1)}, bf16[16,8192]{1,0:T(8,128)(2,1)S(1)}, u32[]{:S(2)}, u32[]{:S(2)}) %collective-permute-start.5) | collective-permute-done | bytes 262176 | tf_op jit(solution)/shard_map/ppermute | solution.py:417
  85.2 4.5 %collective-permute-done.6.refs_7_ = bf16[16,8192]{1,0:T(8,128)(2,1)} collective-permute-done((bf16[16,8192]{1,0:T(8,128)(2,1)}, bf16[16,8192]{1,0:T(8,128)(2,1)}, u32[]{:S(2)}, u32[]{:S(2)}) %collective-permute-start.6) | collective-permute-done | bytes 262176 | tf_op jit(solution)/shard_map/ppermute | solution.py:417
  89.8 3.0 %shard_map.206.center_ref.yhigh_ref.ylow_ref = bf16[128,8192]{1,0:T(8,128)(2,1)} custom-call(s32[1]{0:T(128)} %bitcast.group_ref, bf16[16,8192]{1,0:T(8,128)(2,1)} %get-tuple-element.45.refs_0_, bf16[16,8192]{1,0:T(8,128)(2,1)} %copy-done, bf16[16,8192]{1,0:T(8,128)(2,1)} %copy-done.1, bf16[16,8192]{1,0:T(8,128)(2,1)} %copy-done.2, ...), custom_call_target="tpu_custom_call" | custom-call | bytes 4194304 | tf_op jit(solution)/shard_map/pallas_call | solution.py:333
  92.8 1.7 collective-permute-start.8
  96.1 12.4 %all-to-all-start.1 = ((bf16[256,2,256]{2,1,0:T(2,128)(2,1)}), bf16[256,2,256]{2,1,0:T(2,128)(2,1)S(1)}, u32[]{:S(2)}, u32[]{:S(2)}) async-start(bf16[256,2,256]{2,1,0:T(2,128)(2,1)} %reshape.62), calls=%async_computation.1 | async-start | bytes 524288 | tf_op jit(solution)/shard_map/all_to_all | solution.py:432
  111.6 0.9 fusion.5
  112.5 5.6 %collective-permute-start.9 = (bf16[128,256]{1,0:T(8,128)(2,1)S(1)}, bf16[128,256]{1,0:T(8,128)(2,1)S(1)}, u32[]{:S(2)}, u32[]{:S(2)}) collective-permute-start(bf16[128,256]{1,0:T(8,128)(2,1)S(1)} %get-tuple-element.79), channel_id=1, source_target_pairs={{0,1},{1,2},{2,3},{3,4},{4,5},{5,6},{6,7},{7,0},{8,9},{9,10},{10,1... | collective-permute-start | bytes 196616 | tf_op jit(solution)/shard_map/ppermute | solution.py:437
  118.1 2.5 %shard_map.208.weight_ref = bf16[128,1536]{1,0:T(8,128)(2,1)} custom-call(f32[3,256]{1,0:T(4,128)} %constant.113.clone.dir_ref, bf16[256,128]{1,0:T(8,128)(2,1)} %copy.41.synth_ref, bf16[128,256]{1,0:T(8,128)(2,1)} %bitcast.39, bf16[3,128,256]{2,1,0:T(8,128)(2,1)} %bitcast.37), custom_call_target="tpu_custom_call" | custom-call | flops 268435456 | bytes 1048576 | tf_op jit(solution)/shard_map/pallas_call | solution.py:333
  120.5 13.2 %all-to-all-done.1 = bf16[256,2,256]{2,1,0:T(2,128)(2,1)S(1)} async-done(((bf16[256,2,256]{2,1,0:T(2,128)(2,1)}), bf16[256,2,256]{2,1,0:T(2,128)(2,1)S(1)}, u32[]{:S(2)}, u32[]{:S(2)}) %all-to-all-start.1) | async-done | bytes 262176 | tf_op jit(solution)/shard_map/all_to_all | solution.py:432
  134.7 2.8 %shard_map.207.flow_ref = f32[11,32,256]{2,1,0:T(8,128)} custom-call(bf16[256,512]{1,0:T(8,128)(2,1)} %bitcast.34, bf16[256,1024]{1,0:T(8,128)(2,1)} %constant.114.clone.high_ref, bf16[256,1024]{1,0:T(8,128)(2,1)} %constant.115.clone.low_ref), custom_call_target="tpu_custom_call" | custom-call | flops 536870912 | bytes 2097152 | tf_op jit(solution)/shard_map/pallas_call | solution.py:333
  137.4 0.9 slice.26
  139.7 8.7 %shard_map.209 = (bf16[15,16,256]{2,1,0:T(8,128)(2,1)}, bf16[15,16,256]{2,1,0:T(8,128)(2,1)}, bf16[15,16,256]{2,1,0:T(8,128)(2,1)}, bf16[15,16,256]{2,1,0:T(8,12...) custom-call(s32[1]{0:T(128)} %bitcast.group_ref, ...), custom_call_target="tpu_custom_call" | custom-call | flops 3758096384 | bytes 4718592 | tf_op jit(solution)/shard_map/pallas_call | solution.py:333
  148.8 1.9 collective-permute-start.11
  150.7 2.4 %collective-permute-start.12 = (bf16[15,16,256]{2,1,0:T(8,128)(2,1)}, bf16[15,16,256]{2,1,0:T(8,128)(2,1)S(1)}, u32[]{:S(2)}, u32[]{:S(2)}) collective-permute-start(bf16[15,16,256]{2,1,0:T(8,128)(2,1)} %get-tuple-element.56), channel_id=1, source_target_pairs={{0,3},{1,2},{2,1},{3,0},{4,7},{5,6},{6,5},{7,4},{8,11},{9,10},{10,... | collective-permute-start | bytes 368648 | tf_op jit(solution)/shard_map/ppermute | solution.py:479
  153.1 2.8 %collective-permute-start.13 = (bf16[15,16,256]{2,1,0:T(8,128)(2,1)}, bf16[15,16,256]{2,1,0:T(8,128)(2,1)S(1)}, u32[]{:S(2)}, u32[]{:S(2)}) collective-permute-start(bf16[15,16,256]{2,1,0:T(8,128)(2,1)} %get-tuple-element.57), channel_id=1, source_target_pairs={{0,4},{1,5},{2,6},{3,7},{4,0},{5,1},{6,2},{7,3},{8,12},{9,13},{10,... | collective-permute-start | bytes 368648 | tf_op jit(solution)/shard_map/ppermute | solution.py:479
  156.5 8.7 %shard_map.210 = (bf16[15,16,256]{2,1,0:T(8,128)(2,1)}, bf16[15,16,256]{2,1,0:T(8,128)(2,1)}, bf16[15,16,256]{2,1,0:T(8,128)(2,1)}, bf16[15,16,256]{2,1,0:T(8,12...) custom-call(s32[1]{0:T(128)} %bitcast.group_ref, ...), custom_call_target="tpu_custom_call" | custom-call | flops 3758096384 | bytes 4718592 | tf_op jit(solution)/shard_map/pallas_call | solution.py:333
  165.2 5.1 %collective-permute-start.25 = (f32[3,32,256]{2,1,0:T(8,128)S(1)}, f32[3,32,256]{2,1,0:T(8,128)S(1)}, u32[]{:S(2)}, u32[]{:S(2)}) collective-permute-start(f32[3,32,256]{2,1,0:T(8,128)S(1)} %slice.26), channel_id=1, source_target_pairs={{0,0},{1,1},{2,2},{3,3},{4,4},{5,5},{6,6},{7,7},{8,8},{9,9},{10,10... | collective-permute-start | bytes 294920 | tf_op jit(solution)/shard_map/ppermute | solution.py:482
  170.3 6.4 %collective-permute-done.25 = f32[3,32,256]{2,1,0:T(8,128)S(1)} collective-permute-done((f32[3,32,256]{2,1,0:T(8,128)S(1)}, f32[3,32,256]{2,1,0:T(8,128)S(1)}, u32[]{:S(2)}, u32[]{:S(2)}) %collective-permute-start.25) | collective-permute-done | bytes 98336 | tf_op jit(solution)/shard_map/ppermute | solution.py:482
  176.6 2.0 collective-permute-start.14
  178.6 4.9 %collective-permute-start.15 = (bf16[15,16,256]{2,1,0:T(8,128)(2,1)S(1)}, bf16[15,16,256]{2,1,0:T(8,128)(2,1)S(1)}, u32[]{:S(2)}, u32[]{:S(2)}) collective-permute-start(bf16[15,16,256]{2,1,0:T(8,128)(2,1)S(1)} %copy-done.27), channel_id=1, source_target_pairs={{0,6},{1,7},{2,4},{3,5},{4,2},{5,3},{6,0},{7,1},{8,14},{9,15},{10,... | collective-permute-start | bytes 368648 | tf_op jit(solution)/shard_map/ppermute | solution.py:479
  183.5 5.1 %collective-permute-start.16 = (bf16[15,16,256]{2,1,0:T(8,128)(2,1)S(1)}, bf16[15,16,256]{2,1,0:T(8,128)(2,1)S(1)}, u32[]{:S(2)}, u32[]{:S(2)}) collective-permute-start(bf16[15,16,256]{2,1,0:T(8,128)(2,1)S(1)} %copy-done.26), channel_id=1, source_target_pairs={{0,7},{1,6},{2,5},{3,4},{4,3},{5,2},{6,1},{7,0},{8,15},{9,14},{10,... | collective-permute-start | bytes 368648 | tf_op jit(solution)/shard_map/ppermute | solution.py:479
  188.6 2.6 %collective-permute-start.19 = (bf16[15,16,256]{2,1,0:T(8,128)(2,1)}, bf16[15,16,256]{2,1,0:T(8,128)(2,1)S(1)}, u32[]{:S(2)}, u32[]{:S(2)}) collective-permute-start(bf16[15,16,256]{2,1,0:T(8,128)(2,1)} %get-tuple-element.63), channel_id=1, source_target_pairs={{0,2},{1,3},{2,0},{3,1},{4,6},{5,7},{6,4},{7,5},{8,10},{9,11},{10,... | collective-permute-start | bytes 368648 | tf_op jit(solution)/shard_map/ppermute | solution.py:479
  191.2 2.1 collective-permute-start.20
  193.3 2.9 %collective-permute-done.15.refs_6_ = bf16[15,16,256]{2,1,0:T(8,128)(2,1)S(1)} collective-permute-done((bf16[15,16,256]{2,1,0:T(8,128)(2,1)S(1)}, bf16[15,16,256]{2,1,0:T(8,128)(2,1)S(1)}, u32[]{:S(2)}, u32[]{:S(2)}) %collective-permute-start.15) | collective-permute-done | bytes 122912 | tf_op jit(solution)/shard_map/ppermute | solution.py:479
  196.2 3.2 %collective-permute-start.21 = (bf16[15,16,256]{2,1,0:T(8,128)(2,1)}, bf16[15,16,256]{2,1,0:T(8,128)(2,1)S(1)}, u32[]{:S(2)}, u32[]{:S(2)}) collective-permute-start(bf16[15,16,256]{2,1,0:T(8,128)(2,1)} %get-tuple-element.65), channel_id=1, source_target_pairs={{0,4},{1,5},{2,6},{3,7},{4,0},{5,1},{6,2},{7,3},{8,12},{9,13},{10,... | collective-permute-start | bytes 368648 | tf_op jit(solution)/shard_map/ppermute | solution.py:479
  199.8 4.0 %collective-permute-start.22 = (bf16[15,16,256]{2,1,0:T(8,128)(2,1)}, bf16[15,16,256]{2,1,0:T(8,128)(2,1)S(1)}, u32[]{:S(2)}, u32[]{:S(2)}) collective-permute-start(bf16[15,16,256]{2,1,0:T(8,128)(2,1)} %get-tuple-element.66), channel_id=1, source_target_pairs={{0,5},{1,4},{2,7},{3,6},{4,1},{5,0},{6,3},{7,2},{8,13},{9,12},{10,... | collective-permute-start | bytes 368648 | tf_op jit(solution)/shard_map/ppermute | solution.py:479
  203.8 3.8 %collective-permute-start.23 = (bf16[15,16,256]{2,1,0:T(8,128)(2,1)}, bf16[15,16,256]{2,1,0:T(8,128)(2,1)S(1)}, u32[]{:S(2)}, u32[]{:S(2)}) collective-permute-start(bf16[15,16,256]{2,1,0:T(8,128)(2,1)} %get-tuple-element.67), channel_id=1, source_target_pairs={{0,6},{1,7},{2,4},{3,5},{4,2},{5,3},{6,0},{7,1},{8,14},{9,15},{10,... | collective-permute-start | bytes 368648 | tf_op jit(solution)/shard_map/ppermute | solution.py:479
  207.6 4.7 %collective-permute-start.24 = (bf16[15,16,256]{2,1,0:T(8,128)(2,1)}, bf16[15,16,256]{2,1,0:T(8,128)(2,1)S(1)}, u32[]{:S(2)}, u32[]{:S(2)}) collective-permute-start(bf16[15,16,256]{2,1,0:T(8,128)(2,1)} %get-tuple-element.68), channel_id=1, source_target_pairs={{0,7},{1,6},{2,5},{3,4},{4,3},{5,2},{6,1},{7,0},{8,15},{9,14},{10,... | collective-permute-start | bytes 368648 | tf_op jit(solution)/shard_map/ppermute | solution.py:479
  212.3 2.8 %collective-permute-done.22.refs_13_ = bf16[15,16,256]{2,1,0:T(8,128)(2,1)S(1)} collective-permute-done((bf16[15,16,256]{2,1,0:T(8,128)(2,1)}, bf16[15,16,256]{2,1,0:T(8,128)(2,1)S(1)}, u32[]{:S(2)}, u32[]{:S(2)}) %collective-permute-start.22) | collective-permute-done | bytes 122912 | tf_op jit(solution)/shard_map/ppermute | solution.py:479
  215.1 4.7 %collective-permute-done.23.refs_14_ = bf16[15,16,256]{2,1,0:T(8,128)(2,1)S(1)} collective-permute-done((bf16[15,16,256]{2,1,0:T(8,128)(2,1)}, bf16[15,16,256]{2,1,0:T(8,128)(2,1)S(1)}, u32[]{:S(2)}, u32[]{:S(2)}) %collective-permute-start.23) | collective-permute-done | bytes 122912 | tf_op jit(solution)/shard_map/ppermute | solution.py:479
  221.1 3.0 %shard_map.211 = bf16[15,256,256]{2,1,0:T(8,128)(2,1)} custom-call(s32[1]{0:T(128)S(6)} %xor.7.block_ref, bf16[15,16,256]{2,1,0:T(8,128)(2,1)} %get-tuple-element.53.refs_0_, bf16[15,16,256]{2,1,0:T(8,128)(2,1)} %copy-done.8, bf16[15,16,256]{2,1,0:T(8,128)(2,1)} %copy-done.9, bf16[15,16,256]{2,1,0:T(8,128)(2,1)} %copy-done.10, ...), custom_call_target="tpu_custom_call" | custom-call | bytes 4194304 | tf_op jit(solution)/shard_map/pallas_call | solution.py:333
  (106 shorter events, 12.2 us)
Async XLA Ops:
  10.7 44.1 %all-to-all-start = ((bf16[256,2,640]{2,1,0:T(2,128)(2,1)}), bf16[256,2,640]{2,1,0:T(2,128)(2,1)S(1)}, u32[]{:S(2)}, u32[]{:S(2)}) async-start(bf16[256,2,640]{2,1,0:T(2,128)(2,1)} %reshape.60), calls=%async_computation | async-start | bytes 1310720 | tf_op jit(solution)/shard_map/all_to_all | solution.py:408
  30.9 11.9 %collective-permute-start = (bf16[16,8192]{1,0:T(8,128)(2,1)}, bf16[16,8192]{1,0:T(8,128)(2,1)S(1)}, u32[]{:S(2)}, u32[]{:S(2)}) collective-permute-start(bf16[16,8192]{1,0:T(8,128)(2,1)} %get-tuple-element.38), channel_id=1, source_target_pairs={{0,1},{1,0},{2,3},{3,2},{4,5},{5,4},{6,7},{7,6},{8,9},{9,8},{10,11... | collective-permute-start | bytes 786440 | tf_op jit(solution)/shard_map/ppermute | solution.py:417
  31.7 16.8 %collective-permute-start.1 = (bf16[16,8192]{1,0:T(8,128)(2,1)}, bf16[16,8192]{1,0:T(8,128)(2,1)S(1)}, u32[]{:S(2)}, u32[]{:S(2)}) collective-permute-start(bf16[16,8192]{1,0:T(8,128)(2,1)} %get-tuple-element.39), channel_id=1, source_target_pairs={{0,2},{1,3},{2,0},{3,1},{4,6},{5,7},{6,4},{7,5},{8,10},{9,11},{10,... | collective-permute-start | bytes 786440 | tf_op jit(solution)/shard_map/ppermute | solution.py:417
  32.9 27.4 %collective-permute-start.2 = (bf16[16,8192]{1,0:T(8,128)(2,1)}, bf16[16,8192]{1,0:T(8,128)(2,1)S(1)}, u32[]{:S(2)}, u32[]{:S(2)}) collective-permute-start(bf16[16,8192]{1,0:T(8,128)(2,1)} %get-tuple-element.40), channel_id=1, source_target_pairs={{0,3},{1,2},{2,1},{3,0},{4,7},{5,6},{6,5},{7,4},{8,11},{9,10},{10,... | collective-permute-start | bytes 786440 | tf_op jit(solution)/shard_map/ppermute | solution.py:417
  35.6 31.5 %collective-permute-start.3 = (bf16[16,8192]{1,0:T(8,128)(2,1)}, bf16[16,8192]{1,0:T(8,128)(2,1)S(1)}, u32[]{:S(2)}, u32[]{:S(2)}) collective-permute-start(bf16[16,8192]{1,0:T(8,128)(2,1)} %get-tuple-element.41), channel_id=1, source_target_pairs={{0,4},{1,5},{2,6},{3,7},{4,0},{5,1},{6,2},{7,3},{8,12},{9,13},{10,... | collective-permute-start | bytes 786440 | tf_op jit(solution)/shard_map/ppermute | solution.py:417
  41.1 37.0 %collective-permute-start.4 = (bf16[16,8192]{1,0:T(8,128)(2,1)}, bf16[16,8192]{1,0:T(8,128)(2,1)S(1)}, u32[]{:S(2)}, u32[]{:S(2)}) collective-permute-start(bf16[16,8192]{1,0:T(8,128)(2,1)} %get-tuple-element.42), channel_id=1, source_target_pairs={{0,5},{1,4},{2,7},{3,6},{4,1},{5,0},{6,3},{7,2},{8,13},{9,12},{10,... | collective-permute-start | bytes 786440 | tf_op jit(solution)/shard_map/ppermute | solution.py:417
  42.8 17.4 %copy-start = (bf16[16,8192]{1,0:T(8,128)(2,1)}, bf16[16,8192]{1,0:T(8,128)(2,1)S(1)}, u32[]{:S(2)}) copy-start(bf16[16,8192]{1,0:T(8,128)(2,1)S(1)} %collective-permute-done.refs_1_) | copy-start | bytes 786436
  42.8 42.4 %collective-permute-start.5 = (bf16[16,8192]{1,0:T(8,128)(2,1)}, bf16[16,8192]{1,0:T(8,128)(2,1)S(1)}, u32[]{:S(2)}, u32[]{:S(2)}) collective-permute-start(bf16[16,8192]{1,0:T(8,128)(2,1)} %get-tuple-element.43), channel_id=1, source_target_pairs={{0,6},{1,7},{2,4},{3,5},{4,2},{5,3},{6,0},{7,1},{8,14},{9,15},{10,... | collective-permute-start | bytes 786440 | tf_op jit(solution)/shard_map/ppermute | solution.py:417
  48.5 11.8 %copy-start.1 = (bf16[16,8192]{1,0:T(8,128)(2,1)}, bf16[16,8192]{1,0:T(8,128)(2,1)S(1)}, u32[]{:S(2)}) copy-start(bf16[16,8192]{1,0:T(8,128)(2,1)S(1)} %collective-permute-done.1.refs_2_) | copy-start | bytes 786436
  48.5 41.2 %collective-permute-start.6 = (bf16[16,8192]{1,0:T(8,128)(2,1)}, bf16[16,8192]{1,0:T(8,128)(2,1)}, u32[]{:S(2)}, u32[]{:S(2)}) collective-permute-start(bf16[16,8192]{1,0:T(8,128)(2,1)} %get-tuple-element.44), channel_id=1, source_target_pairs={{0,7},{1,6},{2,5},{3,4},{4,3},{5,2},{6,1},{7,0},{8,15},{9,14},{10,... | collective-permute-start | bytes 786440 | tf_op jit(solution)/shard_map/ppermute | solution.py:417
  60.3 29.5 %copy-start.2 = (bf16[16,8192]{1,0:T(8,128)(2,1)}, bf16[16,8192]{1,0:T(8,128)(2,1)S(1)}, u32[]{:S(2)}) copy-start(bf16[16,8192]{1,0:T(8,128)(2,1)S(1)} %collective-permute-done.2.refs_3_) | copy-start | bytes 786436
  67.1 22.6 %copy-start.3 = (bf16[16,8192]{1,0:T(8,128)(2,1)}, bf16[16,8192]{1,0:T(8,128)(2,1)S(1)}, u32[]{:S(2)}) copy-start(bf16[16,8192]{1,0:T(8,128)(2,1)S(1)} %collective-permute-done.3.refs_4_) | copy-start | bytes 786436
  89.8 18.8 %copy-start.22 = (bf16[256,120]{0,1:T(8,128)(2,1)S(1)}, bf16[256,120]{0,1:T(8,128)(2,1)}, u32[]{:S(2)}) copy-start(bf16[256,120]{0,1:T(8,128)(2,1)} %param.21) | copy-start | bytes 184324
  89.8 19.6 %copy-start.23 = (bf16[120,256]{1,0:T(8,128)(2,1)S(1)}, bf16[120,256]{1,0:T(8,128)(2,1)}, u32[]{:S(2)}) copy-start(bf16[120,256]{1,0:T(8,128)(2,1)} %param.22) | copy-start | bytes 184324
  92.8 17.2 %copy-start.7 = (bf16[3,120,256]{2,1,0:T(8,128)(2,1)S(1)}, bf16[3,120,256]{2,1,0:T(8,128)(2,1)}, u32[]{:S(2)}) copy-start(bf16[3,120,256]{2,1,0:T(8,128)(2,1)} %param.23) | copy-start | bytes 552964
  92.8 18.0 %copy-start.24 = (f32[120]{0:T(128)S(1)}, f32[120]{0:T(128)}, u32[]{:S(2)}) copy-start(f32[120]{0:T(128)} %param.24) | copy-start | bytes 1444
  92.8 45.5 %collective-permute-start.7 = (bf16[128,8192]{1,0:T(8,128)(2,1)}, bf16[128,8192]{1,0:T(8,128)(2,1)S(1)}, u32[]{:S(2)}, u32[]{:S(2)}) collective-permute-start(bf16[128,8192]{1,0:T(8,128)(2,1)} %shard_map.206.center_ref.yhigh_ref.ylow_ref), channel_id=1, source_target_pairs={{0,8},{1,9},{2,10},{3,11},{4,12},{5,13},{6,14},{7,15},{8,16},{9,17... | collective-permute-start | bytes 6291464 | tf_op jit(solution)/shard_map/ppermute | solution.py:435
  92.8 45.5 %collective-permute-start.8 = (bf16[128,8192]{1,0:T(8,128)(2,1)}, bf16[128,8192]{1,0:T(8,128)(2,1)}, u32[]{:S(2)}, u32[]{:S(2)}) collective-permute-start(bf16[128,8192]{1,0:T(8,128)(2,1)} %shard_map.206.center_ref.yhigh_ref.ylow_ref), channel_id=1, source_target_pairs={{0,252},{1,253},{2,254},{3,255},{4,248},{5,249},{6,250},{7,251},{8... | collective-permute-start | bytes 6291464 | tf_op jit(solution)/shard_map/ppermute | solution.py:436
  96.1 37.6 %all-to-all-start.1 = ((bf16[256,2,256]{2,1,0:T(2,128)(2,1)}), bf16[256,2,256]{2,1,0:T(2,128)(2,1)S(1)}, u32[]{:S(2)}, u32[]{:S(2)}) async-start(bf16[256,2,256]{2,1,0:T(2,128)(2,1)} %reshape.62), calls=%async_computation.1 | async-start | bytes 524288 | tf_op jit(solution)/shard_map/all_to_all | solution.py:432
  112.5 25.9 %collective-permute-start.9 = (bf16[128,256]{1,0:T(8,128)(2,1)S(1)}, bf16[128,256]{1,0:T(8,128)(2,1)S(1)}, u32[]{:S(2)}, u32[]{:S(2)}) collective-permute-start(bf16[128,256]{1,0:T(8,128)(2,1)S(1)} %get-tuple-element.79), channel_id=1, source_target_pairs={{0,1},{1,2},{2,3},{3,4},{4,5},{5,6},{6,7},{7,0},{8,9},{9,10},{10,1... | collective-permute-start | bytes 196616 | tf_op jit(solution)/shard_map/ppermute | solution.py:437
  120.5 35.3 %collective-permute-start.17 = (bf16[128,256]{1,0:T(8,128)(2,1)S(1)}, bf16[128,256]{1,0:T(8,128)(2,1)S(1)}, u32[]{:S(2)}, u32[]{:S(2)}) collective-permute-start(bf16[128,256]{1,0:T(8,128)(2,1)S(1)} %get-tuple-element.78), channel_id=1, source_target_pairs={{0,7},{1,0},{2,1},{3,2},{4,3},{5,4},{6,5},{7,6},{8,15},{9,8},{10,9... | collective-permute-start | bytes 196616 | tf_op jit(solution)/shard_map/ppermute | solution.py:438
  148.4 30.2 %collective-permute-start.10 = (bf16[15,16,256]{2,1,0:T(8,128)(2,1)}, bf16[15,16,256]{2,1,0:T(8,128)(2,1)S(1)}, u32[]{:S(2)}, u32[]{:S(2)}) collective-permute-start(bf16[15,16,256]{2,1,0:T(8,128)(2,1)} %get-tuple-element.54), channel_id=1, source_target_pairs={{0,1},{1,0},{2,3},{3,2},{4,5},{5,4},{6,7},{7,6},{8,9},{9,8},{10,11... | collective-permute-start | bytes 368648 | tf_op jit(solution)/shard_map/ppermute | solution.py:479
  148.8 34.7 %collective-permute-start.11 = (bf16[15,16,256]{2,1,0:T(8,128)(2,1)}, bf16[15,16,256]{2,1,0:T(8,128)(2,1)S(1)}, u32[]{:S(2)}, u32[]{:S(2)}) collective-permute-start(bf16[15,16,256]{2,1,0:T(8,128)(2,1)} %get-tuple-element.55), channel_id=1, source_target_pairs={{0,2},{1,3},{2,0},{3,1},{4,6},{5,7},{6,4},{7,5},{8,10},{9,11},{10,... | collective-permute-start | bytes 368648 | tf_op jit(solution)/shard_map/ppermute | solution.py:479
  150.7 37.9 %collective-permute-start.12 = (bf16[15,16,256]{2,1,0:T(8,128)(2,1)}, bf16[15,16,256]{2,1,0:T(8,128)(2,1)S(1)}, u32[]{:S(2)}, u32[]{:S(2)}) collective-permute-start(bf16[15,16,256]{2,1,0:T(8,128)(2,1)} %get-tuple-element.56), channel_id=1, source_target_pairs={{0,3},{1,2},{2,1},{3,0},{4,7},{5,6},{6,5},{7,4},{8,11},{9,10},{10,... | collective-permute-start | bytes 368648 | tf_op jit(solution)/shard_map/ppermute | solution.py:479
  153.1 23.5 %copy-start.28 = (bf16[15,16,256]{2,1,0:T(8,128)(2,1)S(1)}, bf16[15,16,256]{2,1,0:T(8,128)(2,1)}, u32[]{:S(2)}) copy-start(bf16[15,16,256]{2,1,0:T(8,128)(2,1)} %get-tuple-element.58) | copy-start | bytes 368644
  153.1 25.6 %copy-start.27 = (bf16[15,16,256]{2,1,0:T(8,128)(2,1)S(1)}, bf16[15,16,256]{2,1,0:T(8,128)(2,1)}, u32[]{:S(2)}) copy-start(bf16[15,16,256]{2,1,0:T(8,128)(2,1)} %get-tuple-element.59) | copy-start | bytes 368644
  153.1 30.4 %copy-start.26 = (bf16[15,16,256]{2,1,0:T(8,128)(2,1)S(1)}, bf16[15,16,256]{2,1,0:T(8,128)(2,1)}, u32[]{:S(2)}) copy-start(bf16[15,16,256]{2,1,0:T(8,128)(2,1)} %get-tuple-element.60) | copy-start | bytes 368644
  153.1 35.5 %collective-permute-start.13 = (bf16[15,16,256]{2,1,0:T(8,128)(2,1)}, bf16[15,16,256]{2,1,0:T(8,128)(2,1)S(1)}, u32[]{:S(2)}, u32[]{:S(2)}) collective-permute-start(bf16[15,16,256]{2,1,0:T(8,128)(2,1)} %get-tuple-element.57), channel_id=1, source_target_pairs={{0,4},{1,5},{2,6},{3,7},{4,0},{5,1},{6,2},{7,3},{8,12},{9,13},{10,... | collective-permute-start | bytes 368648 | tf_op jit(solution)/shard_map/ppermute | solution.py:479
  165.2 11.4 %collective-permute-start.25 = (f32[3,32,256]{2,1,0:T(8,128)S(1)}, f32[3,32,256]{2,1,0:T(8,128)S(1)}, u32[]{:S(2)}, u32[]{:S(2)}) collective-permute-start(f32[3,32,256]{2,1,0:T(8,128)S(1)} %slice.26), channel_id=1, source_target_pairs={{0,0},{1,1},{2,2},{3,3},{4,4},{5,5},{6,6},{7,7},{8,8},{9,9},{10,10... | collective-permute-start | bytes 294920 | tf_op jit(solution)/shard_map/ppermute | solution.py:482
  176.6 14.6 %collective-permute-start.14 = (bf16[15,16,256]{2,1,0:T(8,128)(2,1)S(1)}, bf16[15,16,256]{2,1,0:T(8,128)(2,1)S(1)}, u32[]{:S(2)}, u32[]{:S(2)}) collective-permute-start(bf16[15,16,256]{2,1,0:T(8,128)(2,1)S(1)} %copy-done.28), channel_id=1, source_target_pairs={{0,5},{1,4},{2,7},{3,6},{4,1},{5,0},{6,3},{7,2},{8,13},{9,12},{10,... | collective-permute-start | bytes 368648 | tf_op jit(solution)/shard_map/ppermute | solution.py:479
  178.6 41.7 %copy-start.8 = (bf16[15,16,256]{2,1,0:T(8,128)(2,1)}, bf16[15,16,256]{2,1,0:T(8,128)(2,1)S(1)}, u32[]{:S(2)}) copy-start(bf16[15,16,256]{2,1,0:T(8,128)(2,1)S(1)} %collective-permute-done.10.refs_1_) | copy-start | bytes 368644
  178.6 17.5 %collective-permute-start.15 = (bf16[15,16,256]{2,1,0:T(8,128)(2,1)S(1)}, bf16[15,16,256]{2,1,0:T(8,128)(2,1)S(1)}, u32[]{:S(2)}, u32[]{:S(2)}) collective-permute-start(bf16[15,16,256]{2,1,0:T(8,128)(2,1)S(1)} %copy-done.27), channel_id=1, source_target_pairs={{0,6},{1,7},{2,4},{3,5},{4,2},{5,3},{6,0},{7,1},{8,14},{9,15},{10,... | collective-permute-start | bytes 368648 | tf_op jit(solution)/shard_map/ppermute | solution.py:479
  183.5 36.8 %copy-start.9 = (bf16[15,16,256]{2,1,0:T(8,128)(2,1)}, bf16[15,16,256]{2,1,0:T(8,128)(2,1)S(1)}, u32[]{:S(2)}) copy-start(bf16[15,16,256]{2,1,0:T(8,128)(2,1)S(1)} %collective-permute-done.11.refs_2_) | copy-start | bytes 368644
  183.5 16.2 %collective-permute-start.16 = (bf16[15,16,256]{2,1,0:T(8,128)(2,1)S(1)}, bf16[15,16,256]{2,1,0:T(8,128)(2,1)S(1)}, u32[]{:S(2)}, u32[]{:S(2)}) collective-permute-start(bf16[15,16,256]{2,1,0:T(8,128)(2,1)S(1)} %copy-done.26), channel_id=1, source_target_pairs={{0,7},{1,6},{2,5},{3,4},{4,3},{5,2},{6,1},{7,0},{8,15},{9,14},{10,... | collective-permute-start | bytes 368648 | tf_op jit(solution)/shard_map/ppermute | solution.py:479
  188.6 31.8 %copy-start.10 = (bf16[15,16,256]{2,1,0:T(8,128)(2,1)}, bf16[15,16,256]{2,1,0:T(8,128)(2,1)S(1)}, u32[]{:S(2)}) copy-start(bf16[15,16,256]{2,1,0:T(8,128)(2,1)S(1)} %collective-permute-done.12.refs_3_) | copy-start | bytes 368644
  188.6 15.2 %collective-permute-start.18 = (bf16[15,16,256]{2,1,0:T(8,128)(2,1)}, bf16[15,16,256]{2,1,0:T(8,128)(2,1)S(1)}, u32[]{:S(2)}, u32[]{:S(2)}) collective-permute-start(bf16[15,16,256]{2,1,0:T(8,128)(2,1)} %get-tuple-element.62), channel_id=1, source_target_pairs={{0,1},{1,0},{2,3},{3,2},{4,5},{5,4},{6,7},{7,6},{8,9},{9,8},{10,11... | collective-permute-start | bytes 368648 | tf_op jit(solution)/shard_map/ppermute | solution.py:479
  188.6 31.7 %copy-start.11 = (bf16[15,16,256]{2,1,0:T(8,128)(2,1)}, bf16[15,16,256]{2,1,0:T(8,128)(2,1)S(1)}, u32[]{:S(2)}) copy-start(bf16[15,16,256]{2,1,0:T(8,128)(2,1)S(1)} %collective-permute-done.13.refs_4_) | copy-start | bytes 368644
  188.6 19.0 %collective-permute-start.19 = (bf16[15,16,256]{2,1,0:T(8,128)(2,1)}, bf16[15,16,256]{2,1,0:T(8,128)(2,1)S(1)}, u32[]{:S(2)}, u32[]{:S(2)}) collective-permute-start(bf16[15,16,256]{2,1,0:T(8,128)(2,1)} %get-tuple-element.63), channel_id=1, source_target_pairs={{0,2},{1,3},{2,0},{3,1},{4,6},{5,7},{6,4},{7,5},{8,10},{9,11},{10,... | collective-permute-start | bytes 368648 | tf_op jit(solution)/shard_map/ppermute | solution.py:479
  191.2 29.2 %copy-start.12 = (bf16[15,16,256]{2,1,0:T(8,128)(2,1)}, bf16[15,16,256]{2,1,0:T(8,128)(2,1)S(1)}, u32[]{:S(2)}) copy-start(bf16[15,16,256]{2,1,0:T(8,128)(2,1)S(1)} %collective-permute-done.14.refs_5_) | copy-start | bytes 368644
  191.2 21.1 %collective-permute-start.20 = (bf16[15,16,256]{2,1,0:T(8,128)(2,1)}, bf16[15,16,256]{2,1,0:T(8,128)(2,1)S(1)}, u32[]{:S(2)}, u32[]{:S(2)}) collective-permute-start(bf16[15,16,256]{2,1,0:T(8,128)(2,1)} %get-tuple-element.64), channel_id=1, source_target_pairs={{0,3},{1,2},{2,1},{3,0},{4,7},{5,6},{6,5},{7,4},{8,11},{9,10},{10,... | collective-permute-start | bytes 368648 | tf_op jit(solution)/shard_map/ppermute | solution.py:479
  196.2 24.2 %copy-start.13 = (bf16[15,16,256]{2,1,0:T(8,128)(2,1)}, bf16[15,16,256]{2,1,0:T(8,128)(2,1)S(1)}, u32[]{:S(2)}) copy-start(bf16[15,16,256]{2,1,0:T(8,128)(2,1)S(1)} %collective-permute-done.15.refs_6_) | copy-start | bytes 368644
  196.2 16.1 %collective-permute-start.21 = (bf16[15,16,256]{2,1,0:T(8,128)(2,1)}, bf16[15,16,256]{2,1,0:T(8,128)(2,1)S(1)}, u32[]{:S(2)}, u32[]{:S(2)}) collective-permute-start(bf16[15,16,256]{2,1,0:T(8,128)(2,1)} %get-tuple-element.65), channel_id=1, source_target_pairs={{0,4},{1,5},{2,6},{3,7},{4,0},{5,1},{6,2},{7,3},{8,12},{9,13},{10,... | collective-permute-start | bytes 368648 | tf_op jit(solution)/shard_map/ppermute | solution.py:479
  199.8 20.6 %copy-start.14 = (bf16[15,16,256]{2,1,0:T(8,128)(2,1)}, bf16[15,16,256]{2,1,0:T(8,128)(2,1)S(1)}, u32[]{:S(2)}) copy-start(bf16[15,16,256]{2,1,0:T(8,128)(2,1)S(1)} %collective-permute-done.16.refs_7_) | copy-start | bytes 368644
  199.8 15.4 %collective-permute-start.22 = (bf16[15,16,256]{2,1,0:T(8,128)(2,1)}, bf16[15,16,256]{2,1,0:T(8,128)(2,1)S(1)}, u32[]{:S(2)}, u32[]{:S(2)}) collective-permute-start(bf16[15,16,256]{2,1,0:T(8,128)(2,1)} %get-tuple-element.66), channel_id=1, source_target_pairs={{0,5},{1,4},{2,7},{3,6},{4,1},{5,0},{6,3},{7,2},{8,13},{9,12},{10,... | collective-permute-start | bytes 368648 | tf_op jit(solution)/shard_map/ppermute | solution.py:479
  203.8 16.6 %copy-start.15 = (bf16[15,16,256]{2,1,0:T(8,128)(2,1)}, bf16[15,16,256]{2,1,0:T(8,128)(2,1)S(1)}, u32[]{:S(2)}) copy-start(bf16[15,16,256]{2,1,0:T(8,128)(2,1)S(1)} %collective-permute-done.18.refs_9_) | copy-start | bytes 368644
  203.8 16.0 %collective-permute-start.23 = (bf16[15,16,256]{2,1,0:T(8,128)(2,1)}, bf16[15,16,256]{2,1,0:T(8,128)(2,1)S(1)}, u32[]{:S(2)}, u32[]{:S(2)}) collective-permute-start(bf16[15,16,256]{2,1,0:T(8,128)(2,1)} %get-tuple-element.67), channel_id=1, source_target_pairs={{0,6},{1,7},{2,4},{3,5},{4,2},{5,3},{6,0},{7,1},{8,14},{9,15},{10,... | collective-permute-start | bytes 368648 | tf_op jit(solution)/shard_map/ppermute | solution.py:479
  207.6 12.8 %copy-start.16 = (bf16[15,16,256]{2,1,0:T(8,128)(2,1)}, bf16[15,16,256]{2,1,0:T(8,128)(2,1)S(1)}, u32[]{:S(2)}) copy-start(bf16[15,16,256]{2,1,0:T(8,128)(2,1)S(1)} %collective-permute-done.19.refs_10_) | copy-start | bytes 368644
  207.6 12.7 %collective-permute-start.24 = (bf16[15,16,256]{2,1,0:T(8,128)(2,1)}, bf16[15,16,256]{2,1,0:T(8,128)(2,1)S(1)}, u32[]{:S(2)}, u32[]{:S(2)}) collective-permute-start(bf16[15,16,256]{2,1,0:T(8,128)(2,1)} %get-tuple-element.68), channel_id=1, source_target_pairs={{0,7},{1,6},{2,5},{3,4},{4,3},{5,2},{6,1},{7,0},{8,15},{9,14},{10,... | collective-permute-start | bytes 368648 | tf_op jit(solution)/shard_map/ppermute | solution.py:479
  (11 other events, 46.3 us)

commit v2 on v1

--- a/solution.py
+++ b/solution.py
@@ -22,7 +22,8 @@
 OWN = COEFS // GROUPS
 PAD = 16
 ROWS = NY // GROUPS
-CELLS = ROWS * NX
+EDGED = ROWS + 2
+CELLS = EDGED * NX
 HALF = NX // 2
 ALL_PAD = GROUPS * PAD
 LANES = 128
@@ -30,7 +31,7 @@
 FLIP = GROUPS // 2
 PARTS = 2
 CHUNK = ROWS // PARTS
-BLOCKS = 12
+BLOCKS = 13
 bf16, f32 = jnp.bfloat16, jnp.float32
 VMEM = pl.BlockSpec(memory_space=pltpu.VMEM)
 SMEM = pl.BlockSpec(memory_space=pltpu.SMEM)
@@ -107,19 +108,28 @@
 
 
 def regroup_kernel(block_ref, coef_ref, *refs):
-    outs, stages = refs[:GROUPS], refs[GROUPS:]
+    near, far, stages = refs[:FLIP], refs[FLIP], refs[FLIP + 1 :]
     block = block_ref[0]
+    height = ROWS + 2 * PAD
     for stage in stages:
-        stage[pl.ds(OWN * ROWS, ROWS), :] = jnp.zeros((ROWS, LANES), f32)
+        stage[pl.ds(OWN * height, height), :] = jnp.zeros((height, LANES), f32)
     for j in range(GROUPS):
-        first = pl.multiple_of((block ^ j) * ROWS, ROWS)
-        rows = coef_ref[:, pl.ds(first, ROWS), :].astype(f32)
-        rows = rows.reshape(OWN * ROWS, NX)
+        first = (block ^ j) * ROWS
+        for start, size, at in ((NY - PAD, PAD, 0), (0, ROWS, PAD), (ROWS, PAD, PAD + ROWS)):
+            rows = coef_ref[:, pl.ds(pl.multiple_of((first + start) % NY, PAD), size), :].astype(f32)
+            for side, stage in enumerate(stages):
+                for c in range(OWN):
+                    stage[c * height + at : c * height + at + size, :] = rows[
+                        c, :, side * LANES : (side + 1) * LANES
+                    ]
         for side, stage in enumerate(stages):
-            stage[pl.ds(0, OWN * ROWS), :] = rows[:, side * LANES : (side + 1) * LANES]
-            for r in range(ROWS):
+            for r in range(EDGED):
                 lane = r * NX + side * LANES
-                outs[j][:, lane : lane + LANES] = stage[pl.ds(r, PAD, stride=ROWS), :].astype(bf16)
+                rows = stage[pl.ds(PAD - 1 + r, PAD, stride=height), :]
+                if j < FLIP:
+                    near[j][:, lane : lane + LANES] = rows.astype(bf16)
+                else:
+                    far[(j - FLIP) * PAD : (j - FLIP + 1) * PAD, lane : lane + LANES] = rows.astype(bf16)
 
 
 def stress_kernel(table_ref, coef_ref, high_ref, low_ref, out_ref, stress_high, stress_low):
@@ -252,11 +262,12 @@
     def strain(i, j):
         return same * plain(i, j) + swap * plain(j, i)
 
-    left = [-0.5 * swim_speed * proj * p[j] for j in range(3)] + [-0.5 * proj]
+    left = [-0.5 * swim_speed * proj * p[j] for j in range(2)] + [-0.5 * proj]
     trace = strain(2, 2)
     left += [strain(0, 0) - trace, strain(1, 0), strain(2, 0)]
     left += [strain(0, 1), strain(1, 1) - trace, strain(2, 1)]
     left += [strain(0, 2), strain(1, 2)]
+    left += [-0.5 * swim_speed * proj * p[2], -0.5 * proj]
     for n, value in enumerate(left):
         high, low = halves(value)
         out_ref[:, n * ALL_PAD : (n + 1) * ALL_PAD] = (dot(high, synth) + dot(low, synth)).astype(bf16)
@@ -269,34 +280,24 @@
         out_ref[pl.ds(pl.multiple_of((group ^ j) * PAD, PAD), PAD), :] = refs[j][...]
 
 
-def rate_kernel(
-    group_ref, center_ref, zlow_ref, zhigh_ref, ylow_ref, yhigh_ref, flow_ref, weight_ref, damp_ref,
-    *refs,
-):
-    outs, (padded, operands, locals_, *stages) = refs[:GROUPS], refs[GROUPS:]
-    group = group_ref[0]
-    cells = CHUNK * NX
-    padded[:, :NX] = ylow_ref[...]
-    padded[:, NX : NX + cells] = center_ref[...]
-    padded[:, NX + cells :] = yhigh_ref[...]
+def inner_kernel(center_ref, flow_ref, weight_ref, damp_ref, out_ref, operands, locals_):
+    blocks = BLOCKS - 2
 
     def build(r, operand, local_terms):
         here = pl.multiple_of(r * NX, NX)
         flow = [flow_ref[f, pl.ds(r, 1), :] for f in range(11)]
         for g in range(GROUPS):
             rows = slice(g * PAD, (g + 1) * PAD)
-            value = padded[rows, pl.ds(here + NX, NX)].astype(f32)
-            y_low = padded[rows, pl.ds(here, NX)].astype(f32)
-            y_high = padded[rows, pl.ds(here + 2 * NX, NX)].astype(f32)
-            z_low = zlow_ref[rows, pl.ds(here, NX)].astype(f32)
-            z_high = zhigh_ref[rows, pl.ds(here, NX)].astype(f32)
+            value = center_ref[rows, pl.ds(here + NX, NX)].astype(f32)
+            y_low = center_ref[rows, pl.ds(here, NX)].astype(f32)
+            y_high = center_ref[rows, pl.ds(here + 2 * NX, NX)].astype(f32)
             x_low = pltpu.roll(value, 1, 1)
             x_high = pltpu.roll(value, NX - 1, 1)
-            diffs = (x_high - x_low, y_high - y_low, z_high - z_low)
-            drift = flow[0] * diffs[0] + flow[1] * diffs[1] + flow[2] * diffs[2]
-            lap = x_high + x_low + y_high + y_low + z_high + z_low - 6.0 * value
+            diff_x, diff_y = x_high - x_low, y_high - y_low
+            lap = x_high + x_low + y_high + y_low - 6.0 * value
             local_terms[rows, :] = transl_diff * lap - damp_ref[rows, :] * value
-            terms = list(diffs) + [drift] + [flow[3 + n] * value for n in range(8)]
+            terms = [diff_x, diff_y, flow[0] * diff_x + flow[1] * diff_y]
+            terms += [flow[3 + n] * value for n in range(8)]
             for n, term in enumerate(terms):
                 operand[n * ALL_PAD + g * PAD : n * ALL_PAD + (g + 1) * PAD, :] = term.astype(bf16)
 
@@ -304,7 +305,35 @@
         for n in range(2):
             build(2 * i + n, operands.at[n], locals_.at[n])
         for n in range(2):
-            result = dot(weight_ref[...], operands[n]) + locals_[n]
+            where = pl.ds(pl.multiple_of((2 * i + n) * NX, NX), NX)
+            out_ref[:, where] = locals_[n] + dot(weight_ref[:, : blocks * ALL_PAD], operands[n])
+        return carry
+
+    lax.fori_loop(0, ROWS // 2, rows, 0)
+
+
+def rate_kernel(group_ref, inner_ref, zlow_ref, zhigh_ref, flow_ref, weight_ref, *refs):
+    outs, (operands, locals_, *stages) = refs[:GROUPS], refs[GROUPS:]
+    group = group_ref[0]
+    skip = (BLOCKS - 2) * ALL_PAD
+
+    def build(r, operand, local_terms):
+        here = pl.multiple_of(r * NX, NX)
+        drift = flow_ref[2, pl.ds(r, 1), :]
+        for g in range(GROUPS):
+            rows = slice(g * PAD, (g + 1) * PAD)
+            z_low = zlow_ref[rows, pl.ds(here, NX)].astype(f32)
+            z_high = zhigh_ref[rows, pl.ds(here, NX)].astype(f32)
+            diff_z = z_high - z_low
+            local_terms[rows, :] = transl_diff * (z_high + z_low) + inner_ref[rows, pl.ds(here, NX)]
+            operand[rows, :] = diff_z.astype(bf16)
+            operand[ALL_PAD + g * PAD : ALL_PAD + (g + 1) * PAD, :] = (drift * diff_z).astype(bf16)
+
+    def rows(i, carry):
+        for n in range(2):
+            build(2 * i + n, operands.at[n], locals_.at[n])
+        for n in range(2):
+            result = dot(weight_ref[:, skip:], operands[n]) + locals_[n]
             for side, stage in enumerate(stages):
                 stage[pl.ds(2 * i + n, ALL_PAD, stride=CHUNK), :] = result[
                     :, side * LANES : (side + 1) * LANES
@@ -373,6 +402,14 @@
     return jnp.concatenate([table[0:2] - table[2:3], table[3:6]])
 
 
+def partner(j):
+    return [(i, i ^ j) for i in range(GROUPS)]
+
+
+def exchanged(chunks):
+    return [chunks[0]] + [lax.ppermute(c, "harm", partner(j + 1)) for j, c in enumerate(chunks[1:])]
+
+
 def odd(plane):
     return (plane // RUN) % 2
 
@@ -409,12 +446,12 @@
 
     later, _ = lax.optimization_barrier((own, sent))
     chunks = call(
-        regroup_kernel, [shape(PAD, CELLS)] * GROUPS, [block_arg, later],
-        [pltpu.VMEM((PAD * ROWS, LANES), f32)] * 2, 1, 0, 4 << 20,
+        regroup_kernel, [shape(PAD, CELLS)] * FLIP + [shape(FLIP * PAD, CELLS)], [block_arg, later],
+        [pltpu.VMEM((PAD * (ROWS + 2 * PAD), LANES), f32)] * 2, 1, 0, 4 << 20,
     )
-    arrived = [chunks[0]]
-    for j in range(1, GROUPS):
-        arrived.append(lax.ppermute(chunks[j], "harm", [(i, i ^ j) for i in range(GROUPS)]))
+    crossed = lax.ppermute(chunks[FLIP], "harm", partner(FLIP))
+    arrived = exchanged(chunks[:FLIP])
+    arrived += exchanged([crossed[m * PAD : (m + 1) * PAD] for m in range(FLIP)])
 
     wave = (position % HALF).astype(f32) * (2.0 * math.pi / NX)
     half = (position // HALF).astype(jnp.int32)
@@ -430,12 +467,10 @@
         (), 2, 1 << 30, 3 << 20,
     )
     mixed = lax.all_to_all(sent, everyone, 0, 0, tiled=True)
-    arrived, _ = lax.optimization_barrier((arrived, sent))
+    arrived, _ = lax.optimization_barrier((arrived, mixed))
     center = call(assemble_kernel, shape(ALL_PAD, CELLS), [group_arg, *arrived], (), 1, 0, 4 << 20)
     z_low = lax.ppermute(center, both, pairs(lambda s, b: ((s + 1) % SPACES, b)))
     z_high = lax.ppermute(center, both, pairs(lambda s, b: ((s - 1) % SPACES, b)))
-    y_low = lax.ppermute(center[:, -NX:], both, pairs(lambda s, b: (s, (b + 1) % GROUPS)))
-    y_high = lax.ppermute(center[:, :NX], both, pairs(lambda s, b: (s, (b - 1) % GROUPS)))
 
     weights = call(
         weights_kernel, shape(ALL_PAD, BLOCKS * ALL_PAD),
@@ -446,40 +481,38 @@
         (), 0, 1 << 28, 1 << 20,
     )
     flow = call(fields_kernel, shape(11, ROWS, NX, dtype=f32), [mixed, *split_table(back_x)], (), 0, 1 << 29, 2 << 20)
+    swap = pairs(lambda s, b: (s, b ^ (FLIP * odd(s))))
+    velocity = lax.ppermute(flow[0:3], both, swap)
+    flow, velocity = lax.optimization_barrier((flow, velocity))
+
     damp = pad_groups(damping, 0)[:, None]
-    returned, parts = [], []
+    inner = call(
+        inner_kernel, shape(ALL_PAD, ROWS * NX, dtype=f32), [center, flow, weights, damp],
+        [pltpu.VMEM((2, (BLOCKS - 2) * ALL_PAD, NX), bf16), pltpu.VMEM((2, ALL_PAD, NX), f32)],
+        0, 6 << 30, 7 << 20,
+    )
+    returned = []
     for part in range(PARTS):
         here = pl.BlockSpec((ALL_PAD, CHUNK * NX), lambda i, part=part: (0, part))
-        first, last = part * CHUNK, (part + 1) * CHUNK
-
-        def edge(row):
-            return pl.BlockSpec((ALL_PAD, NX), lambda i: (0, row))
-
-        low = (y_low, VMEM) if first == 0 else (center, edge(first - 1))
-        high = (y_high, VMEM) if last == ROWS else (center, edge(last))
+        beyond = pl.BlockSpec(
+            (pl.Element(ALL_PAD), pl.Element(CHUNK * NX)), lambda i, part=part: (0, (part * CHUNK + 1) * NX)
+        )
         rates = call(
             rate_kernel, [shape(OWN, CHUNK, NX)] * GROUPS,
-            [group_arg, center, z_low, z_high, low[0], high[0], flow, weights, damp],
+            [group_arg, inner, z_low, z_high, flow, weights],
             [
-                pltpu.VMEM((ALL_PAD, (CHUNK + 2) * NX), bf16),
-                pltpu.VMEM((2, BLOCKS * ALL_PAD, NX), bf16),
+                pltpu.VMEM((2, 2 * ALL_PAD, NX), bf16),
                 pltpu.VMEM((2, ALL_PAD, NX), f32),
                 pltpu.VMEM((ALL_PAD * CHUNK, LANES), f32),
                 pltpu.VMEM((ALL_PAD * CHUNK, LANES), f32),
             ],
-            1, 7 << 29, 9 << 19,
+            1, 1 << 29, 9 << 19,
             [
-                SMEM, here, here, here, low[1], high[1],
-                pl.BlockSpec((11, CHUNK, NX), lambda i, part=part: (0, part, 0)), VMEM, VMEM,
+                SMEM, here, beyond, beyond,
+                pl.BlockSpec((11, CHUNK, NX), lambda i, part=part: (0, part, 0)), VMEM,
             ],
         )
-        parts.append(rates[0])
-        returned.append(rates[0])
-        for j in range(1, GROUPS):
-            returned.append(lax.ppermute(rates[j], "harm", [(i, i ^ j) for i in range(GROUPS)]))
-    swap = pairs(lambda s, b: (s, b ^ (FLIP * odd(s))))
-    late, _ = lax.optimization_barrier((flow[0:3], parts))
-    velocity = lax.ppermute(late, both, swap)
+        returned += exchanged(rates)
     rate = call(place_kernel, shape(OWN, NY, NX), [block_arg, *returned], (), 1, 0, 4 << 20)
     return (rate.reshape(OWN, 1, NY, NX), velocity.reshape(3, 1, ROWS, NX))
 

time: 227 us -> 249 us (1.097)
  starting transfers between devices: 101 us -> 130 us
  waiting for transfers between devices: 62.1 us -> 46.4 us
  Pallas kernels: 43.4 us -> 50.3 us
    all_to_all x1, starting transfers between devices: 12.4 us -> 54.9 us  [local(): mixed = lax.all_to_all(sent, everyone, 0, 0, tiled=True)]
    ppermute x24 -> x22, starting transfers between devices: 72.5 us -> 59.1 us  [the longest x20 47 us: exchanged(): lax.ppermute(c, 'harm', partner(j + 1))]
    ppermute x24 -> x22, waiting for transfers between devices: 48.9 us -> 35.6 us  [the longest x1 18 us: local(): velocity = lax.ppermute(flow[0:3], both, swap)]
    pallas_call x9 -> x10, Pallas kernels: 43.4 us -> 50.3 us  [call(): pl.pallas_call(kernel, out_shape=out_shape, grid=(1,) if specs else (), i...]
    all_to_all x1, waiting for transfers between devices: 13.2 us -> 6.44 us  [local(): mixed = lax.all_to_all(sent, everyone, 0, 0, tiled=True)]
    all_to_all x1, waiting for transfers between devices: 0.01 us -> 4.36 us  [local(): columns = lax.all_to_all(sent, everyone, 0, 0, tiled=True)]
    unnamed x69 -> x57, local copies, waits for them, and re-layouts: 7.52 us -> 7.58 us
  transfers between devices with their start and end apart: 28 -> 26, of which waited for: 13 -> 7; matrix products, arithmetic and copies ran while one was open for 4% -> 4% of each run, Pallas kernels for 14% -> 14%
where the time goes in v2:
time: 249 us; the launch traced here: 246 us
  starting transfers between devices  130 us (52%)
  Pallas kernels  50.3 us (20%)
  waiting for transfers between devices  46.4 us (19%)
  local copies, waits for them, and re-layouts  13 us (5%)
  other arithmetic  4.6 us (2%)
    all_to_all x1, starting transfers between devices, local(): mixed = lax.all_to_all(sent, everyone, 0, 0, tiled=True)  54.9 us
    pallas_call x10, Pallas kernels, call(): pl.pallas_call(kernel, out_shape=out_shape, grid=(1,) if specs else (), i...  50.3 us
    ppermute x20, starting transfers between devices, exchanged(): lax.ppermute(c, 'harm', partner(j + 1))  47 us
    ppermute x1, waiting for transfers between devices, local(): velocity = lax.ppermute(flow[0:3], both, swap)  18 us
    ppermute x20, waiting for transfers between devices, exchanged(): lax.ppermute(c, 'harm', partner(j + 1))  17.6 us
    all_to_all x1, starting transfers between devices, local(): columns = lax.all_to_all(sent, everyone, 0, 0, tiled=True)  14.2 us
    unnamed x57, local copies, waits for them, and re-layouts  7.58 us
    ppermute x1, starting transfers between devices, local(): velocity = lax.ppermute(flow[0:3], both, swap)  6.53 us
  transfers between devices with their start and end apart: 26, of which 7 were waited for; matrix products, arithmetic and copies ran while one was open for 4% of the time, Pallas kernels for 14%

profile of v2, /device:TPU:62, one launch (start us, length us, event | category | flops | bytes accessed | tf_op | source)
XLA Modules:
  0.0 246.2 jit_solution(18251366012798529358)
XLA Ops:
  0.6 0.8 fusion.2
  2.1 4.8 %shard_map.203 = bf16[256,1280]{1,0:T(8,128)(2,1)} custom-call(f32[5,15]{1,0:T(8,128)} %pad_maximum_fusion.table_ref, bf16[15,256,256]{2,1,0:T(8,128)(2,1)} %bitcast.29, bf16[256,256]{1,0:T(8,128)(2,1)} %constant.102.clone.high_ref, bf16[256,256]{1,0:T(8,128)(2,1)} %constant.103.clone.low_ref), custom_call_target="tpu_custom_call" | custom-call | flops 1073741824 | bytes 3145728 | tf_op jit(solution)/shard_map/pallas_call | solution.py:362
  7.5 2.2 reduce
  9.8 1.0 reshape.60
  10.8 14.2 %all-to-all-start = ((bf16[256,2,640]{2,1,0:T(2,128)(2,1)}), bf16[256,2,640]{2,1,0:T(2,128)(2,1)S(1)}, u32[]{:S(2)}, u32[]{:S(2)}) async-start(bf16[256,2,640]{2,1,0:T(2,128)(2,1)} %reshape.60), calls=%async_computation | async-start | bytes 1310720 | tf_op jit(solution)/shard_map/all_to_all | solution.py:445
  25.0 6.3 %shard_map.204 = (bf16[16,8704]{1,0:T(8,128)(2,1)}, bf16[16,8704]{1,0:T(8,128)(2,1)}, bf16[16,8704]{1,0:T(8,128)(2,1)}, bf16[16,8704]{1,0:T(8,128)(2,1)}, bf16[64,8704]{1,0:T(8,128)(2,1)}) custom-call(s32[1]{0:T(128)S(6)} %xor.7.block_ref, bf16[15,256,256]{2,1,0:T(8,128)(2,1)} %bitcast.30), custom_call_target="tpu_custom_call" | custom-call | bytes 4194304 | tf_op jit(solution)/shard_map/pallas_call | solution.py:362
  31.3 5.5 %collective-permute-start.3 = (bf16[64,8704]{1,0:T(8,128)(2,1)}, bf16[64,8704]{1,0:T(8,128)(2,1)S(1)}, u32[]{:S(2)}, u32[]{:S(2)}) collective-permute-start(bf16[64,8704]{1,0:T(8,128)(2,1)} %get-tuple-element.39), channel_id=1, source_target_pairs={{0,4},{1,5},{2,6},{3,7},{4,0},{5,1},{6,2},{7,3},{8,12},{9,13},{10,... | collective-permute-start | bytes 3342344 | tf_op jit(solution)/shard_map/ppermute | solution.py:452
  36.9 0.8 collective-permute-start
  37.7 1.1 collective-permute-start.1
  38.8 2.7 %collective-permute-start.2 = (bf16[16,8704]{1,0:T(8,128)(2,1)}, bf16[16,8704]{1,0:T(8,128)(2,1)}, u32[]{:S(2)}, u32[]{:S(2)}) collective-permute-start(bf16[16,8704]{1,0:T(8,128)(2,1)} %get-tuple-element.38), channel_id=1, source_target_pairs={{0,3},{1,2},{2,1},{3,0},{4,7},{5,6},{6,5},{7,4},{8,11},{9,10},{10,... | collective-permute-start | bytes 835592 | tf_op jit(solution)/shard_map/ppermute | solution.py:410
  41.6 4.4 %all-to-all-done = bf16[256,2,640]{2,1,0:T(2,128)(2,1)S(1)} async-done(((bf16[256,2,640]{2,1,0:T(2,128)(2,1)}), bf16[256,2,640]{2,1,0:T(2,128)(2,1)S(1)}, u32[]{:S(2)}, u32[]{:S(2)}) %all-to-all-start) | async-done | bytes 655392 | tf_op jit(solution)/shard_map/all_to_all | solution.py:445
  46.4 0.9 copy.46
  47.4 4.0 %shard_map.205 = bf16[256,512]{1,0:T(8,128)(2,1)} custom-call(f32[1]{0:T(128)} %bitcast.5.wave_ref, s32[1]{0:T(128)} %bitcast.6.half_ref, f32[1,256]{1,0:T(1,128)} %constant.104.clone.ky_ref, f32[32,1]{1,0:T(8,128)} %constant.105.clone.kz_ref, bf16[256,1280]{1,0:T(8,128)(2,1)} %bitcast.33, bf16[64,256]{1,0:T(8,128)(2,1)} %constant.106.clone.fz_high, ...), custom_call_target="tpu_custom_call" | custom-call | flops 1073741824 | bytes 3145728 | tf_op jit(solution)/shard_map/pallas_call | solution.py:362
  51.4 1.8 reduce.1
  53.2 0.8 reshape.62
  53.9 54.9 %all-to-all-start.1 = ((bf16[256,2,256]{2,1,0:T(2,128)(2,1)}), bf16[256,2,256]{2,1,0:T(2,128)(2,1)S(1)}, u32[]{:S(2)}, u32[]{:S(2)}) async-start(bf16[256,2,256]{2,1,0:T(2,128)(2,1)} %reshape.62), calls=%async_computation.1 | async-start | bytes 524288 | tf_op jit(solution)/shard_map/all_to_all | solution.py:469
  108.8 0.9 fusion.5
  109.7 0.8 collective-permute-start.4
  110.6 1.1 collective-permute-start.5
  111.7 2.7 %collective-permute-start.6 = (bf16[16,8704]{1,0:T(8,128)(2,1)S(1)}, bf16[16,8704]{1,0:T(8,128)(2,1)S(1)}, u32[]{:S(2)}, u32[]{:S(2)}) collective-permute-start(bf16[16,8704]{1,0:T(8,128)(2,1)S(1)} %get-tuple-element.74), channel_id=1, source_target_pairs={{0,3},{1,2},{2,1},{3,0},{4,7},{5,6},{6,5},{7,4},{8,11},{9,10},{10,... | collective-permute-start | bytes 835592 | tf_op jit(solution)/shard_map/ppermute | solution.py:410
  114.4 6.4 %all-to-all-done.1 = bf16[256,2,256]{2,1,0:T(2,128)(2,1)S(1)} async-done(((bf16[256,2,256]{2,1,0:T(2,128)(2,1)}), bf16[256,2,256]{2,1,0:T(2,128)(2,1)S(1)}, u32[]{:S(2)}, u32[]{:S(2)}) %all-to-all-start.1) | async-done | bytes 262176 | tf_op jit(solution)/shard_map/all_to_all | solution.py:469
  121.1 0.8 copy.47
  121.9 4.6 %collective-permute-done.5.refs_6_ = bf16[16,8704]{1,0:T(8,128)(2,1)S(1)} collective-permute-done((bf16[16,8704]{1,0:T(8,128)(2,1)S(1)}, bf16[16,8704]{1,0:T(8,128)(2,1)S(1)}, u32[]{:S(2)}, u32[]{:S(2)}) %collective-permute-start.5) | collective-permute-done | bytes 278560 | tf_op jit(solution)/shard_map/ppermute | solution.py:410
  126.5 1.5 collective-permute-done.6.refs_7_
  128.7 3.0 %shard_map.206.center_ref = bf16[128,8704]{1,0:T(8,128)(2,1)} custom-call(s32[1]{0:T(128)} %bitcast.group_ref, bf16[16,8704]{1,0:T(8,128)(2,1)} %get-tuple-element.40.refs_0_, bf16[16,8704]{1,0:T(8,128)(2,1)} %copy-done.1, bf16[16,8704]{1,0:T(8,128)(2,1)} %collective-permute-done.1.refs_2_, bf16[16,8704]{1,0:T(8,128)(2,1)} %collective-permute-done.2.refs_3_, ...), custom_call_target="tpu_custom_call" | custom-call | bytes 4194304 | tf_op jit(solution)/shard_map/pallas_call | solution.py:362
  131.8 1.7 collective-permute-start.9
  133.6 2.8 %shard_map.207.flow_ref = f32[11,32,256]{2,1,0:T(8,128)} custom-call(bf16[256,512]{1,0:T(8,128)(2,1)} %bitcast.34, bf16[256,1024]{1,0:T(8,128)(2,1)} %constant.114.clone.high_ref, bf16[256,1024]{1,0:T(8,128)(2,1)} %constant.115.clone.low_ref), custom_call_target="tpu_custom_call" | custom-call | flops 536870912 | bytes 2097152 | tf_op jit(solution)/shard_map/pallas_call | solution.py:362
  136.3 0.9 slice.36
  137.2 6.5 %collective-permute-start.7 = (f32[3,32,256]{2,1,0:T(8,128)S(1)}, f32[3,32,256]{2,1,0:T(8,128)S(1)}, u32[]{:S(2)}, u32[]{:S(2)}) collective-permute-start(f32[3,32,256]{2,1,0:T(8,128)S(1)} %slice.36), channel_id=1, source_target_pairs={{0,0},{1,1},{2,2},{3,3},{4,4},{5,5},{6,6},{7,7},{8,8},{9,9},{10,10... | collective-permute-start | bytes 294920 | tf_op jit(solution)/shard_map/ppermute | solution.py:485
  144.6 0.7 copy.38.synth_ref
  146.8 2.5 %shard_map.208.weight_ref = bf16[128,1664]{1,0:T(8,128)(2,1)} custom-call(f32[3,256]{1,0:T(4,128)} %constant.113.clone.dir_ref, bf16[256,128]{1,0:T(8,128)(2,1)} %copy.38.synth_ref, bf16[128,256]{1,0:T(8,128)(2,1)} %bitcast.39, bf16[3,128,256]{2,1,0:T(8,128)(2,1)} %bitcast.37), custom_call_target="tpu_custom_call" | custom-call | flops 268435456 | bytes 1048576 | tf_op jit(solution)/shard_map/pallas_call | solution.py:362
  149.3 18.0 %collective-permute-done.7 = f32[3,32,256]{2,1,0:T(8,128)S(1)} collective-permute-done((f32[3,32,256]{2,1,0:T(8,128)S(1)}, f32[3,32,256]{2,1,0:T(8,128)S(1)}, u32[]{:S(2)}, u32[]{:S(2)}) %collective-permute-start.7) | collective-permute-done | bytes 98336 | tf_op jit(solution)/shard_map/ppermute | solution.py:485
  167.3 12.4 %shard_map.209.inner_ref = f32[128,8192]{1,0:T(8,128)} custom-call(bf16[128,8704]{1,0:T(8,128)(2,1)} %shard_map.206.center_ref, f32[11,32,256]{2,1,0:T(8,128)} %shard_map.207.flow_ref, bf16[128,1664]{1,0:T(8,128)(2,1)} %shard_map.208.weight_ref, f32[128,1]{1,0:T(8,128)} %broadcast_in_dim_reshape.4.damp_ref), custom_call_target="tpu_custom_call" | custom-call | flops 6442450944 | bytes 7340032 | tf_op jit(solution)/shard_map/pallas_call | solution.py:362
  179.7 1.4 copy-done
  181.1 5.8 %shard_map.211 = (bf16[15,16,256]{2,1,0:T(8,128)(2,1)}, bf16[15,16,256]{2,1,0:T(8,128)(2,1)}, bf16[15,16,256]{2,1,0:T(8,128)(2,1)}, bf16[15,16,256]{2,1,0:T(8,12...) custom-call(s32[1]{0:T(128)} %bitcast.group_ref, ...), custom_call_target="tpu_custom_call" | custom-call | flops 536870912 | bytes 4718592 | tf_op jit(solution)/shard_map/pallas_call | solution.py:362
  186.9 4.1 %collective-permute-start.18 = (bf16[15,16,256]{2,1,0:T(8,128)(2,1)}, bf16[15,16,256]{2,1,0:T(8,128)(2,1)S(1)}, u32[]{:S(2)}, u32[]{:S(2)}) collective-permute-start(bf16[15,16,256]{2,1,0:T(8,128)(2,1)} %get-tuple-element.59), channel_id=1, source_target_pairs={{0,2},{1,3},{2,0},{3,1},{4,6},{5,7},{6,4},{7,5},{8,10},{9,11},{10,... | collective-permute-start | bytes 368648 | tf_op jit(solution)/shard_map/ppermute | solution.py:410
  191.6 1.1 collective-permute-start.20
  192.7 3.7 %collective-permute-start.21 = (bf16[15,16,256]{2,1,0:T(8,128)(2,1)}, bf16[15,16,256]{2,1,0:T(8,128)(2,1)S(1)}, u32[]{:S(2)}, u32[]{:S(2)}) collective-permute-start(bf16[15,16,256]{2,1,0:T(8,128)(2,1)} %get-tuple-element.62), channel_id=1, source_target_pairs={{0,5},{1,4},{2,7},{3,6},{4,1},{5,0},{6,3},{7,2},{8,13},{9,12},{10,... | collective-permute-start | bytes 368648 | tf_op jit(solution)/shard_map/ppermute | solution.py:410
  196.4 5.8 %shard_map.210 = (bf16[15,16,256]{2,1,0:T(8,128)(2,1)}, bf16[15,16,256]{2,1,0:T(8,128)(2,1)}, bf16[15,16,256]{2,1,0:T(8,128)(2,1)}, bf16[15,16,256]{2,1,0:T(8,12...) custom-call(s32[1]{0:T(128)} %bitcast.group_ref, ...), custom_call_target="tpu_custom_call" | custom-call | flops 536870912 | bytes 4718592 | tf_op jit(solution)/shard_map/pallas_call | solution.py:362
  202.1 5.3 %collective-permute-start.22 = (bf16[15,16,256]{2,1,0:T(8,128)(2,1)S(1)}, bf16[15,16,256]{2,1,0:T(8,128)(2,1)S(1)}, u32[]{:S(2)}, u32[]{:S(2)}) collective-permute-start(bf16[15,16,256]{2,1,0:T(8,128)(2,1)S(1)} %copy-done.24), channel_id=1, source_target_pairs={{0,6},{1,7},{2,4},{3,5},{4,2},{5,3},{6,0},{7,1},{8,14},{9,15},{10,... | collective-permute-start | bytes 368648 | tf_op jit(solution)/shard_map/ppermute | solution.py:410
  207.5 5.0 %collective-permute-start.23 = (bf16[15,16,256]{2,1,0:T(8,128)(2,1)S(1)}, bf16[15,16,256]{2,1,0:T(8,128)(2,1)S(1)}, u32[]{:S(2)}, u32[]{:S(2)}) collective-permute-start(bf16[15,16,256]{2,1,0:T(8,128)(2,1)S(1)} %copy-done.23), channel_id=1, source_target_pairs={{0,7},{1,6},{2,5},{3,4},{4,3},{5,2},{6,1},{7,0},{8,15},{9,14},{10,... | collective-permute-start | bytes 368648 | tf_op jit(solution)/shard_map/ppermute | solution.py:410
  212.5 4.1 %collective-permute-start.11 = (bf16[15,16,256]{2,1,0:T(8,128)(2,1)}, bf16[15,16,256]{2,1,0:T(8,128)(2,1)S(1)}, u32[]{:S(2)}, u32[]{:S(2)}) collective-permute-start(bf16[15,16,256]{2,1,0:T(8,128)(2,1)} %get-tuple-element.51), channel_id=1, source_target_pairs={{0,2},{1,3},{2,0},{3,1},{4,6},{5,7},{6,4},{7,5},{8,10},{9,11},{10,... | collective-permute-start | bytes 368648 | tf_op jit(solution)/shard_map/ppermute | solution.py:410
  217.2 1.1 collective-permute-start.13
  218.3 4.4 %collective-permute-done.23.refs_15_ = bf16[15,16,256]{2,1,0:T(8,128)(2,1)S(1)} collective-permute-done((bf16[15,16,256]{2,1,0:T(8,128)(2,1)S(1)}, bf16[15,16,256]{2,1,0:T(8,128)(2,1)S(1)}, u32[]{:S(2)}, u32[]{:S(2)}) %collective-permute-start.23) | collective-permute-done | bytes 122912 | tf_op jit(solution)/shard_map/ppermute | solution.py:410
  222.8 6.6 %collective-permute-start.15 = (bf16[15,16,256]{2,1,0:T(8,128)(2,1)}, bf16[15,16,256]{2,1,0:T(8,128)(2,1)S(1)}, u32[]{:S(2)}, u32[]{:S(2)}) collective-permute-start(bf16[15,16,256]{2,1,0:T(8,128)(2,1)} %get-tuple-element.55), channel_id=1, source_target_pairs={{0,6},{1,7},{2,4},{3,5},{4,2},{5,3},{6,0},{7,1},{8,14},{9,15},{10,... | collective-permute-start | bytes 368648 | tf_op jit(solution)/shard_map/ppermute | solution.py:410
  229.4 5.4 %collective-permute-start.16 = (bf16[15,16,256]{2,1,0:T(8,128)(2,1)}, bf16[15,16,256]{2,1,0:T(8,128)(2,1)S(1)}, u32[]{:S(2)}, u32[]{:S(2)}) collective-permute-start(bf16[15,16,256]{2,1,0:T(8,128)(2,1)} %get-tuple-element.56), channel_id=1, source_target_pairs={{0,7},{1,6},{2,5},{3,4},{4,3},{5,2},{6,1},{7,0},{8,15},{9,14},{10,... | collective-permute-start | bytes 368648 | tf_op jit(solution)/shard_map/ppermute | solution.py:410
  234.9 7.1 %collective-permute-done.16.refs_7_ = bf16[15,16,256]{2,1,0:T(8,128)(2,1)S(1)} collective-permute-done((bf16[15,16,256]{2,1,0:T(8,128)(2,1)}, bf16[15,16,256]{2,1,0:T(8,128)(2,1)S(1)}, u32[]{:S(2)}, u32[]{:S(2)}) %collective-permute-start.16) | collective-permute-done | bytes 122912 | tf_op jit(solution)/shard_map/ppermute | solution.py:410
  242.6 3.0 %shard_map.212 = bf16[15,256,256]{2,1,0:T(8,128)(2,1)} custom-call(s32[1]{0:T(128)S(6)} %xor.7.block_ref, bf16[15,16,256]{2,1,0:T(8,128)(2,1)} %get-tuple-element.49.refs_0_, bf16[15,16,256]{2,1,0:T(8,128)(2,1)} %copy-done.13, bf16[15,16,256]{2,1,0:T(8,128)(2,1)} %copy-done.14, bf16[15,16,256]{2,1,0:T(8,128)(2,1)} %copy-done.15, ...), custom_call_target="tpu_custom_call" | custom-call | bytes 4194304 | tf_op jit(solution)/shard_map/pallas_call | solution.py:362
  (91 shorter events, 7.7 us)
Async XLA Ops:
  10.8 35.1 %all-to-all-start = ((bf16[256,2,640]{2,1,0:T(2,128)(2,1)}), bf16[256,2,640]{2,1,0:T(2,128)(2,1)S(1)}, u32[]{:S(2)}, u32[]{:S(2)}) async-start(bf16[256,2,640]{2,1,0:T(2,128)(2,1)} %reshape.60), calls=%async_computation | async-start | bytes 1310720 | tf_op jit(solution)/shard_map/all_to_all | solution.py:445
  31.3 77.5 %collective-permute-start.3 = (bf16[64,8704]{1,0:T(8,128)(2,1)}, bf16[64,8704]{1,0:T(8,128)(2,1)S(1)}, u32[]{:S(2)}, u32[]{:S(2)}) collective-permute-start(bf16[64,8704]{1,0:T(8,128)(2,1)} %get-tuple-element.39), channel_id=1, source_target_pairs={{0,4},{1,5},{2,6},{3,7},{4,0},{5,1},{6,2},{7,3},{8,12},{9,13},{10,... | collective-permute-start | bytes 3342344 | tf_op jit(solution)/shard_map/ppermute | solution.py:452
  36.9 74.9 %collective-permute-start = (bf16[16,8704]{1,0:T(8,128)(2,1)}, bf16[16,8704]{1,0:T(8,128)(2,1)S(1)}, u32[]{:S(2)}, u32[]{:S(2)}) collective-permute-start(bf16[16,8704]{1,0:T(8,128)(2,1)} %get-tuple-element.36), channel_id=1, source_target_pairs={{0,1},{1,0},{2,3},{3,2},{4,5},{5,4},{6,7},{7,6},{8,9},{9,8},{10,11... | collective-permute-start | bytes 835592 | tf_op jit(solution)/shard_map/ppermute | solution.py:410
  37.7 84.2 %collective-permute-start.1 = (bf16[16,8704]{1,0:T(8,128)(2,1)}, bf16[16,8704]{1,0:T(8,128)(2,1)}, u32[]{:S(2)}, u32[]{:S(2)}) collective-permute-start(bf16[16,8704]{1,0:T(8,128)(2,1)} %get-tuple-element.37), channel_id=1, source_target_pairs={{0,2},{1,3},{2,0},{3,1},{4,6},{5,7},{6,4},{7,5},{8,10},{9,11},{10,... | collective-permute-start | bytes 835592 | tf_op jit(solution)/shard_map/ppermute | solution.py:410
  38.8 83.0 %collective-permute-start.2 = (bf16[16,8704]{1,0:T(8,128)(2,1)}, bf16[16,8704]{1,0:T(8,128)(2,1)}, u32[]{:S(2)}, u32[]{:S(2)}) collective-permute-start(bf16[16,8704]{1,0:T(8,128)(2,1)} %get-tuple-element.38), channel_id=1, source_target_pairs={{0,3},{1,2},{2,1},{3,0},{4,7},{5,6},{6,5},{7,4},{8,11},{9,10},{10,... | collective-permute-start | bytes 835592 | tf_op jit(solution)/shard_map/ppermute | solution.py:410
  53.9 66.9 %all-to-all-start.1 = ((bf16[256,2,256]{2,1,0:T(2,128)(2,1)}), bf16[256,2,256]{2,1,0:T(2,128)(2,1)S(1)}, u32[]{:S(2)}, u32[]{:S(2)}) async-start(bf16[256,2,256]{2,1,0:T(2,128)(2,1)} %reshape.62), calls=%async_computation.1 | async-start | bytes 524288 | tf_op jit(solution)/shard_map/all_to_all | solution.py:469
  109.7 12.2 %collective-permute-start.4 = (bf16[16,8704]{1,0:T(8,128)(2,1)}, bf16[16,8704]{1,0:T(8,128)(2,1)S(1)}, u32[]{:S(2)}, u32[]{:S(2)}) collective-permute-start(bf16[16,8704]{1,0:T(8,128)(2,1)} %get-tuple-element.76), channel_id=1, source_target_pairs={{0,1},{1,0},{2,3},{3,2},{4,5},{5,4},{6,7},{7,6},{8,9},{9,8},{10,11... | collective-permute-start | bytes 835592 | tf_op jit(solution)/shard_map/ppermute | solution.py:410
  110.6 15.9 %collective-permute-start.5 = (bf16[16,8704]{1,0:T(8,128)(2,1)S(1)}, bf16[16,8704]{1,0:T(8,128)(2,1)S(1)}, u32[]{:S(2)}, u32[]{:S(2)}) collective-permute-start(bf16[16,8704]{1,0:T(8,128)(2,1)S(1)} %get-tuple-element.75), channel_id=1, source_target_pairs={{0,2},{1,3},{2,0},{3,1},{4,6},{5,7},{6,4},{7,5},{8,10},{9,11},{10,... | collective-permute-start | bytes 835592 | tf_op jit(solution)/shard_map/ppermute | solution.py:410
  111.7 16.3 %copy-start.1 = (bf16[16,8704]{1,0:T(8,128)(2,1)}, bf16[16,8704]{1,0:T(8,128)(2,1)S(1)}, u32[]{:S(2)}) copy-start(bf16[16,8704]{1,0:T(8,128)(2,1)S(1)} %collective-permute-done.refs_1_) | copy-start | bytes 835588
  111.7 16.3 %collective-permute-start.6 = (bf16[16,8704]{1,0:T(8,128)(2,1)S(1)}, bf16[16,8704]{1,0:T(8,128)(2,1)S(1)}, u32[]{:S(2)}, u32[]{:S(2)}) collective-permute-start(bf16[16,8704]{1,0:T(8,128)(2,1)S(1)} %get-tuple-element.74), channel_id=1, source_target_pairs={{0,3},{1,2},{2,1},{3,0},{4,7},{5,6},{6,5},{7,4},{8,11},{9,10},{10,... | collective-permute-start | bytes 835592 | tf_op jit(solution)/shard_map/ppermute | solution.py:410
  121.9 6.1 %copy-start.2 = (bf16[16,8704]{1,0:T(8,128)(2,1)}, bf16[16,8704]{1,0:T(8,128)(2,1)S(1)}, u32[]{:S(2)}) copy-start(bf16[16,8704]{1,0:T(8,128)(2,1)S(1)} %collective-permute-done.4.refs_5_) | copy-start | bytes 835588
  126.5 1.5 copy-start.3
  131.7 12.0 %copy-start.20 = (bf16[256,120]{0,1:T(8,128)(2,1)S(1)}, bf16[256,120]{0,1:T(8,128)(2,1)}, u32[]{:S(2)}) copy-start(bf16[256,120]{0,1:T(8,128)(2,1)} %param.21) | copy-start | bytes 184324
  131.7 12.1 %copy-start.5 = (bf16[3,120,256]{2,1,0:T(8,128)(2,1)S(1)}, bf16[3,120,256]{2,1,0:T(8,128)(2,1)}, u32[]{:S(2)}) copy-start(bf16[3,120,256]{2,1,0:T(8,128)(2,1)} %param.23) | copy-start | bytes 552964
  131.7 13.6 %copy-start.21 = (bf16[120,256]{1,0:T(8,128)(2,1)S(1)}, bf16[120,256]{1,0:T(8,128)(2,1)}, u32[]{:S(2)}) copy-start(bf16[120,256]{1,0:T(8,128)(2,1)} %param.22) | copy-start | bytes 184324
  131.7 14.3 %copy-start.22 = (f32[120]{0:T(128)S(1)}, f32[120]{0:T(128)}, u32[]{:S(2)}) copy-start(f32[120]{0:T(128)} %param.24) | copy-start | bytes 1444
  131.8 47.9 %collective-permute-start.8 = (bf16[128,8704]{1,0:T(8,128)(2,1)}, bf16[128,8704]{1,0:T(8,128)(2,1)S(1)}, u32[]{:S(2)}, u32[]{:S(2)}) collective-permute-start(bf16[128,8704]{1,0:T(8,128)(2,1)} %shard_map.206.center_ref), channel_id=1, source_target_pairs={{0,8},{1,9},{2,10},{3,11},{4,12},{5,13},{6,14},{7,15},{8,16},{9,17... | collective-permute-start | bytes 6684680 | tf_op jit(solution)/shard_map/ppermute | solution.py:472
  131.8 47.9 %collective-permute-start.9 = (bf16[128,8704]{1,0:T(8,128)(2,1)}, bf16[128,8704]{1,0:T(8,128)(2,1)}, u32[]{:S(2)}, u32[]{:S(2)}) collective-permute-start(bf16[128,8704]{1,0:T(8,128)(2,1)} %shard_map.206.center_ref), channel_id=1, source_target_pairs={{0,252},{1,253},{2,254},{3,255},{4,248},{5,249},{6,250},{7,251},{8... | collective-permute-start | bytes 6684680 | tf_op jit(solution)/shard_map/ppermute | solution.py:473
  137.2 30.1 %collective-permute-start.7 = (f32[3,32,256]{2,1,0:T(8,128)S(1)}, f32[3,32,256]{2,1,0:T(8,128)S(1)}, u32[]{:S(2)}, u32[]{:S(2)}) collective-permute-start(f32[3,32,256]{2,1,0:T(8,128)S(1)} %slice.36), channel_id=1, source_target_pairs={{0,0},{1,1},{2,2},{3,3},{4,4},{5,5},{6,6},{7,7},{8,8},{9,9},{10,10... | collective-permute-start | bytes 294920 | tf_op jit(solution)/shard_map/ppermute | solution.py:485
  186.9 15.2 %collective-permute-start.17 = (bf16[15,16,256]{2,1,0:T(8,128)(2,1)}, bf16[15,16,256]{2,1,0:T(8,128)(2,1)S(1)}, u32[]{:S(2)}, u32[]{:S(2)}) collective-permute-start(bf16[15,16,256]{2,1,0:T(8,128)(2,1)} %get-tuple-element.58), channel_id=1, source_target_pairs={{0,1},{1,0},{2,3},{3,2},{4,5},{5,4},{6,7},{7,6},{8,9},{9,8},{10,11... | collective-permute-start | bytes 368648 | tf_op jit(solution)/shard_map/ppermute | solution.py:410
  186.9 20.5 %collective-permute-start.18 = (bf16[15,16,256]{2,1,0:T(8,128)(2,1)}, bf16[15,16,256]{2,1,0:T(8,128)(2,1)S(1)}, u32[]{:S(2)}, u32[]{:S(2)}) collective-permute-start(bf16[15,16,256]{2,1,0:T(8,128)(2,1)} %get-tuple-element.59), channel_id=1, source_target_pairs={{0,2},{1,3},{2,0},{3,1},{4,6},{5,7},{6,4},{7,5},{8,10},{9,11},{10,... | collective-permute-start | bytes 368648 | tf_op jit(solution)/shard_map/ppermute | solution.py:410
  191.0 21.4 %collective-permute-start.19 = (bf16[15,16,256]{2,1,0:T(8,128)(2,1)}, bf16[15,16,256]{2,1,0:T(8,128)(2,1)S(1)}, u32[]{:S(2)}, u32[]{:S(2)}) collective-permute-start(bf16[15,16,256]{2,1,0:T(8,128)(2,1)} %get-tuple-element.60), channel_id=1, source_target_pairs={{0,3},{1,2},{2,1},{3,0},{4,7},{5,6},{6,5},{7,4},{8,11},{9,10},{10,... | collective-permute-start | bytes 368648 | tf_op jit(solution)/shard_map/ppermute | solution.py:410
  191.6 20.8 %collective-permute-start.20 = (bf16[15,16,256]{2,1,0:T(8,128)(2,1)}, bf16[15,16,256]{2,1,0:T(8,128)(2,1)S(1)}, u32[]{:S(2)}, u32[]{:S(2)}) collective-permute-start(bf16[15,16,256]{2,1,0:T(8,128)(2,1)} %get-tuple-element.61), channel_id=1, source_target_pairs={{0,4},{1,5},{2,6},{3,7},{4,0},{5,1},{6,2},{7,3},{8,12},{9,13},{10,... | collective-permute-start | bytes 368648 | tf_op jit(solution)/shard_map/ppermute | solution.py:410
  192.7 9.4 %copy-start.24 = (bf16[15,16,256]{2,1,0:T(8,128)(2,1)S(1)}, bf16[15,16,256]{2,1,0:T(8,128)(2,1)}, u32[]{:S(2)}) copy-start(bf16[15,16,256]{2,1,0:T(8,128)(2,1)} %get-tuple-element.63) | copy-start | bytes 368644
  192.7 14.8 %copy-start.23 = (bf16[15,16,256]{2,1,0:T(8,128)(2,1)S(1)}, bf16[15,16,256]{2,1,0:T(8,128)(2,1)}, u32[]{:S(2)}) copy-start(bf16[15,16,256]{2,1,0:T(8,128)(2,1)} %get-tuple-element.64) | copy-start | bytes 368644
  192.7 23.9 %collective-permute-start.21 = (bf16[15,16,256]{2,1,0:T(8,128)(2,1)}, bf16[15,16,256]{2,1,0:T(8,128)(2,1)S(1)}, u32[]{:S(2)}, u32[]{:S(2)}) collective-permute-start(bf16[15,16,256]{2,1,0:T(8,128)(2,1)} %get-tuple-element.62), channel_id=1, source_target_pairs={{0,5},{1,4},{2,7},{3,6},{4,1},{5,0},{6,3},{7,2},{8,13},{9,12},{10,... | collective-permute-start | bytes 368648 | tf_op jit(solution)/shard_map/ppermute | solution.py:410
  202.1 39.8 %copy-start.6 = (bf16[15,16,256]{2,1,0:T(8,128)(2,1)}, bf16[15,16,256]{2,1,0:T(8,128)(2,1)S(1)}, u32[]{:S(2)}) copy-start(bf16[15,16,256]{2,1,0:T(8,128)(2,1)S(1)} %collective-permute-done.17.refs_9_) | copy-start | bytes 368644
  202.1 15.0 %collective-permute-start.22 = (bf16[15,16,256]{2,1,0:T(8,128)(2,1)S(1)}, bf16[15,16,256]{2,1,0:T(8,128)(2,1)S(1)}, u32[]{:S(2)}, u32[]{:S(2)}) collective-permute-start(bf16[15,16,256]{2,1,0:T(8,128)(2,1)S(1)} %copy-done.24), channel_id=1, source_target_pairs={{0,6},{1,7},{2,4},{3,5},{4,2},{5,3},{6,0},{7,1},{8,14},{9,15},{10,... | collective-permute-start | bytes 368648 | tf_op jit(solution)/shard_map/ppermute | solution.py:410
  207.5 34.5 %copy-start.7 = (bf16[15,16,256]{2,1,0:T(8,128)(2,1)}, bf16[15,16,256]{2,1,0:T(8,128)(2,1)S(1)}, u32[]{:S(2)}) copy-start(bf16[15,16,256]{2,1,0:T(8,128)(2,1)S(1)} %collective-permute-done.18.refs_10_) | copy-start | bytes 368644
  207.5 15.2 %collective-permute-start.23 = (bf16[15,16,256]{2,1,0:T(8,128)(2,1)S(1)}, bf16[15,16,256]{2,1,0:T(8,128)(2,1)S(1)}, u32[]{:S(2)}, u32[]{:S(2)}) collective-permute-start(bf16[15,16,256]{2,1,0:T(8,128)(2,1)S(1)} %copy-done.23), channel_id=1, source_target_pairs={{0,7},{1,6},{2,5},{3,4},{4,3},{5,2},{6,1},{7,0},{8,15},{9,14},{10,... | collective-permute-start | bytes 368648 | tf_op jit(solution)/shard_map/ppermute | solution.py:410
  212.5 29.5 %copy-start.8 = (bf16[15,16,256]{2,1,0:T(8,128)(2,1)}, bf16[15,16,256]{2,1,0:T(8,128)(2,1)S(1)}, u32[]{:S(2)}) copy-start(bf16[15,16,256]{2,1,0:T(8,128)(2,1)S(1)} %collective-permute-done.19.refs_11_) | copy-start | bytes 368644
  212.5 10.3 %collective-permute-start.10 = (bf16[15,16,256]{2,1,0:T(8,128)(2,1)}, bf16[15,16,256]{2,1,0:T(8,128)(2,1)S(1)}, u32[]{:S(2)}, u32[]{:S(2)}) collective-permute-start(bf16[15,16,256]{2,1,0:T(8,128)(2,1)} %get-tuple-element.50), channel_id=1, source_target_pairs={{0,1},{1,0},{2,3},{3,2},{4,5},{5,4},{6,7},{7,6},{8,9},{9,8},{10,11... | collective-permute-start | bytes 368648 | tf_op jit(solution)/shard_map/ppermute | solution.py:410
  212.5 29.5 %copy-start.9 = (bf16[15,16,256]{2,1,0:T(8,128)(2,1)}, bf16[15,16,256]{2,1,0:T(8,128)(2,1)S(1)}, u32[]{:S(2)}) copy-start(bf16[15,16,256]{2,1,0:T(8,128)(2,1)S(1)} %collective-permute-done.20.refs_12_) | copy-start | bytes 368644
  212.5 16.9 %collective-permute-start.11 = (bf16[15,16,256]{2,1,0:T(8,128)(2,1)}, bf16[15,16,256]{2,1,0:T(8,128)(2,1)S(1)}, u32[]{:S(2)}, u32[]{:S(2)}) collective-permute-start(bf16[15,16,256]{2,1,0:T(8,128)(2,1)} %get-tuple-element.51), channel_id=1, source_target_pairs={{0,2},{1,3},{2,0},{3,1},{4,6},{5,7},{6,4},{7,5},{8,10},{9,11},{10,... | collective-permute-start | bytes 368648 | tf_op jit(solution)/shard_map/ppermute | solution.py:410
  216.6 25.4 %copy-start.10 = (bf16[15,16,256]{2,1,0:T(8,128)(2,1)}, bf16[15,16,256]{2,1,0:T(8,128)(2,1)S(1)}, u32[]{:S(2)}) copy-start(bf16[15,16,256]{2,1,0:T(8,128)(2,1)S(1)} %collective-permute-done.21.refs_13_) | copy-start | bytes 368644
  216.6 18.2 %collective-permute-start.12 = (bf16[15,16,256]{2,1,0:T(8,128)(2,1)}, bf16[15,16,256]{2,1,0:T(8,128)(2,1)S(1)}, u32[]{:S(2)}, u32[]{:S(2)}) collective-permute-start(bf16[15,16,256]{2,1,0:T(8,128)(2,1)} %get-tuple-element.52), channel_id=1, source_target_pairs={{0,3},{1,2},{2,1},{3,0},{4,7},{5,6},{6,5},{7,4},{8,11},{9,10},{10,... | collective-permute-start | bytes 368648 | tf_op jit(solution)/shard_map/ppermute | solution.py:410
  217.2 24.8 %copy-start.11 = (bf16[15,16,256]{2,1,0:T(8,128)(2,1)}, bf16[15,16,256]{2,1,0:T(8,128)(2,1)S(1)}, u32[]{:S(2)}) copy-start(bf16[15,16,256]{2,1,0:T(8,128)(2,1)S(1)} %collective-permute-done.22.refs_14_) | copy-start | bytes 368644
  217.2 17.6 %collective-permute-start.13 = (bf16[15,16,256]{2,1,0:T(8,128)(2,1)}, bf16[15,16,256]{2,1,0:T(8,128)(2,1)S(1)}, u32[]{:S(2)}, u32[]{:S(2)}) collective-permute-start(bf16[15,16,256]{2,1,0:T(8,128)(2,1)} %get-tuple-element.53), channel_id=1, source_target_pairs={{0,4},{1,5},{2,6},{3,7},{4,0},{5,1},{6,2},{7,3},{8,12},{9,13},{10,... | collective-permute-start | bytes 368648 | tf_op jit(solution)/shard_map/ppermute | solution.py:410
  222.7 19.3 %copy-start.12 = (bf16[15,16,256]{2,1,0:T(8,128)(2,1)}, bf16[15,16,256]{2,1,0:T(8,128)(2,1)S(1)}, u32[]{:S(2)}) copy-start(bf16[15,16,256]{2,1,0:T(8,128)(2,1)S(1)} %collective-permute-done.23.refs_15_) | copy-start | bytes 368644
  222.7 12.2 %collective-permute-start.14 = (bf16[15,16,256]{2,1,0:T(8,128)(2,1)}, bf16[15,16,256]{2,1,0:T(8,128)(2,1)S(1)}, u32[]{:S(2)}, u32[]{:S(2)}) collective-permute-start(bf16[15,16,256]{2,1,0:T(8,128)(2,1)} %get-tuple-element.54), channel_id=1, source_target_pairs={{0,5},{1,4},{2,7},{3,6},{4,1},{5,0},{6,3},{7,2},{8,13},{9,12},{10,... | collective-permute-start | bytes 368648 | tf_op jit(solution)/shard_map/ppermute | solution.py:410
  222.8 19.2 %copy-start.13 = (bf16[15,16,256]{2,1,0:T(8,128)(2,1)}, bf16[15,16,256]{2,1,0:T(8,128)(2,1)S(1)}, u32[]{:S(2)}) copy-start(bf16[15,16,256]{2,1,0:T(8,128)(2,1)S(1)} %collective-permute-done.10.refs_1_) | copy-start | bytes 368644
  222.8 12.0 %collective-permute-start.15 = (bf16[15,16,256]{2,1,0:T(8,128)(2,1)}, bf16[15,16,256]{2,1,0:T(8,128)(2,1)S(1)}, u32[]{:S(2)}, u32[]{:S(2)}) collective-permute-start(bf16[15,16,256]{2,1,0:T(8,128)(2,1)} %get-tuple-element.55), channel_id=1, source_target_pairs={{0,6},{1,7},{2,4},{3,5},{4,2},{5,3},{6,0},{7,1},{8,14},{9,15},{10,... | collective-permute-start | bytes 368648 | tf_op jit(solution)/shard_map/ppermute | solution.py:410
  229.4 12.6 %copy-start.14 = (bf16[15,16,256]{2,1,0:T(8,128)(2,1)}, bf16[15,16,256]{2,1,0:T(8,128)(2,1)S(1)}, u32[]{:S(2)}) copy-start(bf16[15,16,256]{2,1,0:T(8,128)(2,1)S(1)} %collective-permute-done.11.refs_2_) | copy-start | bytes 368644
  229.4 12.5 %collective-permute-start.16 = (bf16[15,16,256]{2,1,0:T(8,128)(2,1)}, bf16[15,16,256]{2,1,0:T(8,128)(2,1)S(1)}, u32[]{:S(2)}, u32[]{:S(2)}) collective-permute-start(bf16[15,16,256]{2,1,0:T(8,128)(2,1)} %get-tuple-element.56), channel_id=1, source_target_pairs={{0,7},{1,6},{2,5},{3,4},{4,3},{5,2},{6,1},{7,0},{8,15},{9,14},{10,... | collective-permute-start | bytes 368648 | tf_op jit(solution)/shard_map/ppermute | solution.py:410
  234.8 7.2 %copy-start.15 = (bf16[15,16,256]{2,1,0:T(8,128)(2,1)}, bf16[15,16,256]{2,1,0:T(8,128)(2,1)S(1)}, u32[]{:S(2)}) copy-start(bf16[15,16,256]{2,1,0:T(8,128)(2,1)S(1)} %collective-permute-done.12.refs_3_) | copy-start | bytes 368644
  234.8 7.2 %copy-start.16 = (bf16[15,16,256]{2,1,0:T(8,128)(2,1)}, bf16[15,16,256]{2,1,0:T(8,128)(2,1)S(1)}, u32[]{:S(2)}) copy-start(bf16[15,16,256]{2,1,0:T(8,128)(2,1)S(1)} %collective-permute-done.13.refs_4_) | copy-start | bytes 368644
  234.8 7.2 %copy-start.17 = (bf16[15,16,256]{2,1,0:T(8,128)(2,1)}, bf16[15,16,256]{2,1,0:T(8,128)(2,1)S(1)}, u32[]{:S(2)}) copy-start(bf16[15,16,256]{2,1,0:T(8,128)(2,1)S(1)} %collective-permute-done.14.refs_5_) | copy-start | bytes 368644
  234.8 7.2 %copy-start.18 = (bf16[15,16,256]{2,1,0:T(8,128)(2,1)}, bf16[15,16,256]{2,1,0:T(8,128)(2,1)S(1)}, u32[]{:S(2)}) copy-start(bf16[15,16,256]{2,1,0:T(8,128)(2,1)S(1)} %collective-permute-done.15.refs_6_) | copy-start | bytes 368644
  (3 other events, 2.8 us)

commit v3 on v1

--- a/solution.py
+++ b/solution.py
@@ -270,11 +270,10 @@
 
 
 def rate_kernel(
-    group_ref, center_ref, zlow_ref, zhigh_ref, ylow_ref, yhigh_ref, flow_ref, weight_ref, damp_ref,
+    center_ref, zlow_ref, zhigh_ref, ylow_ref, yhigh_ref, flow_ref, weight_ref, damp_ref,
     *refs,
 ):
-    outs, (padded, operands, locals_, *stages) = refs[:GROUPS], refs[GROUPS:]
-    group = group_ref[0]
+    out_ref, padded, operands, locals_, *stages = refs
     cells = CHUNK * NX
     padded[:, :NX] = ylow_ref[...]
     padded[:, NX : NX + cells] = center_ref[...]
@@ -312,21 +311,21 @@
         return carry
 
     lax.fori_loop(0, CHUNK // 2, rows, 0)
-    for j in range(GROUPS):
+    for g in range(GROUPS):
         for c in range(OWN):
-            first = pl.multiple_of(((group ^ j) * PAD + c) * CHUNK, CHUNK)
+            first = (g * PAD + c) * CHUNK
             for side, stage in enumerate(stages):
-                outs[j][c, :, side * LANES : (side + 1) * LANES] = stage[
-                    pl.ds(first, CHUNK), :
+                out_ref[g, c, :, side * LANES : (side + 1) * LANES] = stage[
+                    first : first + CHUNK, :
                 ].astype(bf16)
 
 
-def place_kernel(block_ref, *refs):
+def place_kernel(swap_ref, *refs):
     out_ref = refs[-1]
     for part in range(PARTS):
-        for j in range(GROUPS):
-            first = pl.multiple_of((block_ref[0] ^ j) * ROWS + part * CHUNK, CHUNK)
-            out_ref[:, pl.ds(first, CHUNK), :] = refs[part * GROUPS + j][...]
+        for g in range(GROUPS):
+            first = pl.multiple_of((swap_ref[0] ^ g) * ROWS + part * CHUNK, CHUNK)
+            out_ref[:, pl.ds(first, CHUNK), :] = refs[part][g]
 
 
 def call(kernel, out_shape, ins, scratch=(), scalars=0, flops=0, byte_count=0, specs=None):
@@ -437,6 +436,7 @@
     y_low = lax.ppermute(center[:, -NX:], both, pairs(lambda s, b: (s, (b + 1) % GROUPS)))
     y_high = lax.ppermute(center[:, :NX], both, pairs(lambda s, b: (s, (b - 1) % GROUPS)))
 
+    z_low, z_high, y_low, y_high = lax.optimization_barrier((z_low, z_high, y_low, y_high))
     weights = call(
         weights_kernel, shape(ALL_PAD, BLOCKS * ALL_PAD),
         [
@@ -458,8 +458,8 @@
         low = (y_low, VMEM) if first == 0 else (center, edge(first - 1))
         high = (y_high, VMEM) if last == ROWS else (center, edge(last))
         rates = call(
-            rate_kernel, [shape(OWN, CHUNK, NX)] * GROUPS,
-            [group_arg, center, z_low, z_high, low[0], high[0], flow, weights, damp],
+            rate_kernel, shape(GROUPS, OWN, CHUNK, NX),
+            [center, z_low, z_high, low[0], high[0], flow, weights, damp],
             [
                 pltpu.VMEM((ALL_PAD, (CHUNK + 2) * NX), bf16),
                 pltpu.VMEM((2, BLOCKS * ALL_PAD, NX), bf16),
@@ -467,20 +467,18 @@
                 pltpu.VMEM((ALL_PAD * CHUNK, LANES), f32),
                 pltpu.VMEM((ALL_PAD * CHUNK, LANES), f32),
             ],
-            1, 7 << 29, 9 << 19,
+            0, 7 << 29, 9 << 19,
             [
-                SMEM, here, here, here, low[1], high[1],
+                here, here, here, low[1], high[1],
                 pl.BlockSpec((11, CHUNK, NX), lambda i, part=part: (0, part, 0)), VMEM, VMEM,
             ],
         )
-        parts.append(rates[0])
-        returned.append(rates[0])
-        for j in range(1, GROUPS):
-            returned.append(lax.ppermute(rates[j], "harm", [(i, i ^ j) for i in range(GROUPS)]))
+        parts.append(rates)
+        returned.append(lax.all_to_all(rates, "harm", 0, 0, tiled=True))
     swap = pairs(lambda s, b: (s, b ^ (FLIP * odd(s))))
-    late, _ = lax.optimization_barrier((flow[0:3], parts))
+    late, _ = lax.optimization_barrier((flow[0:3], parts[0]))
     velocity = lax.ppermute(late, both, swap)
-    rate = call(place_kernel, shape(OWN, NY, NX), [block_arg, *returned], (), 1, 0, 4 << 20)
+    rate = call(place_kernel, shape(OWN, NY, NX), [group_arg ^ block_arg, *returned], (), 1, 0, 4 << 20)
     return (rate.reshape(OWN, 1, NY, NX), velocity.reshape(3, 1, ROWS, NX))
 
 

time: 227 us -> 213 us (0.938)
  starting transfers between devices: 101 us -> 76.7 us
  waiting for transfers between devices: 62.1 us -> 74.4 us
    ppermute x14 -> x0, starting transfers between devices: 39.8 us -> none  [local(): lax.ppermute(rates[j], 'harm', [(i, i ^ j) for i in range(GROUPS)])]
    all_to_all x0 -> x2, waiting for transfers between devices: none -> 18.2 us  [local(): returned.append(lax.all_to_all(rates, 'harm', 0, 0, tiled=True))]
    all_to_all x0 -> x2, starting transfers between devices: none -> 13.6 us  [local(): returned.append(lax.all_to_all(rates, 'harm', 0, 0, tiled=True))]
    ppermute x14 -> x0, waiting for transfers between devices: 11.3 us -> none  [local(): lax.ppermute(rates[j], 'harm', [(i, i ^ j) for i in range(GROUPS)])]
    ppermute x1, waiting for transfers between devices: 6.37 us -> 16.5 us  [local(): velocity = lax.ppermute(late, both, swap)]
    all_to_all x1, waiting for transfers between devices: 13.2 us -> 8.39 us  [local(): mixed = lax.all_to_all(sent, everyone, 0, 0, tiled=True)]
    unnamed x69 -> x39, local copies, waits for them, and re-layouts: 7.52 us -> 7.16 us
  transfers between devices with their start and end apart: 28 -> 16, of which waited for: 13 -> 9; matrix products, arithmetic and copies ran while one was open for 4% -> 4% of each run, Pallas kernels for 14% -> 11%
where the time goes in v3:
time: 213 us; the launch traced here: 212 us
  starting transfers between devices  76.7 us (36%)
  waiting for transfers between devices  74.4 us (35%)
  Pallas kernels  43.3 us (20%)
  local copies, waits for them, and re-layouts  12.5 us (6%)
  other arithmetic  3.54 us (2%)
    pallas_call x9, Pallas kernels, call(): pl.pallas_call(kernel, out_shape=out_shape, grid=(1,) if specs else (), i...  43.3 us
    ppermute x7, waiting for transfers between devices, local(): lax.ppermute(chunks[j], 'harm', [(i, i ^ j) for i in range(GROUPS)])  31.2 us
    ppermute x7, starting transfers between devices, local(): lax.ppermute(chunks[j], 'harm', [(i, i ^ j) for i in range(GROUPS)])  22.1 us
    all_to_all x2, waiting for transfers between devices, local(): returned.append(lax.all_to_all(rates, 'harm', 0, 0, tiled=True))  18.2 us
    ppermute x1, waiting for transfers between devices, local(): velocity = lax.ppermute(late, both, swap)  16.5 us
    all_to_all x1, starting transfers between devices, local(): columns = lax.all_to_all(sent, everyone, 0, 0, tiled=True)  14.2 us
    all_to_all x2, starting transfers between devices, local(): returned.append(lax.all_to_all(rates, 'harm', 0, 0, tiled=True))  13.6 us
    all_to_all x1, starting transfers between devices, local(): mixed = lax.all_to_all(sent, everyone, 0, 0, tiled=True)  10.9 us
  transfers between devices with their start and end apart: 16, of which 9 were waited for; matrix products, arithmetic and copies ran while one was open for 4% of the time, Pallas kernels for 11%

profile of v3, /device:TPU:62, one launch (start us, length us, event | category | flops | bytes accessed | tf_op | source)
XLA Modules:
  0.0 212.2 jit_solution(16556739030289666818)
XLA Ops:
  0.6 0.8 fusion.2
  1.5 0.6 pad_maximum_fusion.table_ref
  2.1 4.8 %shard_map.203 = bf16[256,1280]{1,0:T(8,128)(2,1)} custom-call(f32[5,15]{1,0:T(8,128)} %pad_maximum_fusion.table_ref, bf16[15,256,256]{2,1,0:T(8,128)(2,1)} %bitcast.29, bf16[256,256]{1,0:T(8,128)(2,1)} %constant.102.clone.high_ref, bf16[256,256]{1,0:T(8,128)(2,1)} %constant.103.clone.low_ref), custom_call_target="tpu_custom_call" | custom-call | flops 1073741824 | bytes 3145728 | tf_op jit(solution)/shard_map/pallas_call | solution.py:332
  7.5 2.2 %reduce = bf16[256,1280]{1,0:T(8,128)(2,1)S(1)} reduce(bf16[256,1,1280]{2,0,1:T(8,128)(2,1)} %bitcast.32, bf16[]{:T(256)} %broadcast.14), dimensions={1}, to_apply=%copy.39.reduce_sub_computation | reduce | bytes 1310722 | tf_op jit(solution)/shard_map/all_to_all | solution.py:407
  9.7 1.0 reshape.60
  10.7 14.2 %all-to-all-start = ((bf16[256,2,640]{2,1,0:T(2,128)(2,1)}), bf16[256,2,640]{2,1,0:T(2,128)(2,1)S(1)}, u32[]{:S(2)}, u32[]{:S(2)}) async-start(bf16[256,2,640]{2,1,0:T(2,128)(2,1)} %reshape.60), calls=%async_computation | async-start | bytes 1310720 | tf_op jit(solution)/shard_map/all_to_all | solution.py:407
  24.9 6.0 %shard_map.204 = (bf16[16,8192]{1,0:T(8,128)(2,1)}, bf16[16,8192]{1,0:T(8,128)(2,1)}, bf16[16,8192]{1,0:T(8,128)(2,1)}, bf16[16,8192]{1,0:T(8,128)(2,1)}, bf16[1...) custom-call(s32[1]{0:T(128)S(6)} %xor.10.block_ref, ...), custom_call_target="tpu_custom_call" | custom-call | bytes 4194304 | tf_op jit(solution)/shard_map/pallas_call | solution.py:332
  30.9 0.8 collective-permute-start
  31.7 1.1 collective-permute-start.1
  32.9 2.7 %collective-permute-start.2 = (bf16[16,8192]{1,0:T(8,128)(2,1)}, bf16[16,8192]{1,0:T(8,128)(2,1)S(1)}, u32[]{:S(2)}, u32[]{:S(2)}) collective-permute-start(bf16[16,8192]{1,0:T(8,128)(2,1)} %get-tuple-element.28), channel_id=1, source_target_pairs={{0,3},{1,2},{2,1},{3,0},{4,7},{5,6},{6,5},{7,4},{8,11},{9,10},{10,... | collective-permute-start | bytes 786440 | tf_op jit(solution)/shard_map/ppermute | solution.py:416
  35.6 5.5 %collective-permute-start.3 = (bf16[16,8192]{1,0:T(8,128)(2,1)}, bf16[16,8192]{1,0:T(8,128)(2,1)S(1)}, u32[]{:S(2)}, u32[]{:S(2)}) collective-permute-start(bf16[16,8192]{1,0:T(8,128)(2,1)} %get-tuple-element.29), channel_id=1, source_target_pairs={{0,4},{1,5},{2,6},{3,7},{4,0},{5,1},{6,2},{7,3},{8,12},{9,13},{10,... | collective-permute-start | bytes 786440 | tf_op jit(solution)/shard_map/ppermute | solution.py:416
  41.1 1.7 collective-permute-done.refs_1_
  42.8 5.5 %collective-permute-start.5 = (bf16[16,8192]{1,0:T(8,128)(2,1)}, bf16[16,8192]{1,0:T(8,128)(2,1)S(1)}, u32[]{:S(2)}, u32[]{:S(2)}) collective-permute-start(bf16[16,8192]{1,0:T(8,128)(2,1)} %get-tuple-element.31), channel_id=1, source_target_pairs={{0,6},{1,7},{2,4},{3,5},{4,2},{5,3},{6,0},{7,1},{8,14},{9,15},{10,... | collective-permute-start | bytes 786440 | tf_op jit(solution)/shard_map/ppermute | solution.py:416
  48.5 6.3 %collective-permute-start.6 = (bf16[16,8192]{1,0:T(8,128)(2,1)}, bf16[16,8192]{1,0:T(8,128)(2,1)}, u32[]{:S(2)}, u32[]{:S(2)}) collective-permute-start(bf16[16,8192]{1,0:T(8,128)(2,1)} %get-tuple-element.32), channel_id=1, source_target_pairs={{0,7},{1,6},{2,5},{3,4},{4,3},{5,2},{6,1},{7,0},{8,15},{9,14},{10,... | collective-permute-start | bytes 786440 | tf_op jit(solution)/shard_map/ppermute | solution.py:416
  55.3 0.9 copy.50
  56.2 4.0 %shard_map.205 = bf16[256,512]{1,0:T(8,128)(2,1)} custom-call(f32[1]{0:T(128)} %bitcast.5.wave_ref, s32[1]{0:T(128)} %bitcast.6.half_ref, f32[1,256]{1,0:T(1,128)} %constant.104.clone.ky_ref, f32[32,1]{1,0:T(8,128)} %constant.105.clone.kz_ref, bf16[256,1280]{1,0:T(8,128)(2,1)} %bitcast.33, bf16[64,256]{1,0:T(8,128)(2,1)} %constant.106.clone.fz_high, ...), custom_call_target="tpu_custom_call" | custom-call | flops 1073741824 | bytes 3145728 | tf_op jit(solution)/shard_map/pallas_call | solution.py:332
  60.3 6.8 %collective-permute-done.3.refs_4_ = bf16[16,8192]{1,0:T(8,128)(2,1)S(1)} collective-permute-done((bf16[16,8192]{1,0:T(8,128)(2,1)}, bf16[16,8192]{1,0:T(8,128)(2,1)S(1)}, u32[]{:S(2)}, u32[]{:S(2)}) %collective-permute-start.3) | collective-permute-done | bytes 262176 | tf_op jit(solution)/shard_map/ppermute | solution.py:416
  67.1 11.0 %collective-permute-done.4.refs_5_ = bf16[16,8192]{1,0:T(8,128)(2,1)S(1)} collective-permute-done((bf16[16,8192]{1,0:T(8,128)(2,1)}, bf16[16,8192]{1,0:T(8,128)(2,1)S(1)}, u32[]{:S(2)}, u32[]{:S(2)}) %collective-permute-start.4) | collective-permute-done | bytes 262176 | tf_op jit(solution)/shard_map/ppermute | solution.py:416
  78.1 7.1 %collective-permute-done.5.refs_6_ = bf16[16,8192]{1,0:T(8,128)(2,1)S(1)} collective-permute-done((bf16[16,8192]{1,0:T(8,128)(2,1)}, bf16[16,8192]{1,0:T(8,128)(2,1)S(1)}, u32[]{:S(2)}, u32[]{:S(2)}) %collective-permute-start.5) | collective-permute-done | bytes 262176 | tf_op jit(solution)/shard_map/ppermute | solution.py:416
  85.2 4.5 %collective-permute-done.6.refs_7_ = bf16[16,8192]{1,0:T(8,128)(2,1)} collective-permute-done((bf16[16,8192]{1,0:T(8,128)(2,1)}, bf16[16,8192]{1,0:T(8,128)(2,1)}, u32[]{:S(2)}, u32[]{:S(2)}) %collective-permute-start.6) | collective-permute-done | bytes 262176 | tf_op jit(solution)/shard_map/ppermute | solution.py:416
  89.8 3.0 %shard_map.206.center_ref.yhigh_ref.ylow_ref = bf16[128,8192]{1,0:T(8,128)(2,1)} custom-call(s32[1]{0:T(128)} %bitcast.group_ref, bf16[16,8192]{1,0:T(8,128)(2,1)} %get-tuple-element.33.refs_0_, bf16[16,8192]{1,0:T(8,128)(2,1)} %copy-done.2, bf16[16,8192]{1,0:T(8,128)(2,1)} %copy-done.3, bf16[16,8192]{1,0:T(8,128)(2,1)} %copy-done.4, ...), custom_call_target="tpu_custom_call" | custom-call | bytes 4194304 | tf_op jit(solution)/shard_map/pallas_call | solution.py:332
  93.3 0.8 reduce.1
  94.1 0.8 reshape.62
  94.9 10.9 %all-to-all-start.1 = ((bf16[256,2,256]{2,1,0:T(2,128)(2,1)}), bf16[256,2,256]{2,1,0:T(2,128)(2,1)S(1)}, u32[]{:S(2)}, u32[]{:S(2)}) async-start(bf16[256,2,256]{2,1,0:T(2,128)(2,1)} %reshape.62), calls=%async_computation.1 | async-start | bytes 524288 | tf_op jit(solution)/shard_map/all_to_all | solution.py:431
  106.0 0.7 broadcast_in_dim_reshape.4.damp_ref
  106.7 0.6 pad.17
  107.4 0.7 copy.41.synth_ref
  108.2 0.7 pad.18
  108.9 0.9 fusion.5
  109.8 0.9 collective-permute-start.10
  110.7 7.2 %collective-permute-start.9 = (bf16[128,256]{1,0:T(8,128)(2,1)S(1)}, bf16[128,256]{1,0:T(8,128)(2,1)S(1)}, u32[]{:S(2)}, u32[]{:S(2)}) collective-permute-start(bf16[128,256]{1,0:T(8,128)(2,1)S(1)} %get-tuple-element.55), channel_id=1, source_target_pairs={{0,1},{1,2},{2,3},{3,4},{4,5},{5,6},{6,7},{7,0},{8,9},{9,10},{10,1... | collective-permute-start | bytes 196616 | tf_op jit(solution)/shard_map/ppermute | solution.py:436
  117.9 2.5 %shard_map.208.weight_ref = bf16[128,1536]{1,0:T(8,128)(2,1)} custom-call(f32[3,256]{1,0:T(4,128)} %constant.113.clone.dir_ref, bf16[256,128]{1,0:T(8,128)(2,1)} %copy.41.synth_ref, bf16[128,256]{1,0:T(8,128)(2,1)} %bitcast.39, bf16[3,128,256]{2,1,0:T(8,128)(2,1)} %bitcast.37), custom_call_target="tpu_custom_call" | custom-call | flops 268435456 | bytes 1048576 | tf_op jit(solution)/shard_map/pallas_call | solution.py:332
  120.4 8.4 %all-to-all-done.1 = bf16[256,2,256]{2,1,0:T(2,128)(2,1)S(1)} async-done(((bf16[256,2,256]{2,1,0:T(2,128)(2,1)}), bf16[256,2,256]{2,1,0:T(2,128)(2,1)S(1)}, u32[]{:S(2)}, u32[]{:S(2)}) %all-to-all-start.1) | async-done | bytes 262176 | tf_op jit(solution)/shard_map/all_to_all | solution.py:431
  129.0 0.7 copy.51
  129.7 2.8 %shard_map.207.flow_ref = f32[11,32,256]{2,1,0:T(8,128)} custom-call(bf16[256,512]{1,0:T(8,128)(2,1)} %bitcast.34, bf16[256,1024]{1,0:T(8,128)(2,1)} %constant.114.clone.high_ref, bf16[256,1024]{1,0:T(8,128)(2,1)} %constant.115.clone.low_ref), custom_call_target="tpu_custom_call" | custom-call | flops 536870912 | bytes 2097152 | tf_op jit(solution)/shard_map/pallas_call | solution.py:332
  132.6 0.6 copy-done.15
  133.2 0.8 copy-done.13
  134.0 8.6 %shard_map.210 = bf16[8,15,16,256]{3,2,1,0:T(8,128)(2,1)} custom-call(bf16[128,8192]{1,0:T(8,128)(2,1)} %shard_map.206.center_ref.yhigh_ref.ylow_ref, bf16[128,8192]{1,0:T(8,128)(2,1)} %collective-permute-done.7.zlow_ref, bf16[128,8192]{1,0:T(8,128)(2,1)} %copy-done.13, bf16[128,8192]{1,0:T(8,128)(2,1)} %shard_map.206.center_ref.yhigh_ref.ylow_ref, ...), custom_call_target="tpu_custom_call" | custom-call | flops 3758096384 | bytes 4718592 | tf_op jit(solution)/shard_map/pallas_call | solution.py:332
  142.6 9.1 %all-to-all-start.3 = ((bf16[8,15,16,256]{3,2,1,0:T(8,128)(2,1)}), bf16[8,15,16,256]{3,2,1,0:T(8,128)(2,1)S(1)}, u32[]{:S(2)}, u32[]{:S(2)}) async-start(bf16[8,15,16,256]{3,2,1,0:T(8,128)(2,1)} %shard_map.210), calls=%async_computation.3 | async-start | bytes 1966080 | tf_op jit(solution)/shard_map/all_to_all | solution.py:477
  151.7 8.6 %shard_map.209 = bf16[8,15,16,256]{3,2,1,0:T(8,128)(2,1)} custom-call(bf16[128,8192]{1,0:T(8,128)(2,1)} %shard_map.206.center_ref.yhigh_ref.ylow_ref, bf16[128,8192]{1,0:T(8,128)(2,1)} %collective-permute-done.7.zlow_ref, bf16[128,8192]{1,0:T(8,128)(2,1)} %copy-done.13, bf16[128,256]{1,0:T(8,128)(2,1)} %copy-done.14, ...), custom_call_target="tpu_custom_call" | custom-call | flops 3758096384 | bytes 4718592 | tf_op jit(solution)/shard_map/pallas_call | solution.py:332
  160.3 18.2 %all-to-all-done.3.refs_1_ = bf16[8,15,16,256]{3,2,1,0:T(8,128)(2,1)S(1)} async-done(((bf16[8,15,16,256]{3,2,1,0:T(8,128)(2,1)}), bf16[8,15,16,256]{3,2,1,0:T(8,128)(2,1)S(1)}, u32[]{:S(2)}, u32[]{:S(2)}) %all-to-all-start.3) | async-done | bytes 983072 | tf_op jit(solution)/shard_map/all_to_all | solution.py:477
  178.5 4.5 %all-to-all-start.2 = ((bf16[8,15,16,256]{3,2,1,0:T(8,128)(2,1)}), bf16[8,15,16,256]{3,2,1,0:T(8,128)(2,1)S(1)}, u32[]{:S(2)}, u32[]{:S(2)}) async-start(bf16[8,15,16,256]{3,2,1,0:T(8,128)(2,1)} %shard_map.209), calls=%async_computation.2 | async-start | bytes 1966080 | tf_op jit(solution)/shard_map/all_to_all | solution.py:477
  183.0 0.9 slice.26
  183.9 7.3 %collective-permute-start.11 = (f32[3,32,256]{2,1,0:T(8,128)S(1)}, f32[3,32,256]{2,1,0:T(8,128)S(1)}, u32[]{:S(2)}, u32[]{:S(2)}) collective-permute-start(f32[3,32,256]{2,1,0:T(8,128)S(1)} %slice.26), channel_id=1, source_target_pairs={{0,0},{1,1},{2,2},{3,3},{4,4},{5,5},{6,6},{7,7},{8,8},{9,9},{10,10... | collective-permute-start | bytes 294920 | tf_op jit(solution)/shard_map/ppermute | solution.py:480
  191.2 16.5 %collective-permute-done.11 = f32[3,32,256]{2,1,0:T(8,128)S(1)} collective-permute-done((f32[3,32,256]{2,1,0:T(8,128)S(1)}, f32[3,32,256]{2,1,0:T(8,128)S(1)}, u32[]{:S(2)}, u32[]{:S(2)}) %collective-permute-start.11) | collective-permute-done | bytes 98336 | tf_op jit(solution)/shard_map/ppermute | solution.py:480
  207.7 0.9 copy-done.1
  208.7 2.9 %shard_map.211 = bf16[15,256,256]{2,1,0:T(8,128)(2,1)} custom-call(s32[1]{0:T(128)S(6)} %xor.11.swap_ref, bf16[8,15,16,256]{3,2,1,0:T(8,128)(2,1)} %copy-done.1, bf16[8,15,16,256]{3,2,1,0:T(8,128)(2,1)} %copy-done), custom_call_target="tpu_custom_call" | custom-call | bytes 4194304 | tf_op jit(solution)/shard_map/pallas_call | solution.py:332
  211.6 0.6 copy.55
  (52 shorter events, 2.3 us)
Async XLA Ops:
  10.7 44.1 %all-to-all-start = ((bf16[256,2,640]{2,1,0:T(2,128)(2,1)}), bf16[256,2,640]{2,1,0:T(2,128)(2,1)S(1)}, u32[]{:S(2)}, u32[]{:S(2)}) async-start(bf16[256,2,640]{2,1,0:T(2,128)(2,1)} %reshape.60), calls=%async_computation | async-start | bytes 1310720 | tf_op jit(solution)/shard_map/all_to_all | solution.py:407
  30.9 11.9 %collective-permute-start = (bf16[16,8192]{1,0:T(8,128)(2,1)}, bf16[16,8192]{1,0:T(8,128)(2,1)S(1)}, u32[]{:S(2)}, u32[]{:S(2)}) collective-permute-start(bf16[16,8192]{1,0:T(8,128)(2,1)} %get-tuple-element.26), channel_id=1, source_target_pairs={{0,1},{1,0},{2,3},{3,2},{4,5},{5,4},{6,7},{7,6},{8,9},{9,8},{10,11... | collective-permute-start | bytes 786440 | tf_op jit(solution)/shard_map/ppermute | solution.py:416
  31.7 16.8 %collective-permute-start.1 = (bf16[16,8192]{1,0:T(8,128)(2,1)}, bf16[16,8192]{1,0:T(8,128)(2,1)S(1)}, u32[]{:S(2)}, u32[]{:S(2)}) collective-permute-start(bf16[16,8192]{1,0:T(8,128)(2,1)} %get-tuple-element.27), channel_id=1, source_target_pairs={{0,2},{1,3},{2,0},{3,1},{4,6},{5,7},{6,4},{7,5},{8,10},{9,11},{10,... | collective-permute-start | bytes 786440 | tf_op jit(solution)/shard_map/ppermute | solution.py:416
  32.9 27.4 %collective-permute-start.2 = (bf16[16,8192]{1,0:T(8,128)(2,1)}, bf16[16,8192]{1,0:T(8,128)(2,1)S(1)}, u32[]{:S(2)}, u32[]{:S(2)}) collective-permute-start(bf16[16,8192]{1,0:T(8,128)(2,1)} %get-tuple-element.28), channel_id=1, source_target_pairs={{0,3},{1,2},{2,1},{3,0},{4,7},{5,6},{6,5},{7,4},{8,11},{9,10},{10,... | collective-permute-start | bytes 786440 | tf_op jit(solution)/shard_map/ppermute | solution.py:416
  35.6 31.5 %collective-permute-start.3 = (bf16[16,8192]{1,0:T(8,128)(2,1)}, bf16[16,8192]{1,0:T(8,128)(2,1)S(1)}, u32[]{:S(2)}, u32[]{:S(2)}) collective-permute-start(bf16[16,8192]{1,0:T(8,128)(2,1)} %get-tuple-element.29), channel_id=1, source_target_pairs={{0,4},{1,5},{2,6},{3,7},{4,0},{5,1},{6,2},{7,3},{8,12},{9,13},{10,... | collective-permute-start | bytes 786440 | tf_op jit(solution)/shard_map/ppermute | solution.py:416
  41.1 37.0 %collective-permute-start.4 = (bf16[16,8192]{1,0:T(8,128)(2,1)}, bf16[16,8192]{1,0:T(8,128)(2,1)S(1)}, u32[]{:S(2)}, u32[]{:S(2)}) collective-permute-start(bf16[16,8192]{1,0:T(8,128)(2,1)} %get-tuple-element.30), channel_id=1, source_target_pairs={{0,5},{1,4},{2,7},{3,6},{4,1},{5,0},{6,3},{7,2},{8,13},{9,12},{10,... | collective-permute-start | bytes 786440 | tf_op jit(solution)/shard_map/ppermute | solution.py:416
  42.8 17.4 %copy-start.2 = (bf16[16,8192]{1,0:T(8,128)(2,1)}, bf16[16,8192]{1,0:T(8,128)(2,1)S(1)}, u32[]{:S(2)}) copy-start(bf16[16,8192]{1,0:T(8,128)(2,1)S(1)} %collective-permute-done.refs_1_) | copy-start | bytes 786436
  42.8 42.4 %collective-permute-start.5 = (bf16[16,8192]{1,0:T(8,128)(2,1)}, bf16[16,8192]{1,0:T(8,128)(2,1)S(1)}, u32[]{:S(2)}, u32[]{:S(2)}) collective-permute-start(bf16[16,8192]{1,0:T(8,128)(2,1)} %get-tuple-element.31), channel_id=1, source_target_pairs={{0,6},{1,7},{2,4},{3,5},{4,2},{5,3},{6,0},{7,1},{8,14},{9,15},{10,... | collective-permute-start | bytes 786440 | tf_op jit(solution)/shard_map/ppermute | solution.py:416
  48.5 11.8 %copy-start.3 = (bf16[16,8192]{1,0:T(8,128)(2,1)}, bf16[16,8192]{1,0:T(8,128)(2,1)S(1)}, u32[]{:S(2)}) copy-start(bf16[16,8192]{1,0:T(8,128)(2,1)S(1)} %collective-permute-done.1.refs_2_) | copy-start | bytes 786436
  48.5 41.2 %collective-permute-start.6 = (bf16[16,8192]{1,0:T(8,128)(2,1)}, bf16[16,8192]{1,0:T(8,128)(2,1)}, u32[]{:S(2)}, u32[]{:S(2)}) collective-permute-start(bf16[16,8192]{1,0:T(8,128)(2,1)} %get-tuple-element.32), channel_id=1, source_target_pairs={{0,7},{1,6},{2,5},{3,4},{4,3},{5,2},{6,1},{7,0},{8,15},{9,14},{10,... | collective-permute-start | bytes 786440 | tf_op jit(solution)/shard_map/ppermute | solution.py:416
  60.3 29.4 %copy-start.4 = (bf16[16,8192]{1,0:T(8,128)(2,1)}, bf16[16,8192]{1,0:T(8,128)(2,1)S(1)}, u32[]{:S(2)}) copy-start(bf16[16,8192]{1,0:T(8,128)(2,1)S(1)} %collective-permute-done.2.refs_3_) | copy-start | bytes 786436
  67.1 22.7 %copy-start.5 = (bf16[16,8192]{1,0:T(8,128)(2,1)}, bf16[16,8192]{1,0:T(8,128)(2,1)S(1)}, u32[]{:S(2)}) copy-start(bf16[16,8192]{1,0:T(8,128)(2,1)S(1)} %collective-permute-done.3.refs_4_) | copy-start | bytes 786436
  78.1 11.6 %copy-start.6 = (bf16[16,8192]{1,0:T(8,128)(2,1)}, bf16[16,8192]{1,0:T(8,128)(2,1)S(1)}, u32[]{:S(2)}) copy-start(bf16[16,8192]{1,0:T(8,128)(2,1)S(1)} %collective-permute-done.4.refs_5_) | copy-start | bytes 786436
  85.2 4.5 %copy-start.7 = (bf16[16,8192]{1,0:T(8,128)(2,1)}, bf16[16,8192]{1,0:T(8,128)(2,1)S(1)}, u32[]{:S(2)}) copy-start(bf16[16,8192]{1,0:T(8,128)(2,1)S(1)} %collective-permute-done.5.refs_6_) | copy-start | bytes 786436
  89.7 3.6 %copy-start.8 = (bf16[256,512]{1,0:T(8,128)(2,1)S(1)}, bf16[256,512]{1,0:T(8,128)(2,1)}, u32[]{:S(2)}) copy-start(bf16[256,512]{1,0:T(8,128)(2,1)} %shard_map.205) | copy-start | bytes 786436
  89.7 16.1 %copy-start.10 = (bf16[256,120]{0,1:T(8,128)(2,1)S(1)}, bf16[256,120]{0,1:T(8,128)(2,1)}, u32[]{:S(2)}) copy-start(bf16[256,120]{0,1:T(8,128)(2,1)} %param.21) | copy-start | bytes 184324
  89.7 16.1 %copy-start.12 = (f32[120]{0:T(128)S(1)}, f32[120]{0:T(128)}, u32[]{:S(2)}) copy-start(f32[120]{0:T(128)} %param.24) | copy-start | bytes 1444
  89.8 16.9 %copy-start.11 = (bf16[120,256]{1,0:T(8,128)(2,1)S(1)}, bf16[120,256]{1,0:T(8,128)(2,1)}, u32[]{:S(2)}) copy-start(bf16[120,256]{1,0:T(8,128)(2,1)} %param.22) | copy-start | bytes 184324
  92.8 15.3 %copy-start.9 = (bf16[3,120,256]{2,1,0:T(8,128)(2,1)S(1)}, bf16[3,120,256]{2,1,0:T(8,128)(2,1)}, u32[]{:S(2)}) copy-start(bf16[3,120,256]{2,1,0:T(8,128)(2,1)} %param.23) | copy-start | bytes 552964
  92.8 39.8 %collective-permute-start.8 = (bf16[128,8192]{1,0:T(8,128)(2,1)}, bf16[128,8192]{1,0:T(8,128)(2,1)S(1)}, u32[]{:S(2)}, u32[]{:S(2)}) collective-permute-start(bf16[128,8192]{1,0:T(8,128)(2,1)} %shard_map.206.center_ref.yhigh_ref.ylow_ref), channel_id=1, source_target_pairs={{0,252},{1,253},{2,254},{3,255},{4,248},{5,249},{6,250},{7,251},{8... | collective-permute-start | bytes 6291464 | tf_op jit(solution)/shard_map/ppermute | solution.py:435
  92.8 39.8 %collective-permute-start.7 = (bf16[128,8192]{1,0:T(8,128)(2,1)}, bf16[128,8192]{1,0:T(8,128)(2,1)}, u32[]{:S(2)}, u32[]{:S(2)}) collective-permute-start(bf16[128,8192]{1,0:T(8,128)(2,1)} %shard_map.206.center_ref.yhigh_ref.ylow_ref), channel_id=1, source_target_pairs={{0,8},{1,9},{2,10},{3,11},{4,12},{5,13},{6,14},{7,15},{8,16},{9,17... | collective-permute-start | bytes 6291464 | tf_op jit(solution)/shard_map/ppermute | solution.py:434
  94.9 33.9 %all-to-all-start.1 = ((bf16[256,2,256]{2,1,0:T(2,128)(2,1)}), bf16[256,2,256]{2,1,0:T(2,128)(2,1)S(1)}, u32[]{:S(2)}, u32[]{:S(2)}) async-start(bf16[256,2,256]{2,1,0:T(2,128)(2,1)} %reshape.62), calls=%async_computation.1 | async-start | bytes 524288 | tf_op jit(solution)/shard_map/all_to_all | solution.py:431
  109.8 22.8 %collective-permute-start.10 = (bf16[128,256]{1,0:T(8,128)(2,1)S(1)}, bf16[128,256]{1,0:T(8,128)(2,1)S(1)}, u32[]{:S(2)}, u32[]{:S(2)}) collective-permute-start(bf16[128,256]{1,0:T(8,128)(2,1)S(1)} %get-tuple-element.54), channel_id=1, source_target_pairs={{0,7},{1,0},{2,1},{3,2},{4,3},{5,4},{6,5},{7,6},{8,15},{9,8},{10,9... | collective-permute-start | bytes 196616 | tf_op jit(solution)/shard_map/ppermute | solution.py:437
  110.7 21.9 %collective-permute-start.9 = (bf16[128,256]{1,0:T(8,128)(2,1)S(1)}, bf16[128,256]{1,0:T(8,128)(2,1)S(1)}, u32[]{:S(2)}, u32[]{:S(2)}) collective-permute-start(bf16[128,256]{1,0:T(8,128)(2,1)S(1)} %get-tuple-element.55), channel_id=1, source_target_pairs={{0,1},{1,2},{2,3},{3,4},{4,5},{5,6},{6,7},{7,0},{8,9},{9,10},{10,1... | collective-permute-start | bytes 196616 | tf_op jit(solution)/shard_map/ppermute | solution.py:436
  132.6 0.6 copy-start.15
  132.6 10.0 %copy-start.14 = (bf16[128,256]{1,0:T(8,128)(2,1)}, bf16[128,256]{1,0:T(8,128)(2,1)S(1)}, u32[]{:S(2)}) copy-start(bf16[128,256]{1,0:T(8,128)(2,1)S(1)} %collective-permute-done.9.ylow_ref) | copy-start | bytes 196612
  132.6 1.4 copy-start.13
  142.6 36.0 %all-to-all-start.3 = ((bf16[8,15,16,256]{3,2,1,0:T(8,128)(2,1)}), bf16[8,15,16,256]{3,2,1,0:T(8,128)(2,1)S(1)}, u32[]{:S(2)}, u32[]{:S(2)}) async-start(bf16[8,15,16,256]{3,2,1,0:T(8,128)(2,1)} %shard_map.210), calls=%async_computation.3 | async-start | bytes 1966080 | tf_op jit(solution)/shard_map/all_to_all | solution.py:477
  178.5 29.2 %copy-start = (bf16[8,15,16,256]{3,2,1,0:T(8,128)(2,1)}, bf16[8,15,16,256]{3,2,1,0:T(8,128)(2,1)S(1)}, u32[]{:S(2)}) copy-start(bf16[8,15,16,256]{3,2,1,0:T(8,128)(2,1)S(1)} %all-to-all-done.3.refs_1_) | copy-start | bytes 2949124
  178.5 29.2 %all-to-all-start.2 = ((bf16[8,15,16,256]{3,2,1,0:T(8,128)(2,1)}), bf16[8,15,16,256]{3,2,1,0:T(8,128)(2,1)S(1)}, u32[]{:S(2)}, u32[]{:S(2)}) async-start(bf16[8,15,16,256]{3,2,1,0:T(8,128)(2,1)} %shard_map.209), calls=%async_computation.2 | async-start | bytes 1966080 | tf_op jit(solution)/shard_map/all_to_all | solution.py:477
  183.9 23.8 %collective-permute-start.11 = (f32[3,32,256]{2,1,0:T(8,128)S(1)}, f32[3,32,256]{2,1,0:T(8,128)S(1)}, u32[]{:S(2)}, u32[]{:S(2)}) collective-permute-start(f32[3,32,256]{2,1,0:T(8,128)S(1)} %slice.26), channel_id=1, source_target_pairs={{0,0},{1,1},{2,2},{3,3},{4,4},{5,5},{6,6},{7,7},{8,8},{9,9},{10,10... | collective-permute-start | bytes 294920 | tf_op jit(solution)/shard_map/ppermute | solution.py:480
  207.7 0.9 copy-start.1

commit v4 on v2

--- a/solution.py
+++ b/solution.py
@@ -108,7 +108,7 @@
 
 
 def regroup_kernel(block_ref, coef_ref, *refs):
-    near, far, stages = refs[:FLIP], refs[FLIP], refs[FLIP + 1 :]
+    near, rest, last, stages = refs[:FLIP], refs[FLIP], refs[FLIP + 1], refs[FLIP + 2 :]
     block = block_ref[0]
     height = ROWS + 2 * PAD
     for stage in stages:
@@ -128,8 +128,11 @@
                 rows = stage[pl.ds(PAD - 1 + r, PAD, stride=height), :]
                 if j < FLIP:
                     near[j][:, lane : lane + LANES] = rows.astype(bf16)
+                elif j == FLIP:
+                    last[:, lane : lane + LANES] = rows.astype(bf16)
                 else:
-                    far[(j - FLIP) * PAD : (j - FLIP + 1) * PAD, lane : lane + LANES] = rows.astype(bf16)
+                    at = (j - FLIP - 1) * PAD
+                    rest[at : at + PAD, lane : lane + LANES] = rows.astype(bf16)
 
 
 def stress_kernel(table_ref, coef_ref, high_ref, low_ref, out_ref, stress_high, stress_low):
@@ -312,9 +315,9 @@
     lax.fori_loop(0, ROWS // 2, rows, 0)
 
 
-def rate_kernel(group_ref, inner_ref, zlow_ref, zhigh_ref, flow_ref, weight_ref, *refs):
-    outs, (operands, locals_, *stages) = refs[:GROUPS], refs[GROUPS:]
-    group = group_ref[0]
+def rate_kernel(
+    inner_ref, zlow_ref, zhigh_ref, flow_ref, weight_ref, out_ref, operands, locals_, *stages
+):
     skip = (BLOCKS - 2) * ALL_PAD
 
     def build(r, operand, local_terms):
@@ -341,21 +344,21 @@
         return carry
 
     lax.fori_loop(0, CHUNK // 2, rows, 0)
-    for j in range(GROUPS):
+    for g in range(GROUPS):
         for c in range(OWN):
-            first = pl.multiple_of(((group ^ j) * PAD + c) * CHUNK, CHUNK)
+            first = (g * PAD + c) * CHUNK
             for side, stage in enumerate(stages):
-                outs[j][c, :, side * LANES : (side + 1) * LANES] = stage[
-                    pl.ds(first, CHUNK), :
+                out_ref[g, c, :, side * LANES : (side + 1) * LANES] = stage[
+                    first : first + CHUNK, :
                 ].astype(bf16)
 
 
-def place_kernel(block_ref, *refs):
+def place_kernel(swap_ref, *refs):
     out_ref = refs[-1]
     for part in range(PARTS):
-        for j in range(GROUPS):
-            first = pl.multiple_of((block_ref[0] ^ j) * ROWS + part * CHUNK, CHUNK)
-            out_ref[:, pl.ds(first, CHUNK), :] = refs[part * GROUPS + j][...]
+        for g in range(GROUPS):
+            first = pl.multiple_of((swap_ref[0] ^ g) * ROWS + part * CHUNK, CHUNK)
+            out_ref[:, pl.ds(first, CHUNK), :] = refs[part][g]
 
 
 def call(kernel, out_shape, ins, scratch=(), scalars=0, flops=0, byte_count=0, specs=None):
@@ -446,12 +449,15 @@
 
     later, _ = lax.optimization_barrier((own, sent))
     chunks = call(
-        regroup_kernel, [shape(PAD, CELLS)] * FLIP + [shape(FLIP * PAD, CELLS)], [block_arg, later],
+        regroup_kernel,
+        [shape(PAD, CELLS)] * FLIP + [shape((FLIP - 1) * PAD, CELLS), shape(PAD, CELLS)], [block_arg, later],
         [pltpu.VMEM((PAD * (ROWS + 2 * PAD), LANES), f32)] * 2, 1, 0, 4 << 20,
     )
-    crossed = lax.ppermute(chunks[FLIP], "harm", partner(FLIP))
+    chunks, columns = lax.optimization_barrier((chunks, columns))
+    rest = lax.ppermute(chunks[FLIP], "harm", partner(FLIP))
+    last = lax.ppermute(chunks[FLIP + 1], "harm", partner(FLIP))
     arrived = exchanged(chunks[:FLIP])
-    arrived += exchanged([crossed[m * PAD : (m + 1) * PAD] for m in range(FLIP)])
+    arrived += exchanged([last] + [rest[m * PAD : (m + 1) * PAD] for m in range(FLIP - 1)])
 
     wave = (position % HALF).astype(f32) * (2.0 * math.pi / NX)
     half = (position // HALF).astype(jnp.int32)
@@ -481,39 +487,39 @@
         (), 0, 1 << 28, 1 << 20,
     )
     flow = call(fields_kernel, shape(11, ROWS, NX, dtype=f32), [mixed, *split_table(back_x)], (), 0, 1 << 29, 2 << 20)
-    swap = pairs(lambda s, b: (s, b ^ (FLIP * odd(s))))
-    velocity = lax.ppermute(flow[0:3], both, swap)
-    flow, velocity = lax.optimization_barrier((flow, velocity))
-
     damp = pad_groups(damping, 0)[:, None]
     inner = call(
         inner_kernel, shape(ALL_PAD, ROWS * NX, dtype=f32), [center, flow, weights, damp],
         [pltpu.VMEM((2, (BLOCKS - 2) * ALL_PAD, NX), bf16), pltpu.VMEM((2, ALL_PAD, NX), f32)],
         0, 6 << 30, 7 << 20,
     )
-    returned = []
+    returned, parts = [], []
     for part in range(PARTS):
         here = pl.BlockSpec((ALL_PAD, CHUNK * NX), lambda i, part=part: (0, part))
         beyond = pl.BlockSpec(
             (pl.Element(ALL_PAD), pl.Element(CHUNK * NX)), lambda i, part=part: (0, (part * CHUNK + 1) * NX)
         )
         rates = call(
-            rate_kernel, [shape(OWN, CHUNK, NX)] * GROUPS,
-            [group_arg, inner, z_low, z_high, flow, weights],
+            rate_kernel, shape(GROUPS, OWN, CHUNK, NX),
+            [inner, z_low, z_high, flow, weights],
             [
                 pltpu.VMEM((2, 2 * ALL_PAD, NX), bf16),
                 pltpu.VMEM((2, ALL_PAD, NX), f32),
                 pltpu.VMEM((ALL_PAD * CHUNK, LANES), f32),
                 pltpu.VMEM((ALL_PAD * CHUNK, LANES), f32),
             ],
-            1, 1 << 29, 9 << 19,
+            0, 1 << 29, 9 << 19,
             [
-                SMEM, here, beyond, beyond,
+                here, beyond, beyond,
                 pl.BlockSpec((11, CHUNK, NX), lambda i, part=part: (0, part, 0)), VMEM,
             ],
         )
-        returned += exchanged(rates)
-    rate = call(place_kernel, shape(OWN, NY, NX), [block_arg, *returned], (), 1, 0, 4 << 20)
+        parts.append(rates)
+        returned.append(lax.all_to_all(rates, "harm", 0, 0, tiled=True))
+    swap = pairs(lambda s, b: (s, b ^ (FLIP * odd(s))))
+    late, _ = lax.optimization_barrier((flow[0:3], parts[0]))
+    velocity = lax.ppermute(late, both, swap)
+    rate = call(place_kernel, shape(OWN, NY, NX), [group_arg ^ block_arg, *returned], (), 1, 0, 4 << 20)
     return (rate.reshape(OWN, 1, NY, NX), velocity.reshape(3, 1, ROWS, NX))
 
 

time: 249 us -> 221 us (0.89)
  starting transfers between devices: 130 us -> 63.2 us
  waiting for transfers between devices: 46.4 us -> 84.1 us
    all_to_all x1, starting transfers between devices: 54.9 us -> 12.5 us  [local(): mixed = lax.all_to_all(sent, everyone, 0, 0, tiled=True)]
    ppermute x20 -> x6, starting transfers between devices: 47 us -> 9.64 us  [exchanged(): lax.ppermute(c, 'harm', partner(j + 1))]
    all_to_all x0 -> x2, waiting for transfers between devices: none -> 20 us  [local(): returned.append(lax.all_to_all(rates, 'harm', 0, 0, tiled=True))]
    ppermute x2 -> x3, waiting for transfers between devices: 18 us -> 31.9 us  [the longest x1 18 us: local(): velocity = lax.ppermute(late, both, swap)]
    all_to_all x0 -> x2, starting transfers between devices: none -> 11.3 us  [local(): returned.append(lax.all_to_all(rates, 'harm', 0, 0, tiled=True))]
    ppermute x20 -> x6, waiting for transfers between devices: 17.6 us -> 6.47 us  [exchanged(): lax.ppermute(c, 'harm', partner(j + 1))]
    all_to_all x1, waiting for transfers between devices: 4.36 us -> 14.1 us  [local(): columns = lax.all_to_all(sent, everyone, 0, 0, tiled=True)]
    ppermute x1, waiting for transfers between devices: 0.01 us -> 4.68 us  [local(): lax.ppermute(center, both, pairs(lambda s, b: ((s + 1) % SPACES, b)))]
  transfers between devices with their start and end apart: 26 -> 15, of which waited for: 7 -> 8; matrix products, arithmetic and copies ran while one was open for 4% -> 4% of each run, Pallas kernels for 14% -> 15%
where the time goes in v4:
time: 221 us; the launch traced here: 217 us
  waiting for transfers between devices  84.1 us (38%)
  starting transfers between devices  63.2 us (29%)
  Pallas kernels  50.3 us (23%)
  local copies, waits for them, and re-layouts  13 us (6%)
  other arithmetic  4.37 us (2%)
    pallas_call x10, Pallas kernels, call(): pl.pallas_call(kernel, out_shape=out_shape, grid=(1,) if specs else (), i...  50.3 us
    all_to_all x2, waiting for transfers between devices, local(): returned.append(lax.all_to_all(rates, 'harm', 0, 0, tiled=True))  20 us
    ppermute x1, waiting for transfers between devices, local(): velocity = lax.ppermute(late, both, swap)  18 us
    all_to_all x1, starting transfers between devices, local(): columns = lax.all_to_all(sent, everyone, 0, 0, tiled=True)  14.2 us
    all_to_all x1, waiting for transfers between devices, local(): columns = lax.all_to_all(sent, everyone, 0, 0, tiled=True)  14.1 us
    ppermute x1, waiting for transfers between devices, local(): rest = lax.ppermute(chunks[FLIP], 'harm', partner(FLIP))  13.9 us
    all_to_all x1, starting transfers between devices, local(): mixed = lax.all_to_all(sent, everyone, 0, 0, tiled=True)  12.5 us
    all_to_all x2, starting transfers between devices, local(): returned.append(lax.all_to_all(rates, 'harm', 0, 0, tiled=True))  11.3 us
  transfers between devices with their start and end apart: 15, of which 8 were waited for; matrix products, arithmetic and copies ran while one was open for 4% of the time, Pallas kernels for 15%

profile of v4, /device:TPU:62, one launch (start us, length us, event | category | flops | bytes accessed | tf_op | source)
XLA Modules:
  0.0 216.7 jit_solution(1776050566730843778)
XLA Ops:
  0.6 0.8 fusion.2
  1.5 0.6 pad_maximum_fusion.table_ref
  2.1 4.8 %shard_map.203 = bf16[256,1280]{1,0:T(8,128)(2,1)} custom-call(f32[5,15]{1,0:T(8,128)} %pad_maximum_fusion.table_ref, bf16[15,256,256]{2,1,0:T(8,128)(2,1)} %bitcast.29, bf16[256,256]{1,0:T(8,128)(2,1)} %constant.102.clone.high_ref, bf16[256,256]{1,0:T(8,128)(2,1)} %constant.103.clone.low_ref), custom_call_target="tpu_custom_call" | custom-call | flops 1073741824 | bytes 3145728 | tf_op jit(solution)/shard_map/pallas_call | solution.py:365
  7.5 2.1 reduce
  9.6 1.0 reshape.60
  10.6 14.2 %all-to-all-start = ((bf16[256,2,640]{2,1,0:T(2,128)(2,1)}), bf16[256,2,640]{2,1,0:T(2,128)(2,1)S(1)}, u32[]{:S(2)}, u32[]{:S(2)}) async-start(bf16[256,2,640]{2,1,0:T(2,128)(2,1)} %reshape.60), calls=%async_computation | async-start | bytes 1310720 | tf_op jit(solution)/shard_map/all_to_all | solution.py:448
  24.8 6.2 %shard_map.204 = (bf16[16,8704]{1,0:T(8,128)(2,1)}, bf16[16,8704]{1,0:T(8,128)(2,1)}, bf16[16,8704]{1,0:T(8,128)(2,1)}, bf16[16,8704]{1,0:T(8,128)(2,1)}, bf16[4...) custom-call(s32[1]{0:T(128)S(6)} %xor.10.block_ref, bf16[15,256,256]{2,1,0:T(8,128)(2,1)} %bitcast.30), custom_call_target="tpu_custom_call" | custom-call | bytes 4194304 | tf_op jit(solution)/shard_map/pallas_call | solution.py:365
  31.0 14.1 %all-to-all-done = bf16[256,2,640]{2,1,0:T(2,128)(2,1)S(1)} async-done(((bf16[256,2,640]{2,1,0:T(2,128)(2,1)}), bf16[256,2,640]{2,1,0:T(2,128)(2,1)S(1)}, u32[]{:S(2)}, u32[]{:S(2)}) %all-to-all-start) | async-done | bytes 655392 | tf_op jit(solution)/shard_map/all_to_all | solution.py:448
  45.6 0.9 copy.46
  46.6 1.0 collective-permute-start.4
  47.6 4.0 %shard_map.205 = bf16[256,512]{1,0:T(8,128)(2,1)} custom-call(f32[1]{0:T(128)} %bitcast.6.wave_ref, s32[1]{0:T(128)} %bitcast.7.half_ref, f32[1,256]{1,0:T(1,128)} %constant.104.clone.ky_ref, f32[32,1]{1,0:T(8,128)} %constant.105.clone.kz_ref, bf16[256,1280]{1,0:T(8,128)(2,1)} %bitcast.33, bf16[64,256]{1,0:T(8,128)(2,1)} %constant.106.clone.fz_high, ...), custom_call_target="tpu_custom_call" | custom-call | flops 1073741824 | bytes 3145728 | tf_op jit(solution)/shard_map/pallas_call | solution.py:365
  51.6 1.7 reduce.1
  53.3 0.8 reshape.62
  54.0 12.5 %all-to-all-start.1 = ((bf16[256,2,256]{2,1,0:T(2,128)(2,1)}), bf16[256,2,256]{2,1,0:T(2,128)(2,1)S(1)}, u32[]{:S(2)}, u32[]{:S(2)}) async-start(bf16[256,2,256]{2,1,0:T(2,128)(2,1)} %reshape.62), calls=%async_computation.1 | async-start | bytes 524288 | tf_op jit(solution)/shard_map/all_to_all | solution.py:475
  66.5 0.9 collective-permute-start
  67.5 1.1 collective-permute-start.1
  68.6 2.7 %collective-permute-start.2 = (bf16[16,8704]{1,0:T(8,128)(2,1)}, bf16[16,8704]{1,0:T(8,128)(2,1)S(1)}, u32[]{:S(2)}, u32[]{:S(2)}) collective-permute-start(bf16[16,8704]{1,0:T(8,128)(2,1)} %get-tuple-element.35), channel_id=1, source_target_pairs={{0,3},{1,2},{2,1},{3,0},{4,7},{5,6},{6,5},{7,4},{8,11},{9,10},{10,... | collective-permute-start | bytes 835592 | tf_op jit(solution)/shard_map/ppermute | solution.py:413
  71.3 5.5 %collective-permute-start.3 = (bf16[16,8704]{1,0:T(8,128)(2,1)}, bf16[16,8704]{1,0:T(8,128)(2,1)S(1)}, u32[]{:S(2)}, u32[]{:S(2)}) collective-permute-start(bf16[16,8704]{1,0:T(8,128)(2,1)} %get-tuple-element.36), channel_id=1, source_target_pairs={{0,4},{1,5},{2,6},{3,7},{4,0},{5,1},{6,2},{7,3},{8,12},{9,13},{10,... | collective-permute-start | bytes 835592 | tf_op jit(solution)/shard_map/ppermute | solution.py:458
  76.9 13.9 %collective-permute-done.4 = bf16[48,8704]{1,0:T(8,128)(2,1)S(1)} collective-permute-done((bf16[48,8704]{1,0:T(8,128)(2,1)}, bf16[48,8704]{1,0:T(8,128)(2,1)S(1)}, u32[]{:S(2)}, u32[]{:S(2)}) %collective-permute-start.4) | collective-permute-done | bytes 835616 | tf_op jit(solution)/shard_map/ppermute | solution.py:457
  90.8 0.8 fusion.5
  91.5 4.5 %collective-permute-start.6 = (bf16[16,8704]{1,0:T(8,128)(2,1)S(1)}, bf16[16,8704]{1,0:T(8,128)(2,1)S(1)}, u32[]{:S(2)}, u32[]{:S(2)}) collective-permute-start(bf16[16,8704]{1,0:T(8,128)(2,1)S(1)} %get-tuple-element.57), channel_id=1, source_target_pairs={{0,2},{1,3},{2,0},{3,1},{4,6},{5,7},{6,4},{7,5},{8,10},{9,11},{10,... | collective-permute-start | bytes 835592 | tf_op jit(solution)/shard_map/ppermute | solution.py:413
  96.4 6.9 %all-to-all-done.1 = bf16[256,2,256]{2,1,0:T(2,128)(2,1)S(1)} async-done(((bf16[256,2,256]{2,1,0:T(2,128)(2,1)}), bf16[256,2,256]{2,1,0:T(2,128)(2,1)S(1)}, u32[]{:S(2)}, u32[]{:S(2)}) %all-to-all-start.1) | async-done | bytes 262176 | tf_op jit(solution)/shard_map/all_to_all | solution.py:475
  103.6 0.7 copy.47
  104.3 4.3 %collective-permute-done.6.refs_6_ = bf16[16,8704]{1,0:T(8,128)(2,1)S(1)} collective-permute-done((bf16[16,8704]{1,0:T(8,128)(2,1)S(1)}, bf16[16,8704]{1,0:T(8,128)(2,1)S(1)}, u32[]{:S(2)}, u32[]{:S(2)}) %collective-permute-start.6) | collective-permute-done | bytes 278560 | tf_op jit(solution)/shard_map/ppermute | solution.py:413
  108.6 2.2 %collective-permute-done.7.refs_7_ = bf16[16,8704]{1,0:T(8,128)(2,1)S(1)} collective-permute-done((bf16[16,8704]{1,0:T(8,128)(2,1)S(1)}, bf16[16,8704]{1,0:T(8,128)(2,1)S(1)}, u32[]{:S(2)}, u32[]{:S(2)}) %collective-permute-start.7) | collective-permute-done | bytes 278560 | tf_op jit(solution)/shard_map/ppermute | solution.py:413
  110.9 0.7 copy-done.9
  111.5 3.2 %shard_map.206.center_ref = bf16[128,8704]{1,0:T(8,128)(2,1)} custom-call(s32[1]{0:T(128)} %bitcast.group_ref, bf16[16,8704]{1,0:T(8,128)(2,1)} %get-tuple-element.39.refs_0_, bf16[16,8704]{1,0:T(8,128)(2,1)} %copy-done.3, bf16[16,8704]{1,0:T(8,128)(2,1)} %copy-done.4, bf16[16,8704]{1,0:T(8,128)(2,1)} %copy-done.5, bf16[16,8704]{1,0:T(8,128)(2,1)} %copy-done.6, ...), custom_call_target="tpu_custom_call" | custom-call | bytes 4194304 | tf_op jit(solution)/shard_map/pallas_call | solution.py:365
  114.7 1.7 collective-permute-start.9
  116.6 0.7 pad.18
  117.3 0.7 copy.38.synth_ref
  118.0 0.6 pad.17
  118.8 0.7 broadcast_in_dim_reshape.4.damp_ref
  119.5 2.5 %shard_map.208.weight_ref = bf16[128,1664]{1,0:T(8,128)(2,1)} custom-call(f32[3,256]{1,0:T(4,128)} %constant.113.clone.dir_ref, bf16[256,128]{1,0:T(8,128)(2,1)} %copy.38.synth_ref, bf16[128,256]{1,0:T(8,128)(2,1)} %bitcast.39, bf16[3,128,256]{2,1,0:T(8,128)(2,1)} %bitcast.37), custom_call_target="tpu_custom_call" | custom-call | flops 268435456 | bytes 1048576 | tf_op jit(solution)/shard_map/pallas_call | solution.py:365
  121.9 2.8 %shard_map.207.flow_ref = f32[11,32,256]{2,1,0:T(8,128)} custom-call(bf16[256,512]{1,0:T(8,128)(2,1)} %bitcast.34, bf16[256,1024]{1,0:T(8,128)(2,1)} %constant.114.clone.high_ref, bf16[256,1024]{1,0:T(8,128)(2,1)} %constant.115.clone.low_ref), custom_call_target="tpu_custom_call" | custom-call | flops 536870912 | bytes 2097152 | tf_op jit(solution)/shard_map/pallas_call | solution.py:365
  124.7 12.4 %shard_map.209.inner_ref = f32[128,8192]{1,0:T(8,128)} custom-call(bf16[128,8704]{1,0:T(8,128)(2,1)} %shard_map.206.center_ref, f32[11,32,256]{2,1,0:T(8,128)} %shard_map.207.flow_ref, bf16[128,1664]{1,0:T(8,128)(2,1)} %shard_map.208.weight_ref, f32[128,1]{1,0:T(8,128)} %broadcast_in_dim_reshape.4.damp_ref), custom_call_target="tpu_custom_call" | custom-call | flops 6442450944 | bytes 7340032 | tf_op jit(solution)/shard_map/pallas_call | solution.py:365
  137.1 4.7 %collective-permute-done.8.zlow_ref = bf16[128,8704]{1,0:T(8,128)(2,1)S(1)} collective-permute-done((bf16[128,8704]{1,0:T(8,128)(2,1)}, bf16[128,8704]{1,0:T(8,128)(2,1)S(1)}, u32[]{:S(2)}, u32[]{:S(2)}) %collective-permute-start.8) | collective-permute-done | bytes 2228256 | tf_op jit(solution)/shard_map/ppermute | solution.py:478
  141.8 1.4 copy-done
  143.1 5.8 %shard_map.211 = bf16[8,15,16,256]{3,2,1,0:T(8,128)(2,1)} custom-call(f32[128,8192]{1,0:T(8,128)} %shard_map.209.inner_ref, bf16[128,8704]{1,0:T(8,128)(2,1)} %copy-done, bf16[128,8704]{1,0:T(8,128)(2,1)} %collective-permute-done.9.zhigh_ref, f32[11,32,256]{2,1,0:T(8,128)} %shard_map.207.flow_ref, bf16[128,1664]{1,0:T(8,128)(2,1)} %shard_map.208.weight_ref), custom_call_target="tpu_custom_call" | custom-call | flops 536870912 | bytes 4718592 | tf_op jit(solution)/shard_map/pallas_call | solution.py:365
  148.9 6.5 %all-to-all-start.3 = ((bf16[8,15,16,256]{3,2,1,0:T(8,128)(2,1)}), bf16[8,15,16,256]{3,2,1,0:T(8,128)(2,1)S(1)}, u32[]{:S(2)}, u32[]{:S(2)}) async-start(bf16[8,15,16,256]{3,2,1,0:T(8,128)(2,1)} %shard_map.211), calls=%async_computation.3 | async-start | bytes 1966080 | tf_op jit(solution)/shard_map/all_to_all | solution.py:518
  155.4 5.8 %shard_map.210 = bf16[8,15,16,256]{3,2,1,0:T(8,128)(2,1)} custom-call(f32[128,8192]{1,0:T(8,128)} %shard_map.209.inner_ref, bf16[128,8704]{1,0:T(8,128)(2,1)} %copy-done, bf16[128,8704]{1,0:T(8,128)(2,1)} %collective-permute-done.9.zhigh_ref, f32[11,32,256]{2,1,0:T(8,128)} %shard_map.207.flow_ref, bf16[128,1664]{1,0:T(8,128)(2,1)} %shard_map.208.weight_ref), custom_call_target="tpu_custom_call" | custom-call | flops 536870912 | bytes 4718592 | tf_op jit(solution)/shard_map/pallas_call | solution.py:365
  161.2 20.0 %all-to-all-done.3.refs_1_ = bf16[8,15,16,256]{3,2,1,0:T(8,128)(2,1)S(1)} async-done(((bf16[8,15,16,256]{3,2,1,0:T(8,128)(2,1)}), bf16[8,15,16,256]{3,2,1,0:T(8,128)(2,1)S(1)}, u32[]{:S(2)}, u32[]{:S(2)}) %all-to-all-start.3) | async-done | bytes 983072 | tf_op jit(solution)/shard_map/all_to_all | solution.py:518
  181.2 4.8 %all-to-all-start.2 = ((bf16[8,15,16,256]{3,2,1,0:T(8,128)(2,1)}), bf16[8,15,16,256]{3,2,1,0:T(8,128)(2,1)S(1)}, u32[]{:S(2)}, u32[]{:S(2)}) async-start(bf16[8,15,16,256]{3,2,1,0:T(8,128)(2,1)} %shard_map.210), calls=%async_computation.2 | async-start | bytes 1966080 | tf_op jit(solution)/shard_map/all_to_all | solution.py:518
  186.0 0.9 slice.31
  186.9 7.3 %collective-permute-start.10 = (f32[3,32,256]{2,1,0:T(8,128)S(1)}, f32[3,32,256]{2,1,0:T(8,128)S(1)}, u32[]{:S(2)}, u32[]{:S(2)}) collective-permute-start(f32[3,32,256]{2,1,0:T(8,128)S(1)} %slice.31), channel_id=1, source_target_pairs={{0,0},{1,1},{2,2},{3,3},{4,4},{5,5},{6,6},{7,7},{8,8},{9,9},{10,10... | collective-permute-start | bytes 294920 | tf_op jit(solution)/shard_map/ppermute | solution.py:521
  194.2 18.0 %collective-permute-done.10 = f32[3,32,256]{2,1,0:T(8,128)S(1)} collective-permute-done((f32[3,32,256]{2,1,0:T(8,128)S(1)}, f32[3,32,256]{2,1,0:T(8,128)S(1)}, u32[]{:S(2)}, u32[]{:S(2)}) %collective-permute-start.10) | collective-permute-done | bytes 98336 | tf_op jit(solution)/shard_map/ppermute | solution.py:521
  212.2 1.0 copy-done.2
  213.2 2.9 %shard_map.212 = bf16[15,256,256]{2,1,0:T(8,128)(2,1)} custom-call(s32[1]{0:T(128)S(6)} %xor.11.swap_ref, bf16[8,15,16,256]{3,2,1,0:T(8,128)(2,1)} %copy-done.2, bf16[8,15,16,256]{3,2,1,0:T(8,128)(2,1)} %copy-done.1), custom_call_target="tpu_custom_call" | custom-call | bytes 4194304 | tf_op jit(solution)/shard_map/pallas_call | solution.py:365
  216.1 0.6 copy.51
  (47 shorter events, 2.0 us)
Async XLA Ops:
  10.6 34.5 %all-to-all-start = ((bf16[256,2,640]{2,1,0:T(2,128)(2,1)}), bf16[256,2,640]{2,1,0:T(2,128)(2,1)S(1)}, u32[]{:S(2)}, u32[]{:S(2)}) async-start(bf16[256,2,640]{2,1,0:T(2,128)(2,1)} %reshape.60), calls=%async_computation | async-start | bytes 1310720 | tf_op jit(solution)/shard_map/all_to_all | solution.py:448
  46.6 44.2 %collective-permute-start.4 = (bf16[48,8704]{1,0:T(8,128)(2,1)}, bf16[48,8704]{1,0:T(8,128)(2,1)S(1)}, u32[]{:S(2)}, u32[]{:S(2)}) collective-permute-start(bf16[48,8704]{1,0:T(8,128)(2,1)} %get-tuple-element.37), channel_id=1, source_target_pairs={{0,4},{1,5},{2,6},{3,7},{4,0},{5,1},{6,2},{7,3},{8,12},{9,13},{10,... | collective-permute-start | bytes 2506760 | tf_op jit(solution)/shard_map/ppermute | solution.py:457
  54.0 49.3 %all-to-all-start.1 = ((bf16[256,2,256]{2,1,0:T(2,128)(2,1)}), bf16[256,2,256]{2,1,0:T(2,128)(2,1)S(1)}, u32[]{:S(2)}, u32[]{:S(2)}) async-start(bf16[256,2,256]{2,1,0:T(2,128)(2,1)} %reshape.62), calls=%async_computation.1 | async-start | bytes 524288 | tf_op jit(solution)/shard_map/all_to_all | solution.py:475
  66.5 25.0 %collective-permute-start = (bf16[16,8704]{1,0:T(8,128)(2,1)}, bf16[16,8704]{1,0:T(8,128)(2,1)S(1)}, u32[]{:S(2)}, u32[]{:S(2)}) collective-permute-start(bf16[16,8704]{1,0:T(8,128)(2,1)} %get-tuple-element.33), channel_id=1, source_target_pairs={{0,1},{1,0},{2,3},{3,2},{4,5},{5,4},{6,7},{7,6},{8,9},{9,8},{10,11... | collective-permute-start | bytes 835592 | tf_op jit(solution)/shard_map/ppermute | solution.py:413
  67.5 28.6 %collective-permute-start.1 = (bf16[16,8704]{1,0:T(8,128)(2,1)}, bf16[16,8704]{1,0:T(8,128)(2,1)S(1)}, u32[]{:S(2)}, u32[]{:S(2)}) collective-permute-start(bf16[16,8704]{1,0:T(8,128)(2,1)} %get-tuple-element.34), channel_id=1, source_target_pairs={{0,2},{1,3},{2,0},{3,1},{4,6},{5,7},{6,4},{7,5},{8,10},{9,11},{10,... | collective-permute-start | bytes 835592 | tf_op jit(solution)/shard_map/ppermute | solution.py:413
  68.6 35.7 %collective-permute-start.2 = (bf16[16,8704]{1,0:T(8,128)(2,1)}, bf16[16,8704]{1,0:T(8,128)(2,1)S(1)}, u32[]{:S(2)}, u32[]{:S(2)}) collective-permute-start(bf16[16,8704]{1,0:T(8,128)(2,1)} %get-tuple-element.35), channel_id=1, source_target_pairs={{0,3},{1,2},{2,1},{3,0},{4,7},{5,6},{6,5},{7,4},{8,11},{9,10},{10,... | collective-permute-start | bytes 835592 | tf_op jit(solution)/shard_map/ppermute | solution.py:413
  71.3 33.0 %collective-permute-start.3 = (bf16[16,8704]{1,0:T(8,128)(2,1)}, bf16[16,8704]{1,0:T(8,128)(2,1)S(1)}, u32[]{:S(2)}, u32[]{:S(2)}) collective-permute-start(bf16[16,8704]{1,0:T(8,128)(2,1)} %get-tuple-element.36), channel_id=1, source_target_pairs={{0,4},{1,5},{2,6},{3,7},{4,0},{5,1},{6,2},{7,3},{8,12},{9,13},{10,... | collective-permute-start | bytes 835592 | tf_op jit(solution)/shard_map/ppermute | solution.py:458
  91.5 12.8 %collective-permute-start.5 = (bf16[16,8704]{1,0:T(8,128)(2,1)}, bf16[16,8704]{1,0:T(8,128)(2,1)S(1)}, u32[]{:S(2)}, u32[]{:S(2)}) collective-permute-start(bf16[16,8704]{1,0:T(8,128)(2,1)} %get-tuple-element.58), channel_id=1, source_target_pairs={{0,1},{1,0},{2,3},{3,2},{4,5},{5,4},{6,7},{7,6},{8,9},{9,8},{10,11... | collective-permute-start | bytes 835592 | tf_op jit(solution)/shard_map/ppermute | solution.py:413
  91.5 19.3 %copy-start.3 = (bf16[16,8704]{1,0:T(8,128)(2,1)}, bf16[16,8704]{1,0:T(8,128)(2,1)S(1)}, u32[]{:S(2)}) copy-start(bf16[16,8704]{1,0:T(8,128)(2,1)S(1)} %collective-permute-done.refs_1_) | copy-start | bytes 835588
  91.5 17.1 %collective-permute-start.6 = (bf16[16,8704]{1,0:T(8,128)(2,1)S(1)}, bf16[16,8704]{1,0:T(8,128)(2,1)S(1)}, u32[]{:S(2)}, u32[]{:S(2)}) collective-permute-start(bf16[16,8704]{1,0:T(8,128)(2,1)S(1)} %get-tuple-element.57), channel_id=1, source_target_pairs={{0,2},{1,3},{2,0},{3,1},{4,6},{5,7},{6,4},{7,5},{8,10},{9,11},{10,... | collective-permute-start | bytes 835592 | tf_op jit(solution)/shard_map/ppermute | solution.py:413
  96.0 14.8 %copy-start.4 = (bf16[16,8704]{1,0:T(8,128)(2,1)}, bf16[16,8704]{1,0:T(8,128)(2,1)S(1)}, u32[]{:S(2)}) copy-start(bf16[16,8704]{1,0:T(8,128)(2,1)S(1)} %collective-permute-done.1.refs_2_) | copy-start | bytes 835588
  96.0 14.8 %collective-permute-start.7 = (bf16[16,8704]{1,0:T(8,128)(2,1)S(1)}, bf16[16,8704]{1,0:T(8,128)(2,1)S(1)}, u32[]{:S(2)}, u32[]{:S(2)}) collective-permute-start(bf16[16,8704]{1,0:T(8,128)(2,1)S(1)} %get-tuple-element.56), channel_id=1, source_target_pairs={{0,3},{1,2},{2,1},{3,0},{4,7},{5,6},{6,5},{7,4},{8,11},{9,10},{10,... | collective-permute-start | bytes 835592 | tf_op jit(solution)/shard_map/ppermute | solution.py:413
  104.3 6.5 %copy-start.5 = (bf16[16,8704]{1,0:T(8,128)(2,1)}, bf16[16,8704]{1,0:T(8,128)(2,1)S(1)}, u32[]{:S(2)}) copy-start(bf16[16,8704]{1,0:T(8,128)(2,1)S(1)} %collective-permute-done.2.refs_3_) | copy-start | bytes 835588
  104.3 6.5 %copy-start.6 = (bf16[16,8704]{1,0:T(8,128)(2,1)}, bf16[16,8704]{1,0:T(8,128)(2,1)S(1)}, u32[]{:S(2)}) copy-start(bf16[16,8704]{1,0:T(8,128)(2,1)S(1)} %collective-permute-done.3.refs_4_) | copy-start | bytes 835588
  104.3 6.5 %copy-start.7 = (bf16[16,8704]{1,0:T(8,128)(2,1)}, bf16[16,8704]{1,0:T(8,128)(2,1)S(1)}, u32[]{:S(2)}) copy-start(bf16[16,8704]{1,0:T(8,128)(2,1)S(1)} %collective-permute-done.5.refs_5_) | copy-start | bytes 835588
  108.6 2.2 %copy-start.8 = (bf16[16,8704]{1,0:T(8,128)(2,1)}, bf16[16,8704]{1,0:T(8,128)(2,1)S(1)}, u32[]{:S(2)}) copy-start(bf16[16,8704]{1,0:T(8,128)(2,1)S(1)} %collective-permute-done.6.refs_6_) | copy-start | bytes 835588
  110.8 0.7 copy-start.9
  111.5 4.9 %copy-start.11 = (bf16[256,120]{0,1:T(8,128)(2,1)S(1)}, bf16[256,120]{0,1:T(8,128)(2,1)}, u32[]{:S(2)}) copy-start(bf16[256,120]{0,1:T(8,128)(2,1)} %param.21) | copy-start | bytes 184324
  111.5 5.0 %copy-start.10 = (bf16[3,120,256]{2,1,0:T(8,128)(2,1)S(1)}, bf16[3,120,256]{2,1,0:T(8,128)(2,1)}, u32[]{:S(2)}) copy-start(bf16[3,120,256]{2,1,0:T(8,128)(2,1)} %param.23) | copy-start | bytes 552964
  111.5 6.5 %copy-start.12 = (bf16[120,256]{1,0:T(8,128)(2,1)S(1)}, bf16[120,256]{1,0:T(8,128)(2,1)}, u32[]{:S(2)}) copy-start(bf16[120,256]{1,0:T(8,128)(2,1)} %param.22) | copy-start | bytes 184324
  111.5 7.1 %copy-start.13 = (f32[120]{0:T(128)S(1)}, f32[120]{0:T(128)}, u32[]{:S(2)}) copy-start(f32[120]{0:T(128)} %param.24) | copy-start | bytes 1444
  114.7 27.1 %collective-permute-start.8 = (bf16[128,8704]{1,0:T(8,128)(2,1)}, bf16[128,8704]{1,0:T(8,128)(2,1)S(1)}, u32[]{:S(2)}, u32[]{:S(2)}) collective-permute-start(bf16[128,8704]{1,0:T(8,128)(2,1)} %shard_map.206.center_ref), channel_id=1, source_target_pairs={{0,8},{1,9},{2,10},{3,11},{4,12},{5,13},{6,14},{7,15},{8,16},{9,17... | collective-permute-start | bytes 6684680 | tf_op jit(solution)/shard_map/ppermute | solution.py:478
  114.7 27.1 %collective-permute-start.9 = (bf16[128,8704]{1,0:T(8,128)(2,1)}, bf16[128,8704]{1,0:T(8,128)(2,1)}, u32[]{:S(2)}, u32[]{:S(2)}) collective-permute-start(bf16[128,8704]{1,0:T(8,128)(2,1)} %shard_map.206.center_ref), channel_id=1, source_target_pairs={{0,252},{1,253},{2,254},{3,255},{4,248},{5,249},{6,250},{7,251},{8... | collective-permute-start | bytes 6684680 | tf_op jit(solution)/shard_map/ppermute | solution.py:479
  141.8 1.4 copy-start
  148.9 32.2 %all-to-all-start.3 = ((bf16[8,15,16,256]{3,2,1,0:T(8,128)(2,1)}), bf16[8,15,16,256]{3,2,1,0:T(8,128)(2,1)S(1)}, u32[]{:S(2)}, u32[]{:S(2)}) async-start(bf16[8,15,16,256]{3,2,1,0:T(8,128)(2,1)} %shard_map.211), calls=%async_computation.3 | async-start | bytes 1966080 | tf_op jit(solution)/shard_map/all_to_all | solution.py:518
  181.2 31.0 %copy-start.1 = (bf16[8,15,16,256]{3,2,1,0:T(8,128)(2,1)}, bf16[8,15,16,256]{3,2,1,0:T(8,128)(2,1)S(1)}, u32[]{:S(2)}) copy-start(bf16[8,15,16,256]{3,2,1,0:T(8,128)(2,1)S(1)} %all-to-all-done.3.refs_1_) | copy-start | bytes 2949124
  181.2 31.0 %all-to-all-start.2 = ((bf16[8,15,16,256]{3,2,1,0:T(8,128)(2,1)}), bf16[8,15,16,256]{3,2,1,0:T(8,128)(2,1)S(1)}, u32[]{:S(2)}, u32[]{:S(2)}) async-start(bf16[8,15,16,256]{3,2,1,0:T(8,128)(2,1)} %shard_map.210), calls=%async_computation.2 | async-start | bytes 1966080 | tf_op jit(solution)/shard_map/all_to_all | solution.py:518
  186.9 25.3 %collective-permute-start.10 = (f32[3,32,256]{2,1,0:T(8,128)S(1)}, f32[3,32,256]{2,1,0:T(8,128)S(1)}, u32[]{:S(2)}, u32[]{:S(2)}) collective-permute-start(f32[3,32,256]{2,1,0:T(8,128)S(1)} %slice.31), channel_id=1, source_target_pairs={{0,0},{1,1},{2,2},{3,3},{4,4},{5,5},{6,6},{7,7},{8,8},{9,9},{10,10... | collective-permute-start | bytes 294920 | tf_op jit(solution)/shard_map/ppermute | solution.py:521
  212.2 1.0 copy-start.2

commit v5 on v3

--- a/solution.py
+++ b/solution.py
@@ -22,12 +22,14 @@
 OWN = COEFS // GROUPS
 PAD = 16
 ROWS = NY // GROUPS
-CELLS = ROWS * NX
+EDGED = ROWS + 2
+CELLS = EDGED * NX
 HALF = NX // 2
 ALL_PAD = GROUPS * PAD
 LANES = 128
 RUN = 8
 FLIP = GROUPS // 2
+AHEAD = 6
 PARTS = 2
 CHUNK = ROWS // PARTS
 BLOCKS = 12
@@ -109,17 +111,23 @@
 def regroup_kernel(block_ref, coef_ref, *refs):
     outs, stages = refs[:GROUPS], refs[GROUPS:]
     block = block_ref[0]
+    height = ROWS + 2 * PAD
     for stage in stages:
-        stage[pl.ds(OWN * ROWS, ROWS), :] = jnp.zeros((ROWS, LANES), f32)
+        stage[pl.ds(OWN * height, height), :] = jnp.zeros((height, LANES), f32)
     for j in range(GROUPS):
-        first = pl.multiple_of((block ^ j) * ROWS, ROWS)
-        rows = coef_ref[:, pl.ds(first, ROWS), :].astype(f32)
-        rows = rows.reshape(OWN * ROWS, NX)
+        first = (block ^ j) * ROWS
+        for start, size, at in ((NY - PAD, PAD, 0), (0, ROWS, PAD), (ROWS, PAD, PAD + ROWS)):
+            rows = coef_ref[:, pl.ds(pl.multiple_of((first + start) % NY, PAD), size), :].astype(f32)
+            for side, stage in enumerate(stages):
+                for c in range(OWN):
+                    stage[c * height + at : c * height + at + size, :] = rows[
+                        c, :, side * LANES : (side + 1) * LANES
+                    ]
         for side, stage in enumerate(stages):
-            stage[pl.ds(0, OWN * ROWS), :] = rows[:, side * LANES : (side + 1) * LANES]
-            for r in range(ROWS):
+            for r in range(EDGED):
                 lane = r * NX + side * LANES
-                outs[j][:, lane : lane + LANES] = stage[pl.ds(r, PAD, stride=ROWS), :].astype(bf16)
+                rows = stage[pl.ds(PAD - 1 + r, PAD, stride=height), :]
+                outs[j][:, lane : lane + LANES] = rows.astype(bf16)
 
 
 def stress_kernel(table_ref, coef_ref, high_ref, low_ref, out_ref, stress_high, stress_low):
@@ -270,23 +278,17 @@
 
 
 def rate_kernel(
-    center_ref, zlow_ref, zhigh_ref, ylow_ref, yhigh_ref, flow_ref, weight_ref, damp_ref,
-    *refs,
+    center_ref, zlow_ref, zhigh_ref, flow_ref, weight_ref, damp_ref,
+    out_ref, operands, locals_, *stages,
 ):
-    out_ref, padded, operands, locals_, *stages = refs
-    cells = CHUNK * NX
-    padded[:, :NX] = ylow_ref[...]
-    padded[:, NX : NX + cells] = center_ref[...]
-    padded[:, NX + cells :] = yhigh_ref[...]
-
     def build(r, operand, local_terms):
         here = pl.multiple_of(r * NX, NX)
         flow = [flow_ref[f, pl.ds(r, 1), :] for f in range(11)]
         for g in range(GROUPS):
             rows = slice(g * PAD, (g + 1) * PAD)
-            value = padded[rows, pl.ds(here + NX, NX)].astype(f32)
-            y_low = padded[rows, pl.ds(here, NX)].astype(f32)
-            y_high = padded[rows, pl.ds(here + 2 * NX, NX)].astype(f32)
+            value = center_ref[rows, pl.ds(here + NX, NX)].astype(f32)
+            y_low = center_ref[rows, pl.ds(here, NX)].astype(f32)
+            y_high = center_ref[rows, pl.ds(here + 2 * NX, NX)].astype(f32)
             z_low = zlow_ref[rows, pl.ds(here, NX)].astype(f32)
             z_high = zhigh_ref[rows, pl.ds(here, NX)].astype(f32)
             x_low = pltpu.roll(value, 1, 1)
@@ -398,22 +400,23 @@
     group_arg = group.astype(jnp.int32).reshape(1)
     block_arg = group_arg ^ (FLIP * odd(plane)).astype(jnp.int32)
 
+    chunks = call(
+        regroup_kernel, [shape(PAD, CELLS)] * GROUPS, [block_arg, own],
+        [pltpu.VMEM((PAD * (ROWS + 2 * PAD), LANES), f32)] * 2, 1, 0, 4 << 20,
+    )
+    arrived = [chunks[0]]
+    for j in range(1, GROUPS):
+        arrived.append(lax.ppermute(chunks[j], "harm", [(i, i ^ j) for i in range(GROUPS)]))
+    own, _ = lax.optimization_barrier((own, chunks))
+
     table = stress_table(synthesis, directions, group)
     high, low = split_table(forward_x)
     sent = call(
         stress_kernel, shape(NX, 10 * HALF), [table, own, high, low],
         [pltpu.VMEM((5, NY, NX), bf16)] * 2, 1, 1 << 30, 3 << 20,
     )
+    sent, arrived[:AHEAD] = lax.optimization_barrier((sent, arrived[:AHEAD]))
     columns = lax.all_to_all(sent, everyone, 0, 0, tiled=True)
-
-    later, _ = lax.optimization_barrier((own, sent))
-    chunks = call(
-        regroup_kernel, [shape(PAD, CELLS)] * GROUPS, [block_arg, later],
-        [pltpu.VMEM((PAD * ROWS, LANES), f32)] * 2, 1, 0, 4 << 20,
-    )
-    arrived = [chunks[0]]
-    for j in range(1, GROUPS):
-        arrived.append(lax.ppermute(chunks[j], "harm", [(i, i ^ j) for i in range(GROUPS)]))
 
     wave = (position % HALF).astype(f32) * (2.0 * math.pi / NX)
     half = (position // HALF).astype(jnp.int32)
@@ -433,10 +436,7 @@
     center = call(assemble_kernel, shape(ALL_PAD, CELLS), [group_arg, *arrived], (), 1, 0, 4 << 20)
     z_low = lax.ppermute(center, both, pairs(lambda s, b: ((s + 1) % SPACES, b)))
     z_high = lax.ppermute(center, both, pairs(lambda s, b: ((s - 1) % SPACES, b)))
-    y_low = lax.ppermute(center[:, -NX:], both, pairs(lambda s, b: (s, (b + 1) % GROUPS)))
-    y_high = lax.ppermute(center[:, :NX], both, pairs(lambda s, b: (s, (b - 1) % GROUPS)))
-
-    z_low, z_high, y_low, y_high = lax.optimization_barrier((z_low, z_high, y_low, y_high))
+
     weights = call(
         weights_kernel, shape(ALL_PAD, BLOCKS * ALL_PAD),
         [
@@ -449,19 +449,14 @@
     damp = pad_groups(damping, 0)[:, None]
     returned, parts = [], []
     for part in range(PARTS):
-        here = pl.BlockSpec((ALL_PAD, CHUNK * NX), lambda i, part=part: (0, part))
-        first, last = part * CHUNK, (part + 1) * CHUNK
-
-        def edge(row):
-            return pl.BlockSpec((ALL_PAD, NX), lambda i: (0, row))
-
-        low = (y_low, VMEM) if first == 0 else (center, edge(first - 1))
-        high = (y_high, VMEM) if last == ROWS else (center, edge(last))
+        def lines(first, count, part=part):
+            size = (pl.Element(ALL_PAD), pl.Element(count * NX))
+            return pl.BlockSpec(size, lambda i: (0, (part * CHUNK + first) * NX))
+
         rates = call(
             rate_kernel, shape(GROUPS, OWN, CHUNK, NX),
-            [center, z_low, z_high, low[0], high[0], flow, weights, damp],
+            [center, z_low, z_high, flow, weights, damp],
             [
-                pltpu.VMEM((ALL_PAD, (CHUNK + 2) * NX), bf16),
                 pltpu.VMEM((2, BLOCKS * ALL_PAD, NX), bf16),
                 pltpu.VMEM((2, ALL_PAD, NX), f32),
                 pltpu.VMEM((ALL_PAD * CHUNK, LANES), f32),
@@ -469,7 +464,7 @@
             ],
             0, 7 << 29, 9 << 19,
             [
-                here, here, here, low[1], high[1],
+                lines(0, CHUNK + 2), lines(1, CHUNK), lines(1, CHUNK),
                 pl.BlockSpec((11, CHUNK, NX), lambda i, part=part: (0, part, 0)), VMEM, VMEM,
             ],
         )

time: 213 us -> 231 us (1.085); the launches traced: 212 us -> 227 us
  waiting for transfers between devices: 74.4 us -> 98.1 us
  starting transfers between devices: 76.7 us -> 68.4 us
    all_to_all x1, waiting for transfers between devices: 0.01 us -> 12.4 us  [local(): columns = lax.all_to_all(sent, everyone, 0, 0, tiled=True)]
    all_to_all x1, waiting for transfers between devices: 8.39 us -> 18.3 us  [local(): mixed = lax.all_to_all(sent, everyone, 0, 0, tiled=True)]
    ppermute x2 -> x0, starting transfers between devices: 8.12 us -> none  [the longest x1 7.2 us: local(): lax.ppermute(center[:, -NX:], both, pairs(lambda s, b: (s, (b + 1) % GROU...]
    all_to_all x1, starting transfers between devices: 10.9 us -> 15.9 us  [local(): mixed = lax.all_to_all(sent, everyone, 0, 0, tiled=True)]
    all_to_all x2, starting transfers between devices: 13.6 us -> 10.9 us  [local(): returned.append(lax.all_to_all(rates, 'harm', 0, 0, tiled=True))]
    ppermute x7, starting transfers between devices: 22.1 us -> 19.4 us  [local(): lax.ppermute(chunks[j], 'harm', [(i, i ^ j) for i in range(GROUPS)])]
    unnamed x39 -> x33, local copies, waits for them, and re-layouts: 7.16 us -> 7.18 us
  transfers between devices with their start and end apart: 16 -> 14, of which waited for: 9 -> 8; matrix products, arithmetic and copies ran while one was open for 4% -> 4% of each run, Pallas kernels for 11% -> 10%
where the time goes in v5:
time: 231 us; the launch traced here: 227 us
  waiting for transfers between devices  98.1 us (42%)
  starting transfers between devices  68.4 us (30%)
  Pallas kernels  43.7 us (19%)
  local copies, waits for them, and re-layouts  11.7 us (5%)
  other arithmetic  3.51 us (2%)
    pallas_call x9, Pallas kernels, call(): pl.pallas_call(kernel, out_shape=out_shape, grid=(1,) if specs else (), i...  43.7 us
    ppermute x7, waiting for transfers between devices, local(): lax.ppermute(chunks[j], 'harm', [(i, i ^ j) for i in range(GROUPS)])  33.4 us
    ppermute x7, starting transfers between devices, local(): lax.ppermute(chunks[j], 'harm', [(i, i ^ j) for i in range(GROUPS)])  19.4 us
    all_to_all x1, waiting for transfers between devices, local(): mixed = lax.all_to_all(sent, everyone, 0, 0, tiled=True)  18.3 us
    all_to_all x2, waiting for transfers between devices, local(): returned.append(lax.all_to_all(rates, 'harm', 0, 0, tiled=True))  18.2 us
    all_to_all x1, starting transfers between devices, local(): mixed = lax.all_to_all(sent, everyone, 0, 0, tiled=True)  15.9 us
    ppermute x1, waiting for transfers between devices, local(): velocity = lax.ppermute(late, both, swap)  15.8 us
    all_to_all x1, starting transfers between devices, local(): columns = lax.all_to_all(sent, everyone, 0, 0, tiled=True)  14.4 us
  transfers between devices with their start and end apart: 14, of which 8 were waited for; matrix products, arithmetic and copies ran while one was open for 4% of the time, Pallas kernels for 10%

profile of v5, /device:TPU:62, one launch (start us, length us, event | category | flops | bytes accessed | tf_op | source)
XLA Modules:
  0.0 227.2 jit_solution(13877547770607431500)
XLA Ops:
  0.7 6.4 %shard_map.203 = (bf16[16,8704]{1,0:T(8,128)(2,1)}, bf16[16,8704]{1,0:T(8,128)(2,1)}, bf16[16,8704]{1,0:T(8,128)(2,1)}, bf16[16,8704]{1,0:T(8,128)(2,1)}, bf16[1...) custom-call(s32[1]{0:T(128)S(6)} %xor.10.block_ref, ...), custom_call_target="tpu_custom_call" | custom-call | bytes 4194304 | tf_op jit(solution)/shard_map/pallas_call | solution.py:334
  7.0 0.8 collective-permute-start
  7.9 1.1 collective-permute-start.1
  9.0 2.8 %collective-permute-start.2 = (bf16[16,8704]{1,0:T(8,128)(2,1)}, bf16[16,8704]{1,0:T(8,128)(2,1)S(1)}, u32[]{:S(2)}, u32[]{:S(2)}) collective-permute-start(bf16[16,8704]{1,0:T(8,128)(2,1)} %get-tuple-element.30), channel_id=1, source_target_pairs={{0,3},{1,2},{2,1},{3,0},{4,7},{5,6},{6,5},{7,4},{8,11},{9,10},{10,... | collective-permute-start | bytes 835592 | tf_op jit(solution)/shard_map/ppermute | solution.py:409
  11.7 6.3 %collective-permute-start.3 = (bf16[16,8704]{1,0:T(8,128)(2,1)}, bf16[16,8704]{1,0:T(8,128)(2,1)S(1)}, u32[]{:S(2)}, u32[]{:S(2)}) collective-permute-start(bf16[16,8704]{1,0:T(8,128)(2,1)} %get-tuple-element.31), channel_id=1, source_target_pairs={{0,4},{1,5},{2,6},{3,7},{4,0},{5,1},{6,2},{7,3},{8,12},{9,13},{10,... | collective-permute-start | bytes 835592 | tf_op jit(solution)/shard_map/ppermute | solution.py:409
  18.0 0.8 fusion.2
  18.9 0.6 pad_maximum_fusion.table_ref
  19.5 4.8 %shard_map.204 = bf16[256,1280]{1,0:T(8,128)(2,1)} custom-call(f32[5,15]{1,0:T(8,128)} %pad_maximum_fusion.table_ref, bf16[15,256,256]{2,1,0:T(8,128)(2,1)} %bitcast.30, bf16[256,256]{1,0:T(8,128)(2,1)} %constant.102.clone.high_ref, bf16[256,256]{1,0:T(8,128)(2,1)} %constant.103.clone.low_ref), custom_call_target="tpu_custom_call" | custom-call | flops 1073741824 | bytes 3145728 | tf_op jit(solution)/shard_map/pallas_call | solution.py:334
  24.4 11.0 %collective-permute-done.3.refs_4_ = bf16[16,8704]{1,0:T(8,128)(2,1)S(1)} collective-permute-done((bf16[16,8704]{1,0:T(8,128)(2,1)}, bf16[16,8704]{1,0:T(8,128)(2,1)S(1)}, u32[]{:S(2)}, u32[]{:S(2)}) %collective-permute-start.3) | collective-permute-done | bytes 278560 | tf_op jit(solution)/shard_map/ppermute | solution.py:409
  35.4 5.9 %collective-permute-done.4.refs_5_ = bf16[16,8704]{1,0:T(8,128)(2,1)S(1)} collective-permute-done((bf16[16,8704]{1,0:T(8,128)(2,1)}, bf16[16,8704]{1,0:T(8,128)(2,1)S(1)}, u32[]{:S(2)}, u32[]{:S(2)}) %collective-permute-start.4) | collective-permute-done | bytes 278560 | tf_op jit(solution)/shard_map/ppermute | solution.py:409
  41.3 0.6 broadcast.14
  41.9 2.1 reduce
  44.0 1.0 reshape.60
  45.0 14.4 %all-to-all-start = ((bf16[256,2,640]{2,1,0:T(2,128)(2,1)}), bf16[256,2,640]{2,1,0:T(2,128)(2,1)S(1)}, u32[]{:S(2)}, u32[]{:S(2)}) async-start(bf16[256,2,640]{2,1,0:T(2,128)(2,1)} %reshape.60), calls=%async_computation | async-start | bytes 1310720 | tf_op jit(solution)/shard_map/all_to_all | solution.py:419
  59.4 6.5 %collective-permute-start.5 = (bf16[16,8704]{1,0:T(8,128)(2,1)}, bf16[16,8704]{1,0:T(8,128)(2,1)}, u32[]{:S(2)}, u32[]{:S(2)}) collective-permute-start(bf16[16,8704]{1,0:T(8,128)(2,1)} %get-tuple-element.33), channel_id=1, source_target_pairs={{0,6},{1,7},{2,4},{3,5},{4,2},{5,3},{6,0},{7,1},{8,14},{9,15},{10,... | collective-permute-start | bytes 835592 | tf_op jit(solution)/shard_map/ppermute | solution.py:409
  65.9 1.9 collective-permute-start.6
  67.8 12.4 %all-to-all-done = bf16[256,2,640]{2,1,0:T(2,128)(2,1)S(1)} async-done(((bf16[256,2,640]{2,1,0:T(2,128)(2,1)}), bf16[256,2,640]{2,1,0:T(2,128)(2,1)S(1)}, u32[]{:S(2)}, u32[]{:S(2)}) %all-to-all-start) | async-done | bytes 655392 | tf_op jit(solution)/shard_map/all_to_all | solution.py:419
  80.2 0.5 reshape.61
  80.8 0.9 copy.50
  81.7 4.0 %shard_map.205 = bf16[256,512]{1,0:T(8,128)(2,1)} custom-call(f32[1]{0:T(128)} %bitcast.5.wave_ref, s32[1]{0:T(128)} %bitcast.6.half_ref, f32[1,256]{1,0:T(1,128)} %constant.104.clone.ky_ref, f32[32,1]{1,0:T(8,128)} %constant.105.clone.kz_ref, bf16[256,1280]{1,0:T(8,128)(2,1)} %bitcast.33, bf16[64,256]{1,0:T(8,128)(2,1)} %constant.106.clone.fz_high, ...), custom_call_target="tpu_custom_call" | custom-call | flops 1073741824 | bytes 3145728 | tf_op jit(solution)/shard_map/pallas_call | solution.py:334
  85.8 9.2 %collective-permute-done.5.refs_6_ = bf16[16,8704]{1,0:T(8,128)(2,1)} collective-permute-done((bf16[16,8704]{1,0:T(8,128)(2,1)}, bf16[16,8704]{1,0:T(8,128)(2,1)}, u32[]{:S(2)}, u32[]{:S(2)}) %collective-permute-start.5) | collective-permute-done | bytes 278560 | tf_op jit(solution)/shard_map/ppermute | solution.py:409
  95.0 7.3 %collective-permute-done.6.refs_7_ = bf16[16,8704]{1,0:T(8,128)(2,1)} collective-permute-done((bf16[16,8704]{1,0:T(8,128)(2,1)}, bf16[16,8704]{1,0:T(8,128)(2,1)}, u32[]{:S(2)}, u32[]{:S(2)}) %collective-permute-start.6) | collective-permute-done | bytes 278560 | tf_op jit(solution)/shard_map/ppermute | solution.py:409
  102.3 3.1 %shard_map.206.center_ref = bf16[128,8704]{1,0:T(8,128)(2,1)} custom-call(s32[1]{0:T(128)} %bitcast.group_ref, bf16[16,8704]{1,0:T(8,128)(2,1)} %get-tuple-element.43.refs_0_, bf16[16,8704]{1,0:T(8,128)(2,1)} %copy-done.2, bf16[16,8704]{1,0:T(8,128)(2,1)} %copy-done.3, bf16[16,8704]{1,0:T(8,128)(2,1)} %copy-done.4, bf16[16,8704]{1,0:T(8,128)(2,1)} %copy-done.5, ...), custom_call_target="tpu_custom_call" | custom-call | bytes 4194304 | tf_op jit(solution)/shard_map/pallas_call | solution.py:334
  105.4 0.5 collective-permute-start.7
  105.9 0.8 reduce.1
  106.6 0.8 reshape.62
  107.4 15.9 %all-to-all-start.1 = ((bf16[256,2,256]{2,1,0:T(2,128)(2,1)}), bf16[256,2,256]{2,1,0:T(2,128)(2,1)S(1)}, u32[]{:S(2)}, u32[]{:S(2)}) async-start(bf16[256,2,256]{2,1,0:T(2,128)(2,1)} %reshape.62), calls=%async_computation.1 | async-start | bytes 524288 | tf_op jit(solution)/shard_map/all_to_all | solution.py:434
  123.5 0.7 broadcast_in_dim_reshape.4.damp_ref
  124.3 0.6 pad.17
  124.9 0.7 copy.41.synth_ref
  125.7 0.7 pad.18
  126.4 2.5 %shard_map.208.weight_ref = bf16[128,1536]{1,0:T(8,128)(2,1)} custom-call(f32[3,256]{1,0:T(4,128)} %constant.113.clone.dir_ref, bf16[256,128]{1,0:T(8,128)(2,1)} %copy.41.synth_ref, bf16[128,256]{1,0:T(8,128)(2,1)} %bitcast.39, bf16[3,128,256]{2,1,0:T(8,128)(2,1)} %bitcast.37), custom_call_target="tpu_custom_call" | custom-call | flops 268435456 | bytes 1048576 | tf_op jit(solution)/shard_map/pallas_call | solution.py:334
  129.0 18.3 %all-to-all-done.1 = bf16[256,2,256]{2,1,0:T(2,128)(2,1)S(1)} async-done(((bf16[256,2,256]{2,1,0:T(2,128)(2,1)}), bf16[256,2,256]{2,1,0:T(2,128)(2,1)S(1)}, u32[]{:S(2)}, u32[]{:S(2)}) %all-to-all-start.1) | async-done | bytes 262176 | tf_op jit(solution)/shard_map/all_to_all | solution.py:434
  147.2 0.2 reshape.63
  147.4 0.7 copy.51
  148.2 2.8 %shard_map.207.flow_ref = f32[11,32,256]{2,1,0:T(8,128)} custom-call(bf16[256,512]{1,0:T(8,128)(2,1)} %bitcast.34, bf16[256,1024]{1,0:T(8,128)(2,1)} %constant.114.clone.high_ref, bf16[256,1024]{1,0:T(8,128)(2,1)} %constant.115.clone.low_ref), custom_call_target="tpu_custom_call" | custom-call | flops 536870912 | bytes 2097152 | tf_op jit(solution)/shard_map/pallas_call | solution.py:334
  151.0 1.4 copy-done.12
  152.4 8.6 %shard_map.210 = bf16[8,15,16,256]{3,2,1,0:T(8,128)(2,1)} custom-call(bf16[128,8704]{1,0:T(8,128)(2,1)} %shard_map.206.center_ref, bf16[128,8704]{1,0:T(8,128)(2,1)} %collective-permute-done.7.zlow_ref, bf16[128,8704]{1,0:T(8,128)(2,1)} %copy-done.12, f32[11,32,256]{2,1,0:T(8,128)} %shard_map.207.flow_ref, bf16[128,1536]{1,0:T(8,128)(2,1)} %shard_map.208.weight_ref, ...), custom_call_target="tpu_custom_call" | custom-call | flops 3758096384 | bytes 4718592 | tf_op jit(solution)/shard_map/pallas_call | solution.py:334
  161.0 6.1 %all-to-all-start.3 = ((bf16[8,15,16,256]{3,2,1,0:T(8,128)(2,1)}), bf16[8,15,16,256]{3,2,1,0:T(8,128)(2,1)S(1)}, u32[]{:S(2)}, u32[]{:S(2)}) async-start(bf16[8,15,16,256]{3,2,1,0:T(8,128)(2,1)} %shard_map.210), calls=%async_computation.3 | async-start | bytes 1966080 | tf_op jit(solution)/shard_map/all_to_all | solution.py:472
  167.1 8.6 %shard_map.209 = bf16[8,15,16,256]{3,2,1,0:T(8,128)(2,1)} custom-call(bf16[128,8704]{1,0:T(8,128)(2,1)} %shard_map.206.center_ref, bf16[128,8704]{1,0:T(8,128)(2,1)} %collective-permute-done.7.zlow_ref, bf16[128,8704]{1,0:T(8,128)(2,1)} %copy-done.12, f32[11,32,256]{2,1,0:T(8,128)} %shard_map.207.flow_ref, bf16[128,1536]{1,0:T(8,128)(2,1)} %shard_map.208.weight_ref, ...), custom_call_target="tpu_custom_call" | custom-call | flops 3758096384 | bytes 4718592 | tf_op jit(solution)/shard_map/pallas_call | solution.py:334
  175.7 18.2 %all-to-all-done.3.refs_1_ = bf16[8,15,16,256]{3,2,1,0:T(8,128)(2,1)S(1)} async-done(((bf16[8,15,16,256]{3,2,1,0:T(8,128)(2,1)}), bf16[8,15,16,256]{3,2,1,0:T(8,128)(2,1)S(1)}, u32[]{:S(2)}, u32[]{:S(2)}) %all-to-all-start.3) | async-done | bytes 983072 | tf_op jit(solution)/shard_map/all_to_all | solution.py:472
  193.9 4.8 %all-to-all-start.2 = ((bf16[8,15,16,256]{3,2,1,0:T(8,128)(2,1)}), bf16[8,15,16,256]{3,2,1,0:T(8,128)(2,1)S(1)}, u32[]{:S(2)}, u32[]{:S(2)}) async-start(bf16[8,15,16,256]{3,2,1,0:T(8,128)(2,1)} %shard_map.209), calls=%async_computation.2 | async-start | bytes 1966080 | tf_op jit(solution)/shard_map/all_to_all | solution.py:472
  198.7 0.9 slice.16
  199.6 7.3 %collective-permute-start.9 = (f32[3,32,256]{2,1,0:T(8,128)S(1)}, f32[3,32,256]{2,1,0:T(8,128)S(1)}, u32[]{:S(2)}, u32[]{:S(2)}) collective-permute-start(f32[3,32,256]{2,1,0:T(8,128)S(1)} %slice.16), channel_id=1, source_target_pairs={{0,0},{1,1},{2,2},{3,3},{4,4},{5,5},{6,6},{7,7},{8,8},{9,9},{10,10... | collective-permute-start | bytes 294920 | tf_op jit(solution)/shard_map/ppermute | solution.py:475
  206.9 15.8 %collective-permute-done.9 = f32[3,32,256]{2,1,0:T(8,128)S(1)} collective-permute-done((f32[3,32,256]{2,1,0:T(8,128)S(1)}, f32[3,32,256]{2,1,0:T(8,128)S(1)}, u32[]{:S(2)}, u32[]{:S(2)}) %collective-permute-start.9) | collective-permute-done | bytes 98336 | tf_op jit(solution)/shard_map/ppermute | solution.py:475
  222.7 0.9 copy-done.1
  223.6 2.9 %shard_map.211 = bf16[15,256,256]{2,1,0:T(8,128)(2,1)} custom-call(s32[1]{0:T(128)S(6)} %xor.11.swap_ref, bf16[8,15,16,256]{3,2,1,0:T(8,128)(2,1)} %copy-done.1, bf16[8,15,16,256]{3,2,1,0:T(8,128)(2,1)} %copy-done), custom_call_target="tpu_custom_call" | custom-call | bytes 4194304 | tf_op jit(solution)/shard_map/pallas_call | solution.py:334
  226.5 0.6 copy.55
  (41 shorter events, 0.3 us)
Async XLA Ops:
  7.0 17.3 %collective-permute-start = (bf16[16,8704]{1,0:T(8,128)(2,1)}, bf16[16,8704]{1,0:T(8,128)(2,1)S(1)}, u32[]{:S(2)}, u32[]{:S(2)}) collective-permute-start(bf16[16,8704]{1,0:T(8,128)(2,1)} %get-tuple-element.28), channel_id=1, source_target_pairs={{0,1},{1,0},{2,3},{3,2},{4,5},{5,4},{6,7},{7,6},{8,9},{9,8},{10,11... | collective-permute-start | bytes 835592 | tf_op jit(solution)/shard_map/ppermute | solution.py:409
  7.9 16.5 %collective-permute-start.1 = (bf16[16,8704]{1,0:T(8,128)(2,1)}, bf16[16,8704]{1,0:T(8,128)(2,1)S(1)}, u32[]{:S(2)}, u32[]{:S(2)}) collective-permute-start(bf16[16,8704]{1,0:T(8,128)(2,1)} %get-tuple-element.29), channel_id=1, source_target_pairs={{0,2},{1,3},{2,0},{3,1},{4,6},{5,7},{6,4},{7,5},{8,10},{9,11},{10,... | collective-permute-start | bytes 835592 | tf_op jit(solution)/shard_map/ppermute | solution.py:409
  9.0 15.4 %collective-permute-start.2 = (bf16[16,8704]{1,0:T(8,128)(2,1)}, bf16[16,8704]{1,0:T(8,128)(2,1)S(1)}, u32[]{:S(2)}, u32[]{:S(2)}) collective-permute-start(bf16[16,8704]{1,0:T(8,128)(2,1)} %get-tuple-element.30), channel_id=1, source_target_pairs={{0,3},{1,2},{2,1},{3,0},{4,7},{5,6},{6,5},{7,4},{8,11},{9,10},{10,... | collective-permute-start | bytes 835592 | tf_op jit(solution)/shard_map/ppermute | solution.py:409
  11.7 23.6 %collective-permute-start.3 = (bf16[16,8704]{1,0:T(8,128)(2,1)}, bf16[16,8704]{1,0:T(8,128)(2,1)S(1)}, u32[]{:S(2)}, u32[]{:S(2)}) collective-permute-start(bf16[16,8704]{1,0:T(8,128)(2,1)} %get-tuple-element.31), channel_id=1, source_target_pairs={{0,4},{1,5},{2,6},{3,7},{4,0},{5,1},{6,2},{7,3},{8,12},{9,13},{10,... | collective-permute-start | bytes 835592 | tf_op jit(solution)/shard_map/ppermute | solution.py:409
  18.0 23.3 %collective-permute-start.4 = (bf16[16,8704]{1,0:T(8,128)(2,1)}, bf16[16,8704]{1,0:T(8,128)(2,1)S(1)}, u32[]{:S(2)}, u32[]{:S(2)}) collective-permute-start(bf16[16,8704]{1,0:T(8,128)(2,1)} %get-tuple-element.32), channel_id=1, source_target_pairs={{0,5},{1,4},{2,7},{3,6},{4,1},{5,0},{6,3},{7,2},{8,13},{9,12},{10,... | collective-permute-start | bytes 835592 | tf_op jit(solution)/shard_map/ppermute | solution.py:409
  24.3 56.5 %copy-start.2 = (bf16[16,8704]{1,0:T(8,128)(2,1)}, bf16[16,8704]{1,0:T(8,128)(2,1)S(1)}, u32[]{:S(2)}) copy-start(bf16[16,8704]{1,0:T(8,128)(2,1)S(1)} %collective-permute-done.refs_1_) | copy-start | bytes 835588
  24.3 56.5 %copy-start.3 = (bf16[16,8704]{1,0:T(8,128)(2,1)}, bf16[16,8704]{1,0:T(8,128)(2,1)S(1)}, u32[]{:S(2)}) copy-start(bf16[16,8704]{1,0:T(8,128)(2,1)S(1)} %collective-permute-done.1.refs_2_) | copy-start | bytes 835588
  24.3 56.5 %copy-start.4 = (bf16[16,8704]{1,0:T(8,128)(2,1)}, bf16[16,8704]{1,0:T(8,128)(2,1)S(1)}, u32[]{:S(2)}) copy-start(bf16[16,8704]{1,0:T(8,128)(2,1)S(1)} %collective-permute-done.2.refs_3_) | copy-start | bytes 835588
  35.4 45.4 %copy-start.5 = (bf16[16,8704]{1,0:T(8,128)(2,1)}, bf16[16,8704]{1,0:T(8,128)(2,1)S(1)}, u32[]{:S(2)}) copy-start(bf16[16,8704]{1,0:T(8,128)(2,1)S(1)} %collective-permute-done.3.refs_4_) | copy-start | bytes 835588
  41.3 39.5 %copy-start.6 = (bf16[16,8704]{1,0:T(8,128)(2,1)}, bf16[16,8704]{1,0:T(8,128)(2,1)S(1)}, u32[]{:S(2)}) copy-start(bf16[16,8704]{1,0:T(8,128)(2,1)S(1)} %collective-permute-done.4.refs_5_) | copy-start | bytes 835588
  45.0 35.2 %all-to-all-start = ((bf16[256,2,640]{2,1,0:T(2,128)(2,1)}), bf16[256,2,640]{2,1,0:T(2,128)(2,1)S(1)}, u32[]{:S(2)}, u32[]{:S(2)}) async-start(bf16[256,2,640]{2,1,0:T(2,128)(2,1)} %reshape.60), calls=%async_computation | async-start | bytes 1310720 | tf_op jit(solution)/shard_map/all_to_all | solution.py:419
  59.4 35.6 %collective-permute-start.5 = (bf16[16,8704]{1,0:T(8,128)(2,1)}, bf16[16,8704]{1,0:T(8,128)(2,1)}, u32[]{:S(2)}, u32[]{:S(2)}) collective-permute-start(bf16[16,8704]{1,0:T(8,128)(2,1)} %get-tuple-element.33), channel_id=1, source_target_pairs={{0,6},{1,7},{2,4},{3,5},{4,2},{5,3},{6,0},{7,1},{8,14},{9,15},{10,... | collective-permute-start | bytes 835592 | tf_op jit(solution)/shard_map/ppermute | solution.py:409
  65.9 36.3 %collective-permute-start.6 = (bf16[16,8704]{1,0:T(8,128)(2,1)}, bf16[16,8704]{1,0:T(8,128)(2,1)}, u32[]{:S(2)}, u32[]{:S(2)}) collective-permute-start(bf16[16,8704]{1,0:T(8,128)(2,1)} %get-tuple-element.34), channel_id=1, source_target_pairs={{0,7},{1,6},{2,5},{3,4},{4,3},{5,2},{6,1},{7,0},{8,15},{9,14},{10,... | collective-permute-start | bytes 835592 | tf_op jit(solution)/shard_map/ppermute | solution.py:409
  85.8 20.1 %copy-start.7 = (bf16[256,512]{1,0:T(8,128)(2,1)S(1)}, bf16[256,512]{1,0:T(8,128)(2,1)}, u32[]{:S(2)}) copy-start(bf16[256,512]{1,0:T(8,128)(2,1)} %shard_map.205) | copy-start | bytes 786436
  85.8 37.6 %copy-start.9 = (bf16[256,120]{0,1:T(8,128)(2,1)S(1)}, bf16[256,120]{0,1:T(8,128)(2,1)}, u32[]{:S(2)}) copy-start(bf16[256,120]{0,1:T(8,128)(2,1)} %param.21) | copy-start | bytes 184324
  85.8 37.6 %copy-start.11 = (f32[120]{0:T(128)S(1)}, f32[120]{0:T(128)}, u32[]{:S(2)}) copy-start(f32[120]{0:T(128)} %param.24) | copy-start | bytes 1444
  85.8 38.4 %copy-start.10 = (bf16[120,256]{1,0:T(8,128)(2,1)S(1)}, bf16[120,256]{1,0:T(8,128)(2,1)}, u32[]{:S(2)}) copy-start(bf16[120,256]{1,0:T(8,128)(2,1)} %param.22) | copy-start | bytes 184324
  105.4 20.3 %copy-start.8 = (bf16[3,120,256]{2,1,0:T(8,128)(2,1)S(1)}, bf16[3,120,256]{2,1,0:T(8,128)(2,1)}, u32[]{:S(2)}) copy-start(bf16[3,120,256]{2,1,0:T(8,128)(2,1)} %param.23) | copy-start | bytes 552964
  105.4 45.7 %collective-permute-start.8 = (bf16[128,8704]{1,0:T(8,128)(2,1)}, bf16[128,8704]{1,0:T(8,128)(2,1)S(1)}, u32[]{:S(2)}, u32[]{:S(2)}) collective-permute-start(bf16[128,8704]{1,0:T(8,128)(2,1)} %shard_map.206.center_ref), channel_id=1, source_target_pairs={{0,252},{1,253},{2,254},{3,255},{4,248},{5,249},{6,250},{7,251},{8... | collective-permute-start | bytes 6684680 | tf_op jit(solution)/shard_map/ppermute | solution.py:438
  105.4 45.7 %collective-permute-start.7 = (bf16[128,8704]{1,0:T(8,128)(2,1)}, bf16[128,8704]{1,0:T(8,128)(2,1)}, u32[]{:S(2)}, u32[]{:S(2)}) collective-permute-start(bf16[128,8704]{1,0:T(8,128)(2,1)} %shard_map.206.center_ref), channel_id=1, source_target_pairs={{0,8},{1,9},{2,10},{3,11},{4,12},{5,13},{6,14},{7,15},{8,16},{9,17... | collective-permute-start | bytes 6684680 | tf_op jit(solution)/shard_map/ppermute | solution.py:437
  107.4 39.8 %all-to-all-start.1 = ((bf16[256,2,256]{2,1,0:T(2,128)(2,1)}), bf16[256,2,256]{2,1,0:T(2,128)(2,1)S(1)}, u32[]{:S(2)}, u32[]{:S(2)}) async-start(bf16[256,2,256]{2,1,0:T(2,128)(2,1)} %reshape.62), calls=%async_computation.1 | async-start | bytes 524288 | tf_op jit(solution)/shard_map/all_to_all | solution.py:434
  151.0 1.4 copy-start.12
  161.0 32.9 %all-to-all-start.3 = ((bf16[8,15,16,256]{3,2,1,0:T(8,128)(2,1)}), bf16[8,15,16,256]{3,2,1,0:T(8,128)(2,1)S(1)}, u32[]{:S(2)}, u32[]{:S(2)}) async-start(bf16[8,15,16,256]{3,2,1,0:T(8,128)(2,1)} %shard_map.210), calls=%async_computation.3 | async-start | bytes 1966080 | tf_op jit(solution)/shard_map/all_to_all | solution.py:472
  193.9 28.8 %copy-start = (bf16[8,15,16,256]{3,2,1,0:T(8,128)(2,1)}, bf16[8,15,16,256]{3,2,1,0:T(8,128)(2,1)S(1)}, u32[]{:S(2)}) copy-start(bf16[8,15,16,256]{3,2,1,0:T(8,128)(2,1)S(1)} %all-to-all-done.3.refs_1_) | copy-start | bytes 2949124
  193.9 28.8 %all-to-all-start.2 = ((bf16[8,15,16,256]{3,2,1,0:T(8,128)(2,1)}), bf16[8,15,16,256]{3,2,1,0:T(8,128)(2,1)S(1)}, u32[]{:S(2)}, u32[]{:S(2)}) async-start(bf16[8,15,16,256]{3,2,1,0:T(8,128)(2,1)} %shard_map.209), calls=%async_computation.2 | async-start | bytes 1966080 | tf_op jit(solution)/shard_map/all_to_all | solution.py:472
  199.6 23.0 %collective-permute-start.9 = (f32[3,32,256]{2,1,0:T(8,128)S(1)}, f32[3,32,256]{2,1,0:T(8,128)S(1)}, u32[]{:S(2)}, u32[]{:S(2)}) collective-permute-start(f32[3,32,256]{2,1,0:T(8,128)S(1)} %slice.16), channel_id=1, source_target_pairs={{0,0},{1,1},{2,2},{3,3},{4,4},{5,5},{6,6},{7,7},{8,8},{9,9},{10,10... | collective-permute-start | bytes 294920 | tf_op jit(solution)/shard_map/ppermute | solution.py:475
  222.7 1.0 copy-start.1

commit v6 on v4

--- a/solution.py
+++ b/solution.py
@@ -108,7 +108,7 @@
 
 
 def regroup_kernel(block_ref, coef_ref, *refs):
-    near, rest, last, stages = refs[:FLIP], refs[FLIP], refs[FLIP + 1], refs[FLIP + 2 :]
+    outs, stages = refs[:GROUPS], refs[GROUPS:]
     block = block_ref[0]
     height = ROWS + 2 * PAD
     for stage in stages:
@@ -126,13 +126,7 @@
             for r in range(EDGED):
                 lane = r * NX + side * LANES
                 rows = stage[pl.ds(PAD - 1 + r, PAD, stride=height), :]
-                if j < FLIP:
-                    near[j][:, lane : lane + LANES] = rows.astype(bf16)
-                elif j == FLIP:
-                    last[:, lane : lane + LANES] = rows.astype(bf16)
-                else:
-                    at = (j - FLIP - 1) * PAD
-                    rest[at : at + PAD, lane : lane + LANES] = rows.astype(bf16)
+                outs[j][:, lane : lane + LANES] = rows.astype(bf16)
 
 
 def stress_kernel(table_ref, coef_ref, high_ref, low_ref, out_ref, stress_high, stress_low):
@@ -449,15 +443,10 @@
 
     later, _ = lax.optimization_barrier((own, sent))
     chunks = call(
-        regroup_kernel,
-        [shape(PAD, CELLS)] * FLIP + [shape((FLIP - 1) * PAD, CELLS), shape(PAD, CELLS)], [block_arg, later],
+        regroup_kernel, [shape(PAD, CELLS)] * GROUPS, [block_arg, later],
         [pltpu.VMEM((PAD * (ROWS + 2 * PAD), LANES), f32)] * 2, 1, 0, 4 << 20,
     )
-    chunks, columns = lax.optimization_barrier((chunks, columns))
-    rest = lax.ppermute(chunks[FLIP], "harm", partner(FLIP))
-    last = lax.ppermute(chunks[FLIP + 1], "harm", partner(FLIP))
-    arrived = exchanged(chunks[:FLIP])
-    arrived += exchanged([last] + [rest[m * PAD : (m + 1) * PAD] for m in range(FLIP - 1)])
+    arrived = exchanged(chunks)
 
     wave = (position % HALF).astype(f32) * (2.0 * math.pi / NX)
     half = (position // HALF).astype(jnp.int32)
@@ -473,8 +462,8 @@
         (), 2, 1 << 30, 3 << 20,
     )
     mixed = lax.all_to_all(sent, everyone, 0, 0, tiled=True)
-    arrived, _ = lax.optimization_barrier((arrived, mixed))
-    center = call(assemble_kernel, shape(ALL_PAD, CELLS), [group_arg, *arrived], (), 1, 0, 4 << 20)
+    arrived, _ = lax.optimization_barrier((arrived, sent))
+    center = call(assemble_kernel, shape(ALL_PAD, CELLS), [group_arg, *arrived], (), 1, 1 << 32, 4 << 20)
     z_low = lax.ppermute(center, both, pairs(lambda s, b: ((s + 1) % SPACES, b)))
     z_high = lax.ppermute(center, both, pairs(lambda s, b: ((s - 1) % SPACES, b)))
 
@@ -491,7 +480,7 @@
     inner = call(
         inner_kernel, shape(ALL_PAD, ROWS * NX, dtype=f32), [center, flow, weights, damp],
         [pltpu.VMEM((2, (BLOCKS - 2) * ALL_PAD, NX), bf16), pltpu.VMEM((2, ALL_PAD, NX), f32)],
-        0, 6 << 30, 7 << 20,
+        0, 1 << 37, 7 << 20,
     )
     returned, parts = [], []
     for part in range(PARTS):

time: 221 us -> 211 us (0.955)
  the two profiles are of different devices: /device:TPU:62 before, /device:TPU:40 now
where the time goes in v6:
time: 211 us; the launch traced here: 210 us
  starting transfers between devices  88.9 us (42%)
  waiting for transfers between devices  52.3 us (25%)
  Pallas kernels  50.4 us (24%)
  local copies, waits for them, and re-layouts  12.4 us (6%)
  other arithmetic  4.36 us (2%)
    pallas_call x10, Pallas kernels, call(): pl.pallas_call(kernel, out_shape=out_shape, grid=(1,) if specs else (), i...  50.4 us
    all_to_all x1, starting transfers between devices, local(): mixed = lax.all_to_all(sent, everyone, 0, 0, tiled=True)  28.8 us
    ppermute x7, starting transfers between devices, exchanged(): lax.ppermute(c, 'harm', partner(j + 1))  22.3 us
    all_to_all x2, waiting for transfers between devices, local(): returned.append(lax.all_to_all(rates, 'harm', 0, 0, tiled=True))  21.2 us
    ppermute x1, waiting for transfers between devices, local(): velocity = lax.ppermute(late, both, swap)  19.3 us
    all_to_all x1, starting transfers between devices, local(): columns = lax.all_to_all(sent, everyone, 0, 0, tiled=True)  14.3 us
    all_to_all x2, starting transfers between devices, local(): returned.append(lax.all_to_all(rates, 'harm', 0, 0, tiled=True))  13.9 us
    unnamed x31, local copies, waits for them, and re-layouts  8.01 us
  transfers between devices with their start and end apart: 14, of which 6 were waited for; matrix products, arithmetic and copies ran while one was open for 4% of the time, Pallas kernels for 18%

profile of v6, /device:TPU:40, one launch (start us, length us, event | category | flops | bytes accessed | tf_op | source)
XLA Modules:
  0.0 210.1 jit_solution(15667752220262636269)
XLA Ops:
  0.6 0.8 fusion.2
  1.5 0.6 pad_maximum_fusion.table_ref
  2.1 4.8 %shard_map.203 = bf16[256,1280]{1,0:T(8,128)(2,1)} custom-call(f32[5,15]{1,0:T(8,128)} %pad_maximum_fusion.table_ref, bf16[15,256,256]{2,1,0:T(8,128)(2,1)} %bitcast.29, bf16[256,256]{1,0:T(8,128)(2,1)} %constant.102.clone.high_ref, bf16[256,256]{1,0:T(8,128)(2,1)} %constant.103.clone.low_ref), custom_call_target="tpu_custom_call" | custom-call | flops 1073741824 | bytes 3145728 | tf_op jit(solution)/shard_map/pallas_call | solution.py:359
  6.9 0.5 broadcast.14
  7.5 2.1 reduce
  9.6 1.0 reshape.60
  10.5 14.3 %all-to-all-start = ((bf16[256,2,640]{2,1,0:T(2,128)(2,1)}), bf16[256,2,640]{2,1,0:T(2,128)(2,1)S(1)}, u32[]{:S(2)}, u32[]{:S(2)}) async-start(bf16[256,2,640]{2,1,0:T(2,128)(2,1)} %reshape.60), calls=%async_computation | async-start | bytes 1310720 | tf_op jit(solution)/shard_map/all_to_all | solution.py:442
  24.9 6.4 %shard_map.204 = (bf16[16,8704]{1,0:T(8,128)(2,1)}, bf16[16,8704]{1,0:T(8,128)(2,1)}, bf16[16,8704]{1,0:T(8,128)(2,1)}, bf16[16,8704]{1,0:T(8,128)(2,1)}, bf16[1...) custom-call(s32[1]{0:T(128)S(6)} %xor.10.block_ref, ...), custom_call_target="tpu_custom_call" | custom-call | bytes 4194304 | tf_op jit(solution)/shard_map/pallas_call | solution.py:359
  31.3 1.5 collective-permute-start
  32.8 2.7 %collective-permute-start.1 = (bf16[16,8704]{1,0:T(8,128)(2,1)}, bf16[16,8704]{1,0:T(8,128)(2,1)S(1)}, u32[]{:S(2)}, u32[]{:S(2)}) collective-permute-start(bf16[16,8704]{1,0:T(8,128)(2,1)} %get-tuple-element.23), channel_id=1, source_target_pairs={{0,2},{1,3},{2,0},{3,1},{4,6},{5,7},{6,4},{7,5},{8,10},{9,11},{10,... | collective-permute-start | bytes 835592 | tf_op jit(solution)/shard_map/ppermute | solution.py:407
  35.5 0.5 collective-permute-start.2
  36.0 5.5 %collective-permute-start.3 = (bf16[16,8704]{1,0:T(8,128)(2,1)}, bf16[16,8704]{1,0:T(8,128)(2,1)S(1)}, u32[]{:S(2)}, u32[]{:S(2)}) collective-permute-start(bf16[16,8704]{1,0:T(8,128)(2,1)} %get-tuple-element.25), channel_id=1, source_target_pairs={{0,4},{1,5},{2,6},{3,7},{4,0},{5,1},{6,2},{7,3},{8,12},{9,13},{10,... | collective-permute-start | bytes 835592 | tf_op jit(solution)/shard_map/ppermute | solution.py:407
  41.6 2.0 collective-permute-done.refs_1_
  43.7 7.1 %collective-permute-start.5 = (bf16[16,8704]{1,0:T(8,128)(2,1)}, bf16[16,8704]{1,0:T(8,128)(2,1)}, u32[]{:S(2)}, u32[]{:S(2)}) collective-permute-start(bf16[16,8704]{1,0:T(8,128)(2,1)} %get-tuple-element.27), channel_id=1, source_target_pairs={{0,6},{1,7},{2,4},{3,5},{4,2},{5,3},{6,0},{7,1},{8,14},{9,15},{10,... | collective-permute-start | bytes 835592 | tf_op jit(solution)/shard_map/ppermute | solution.py:407
  50.8 0.5 collective-permute-done.1.refs_2_
  51.3 4.8 %collective-permute-start.6 = (bf16[16,8704]{1,0:T(8,128)(2,1)}, bf16[16,8704]{1,0:T(8,128)(2,1)}, u32[]{:S(2)}, u32[]{:S(2)}) collective-permute-start(bf16[16,8704]{1,0:T(8,128)(2,1)} %get-tuple-element.28), channel_id=1, source_target_pairs={{0,7},{1,6},{2,5},{3,4},{4,3},{5,2},{6,1},{7,0},{8,15},{9,14},{10,... | collective-permute-start | bytes 835592 | tf_op jit(solution)/shard_map/ppermute | solution.py:407
  56.1 0.5 reshape.61
  56.6 0.9 copy.46
  57.6 4.0 %shard_map.205 = bf16[256,512]{1,0:T(8,128)(2,1)} custom-call(f32[1]{0:T(128)} %bitcast.5.wave_ref, s32[1]{0:T(128)} %bitcast.6.half_ref, f32[1,256]{1,0:T(1,128)} %constant.104.clone.ky_ref, f32[32,1]{1,0:T(8,128)} %constant.105.clone.kz_ref, bf16[256,1280]{1,0:T(8,128)(2,1)} %bitcast.33, bf16[64,256]{1,0:T(8,128)(2,1)} %constant.106.clone.fz_high, ...), custom_call_target="tpu_custom_call" | custom-call | flops 1073741824 | bytes 3145728 | tf_op jit(solution)/shard_map/pallas_call | solution.py:359
  61.6 1.7 reduce.1
  63.3 0.8 reshape.62
  64.1 28.8 %all-to-all-start.1 = ((bf16[256,2,256]{2,1,0:T(2,128)(2,1)}), bf16[256,2,256]{2,1,0:T(2,128)(2,1)S(1)}, u32[]{:S(2)}, u32[]{:S(2)}) async-start(bf16[256,2,256]{2,1,0:T(2,128)(2,1)} %reshape.62), calls=%async_computation.1 | async-start | bytes 524288 | tf_op jit(solution)/shard_map/all_to_all | solution.py:464
  93.0 0.7 pad.18
  93.7 0.7 copy.38.synth_ref
  94.5 0.6 pad.17
  95.2 0.7 broadcast_in_dim_reshape.4.damp_ref
  96.0 2.5 %shard_map.208.weight_ref = bf16[128,1664]{1,0:T(8,128)(2,1)} custom-call(f32[3,256]{1,0:T(4,128)} %constant.113.clone.dir_ref, bf16[256,128]{1,0:T(8,128)(2,1)} %copy.38.synth_ref, bf16[128,256]{1,0:T(8,128)(2,1)} %bitcast.39, bf16[3,128,256]{2,1,0:T(8,128)(2,1)} %bitcast.37), custom_call_target="tpu_custom_call" | custom-call | flops 268435456 | bytes 1048576 | tf_op jit(solution)/shard_map/pallas_call | solution.py:359
  98.5 0.6 copy-done.9
  99.3 3.1 %shard_map.206.center_ref = bf16[128,8704]{1,0:T(8,128)(2,1)} custom-call(s32[1]{0:T(128)} %bitcast.group_ref, bf16[16,8704]{1,0:T(8,128)(2,1)} %get-tuple-element.29.refs_0_, bf16[16,8704]{1,0:T(8,128)(2,1)} %copy-done.7, bf16[16,8704]{1,0:T(8,128)(2,1)} %copy-done.8, bf16[16,8704]{1,0:T(8,128)(2,1)} %copy-done.9, bf16[16,8704]{1,0:T(8,128)(2,1)} %copy-done.10, ...), custom_call_target="tpu_custom_call" | custom-call | flops 4294967296 | bytes 4194304 | tf_op jit(solution)/shard_map/pallas_call | solution.py:359
  102.6 1.6 collective-permute-start.8
  104.2 3.1 %all-to-all-done.1 = bf16[256,2,256]{2,1,0:T(2,128)(2,1)S(1)} async-done(((bf16[256,2,256]{2,1,0:T(2,128)(2,1)}), bf16[256,2,256]{2,1,0:T(2,128)(2,1)S(1)}, u32[]{:S(2)}, u32[]{:S(2)}) %all-to-all-start.1) | async-done | bytes 262176 | tf_op jit(solution)/shard_map/all_to_all | solution.py:464
  107.3 0.2 reshape.63
  107.5 0.7 copy.47
  108.2 2.8 %shard_map.207.flow_ref = f32[11,32,256]{2,1,0:T(8,128)} custom-call(bf16[256,512]{1,0:T(8,128)(2,1)} %bitcast.34, bf16[256,1024]{1,0:T(8,128)(2,1)} %constant.114.clone.high_ref, bf16[256,1024]{1,0:T(8,128)(2,1)} %constant.115.clone.low_ref), custom_call_target="tpu_custom_call" | custom-call | flops 536870912 | bytes 2097152 | tf_op jit(solution)/shard_map/pallas_call | solution.py:359
  111.0 12.3 %shard_map.209.inner_ref = f32[128,8192]{1,0:T(8,128)} custom-call(bf16[128,8704]{1,0:T(8,128)(2,1)} %shard_map.206.center_ref, f32[11,32,256]{2,1,0:T(8,128)} %shard_map.207.flow_ref, bf16[128,1664]{1,0:T(8,128)(2,1)} %shard_map.208.weight_ref, f32[128,1]{1,0:T(8,128)} %broadcast_in_dim_reshape.4.damp_ref), custom_call_target="tpu_custom_call" | custom-call | flops 137438953472 | bytes 7340032 | tf_op jit(solution)/shard_map/pallas_call | solution.py:359
  123.3 6.2 %collective-permute-done.7.zlow_ref = bf16[128,8704]{1,0:T(8,128)(2,1)S(1)} collective-permute-done((bf16[128,8704]{1,0:T(8,128)(2,1)}, bf16[128,8704]{1,0:T(8,128)(2,1)S(1)}, u32[]{:S(2)}, u32[]{:S(2)}) %collective-permute-start.7) | collective-permute-done | bytes 2228256 | tf_op jit(solution)/shard_map/ppermute | solution.py:467
  129.5 1.4 copy-done
  130.9 5.8 %shard_map.211 = bf16[8,15,16,256]{3,2,1,0:T(8,128)(2,1)} custom-call(f32[128,8192]{1,0:T(8,128)} %shard_map.209.inner_ref, bf16[128,8704]{1,0:T(8,128)(2,1)} %copy-done, bf16[128,8704]{1,0:T(8,128)(2,1)} %collective-permute-done.8.zhigh_ref, f32[11,32,256]{2,1,0:T(8,128)} %shard_map.207.flow_ref, bf16[128,1664]{1,0:T(8,128)(2,1)} %shard_map.208.weight_ref), custom_call_target="tpu_custom_call" | custom-call | flops 536870912 | bytes 4718592 | tf_op jit(solution)/shard_map/pallas_call | solution.py:359
  136.7 9.3 %all-to-all-start.3 = ((bf16[8,15,16,256]{3,2,1,0:T(8,128)(2,1)}), bf16[8,15,16,256]{3,2,1,0:T(8,128)(2,1)S(1)}, u32[]{:S(2)}, u32[]{:S(2)}) async-start(bf16[8,15,16,256]{3,2,1,0:T(8,128)(2,1)} %shard_map.211), calls=%async_computation.3 | async-start | bytes 1966080 | tf_op jit(solution)/shard_map/all_to_all | solution.py:507
  145.9 5.8 %shard_map.210 = bf16[8,15,16,256]{3,2,1,0:T(8,128)(2,1)} custom-call(f32[128,8192]{1,0:T(8,128)} %shard_map.209.inner_ref, bf16[128,8704]{1,0:T(8,128)(2,1)} %copy-done, bf16[128,8704]{1,0:T(8,128)(2,1)} %collective-permute-done.8.zhigh_ref, f32[11,32,256]{2,1,0:T(8,128)} %shard_map.207.flow_ref, bf16[128,1664]{1,0:T(8,128)(2,1)} %shard_map.208.weight_ref), custom_call_target="tpu_custom_call" | custom-call | flops 536870912 | bytes 4718592 | tf_op jit(solution)/shard_map/pallas_call | solution.py:359
  151.7 21.2 %all-to-all-done.3.refs_1_ = bf16[8,15,16,256]{3,2,1,0:T(8,128)(2,1)S(1)} async-done(((bf16[8,15,16,256]{3,2,1,0:T(8,128)(2,1)}), bf16[8,15,16,256]{3,2,1,0:T(8,128)(2,1)S(1)}, u32[]{:S(2)}, u32[]{:S(2)}) %all-to-all-start.3) | async-done | bytes 983072 | tf_op jit(solution)/shard_map/all_to_all | solution.py:507
  172.9 4.6 %all-to-all-start.2 = ((bf16[8,15,16,256]{3,2,1,0:T(8,128)(2,1)}), bf16[8,15,16,256]{3,2,1,0:T(8,128)(2,1)S(1)}, u32[]{:S(2)}, u32[]{:S(2)}) async-start(bf16[8,15,16,256]{3,2,1,0:T(8,128)(2,1)} %shard_map.210), calls=%async_computation.2 | async-start | bytes 1966080 | tf_op jit(solution)/shard_map/all_to_all | solution.py:507
  177.5 0.9 slice.16
  178.4 7.8 %collective-permute-start.9 = (f32[3,32,256]{2,1,0:T(8,128)S(1)}, f32[3,32,256]{2,1,0:T(8,128)S(1)}, u32[]{:S(2)}, u32[]{:S(2)}) collective-permute-start(f32[3,32,256]{2,1,0:T(8,128)S(1)} %slice.16), channel_id=1, source_target_pairs={{0,0},{1,1},{2,2},{3,3},{4,4},{5,5},{6,6},{7,7},{8,8},{9,9},{10,10... | collective-permute-start | bytes 294920 | tf_op jit(solution)/shard_map/ppermute | solution.py:510
  186.2 19.3 %collective-permute-done.9 = f32[3,32,256]{2,1,0:T(8,128)S(1)} collective-permute-done((f32[3,32,256]{2,1,0:T(8,128)S(1)}, f32[3,32,256]{2,1,0:T(8,128)S(1)}, u32[]{:S(2)}, u32[]{:S(2)}) %collective-permute-start.9) | collective-permute-done | bytes 98336 | tf_op jit(solution)/shard_map/ppermute | solution.py:510
  205.5 1.0 copy-done.2
  206.5 2.9 %shard_map.212 = bf16[15,256,256]{2,1,0:T(8,128)(2,1)} custom-call(s32[1]{0:T(128)S(6)} %xor.11.swap_ref, bf16[8,15,16,256]{3,2,1,0:T(8,128)(2,1)} %copy-done.2, bf16[8,15,16,256]{3,2,1,0:T(8,128)(2,1)} %copy-done.1), custom_call_target="tpu_custom_call" | custom-call | bytes 4194304 | tf_op jit(solution)/shard_map/pallas_call | solution.py:359
  209.4 0.6 copy.51
  (40 shorter events, 0.7 us)
Async XLA Ops:
  10.5 45.6 %all-to-all-start = ((bf16[256,2,640]{2,1,0:T(2,128)(2,1)}), bf16[256,2,640]{2,1,0:T(2,128)(2,1)S(1)}, u32[]{:S(2)}, u32[]{:S(2)}) async-start(bf16[256,2,640]{2,1,0:T(2,128)(2,1)} %reshape.60), calls=%async_computation | async-start | bytes 1310720 | tf_op jit(solution)/shard_map/all_to_all | solution.py:442
  31.3 12.4 %collective-permute-start = (bf16[16,8704]{1,0:T(8,128)(2,1)}, bf16[16,8704]{1,0:T(8,128)(2,1)S(1)}, u32[]{:S(2)}, u32[]{:S(2)}) collective-permute-start(bf16[16,8704]{1,0:T(8,128)(2,1)} %get-tuple-element.22), channel_id=1, source_target_pairs={{0,1},{1,0},{2,3},{3,2},{4,5},{5,4},{6,7},{7,6},{8,9},{9,8},{10,11... | collective-permute-start | bytes 835592 | tf_op jit(solution)/shard_map/ppermute | solution.py:407
  32.8 18.5 %collective-permute-start.1 = (bf16[16,8704]{1,0:T(8,128)(2,1)}, bf16[16,8704]{1,0:T(8,128)(2,1)S(1)}, u32[]{:S(2)}, u32[]{:S(2)}) collective-permute-start(bf16[16,8704]{1,0:T(8,128)(2,1)} %get-tuple-element.23), channel_id=1, source_target_pairs={{0,2},{1,3},{2,0},{3,1},{4,6},{5,7},{6,4},{7,5},{8,10},{9,11},{10,... | collective-permute-start | bytes 835592 | tf_op jit(solution)/shard_map/ppermute | solution.py:407
  35.5 62.9 %collective-permute-start.2 = (bf16[16,8704]{1,0:T(8,128)(2,1)}, bf16[16,8704]{1,0:T(8,128)(2,1)S(1)}, u32[]{:S(2)}, u32[]{:S(2)}) collective-permute-start(bf16[16,8704]{1,0:T(8,128)(2,1)} %get-tuple-element.24), channel_id=1, source_target_pairs={{0,3},{1,2},{2,1},{3,0},{4,7},{5,6},{6,5},{7,4},{8,11},{9,10},{10,... | collective-permute-start | bytes 835592 | tf_op jit(solution)/shard_map/ppermute | solution.py:407
  36.0 62.4 %collective-permute-start.3 = (bf16[16,8704]{1,0:T(8,128)(2,1)}, bf16[16,8704]{1,0:T(8,128)(2,1)S(1)}, u32[]{:S(2)}, u32[]{:S(2)}) collective-permute-start(bf16[16,8704]{1,0:T(8,128)(2,1)} %get-tuple-element.25), channel_id=1, source_target_pairs={{0,4},{1,5},{2,6},{3,7},{4,0},{5,1},{6,2},{7,3},{8,12},{9,13},{10,... | collective-permute-start | bytes 835592 | tf_op jit(solution)/shard_map/ppermute | solution.py:407
  41.6 56.9 %collective-permute-start.4 = (bf16[16,8704]{1,0:T(8,128)(2,1)}, bf16[16,8704]{1,0:T(8,128)(2,1)S(1)}, u32[]{:S(2)}, u32[]{:S(2)}) collective-permute-start(bf16[16,8704]{1,0:T(8,128)(2,1)} %get-tuple-element.26), channel_id=1, source_target_pairs={{0,5},{1,4},{2,7},{3,6},{4,1},{5,0},{6,3},{7,2},{8,13},{9,12},{10,... | collective-permute-start | bytes 835592 | tf_op jit(solution)/shard_map/ppermute | solution.py:407
  43.7 17.9 %copy-start.7 = (bf16[16,8704]{1,0:T(8,128)(2,1)}, bf16[16,8704]{1,0:T(8,128)(2,1)S(1)}, u32[]{:S(2)}) copy-start(bf16[16,8704]{1,0:T(8,128)(2,1)S(1)} %collective-permute-done.refs_1_) | copy-start | bytes 835588
  43.7 54.8 %collective-permute-start.5 = (bf16[16,8704]{1,0:T(8,128)(2,1)}, bf16[16,8704]{1,0:T(8,128)(2,1)}, u32[]{:S(2)}, u32[]{:S(2)}) collective-permute-start(bf16[16,8704]{1,0:T(8,128)(2,1)} %get-tuple-element.27), channel_id=1, source_target_pairs={{0,6},{1,7},{2,4},{3,5},{4,2},{5,3},{6,0},{7,1},{8,14},{9,15},{10,... | collective-permute-start | bytes 835592 | tf_op jit(solution)/shard_map/ppermute | solution.py:407
  51.3 10.3 %copy-start.8 = (bf16[16,8704]{1,0:T(8,128)(2,1)}, bf16[16,8704]{1,0:T(8,128)(2,1)S(1)}, u32[]{:S(2)}) copy-start(bf16[16,8704]{1,0:T(8,128)(2,1)S(1)} %collective-permute-done.1.refs_2_) | copy-start | bytes 835588
  51.3 47.2 %collective-permute-start.6 = (bf16[16,8704]{1,0:T(8,128)(2,1)}, bf16[16,8704]{1,0:T(8,128)(2,1)}, u32[]{:S(2)}, u32[]{:S(2)}) collective-permute-start(bf16[16,8704]{1,0:T(8,128)(2,1)} %get-tuple-element.28), channel_id=1, source_target_pairs={{0,7},{1,6},{2,5},{3,4},{4,3},{5,2},{6,1},{7,0},{8,15},{9,14},{10,... | collective-permute-start | bytes 835592 | tf_op jit(solution)/shard_map/ppermute | solution.py:407
  57.6 35.3 %copy-start.4 = (bf16[256,120]{0,1:T(8,128)(2,1)S(1)}, bf16[256,120]{0,1:T(8,128)(2,1)}, u32[]{:S(2)}) copy-start(bf16[256,120]{0,1:T(8,128)(2,1)} %param.21) | copy-start | bytes 184324
  57.6 35.4 %copy-start.3 = (bf16[3,120,256]{2,1,0:T(8,128)(2,1)S(1)}, bf16[3,120,256]{2,1,0:T(8,128)(2,1)}, u32[]{:S(2)}) copy-start(bf16[3,120,256]{2,1,0:T(8,128)(2,1)} %param.23) | copy-start | bytes 552964
  61.6 32.9 %copy-start.5 = (bf16[120,256]{1,0:T(8,128)(2,1)S(1)}, bf16[120,256]{1,0:T(8,128)(2,1)}, u32[]{:S(2)}) copy-start(bf16[120,256]{1,0:T(8,128)(2,1)} %param.22) | copy-start | bytes 184324
  61.6 33.5 %copy-start.6 = (f32[120]{0:T(128)S(1)}, f32[120]{0:T(128)}, u32[]{:S(2)}) copy-start(f32[120]{0:T(128)} %param.24) | copy-start | bytes 1444
  64.1 43.2 %all-to-all-start.1 = ((bf16[256,2,256]{2,1,0:T(2,128)(2,1)}), bf16[256,2,256]{2,1,0:T(2,128)(2,1)S(1)}, u32[]{:S(2)}, u32[]{:S(2)}) async-start(bf16[256,2,256]{2,1,0:T(2,128)(2,1)} %reshape.62), calls=%async_computation.1 | async-start | bytes 524288 | tf_op jit(solution)/shard_map/all_to_all | solution.py:464
  98.4 0.7 copy-start.9
  98.4 0.8 copy-start.10
  98.5 0.9 copy-start.11
  102.4 27.1 %collective-permute-start.7 = (bf16[128,8704]{1,0:T(8,128)(2,1)}, bf16[128,8704]{1,0:T(8,128)(2,1)S(1)}, u32[]{:S(2)}, u32[]{:S(2)}) collective-permute-start(bf16[128,8704]{1,0:T(8,128)(2,1)} %shard_map.206.center_ref), channel_id=1, source_target_pairs={{0,8},{1,9},{2,10},{3,11},{4,12},{5,13},{6,14},{7,15},{8,16},{9,17... | collective-permute-start | bytes 6684680 | tf_op jit(solution)/shard_map/ppermute | solution.py:467
  102.6 26.9 %collective-permute-start.8 = (bf16[128,8704]{1,0:T(8,128)(2,1)}, bf16[128,8704]{1,0:T(8,128)(2,1)}, u32[]{:S(2)}, u32[]{:S(2)}) collective-permute-start(bf16[128,8704]{1,0:T(8,128)(2,1)} %shard_map.206.center_ref), channel_id=1, source_target_pairs={{0,252},{1,253},{2,254},{3,255},{4,248},{5,249},{6,250},{7,251},{8... | collective-permute-start | bytes 6684680 | tf_op jit(solution)/shard_map/ppermute | solution.py:468
  129.5 1.4 copy-start
  136.7 36.2 %all-to-all-start.3 = ((bf16[8,15,16,256]{3,2,1,0:T(8,128)(2,1)}), bf16[8,15,16,256]{3,2,1,0:T(8,128)(2,1)S(1)}, u32[]{:S(2)}, u32[]{:S(2)}) async-start(bf16[8,15,16,256]{3,2,1,0:T(8,128)(2,1)} %shard_map.211), calls=%async_computation.3 | async-start | bytes 1966080 | tf_op jit(solution)/shard_map/all_to_all | solution.py:507
  172.9 32.7 %copy-start.1 = (bf16[8,15,16,256]{3,2,1,0:T(8,128)(2,1)}, bf16[8,15,16,256]{3,2,1,0:T(8,128)(2,1)S(1)}, u32[]{:S(2)}) copy-start(bf16[8,15,16,256]{3,2,1,0:T(8,128)(2,1)S(1)} %all-to-all-done.3.refs_1_) | copy-start | bytes 2949124
  172.9 32.7 %all-to-all-start.2 = ((bf16[8,15,16,256]{3,2,1,0:T(8,128)(2,1)}), bf16[8,15,16,256]{3,2,1,0:T(8,128)(2,1)S(1)}, u32[]{:S(2)}, u32[]{:S(2)}) async-start(bf16[8,15,16,256]{3,2,1,0:T(8,128)(2,1)} %shard_map.210), calls=%async_computation.2 | async-start | bytes 1966080 | tf_op jit(solution)/shard_map/all_to_all | solution.py:507
  178.4 27.2 %collective-permute-start.9 = (f32[3,32,256]{2,1,0:T(8,128)S(1)}, f32[3,32,256]{2,1,0:T(8,128)S(1)}, u32[]{:S(2)}, u32[]{:S(2)}) collective-permute-start(f32[3,32,256]{2,1,0:T(8,128)S(1)} %slice.16), channel_id=1, source_target_pairs={{0,0},{1,1},{2,2},{3,3},{4,4},{5,5},{6,6},{7,7},{8,8},{9,9},{10,10... | collective-permute-start | bytes 294920 | tf_op jit(solution)/shard_map/ppermute | solution.py:510
  205.5 1.0 copy-start.2

commit v7 on v6

--- a/solution.py
+++ b/solution.py
@@ -271,10 +271,13 @@
 
 
 def assemble_kernel(group_ref, *refs):
-    out_ref = refs[GROUPS]
+    out_ref, *parts = refs[GROUPS:]
     group = group_ref[0]
     for j in range(GROUPS):
-        out_ref[pl.ds(pl.multiple_of((group ^ j) * PAD, PAD), PAD), :] = refs[j][...]
+        where = pl.ds(pl.multiple_of((group ^ j) * PAD, PAD), PAD)
+        out_ref[where, :] = refs[j][...]
+        for n, part in enumerate(parts):
+            part[where, :] = refs[j][:, (n * CHUNK + 1) * NX : ((n + 1) * CHUNK + 1) * NX]
 
 
 def inner_kernel(center_ref, flow_ref, weight_ref, damp_ref, out_ref, operands, locals_):
@@ -448,6 +451,16 @@
     )
     arrived = exchanged(chunks)
 
+    weights = call(
+        weights_kernel, shape(ALL_PAD, BLOCKS * ALL_PAD),
+        [
+            directions.astype(np.float32), pad_groups(synthesis, 1),
+            pad_groups(projection, 0), pad_groups(turn_projection, 1),
+        ],
+        (), 0, 1 << 28, 1 << 20,
+    )
+    columns, weights = lax.optimization_barrier((columns, weights))
+
     wave = (position % HALF).astype(f32) * (2.0 * math.pi / NX)
     half = (position // HALF).astype(jnp.int32)
     bz_high, bz_low = split_table(back_z)
@@ -463,18 +476,14 @@
     )
     mixed = lax.all_to_all(sent, everyone, 0, 0, tiled=True)
     arrived, _ = lax.optimization_barrier((arrived, sent))
-    center = call(assemble_kernel, shape(ALL_PAD, CELLS), [group_arg, *arrived], (), 1, 1 << 32, 4 << 20)
-    z_low = lax.ppermute(center, both, pairs(lambda s, b: ((s + 1) % SPACES, b)))
-    z_high = lax.ppermute(center, both, pairs(lambda s, b: ((s - 1) % SPACES, b)))
-
-    weights = call(
-        weights_kernel, shape(ALL_PAD, BLOCKS * ALL_PAD),
-        [
-            directions.astype(np.float32), pad_groups(synthesis, 1),
-            pad_groups(projection, 0), pad_groups(turn_projection, 1),
-        ],
-        (), 0, 1 << 28, 1 << 20,
+    center, *own_parts = call(
+        assemble_kernel, [shape(ALL_PAD, CELLS)] + [shape(ALL_PAD, CHUNK * NX)] * PARTS,
+        [group_arg, *arrived], (), 1, 1 << 32, 4 << 20,
     )
+    above = pairs(lambda s, b: ((s + 1) % SPACES, b))
+    below = pairs(lambda s, b: ((s - 1) % SPACES, b))
+    halo = [(lax.ppermute(rows, both, above), lax.ppermute(rows, both, below)) for rows in own_parts]
+
     flow = call(fields_kernel, shape(11, ROWS, NX, dtype=f32), [mixed, *split_table(back_x)], (), 0, 1 << 29, 2 << 20)
     damp = pad_groups(damping, 0)[:, None]
     inner = call(
@@ -482,31 +491,29 @@
         [pltpu.VMEM((2, (BLOCKS - 2) * ALL_PAD, NX), bf16), pltpu.VMEM((2, ALL_PAD, NX), f32)],
         0, 1 << 37, 7 << 20,
     )
-    returned, parts = [], []
+    returned = []
     for part in range(PARTS):
         here = pl.BlockSpec((ALL_PAD, CHUNK * NX), lambda i, part=part: (0, part))
-        beyond = pl.BlockSpec(
-            (pl.Element(ALL_PAD), pl.Element(CHUNK * NX)), lambda i, part=part: (0, (part * CHUNK + 1) * NX)
-        )
         rates = call(
             rate_kernel, shape(GROUPS, OWN, CHUNK, NX),
-            [inner, z_low, z_high, flow, weights],
+            [inner, *halo[part], flow, weights],
             [
                 pltpu.VMEM((2, 2 * ALL_PAD, NX), bf16),
                 pltpu.VMEM((2, ALL_PAD, NX), f32),
                 pltpu.VMEM((ALL_PAD * CHUNK, LANES), f32),
                 pltpu.VMEM((ALL_PAD * CHUNK, LANES), f32),
             ],
-            0, 1 << 29, 9 << 19,
+            0, 1 << 33, 9 << 19,
             [
-                here, beyond, beyond,
+                here, VMEM, VMEM,
                 pl.BlockSpec((11, CHUNK, NX), lambda i, part=part: (0, part, 0)), VMEM,
             ],
         )
-        parts.append(rates)
+        inner, rates = lax.optimization_barrier((inner, rates))
+        returned, rates = lax.optimization_barrier((returned, rates))
         returned.append(lax.all_to_all(rates, "harm", 0, 0, tiled=True))
     swap = pairs(lambda s, b: (s, b ^ (FLIP * odd(s))))
-    late, _ = lax.optimization_barrier((flow[0:3], parts[0]))
+    late, _ = lax.optimization_barrier((flow[0:3], rates))
     velocity = lax.ppermute(late, both, swap)
     rate = call(place_kernel, shape(OWN, NY, NX), [group_arg ^ block_arg, *returned], (), 1, 0, 4 << 20)
     return (rate.reshape(OWN, 1, NY, NX), velocity.reshape(3, 1, ROWS, NX))

time: 211 us -> 198 us (0.938)
  the two profiles are of different devices: /device:TPU:40 before, /device:TPU:56 now
where the time goes in v7:
time: 198 us; the launch traced here: 197 us
  starting transfers between devices  80.6 us (41%)
  Pallas kernels  51.3 us (26%)
  waiting for transfers between devices  46 us (23%)
  local copies, waits for them, and re-layouts  12.9 us (7%)
  other arithmetic  4.37 us (2%)
    pallas_call x10, Pallas kernels, call(): pl.pallas_call(kernel, out_shape=out_shape, grid=(1,) if specs else (), i...  51.3 us
    all_to_all x1, starting transfers between devices, local(): mixed = lax.all_to_all(sent, everyone, 0, 0, tiled=True)  23.9 us
    ppermute x7, starting transfers between devices, exchanged(): lax.ppermute(c, 'harm', partner(j + 1))  22.4 us
    ppermute x1, waiting for transfers between devices, local(): velocity = lax.ppermute(late, both, swap)  20.3 us
    all_to_all x2, waiting for transfers between devices, local(): returned.append(lax.all_to_all(rates, 'harm', 0, 0, tiled=True))  18.8 us
    all_to_all x1, starting transfers between devices, local(): columns = lax.all_to_all(sent, everyone, 0, 0, tiled=True)  14.3 us
    all_to_all x2, starting transfers between devices, local(): returned.append(lax.all_to_all(rates, 'harm', 0, 0, tiled=True))  8.82 us
    unnamed x33, local copies, waits for them, and re-layouts  8.38 us
  transfers between devices with their start and end apart: 16, of which 6 were waited for; matrix products, arithmetic and copies ran while one was open for 4% of the time, Pallas kernels for 22%

profile of v7, /device:TPU:56, one launch (start us, length us, event | category | flops | bytes accessed | tf_op | source)
XLA Modules:
  0.0 196.9 jit_solution(3988736758633748461)
XLA Ops:
  0.6 0.8 fusion.2
  1.5 0.6 pad_maximum_fusion.table_ref
  2.1 4.8 %shard_map.203 = bf16[256,1280]{1,0:T(8,128)(2,1)} custom-call(f32[5,15]{1,0:T(8,128)} %pad_maximum_fusion.table_ref, bf16[15,256,256]{2,1,0:T(8,128)(2,1)} %bitcast.29, bf16[256,256]{1,0:T(8,128)(2,1)} %constant.102.clone.high_ref, bf16[256,256]{1,0:T(8,128)(2,1)} %constant.103.clone.low_ref), custom_call_target="tpu_custom_call" | custom-call | flops 1073741824 | bytes 3145728 | tf_op jit(solution)/shard_map/pallas_call | solution.py:362
  6.9 0.5 broadcast.14
  7.5 2.1 %reduce = bf16[256,1280]{1,0:T(8,128)(2,1)S(1)} reduce(bf16[256,1,1280]{2,0,1:T(8,128)(2,1)} %bitcast.32, bf16[]{:T(256)} %broadcast.14), dimensions={1}, to_apply=%copy.36.reduce_sub_computation | reduce | bytes 1310722 | tf_op jit(solution)/shard_map/all_to_all | solution.py:445
  9.6 1.0 reshape.60
  10.6 14.3 %all-to-all-start = ((bf16[256,2,640]{2,1,0:T(2,128)(2,1)}), bf16[256,2,640]{2,1,0:T(2,128)(2,1)S(1)}, u32[]{:S(2)}, u32[]{:S(2)}) async-start(bf16[256,2,640]{2,1,0:T(2,128)(2,1)} %reshape.60), calls=%async_computation | async-start | bytes 1310720 | tf_op jit(solution)/shard_map/all_to_all | solution.py:445
  24.9 6.4 %shard_map.204 = (bf16[16,8704]{1,0:T(8,128)(2,1)}, bf16[16,8704]{1,0:T(8,128)(2,1)}, bf16[16,8704]{1,0:T(8,128)(2,1)}, bf16[16,8704]{1,0:T(8,128)(2,1)}, bf16[1...) custom-call(s32[1]{0:T(128)S(6)} %xor.10.block_ref, ...), custom_call_target="tpu_custom_call" | custom-call | bytes 4194304 | tf_op jit(solution)/shard_map/pallas_call | solution.py:362
  31.2 1.5 collective-permute-start
  32.7 2.7 %collective-permute-start.1 = (bf16[16,8704]{1,0:T(8,128)(2,1)}, bf16[16,8704]{1,0:T(8,128)(2,1)S(1)}, u32[]{:S(2)}, u32[]{:S(2)}) collective-permute-start(bf16[16,8704]{1,0:T(8,128)(2,1)} %get-tuple-element.33), channel_id=1, source_target_pairs={{0,2},{1,3},{2,0},{3,1},{4,6},{5,7},{6,4},{7,5},{8,10},{9,11},{10,... | collective-permute-start | bytes 835592 | tf_op jit(solution)/shard_map/ppermute | solution.py:410
  35.4 0.5 collective-permute-start.2
  35.9 5.5 %collective-permute-start.3 = (bf16[16,8704]{1,0:T(8,128)(2,1)}, bf16[16,8704]{1,0:T(8,128)(2,1)S(1)}, u32[]{:S(2)}, u32[]{:S(2)}) collective-permute-start(bf16[16,8704]{1,0:T(8,128)(2,1)} %get-tuple-element.35), channel_id=1, source_target_pairs={{0,4},{1,5},{2,6},{3,7},{4,0},{5,1},{6,2},{7,3},{8,12},{9,13},{10,... | collective-permute-start | bytes 835592 | tf_op jit(solution)/shard_map/ppermute | solution.py:410
  41.6 2.2 %collective-permute-done.refs_1_ = bf16[16,8704]{1,0:T(8,128)(2,1)S(1)} collective-permute-done((bf16[16,8704]{1,0:T(8,128)(2,1)}, bf16[16,8704]{1,0:T(8,128)(2,1)S(1)}, u32[]{:S(2)}, u32[]{:S(2)}) %collective-permute-start) | collective-permute-done | bytes 278560 | tf_op jit(solution)/shard_map/ppermute | solution.py:410
  43.8 7.0 %collective-permute-start.5 = (bf16[16,8704]{1,0:T(8,128)(2,1)}, bf16[16,8704]{1,0:T(8,128)(2,1)}, u32[]{:S(2)}, u32[]{:S(2)}) collective-permute-start(bf16[16,8704]{1,0:T(8,128)(2,1)} %get-tuple-element.37), channel_id=1, source_target_pairs={{0,6},{1,7},{2,4},{3,5},{4,2},{5,3},{6,0},{7,1},{8,14},{9,15},{10,... | collective-permute-start | bytes 835592 | tf_op jit(solution)/shard_map/ppermute | solution.py:410
  50.8 0.3 collective-permute-done.1.refs_2_
  51.1 5.1 %collective-permute-start.6 = (bf16[16,8704]{1,0:T(8,128)(2,1)}, bf16[16,8704]{1,0:T(8,128)(2,1)}, u32[]{:S(2)}, u32[]{:S(2)}) collective-permute-start(bf16[16,8704]{1,0:T(8,128)(2,1)} %get-tuple-element.38), channel_id=1, source_target_pairs={{0,7},{1,6},{2,5},{3,4},{4,3},{5,2},{6,1},{7,0},{8,15},{9,14},{10,... | collective-permute-start | bytes 835592 | tf_op jit(solution)/shard_map/ppermute | solution.py:410
  56.3 0.7 copy.37.synth_ref
  57.0 0.6 pad.17
  57.8 0.7 pad.18
  58.5 2.5 %shard_map.205.weight_ref = bf16[128,1664]{1,0:T(8,128)(2,1)} custom-call(f32[3,256]{1,0:T(4,128)} %constant.104.clone.dir_ref, bf16[256,128]{1,0:T(8,128)(2,1)} %copy.37.synth_ref, bf16[128,256]{1,0:T(8,128)(2,1)} %bitcast.39, bf16[3,128,256]{2,1,0:T(8,128)(2,1)} %bitcast.37), custom_call_target="tpu_custom_call" | custom-call | flops 268435456 | bytes 1048576 | tf_op jit(solution)/shard_map/pallas_call | solution.py:362
  61.0 0.5 reshape.61
  61.5 0.9 copy.46
  62.4 4.0 %shard_map.206 = bf16[256,512]{1,0:T(8,128)(2,1)} custom-call(f32[1]{0:T(128)} %bitcast.5.wave_ref, s32[1]{0:T(128)} %bitcast.6.half_ref, f32[1,256]{1,0:T(1,128)} %constant.105.clone.ky_ref, f32[32,1]{1,0:T(8,128)} %constant.106.clone.kz_ref, bf16[256,1280]{1,0:T(8,128)(2,1)} %bitcast.33, bf16[64,256]{1,0:T(8,128)(2,1)} %constant.107.clone.fz_high, ...), custom_call_target="tpu_custom_call" | custom-call | flops 1073741824 | bytes 3145728 | tf_op jit(solution)/shard_map/pallas_call | solution.py:362
  66.5 1.7 reduce.1
  68.1 0.8 reshape.62
  68.9 23.9 %all-to-all-start.1 = ((bf16[256,2,256]{2,1,0:T(2,128)(2,1)}), bf16[256,2,256]{2,1,0:T(2,128)(2,1)S(1)}, u32[]{:S(2)}, u32[]{:S(2)}) async-start(bf16[256,2,256]{2,1,0:T(2,128)(2,1)} %reshape.62), calls=%async_computation.1 | async-start | bytes 524288 | tf_op jit(solution)/shard_map/all_to_all | solution.py:477
  93.0 0.7 broadcast_in_dim_reshape.4.damp_ref
  94.0 0.4 copy-done.10
  94.6 3.9 %shard_map.207 = (bf16[128,8704]{1,0:T(8,128)(2,1)}, bf16[128,4096]{1,0:T(8,128)(2,1)}, bf16[128,4096]{1,0:T(8,128)(2,1)}) custom-call(s32[1]{0:T(128)} %bitcast.group_ref, bf16[16,8704]{1,0:T(8,128)(2,1)} %get-tuple-element.40.refs_0_, bf16[16,8704]{1,0:T(8,128)(2,1)} %copy-done.8, bf16[16,8704]{1,0:T(8,128)(2,1)} %copy-done.9, ...), custom_call_target="tpu_custom_call" | custom-call | flops 4294967296 | bytes 4194304 | tf_op jit(solution)/shard_map/pallas_call | solution.py:362
  98.7 1.6 collective-permute-start.8
  100.4 1.6 collective-permute-start.10
  102.1 4.0 %all-to-all-done.1 = bf16[256,2,256]{2,1,0:T(2,128)(2,1)S(1)} async-done(((bf16[256,2,256]{2,1,0:T(2,128)(2,1)}), bf16[256,2,256]{2,1,0:T(2,128)(2,1)S(1)}, u32[]{:S(2)}, u32[]{:S(2)}) %all-to-all-start.1) | async-done | bytes 262176 | tf_op jit(solution)/shard_map/all_to_all | solution.py:477
  106.3 0.7 copy.47
  107.0 2.8 %shard_map.208.flow_ref = f32[11,32,256]{2,1,0:T(8,128)} custom-call(bf16[256,512]{1,0:T(8,128)(2,1)} %bitcast.34, bf16[256,1024]{1,0:T(8,128)(2,1)} %constant.114.clone.high_ref, bf16[256,1024]{1,0:T(8,128)(2,1)} %constant.115.clone.low_ref), custom_call_target="tpu_custom_call" | custom-call | flops 536870912 | bytes 2097152 | tf_op jit(solution)/shard_map/pallas_call | solution.py:362
  109.8 12.4 %shard_map.209.inner_ref = f32[128,8192]{1,0:T(8,128)} custom-call(bf16[128,8704]{1,0:T(8,128)(2,1)} %get-tuple-element.48.center_ref, f32[11,32,256]{2,1,0:T(8,128)} %shard_map.208.flow_ref, bf16[128,1664]{1,0:T(8,128)(2,1)} %shard_map.205.weight_ref, f32[128,1]{1,0:T(8,128)} %broadcast_in_dim_reshape.4.damp_ref), custom_call_target="tpu_custom_call" | custom-call | flops 137438953472 | bytes 7340032 | tf_op jit(solution)/shard_map/pallas_call | solution.py:362
  122.2 1.0 copy-done.6
  123.2 1.0 copy-done.7
  124.2 5.8 %shard_map.210 = bf16[8,15,16,256]{3,2,1,0:T(8,128)(2,1)} custom-call(f32[128,8192]{1,0:T(8,128)} %shard_map.209.inner_ref, bf16[128,4096]{1,0:T(8,128)(2,1)} %copy-done.6, bf16[128,4096]{1,0:T(8,128)(2,1)} %copy-done.7, f32[11,32,256]{2,1,0:T(8,128)} %shard_map.208.flow_ref, bf16[128,1664]{1,0:T(8,128)(2,1)} %shard_map.205.weight_ref), custom_call_target="tpu_custom_call" | custom-call | flops 8589934592 | bytes 4718592 | tf_op jit(solution)/shard_map/pallas_call | solution.py:362
  129.9 5.3 %all-to-all-start.2 = ((bf16[8,15,16,256]{3,2,1,0:T(8,128)(2,1)}), bf16[8,15,16,256]{3,2,1,0:T(8,128)(2,1)S(1)}, u32[]{:S(2)}, u32[]{:S(2)}) async-start(bf16[8,15,16,256]{3,2,1,0:T(8,128)(2,1)} %shard_map.210), calls=%async_computation.2 | async-start | bytes 1966080 | tf_op jit(solution)/shard_map/all_to_all | solution.py:514
  135.2 5.8 %shard_map.211 = bf16[8,15,16,256]{3,2,1,0:T(8,128)(2,1)} custom-call(f32[128,8192]{1,0:T(8,128)} %shard_map.209.inner_ref, bf16[128,4096]{1,0:T(8,128)(2,1)} %collective-permute-done.9.zlow_ref, bf16[128,4096]{1,0:T(8,128)(2,1)} %collective-permute-done.10.zhigh_ref, f32[11,32,256]{2,1,0:T(8,128)} %shard_map.208.flow_ref, ...), custom_call_target="tpu_custom_call" | custom-call | flops 8589934592 | bytes 4718592 | tf_op jit(solution)/shard_map/pallas_call | solution.py:362
  141.0 18.8 %all-to-all-done.2.refs_0_ = bf16[8,15,16,256]{3,2,1,0:T(8,128)(2,1)S(1)} async-done(((bf16[8,15,16,256]{3,2,1,0:T(8,128)(2,1)}), bf16[8,15,16,256]{3,2,1,0:T(8,128)(2,1)S(1)}, u32[]{:S(2)}, u32[]{:S(2)}) %all-to-all-start.2) | async-done | bytes 983072 | tf_op jit(solution)/shard_map/all_to_all | solution.py:514
  159.8 3.6 %all-to-all-start.3 = ((bf16[8,15,16,256]{3,2,1,0:T(8,128)(2,1)}), bf16[8,15,16,256]{3,2,1,0:T(8,128)(2,1)S(1)}, u32[]{:S(2)}, u32[]{:S(2)}) async-start(bf16[8,15,16,256]{3,2,1,0:T(8,128)(2,1)} %shard_map.211), calls=%async_computation.3 | async-start | bytes 1966080 | tf_op jit(solution)/shard_map/all_to_all | solution.py:514
  163.4 0.9 slice.16
  164.3 7.7 %collective-permute-start.11 = (f32[3,32,256]{2,1,0:T(8,128)S(1)}, f32[3,32,256]{2,1,0:T(8,128)S(1)}, u32[]{:S(2)}, u32[]{:S(2)}) collective-permute-start(f32[3,32,256]{2,1,0:T(8,128)S(1)} %slice.16), channel_id=1, source_target_pairs={{0,0},{1,1},{2,2},{3,3},{4,4},{5,5},{6,6},{7,7},{8,8},{9,9},{10,10... | collective-permute-start | bytes 294920 | tf_op jit(solution)/shard_map/ppermute | solution.py:517
  172.0 20.3 %collective-permute-done.11 = f32[3,32,256]{2,1,0:T(8,128)S(1)} collective-permute-done((f32[3,32,256]{2,1,0:T(8,128)S(1)}, f32[3,32,256]{2,1,0:T(8,128)S(1)}, u32[]{:S(2)}, u32[]{:S(2)}) %collective-permute-start.11) | collective-permute-done | bytes 98336 | tf_op jit(solution)/shard_map/ppermute | solution.py:517
  192.3 1.0 copy-done.1
  193.3 2.9 %shard_map.212 = bf16[15,256,256]{2,1,0:T(8,128)(2,1)} custom-call(s32[1]{0:T(128)S(6)} %xor.11.swap_ref, bf16[8,15,16,256]{3,2,1,0:T(8,128)(2,1)} %copy-done, bf16[8,15,16,256]{3,2,1,0:T(8,128)(2,1)} %copy-done.1), custom_call_target="tpu_custom_call" | custom-call | bytes 4194304 | tf_op jit(solution)/shard_map/pallas_call | solution.py:362
  196.2 0.6 copy.51
  (46 shorter events, 1.3 us)
Async XLA Ops:
  10.6 45.6 %copy-start.3 = (bf16[256,120]{0,1:T(8,128)(2,1)S(1)}, bf16[256,120]{0,1:T(8,128)(2,1)}, u32[]{:S(2)}) copy-start(bf16[256,120]{0,1:T(8,128)(2,1)} %param.21) | copy-start | bytes 184324
  10.6 46.5 %copy-start.4 = (bf16[120,256]{1,0:T(8,128)(2,1)S(1)}, bf16[120,256]{1,0:T(8,128)(2,1)}, u32[]{:S(2)}) copy-start(bf16[120,256]{1,0:T(8,128)(2,1)} %param.22) | copy-start | bytes 184324
  10.6 47.1 %copy-start.2 = (bf16[3,120,256]{2,1,0:T(8,128)(2,1)S(1)}, bf16[3,120,256]{2,1,0:T(8,128)(2,1)}, u32[]{:S(2)}) copy-start(bf16[3,120,256]{2,1,0:T(8,128)(2,1)} %param.23) | copy-start | bytes 552964
  10.6 50.4 %all-to-all-start = ((bf16[256,2,640]{2,1,0:T(2,128)(2,1)}), bf16[256,2,640]{2,1,0:T(2,128)(2,1)S(1)}, u32[]{:S(2)}, u32[]{:S(2)}) async-start(bf16[256,2,640]{2,1,0:T(2,128)(2,1)} %reshape.60), calls=%async_computation | async-start | bytes 1310720 | tf_op jit(solution)/shard_map/all_to_all | solution.py:445
  31.2 12.6 %collective-permute-start = (bf16[16,8704]{1,0:T(8,128)(2,1)}, bf16[16,8704]{1,0:T(8,128)(2,1)S(1)}, u32[]{:S(2)}, u32[]{:S(2)}) collective-permute-start(bf16[16,8704]{1,0:T(8,128)(2,1)} %get-tuple-element.32), channel_id=1, source_target_pairs={{0,1},{1,0},{2,3},{3,2},{4,5},{5,4},{6,7},{7,6},{8,9},{9,8},{10,11... | collective-permute-start | bytes 835592 | tf_op jit(solution)/shard_map/ppermute | solution.py:410
  32.7 18.4 %collective-permute-start.1 = (bf16[16,8704]{1,0:T(8,128)(2,1)}, bf16[16,8704]{1,0:T(8,128)(2,1)S(1)}, u32[]{:S(2)}, u32[]{:S(2)}) collective-permute-start(bf16[16,8704]{1,0:T(8,128)(2,1)} %get-tuple-element.33), channel_id=1, source_target_pairs={{0,2},{1,3},{2,0},{3,1},{4,6},{5,7},{6,4},{7,5},{8,10},{9,11},{10,... | collective-permute-start | bytes 835592 | tf_op jit(solution)/shard_map/ppermute | solution.py:410
  35.4 58.3 %collective-permute-start.2 = (bf16[16,8704]{1,0:T(8,128)(2,1)}, bf16[16,8704]{1,0:T(8,128)(2,1)S(1)}, u32[]{:S(2)}, u32[]{:S(2)}) collective-permute-start(bf16[16,8704]{1,0:T(8,128)(2,1)} %get-tuple-element.34), channel_id=1, source_target_pairs={{0,3},{1,2},{2,1},{3,0},{4,7},{5,6},{6,5},{7,4},{8,11},{9,10},{10,... | collective-permute-start | bytes 835592 | tf_op jit(solution)/shard_map/ppermute | solution.py:410
  35.9 57.8 %collective-permute-start.3 = (bf16[16,8704]{1,0:T(8,128)(2,1)}, bf16[16,8704]{1,0:T(8,128)(2,1)S(1)}, u32[]{:S(2)}, u32[]{:S(2)}) collective-permute-start(bf16[16,8704]{1,0:T(8,128)(2,1)} %get-tuple-element.35), channel_id=1, source_target_pairs={{0,4},{1,5},{2,6},{3,7},{4,0},{5,1},{6,2},{7,3},{8,12},{9,13},{10,... | collective-permute-start | bytes 835592 | tf_op jit(solution)/shard_map/ppermute | solution.py:410
  41.5 52.2 %collective-permute-start.4 = (bf16[16,8704]{1,0:T(8,128)(2,1)}, bf16[16,8704]{1,0:T(8,128)(2,1)S(1)}, u32[]{:S(2)}, u32[]{:S(2)}) collective-permute-start(bf16[16,8704]{1,0:T(8,128)(2,1)} %get-tuple-element.36), channel_id=1, source_target_pairs={{0,5},{1,4},{2,7},{3,6},{4,1},{5,0},{6,3},{7,2},{8,13},{9,12},{10,... | collective-permute-start | bytes 835592 | tf_op jit(solution)/shard_map/ppermute | solution.py:410
  43.8 17.7 %copy-start.8 = (bf16[16,8704]{1,0:T(8,128)(2,1)}, bf16[16,8704]{1,0:T(8,128)(2,1)S(1)}, u32[]{:S(2)}) copy-start(bf16[16,8704]{1,0:T(8,128)(2,1)S(1)} %collective-permute-done.refs_1_) | copy-start | bytes 835588
  43.8 49.9 %collective-permute-start.5 = (bf16[16,8704]{1,0:T(8,128)(2,1)}, bf16[16,8704]{1,0:T(8,128)(2,1)}, u32[]{:S(2)}, u32[]{:S(2)}) collective-permute-start(bf16[16,8704]{1,0:T(8,128)(2,1)} %get-tuple-element.37), channel_id=1, source_target_pairs={{0,6},{1,7},{2,4},{3,5},{4,2},{5,3},{6,0},{7,1},{8,14},{9,15},{10,... | collective-permute-start | bytes 835592 | tf_op jit(solution)/shard_map/ppermute | solution.py:410
  51.1 10.4 %copy-start.9 = (bf16[16,8704]{1,0:T(8,128)(2,1)}, bf16[16,8704]{1,0:T(8,128)(2,1)S(1)}, u32[]{:S(2)}) copy-start(bf16[16,8704]{1,0:T(8,128)(2,1)S(1)} %collective-permute-done.1.refs_2_) | copy-start | bytes 835588
  51.1 42.9 %collective-permute-start.6 = (bf16[16,8704]{1,0:T(8,128)(2,1)}, bf16[16,8704]{1,0:T(8,128)(2,1)}, u32[]{:S(2)}, u32[]{:S(2)}) collective-permute-start(bf16[16,8704]{1,0:T(8,128)(2,1)} %get-tuple-element.38), channel_id=1, source_target_pairs={{0,7},{1,6},{2,5},{3,4},{4,3},{5,2},{6,1},{7,0},{8,15},{9,14},{10,... | collective-permute-start | bytes 835592 | tf_op jit(solution)/shard_map/ppermute | solution.py:410
  62.4 30.5 %copy-start.5 = (f32[120]{0:T(128)S(1)}, f32[120]{0:T(128)}, u32[]{:S(2)}) copy-start(f32[120]{0:T(128)} %param.24) | copy-start | bytes 1444
  68.9 37.1 %all-to-all-start.1 = ((bf16[256,2,256]{2,1,0:T(2,128)(2,1)}), bf16[256,2,256]{2,1,0:T(2,128)(2,1)S(1)}, u32[]{:S(2)}, u32[]{:S(2)}) async-start(bf16[256,2,256]{2,1,0:T(2,128)(2,1)} %reshape.62), calls=%async_computation.1 | async-start | bytes 524288 | tf_op jit(solution)/shard_map/all_to_all | solution.py:477
  93.7 0.7 copy-start.10
  93.7 0.8 copy-start.11
  93.7 0.9 copy-start.12
  98.6 23.6 %collective-permute-start.7 = (bf16[128,4096]{1,0:T(8,128)(2,1)}, bf16[128,4096]{1,0:T(8,128)(2,1)S(1)}, u32[]{:S(2)}, u32[]{:S(2)}) collective-permute-start(bf16[128,4096]{1,0:T(8,128)(2,1)} %get-tuple-element.50), channel_id=1, source_target_pairs={{0,8},{1,9},{2,10},{3,11},{4,12},{5,13},{6,14},{7,15},{8,16},{9,17... | collective-permute-start | bytes 3145736 | tf_op jit(solution)/shard_map/ppermute | solution.py:485
  98.7 23.5 %collective-permute-start.8 = (bf16[128,4096]{1,0:T(8,128)(2,1)}, bf16[128,4096]{1,0:T(8,128)(2,1)S(1)}, u32[]{:S(2)}, u32[]{:S(2)}) collective-permute-start(bf16[128,4096]{1,0:T(8,128)(2,1)} %get-tuple-element.50), channel_id=1, source_target_pairs={{0,252},{1,253},{2,254},{3,255},{4,248},{5,249},{6,250},{7,251},{8... | collective-permute-start | bytes 3145736 | tf_op jit(solution)/shard_map/ppermute | solution.py:485
  100.3 34.9 %collective-permute-start.9 = (bf16[128,4096]{1,0:T(8,128)(2,1)}, bf16[128,4096]{1,0:T(8,128)(2,1)}, u32[]{:S(2)}, u32[]{:S(2)}) collective-permute-start(bf16[128,4096]{1,0:T(8,128)(2,1)} %get-tuple-element.53), channel_id=1, source_target_pairs={{0,8},{1,9},{2,10},{3,11},{4,12},{5,13},{6,14},{7,15},{8,16},{9,17... | collective-permute-start | bytes 3145736 | tf_op jit(solution)/shard_map/ppermute | solution.py:485
  100.4 34.8 %collective-permute-start.10 = (bf16[128,4096]{1,0:T(8,128)(2,1)}, bf16[128,4096]{1,0:T(8,128)(2,1)}, u32[]{:S(2)}, u32[]{:S(2)}) collective-permute-start(bf16[128,4096]{1,0:T(8,128)(2,1)} %get-tuple-element.53), channel_id=1, source_target_pairs={{0,252},{1,253},{2,254},{3,255},{4,248},{5,249},{6,250},{7,251},{8... | collective-permute-start | bytes 3145736 | tf_op jit(solution)/shard_map/ppermute | solution.py:485
  122.2 1.0 copy-start.6
  123.2 1.0 copy-start.7
  129.9 29.9 %all-to-all-start.2 = ((bf16[8,15,16,256]{3,2,1,0:T(8,128)(2,1)}), bf16[8,15,16,256]{3,2,1,0:T(8,128)(2,1)S(1)}, u32[]{:S(2)}, u32[]{:S(2)}) async-start(bf16[8,15,16,256]{3,2,1,0:T(8,128)(2,1)} %shard_map.210), calls=%async_computation.2 | async-start | bytes 1966080 | tf_op jit(solution)/shard_map/all_to_all | solution.py:514
  159.8 32.5 %copy-start = (bf16[8,15,16,256]{3,2,1,0:T(8,128)(2,1)}, bf16[8,15,16,256]{3,2,1,0:T(8,128)(2,1)S(1)}, u32[]{:S(2)}) copy-start(bf16[8,15,16,256]{3,2,1,0:T(8,128)(2,1)S(1)} %all-to-all-done.2.refs_0_) | copy-start | bytes 2949124
  159.8 32.5 %all-to-all-start.3 = ((bf16[8,15,16,256]{3,2,1,0:T(8,128)(2,1)}), bf16[8,15,16,256]{3,2,1,0:T(8,128)(2,1)S(1)}, u32[]{:S(2)}, u32[]{:S(2)}) async-start(bf16[8,15,16,256]{3,2,1,0:T(8,128)(2,1)} %shard_map.211), calls=%async_computation.3 | async-start | bytes 1966080 | tf_op jit(solution)/shard_map/all_to_all | solution.py:514
  164.3 28.1 %collective-permute-start.11 = (f32[3,32,256]{2,1,0:T(8,128)S(1)}, f32[3,32,256]{2,1,0:T(8,128)S(1)}, u32[]{:S(2)}, u32[]{:S(2)}) collective-permute-start(f32[3,32,256]{2,1,0:T(8,128)S(1)} %slice.16), channel_id=1, source_target_pairs={{0,0},{1,1},{2,2},{3,3},{4,4},{5,5},{6,6},{7,7},{8,8},{9,9},{10,10... | collective-permute-start | bytes 294920 | tf_op jit(solution)/shard_map/ppermute | solution.py:517
  192.3 1.0 copy-start.1

commit v8 on v7

--- a/solution.py
+++ b/solution.py
@@ -309,7 +309,7 @@
             out_ref[:, where] = locals_[n] + dot(weight_ref[:, : blocks * ALL_PAD], operands[n])
         return carry
 
-    lax.fori_loop(0, ROWS // 2, rows, 0)
+    lax.fori_loop(0, CHUNK // 2, rows, 0)
 
 
 def rate_kernel(
@@ -486,14 +486,16 @@
 
     flow = call(fields_kernel, shape(11, ROWS, NX, dtype=f32), [mixed, *split_table(back_x)], (), 0, 1 << 29, 2 << 20)
     damp = pad_groups(damping, 0)[:, None]
-    inner = call(
-        inner_kernel, shape(ALL_PAD, ROWS * NX, dtype=f32), [center, flow, weights, damp],
-        [pltpu.VMEM((2, (BLOCKS - 2) * ALL_PAD, NX), bf16), pltpu.VMEM((2, ALL_PAD, NX), f32)],
-        0, 1 << 37, 7 << 20,
-    )
     returned = []
     for part in range(PARTS):
-        here = pl.BlockSpec((ALL_PAD, CHUNK * NX), lambda i, part=part: (0, part))
+        size = (pl.Element(ALL_PAD), pl.Element((CHUNK + 2) * NX))
+        here = pl.BlockSpec(size, lambda i, part=part: (0, part * CHUNK * NX))
+        flow_here = pl.BlockSpec((11, CHUNK, NX), lambda i, part=part: (0, part, 0))
+        inner = call(
+            inner_kernel, shape(ALL_PAD, CHUNK * NX, dtype=f32), [center, flow, weights, damp],
+            [pltpu.VMEM((2, (BLOCKS - 2) * ALL_PAD, NX), bf16), pltpu.VMEM((2, ALL_PAD, NX), f32)],
+            0, 1 << 37, 7 << 19, [here, flow_here, VMEM, VMEM],
+        )
         rates = call(
             rate_kernel, shape(GROUPS, OWN, CHUNK, NX),
             [inner, *halo[part], flow, weights],
@@ -504,12 +506,9 @@
                 pltpu.VMEM((ALL_PAD * CHUNK, LANES), f32),
             ],
             0, 1 << 33, 9 << 19,
-            [
-                here, VMEM, VMEM,
-                pl.BlockSpec((11, CHUNK, NX), lambda i, part=part: (0, part, 0)), VMEM,
-            ],
+            [VMEM, VMEM, VMEM, flow_here, VMEM],
         )
-        inner, rates = lax.optimization_barrier((inner, rates))
+        center, rates = lax.optimization_barrier((center, rates))
         returned, rates = lax.optimization_barrier((returned, rates))
         returned.append(lax.all_to_all(rates, "harm", 0, 0, tiled=True))
     swap = pairs(lambda s, b: (s, b ^ (FLIP * odd(s))))

time: 198 us -> 198 us (level)
  the two profiles are of different devices: /device:TPU:56 before, /device:TPU:62 now
where the time goes in v8:
time: 198 us; the launch traced here: 194 us
  starting transfers between devices  83.3 us (42%)
  Pallas kernels  53 us (27%)
  waiting for transfers between devices  38.1 us (19%)
  local copies, waits for them, and re-layouts  13.2 us (7%)
  other arithmetic  4.57 us (2%)
    pallas_call x11, Pallas kernels, call(): pl.pallas_call(kernel, out_shape=out_shape, grid=(1,) if specs else (), i...  53 us
    all_to_all x1, starting transfers between devices, local(): mixed = lax.all_to_all(sent, everyone, 0, 0, tiled=True)  24.4 us
    ppermute x7, starting transfers between devices, exchanged(): lax.ppermute(c, 'harm', partner(j + 1))  22.2 us
    ppermute x1, waiting for transfers between devices, local(): velocity = lax.ppermute(late, both, swap)  18.3 us
    all_to_all x2, waiting for transfers between devices, local(): returned.append(lax.all_to_all(rates, 'harm', 0, 0, tiled=True))  14.4 us
    all_to_all x1, starting transfers between devices, local(): columns = lax.all_to_all(sent, everyone, 0, 0, tiled=True)  14.2 us
    all_to_all x2, starting transfers between devices, local(): returned.append(lax.all_to_all(rates, 'harm', 0, 0, tiled=True))  11.8 us
    unnamed x31, local copies, waits for them, and re-layouts  8.7 us
  transfers between devices with their start and end apart: 16, of which 5 were waited for; matrix products, arithmetic and copies ran while one was open for 5% of the time, Pallas kernels for 23%

profile of v8, /device:TPU:62, one launch (start us, length us, event | category | flops | bytes accessed | tf_op | source)
XLA Modules:
  0.0 194.0 jit_solution(10196657162645317027)
XLA Ops:
  0.6 0.8 fusion.2
  1.5 0.6 pad_maximum_fusion.table_ref
  2.1 4.8 %shard_map.203 = bf16[256,1280]{1,0:T(8,128)(2,1)} custom-call(f32[5,15]{1,0:T(8,128)} %pad_maximum_fusion.table_ref, bf16[15,256,256]{2,1,0:T(8,128)(2,1)} %bitcast.29, bf16[256,256]{1,0:T(8,128)(2,1)} %constant.102.clone.high_ref, bf16[256,256]{1,0:T(8,128)(2,1)} %constant.103.clone.low_ref), custom_call_target="tpu_custom_call" | custom-call | flops 1073741824 | bytes 3145728 | tf_op jit(solution)/shard_map/pallas_call | solution.py:362
  6.9 0.6 broadcast.14
  7.5 2.2 %reduce = bf16[256,1280]{1,0:T(8,128)(2,1)S(1)} reduce(bf16[256,1,1280]{2,0,1:T(8,128)(2,1)} %bitcast.32, bf16[]{:T(256)} %broadcast.14), dimensions={1}, to_apply=%copy.39.reduce_sub_computation | reduce | bytes 1310722 | tf_op jit(solution)/shard_map/all_to_all | solution.py:445
  9.8 1.0 reshape.60
  10.7 14.2 %all-to-all-start = ((bf16[256,2,640]{2,1,0:T(2,128)(2,1)}), bf16[256,2,640]{2,1,0:T(2,128)(2,1)S(1)}, u32[]{:S(2)}, u32[]{:S(2)}) async-start(bf16[256,2,640]{2,1,0:T(2,128)(2,1)} %reshape.60), calls=%async_computation | async-start | bytes 1310720 | tf_op jit(solution)/shard_map/all_to_all | solution.py:445
  25.0 6.4 %shard_map.204 = (bf16[16,8704]{1,0:T(8,128)(2,1)}, bf16[16,8704]{1,0:T(8,128)(2,1)}, bf16[16,8704]{1,0:T(8,128)(2,1)}, bf16[16,8704]{1,0:T(8,128)(2,1)}, bf16[1...) custom-call(s32[1]{0:T(128)S(6)} %xor.10.block_ref, ...), custom_call_target="tpu_custom_call" | custom-call | bytes 4194304 | tf_op jit(solution)/shard_map/pallas_call | solution.py:362
  31.4 0.8 collective-permute-start
  32.2 1.1 collective-permute-start.1
  33.4 2.7 %collective-permute-start.2 = (bf16[16,8704]{1,0:T(8,128)(2,1)}, bf16[16,8704]{1,0:T(8,128)(2,1)S(1)}, u32[]{:S(2)}, u32[]{:S(2)}) collective-permute-start(bf16[16,8704]{1,0:T(8,128)(2,1)} %get-tuple-element.34), channel_id=1, source_target_pairs={{0,3},{1,2},{2,1},{3,0},{4,7},{5,6},{6,5},{7,4},{8,11},{9,10},{10,... | collective-permute-start | bytes 835592 | tf_op jit(solution)/shard_map/ppermute | solution.py:410
  36.1 5.5 %collective-permute-start.3 = (bf16[16,8704]{1,0:T(8,128)(2,1)}, bf16[16,8704]{1,0:T(8,128)(2,1)S(1)}, u32[]{:S(2)}, u32[]{:S(2)}) collective-permute-start(bf16[16,8704]{1,0:T(8,128)(2,1)} %get-tuple-element.35), channel_id=1, source_target_pairs={{0,4},{1,5},{2,6},{3,7},{4,0},{5,1},{6,2},{7,3},{8,12},{9,13},{10,... | collective-permute-start | bytes 835592 | tf_op jit(solution)/shard_map/ppermute | solution.py:410
  41.6 1.9 collective-permute-done.refs_1_
  43.5 5.5 %collective-permute-start.5 = (bf16[16,8704]{1,0:T(8,128)(2,1)}, bf16[16,8704]{1,0:T(8,128)(2,1)}, u32[]{:S(2)}, u32[]{:S(2)}) collective-permute-start(bf16[16,8704]{1,0:T(8,128)(2,1)} %get-tuple-element.37), channel_id=1, source_target_pairs={{0,6},{1,7},{2,4},{3,5},{4,2},{5,3},{6,0},{7,1},{8,14},{9,15},{10,... | collective-permute-start | bytes 835592 | tf_op jit(solution)/shard_map/ppermute | solution.py:410
  49.5 6.4 %collective-permute-start.6 = (bf16[16,8704]{1,0:T(8,128)(2,1)}, bf16[16,8704]{1,0:T(8,128)(2,1)}, u32[]{:S(2)}, u32[]{:S(2)}) collective-permute-start(bf16[16,8704]{1,0:T(8,128)(2,1)} %get-tuple-element.38), channel_id=1, source_target_pairs={{0,7},{1,6},{2,5},{3,4},{4,3},{5,2},{6,1},{7,0},{8,15},{9,14},{10,... | collective-permute-start | bytes 835592 | tf_op jit(solution)/shard_map/ppermute | solution.py:410
  56.0 0.7 copy.40.synth_ref
  56.8 0.6 pad.17
  57.5 0.7 pad.18
  58.2 2.5 %shard_map.205.weight_ref = bf16[128,1664]{1,0:T(8,128)(2,1)} custom-call(f32[3,256]{1,0:T(4,128)} %constant.104.clone.dir_ref, bf16[256,128]{1,0:T(8,128)(2,1)} %copy.40.synth_ref, bf16[128,256]{1,0:T(8,128)(2,1)} %bitcast.39, bf16[3,128,256]{2,1,0:T(8,128)(2,1)} %bitcast.37), custom_call_target="tpu_custom_call" | custom-call | flops 268435456 | bytes 1048576 | tf_op jit(solution)/shard_map/pallas_call | solution.py:362
  60.7 0.5 reshape.61
  61.2 0.9 copy.50
  62.1 4.0 %shard_map.206 = bf16[256,512]{1,0:T(8,128)(2,1)} custom-call(f32[1]{0:T(128)} %bitcast.5.wave_ref, s32[1]{0:T(128)} %bitcast.6.half_ref, f32[1,256]{1,0:T(1,128)} %constant.105.clone.ky_ref, f32[32,1]{1,0:T(8,128)} %constant.106.clone.kz_ref, bf16[256,1280]{1,0:T(8,128)(2,1)} %bitcast.33, bf16[64,256]{1,0:T(8,128)(2,1)} %constant.107.clone.fz_high, ...), custom_call_target="tpu_custom_call" | custom-call | flops 1073741824 | bytes 3145728 | tf_op jit(solution)/shard_map/pallas_call | solution.py:362
  66.2 1.8 reduce.1
  67.9 0.8 reshape.62
  68.7 24.4 %all-to-all-start.1 = ((bf16[256,2,256]{2,1,0:T(2,128)(2,1)}), bf16[256,2,256]{2,1,0:T(2,128)(2,1)S(1)}, u32[]{:S(2)}, u32[]{:S(2)}) async-start(bf16[256,2,256]{2,1,0:T(2,128)(2,1)} %reshape.62), calls=%async_computation.1 | async-start | bytes 524288 | tf_op jit(solution)/shard_map/all_to_all | solution.py:477
  93.2 0.7 broadcast_in_dim_reshape.4.damp_ref
  94.0 0.6 copy-done.9
  94.8 3.9 %shard_map.207 = (bf16[128,8704]{1,0:T(8,128)(2,1)}, bf16[128,4096]{1,0:T(8,128)(2,1)}, bf16[128,4096]{1,0:T(8,128)(2,1)}) custom-call(s32[1]{0:T(128)} %bitcast.group_ref, bf16[16,8704]{1,0:T(8,128)(2,1)} %get-tuple-element.40.refs_0_, bf16[16,8704]{1,0:T(8,128)(2,1)} %copy-done.7, bf16[16,8704]{1,0:T(8,128)(2,1)} %copy-done.8, bf16[16,8704]{1,0:T(8,128)(2,1)} %copy-done.9, ...), custom_call_target="tpu_custom_call" | custom-call | flops 4294967296 | bytes 4194304 | tf_op jit(solution)/shard_map/pallas_call | solution.py:362
  98.8 1.6 collective-permute-start.8
  100.5 1.6 collective-permute-start.10
  102.2 2.9 %all-to-all-done.1 = bf16[256,2,256]{2,1,0:T(2,128)(2,1)S(1)} async-done(((bf16[256,2,256]{2,1,0:T(2,128)(2,1)}), bf16[256,2,256]{2,1,0:T(2,128)(2,1)S(1)}, u32[]{:S(2)}, u32[]{:S(2)}) %all-to-all-start.1) | async-done | bytes 262176 | tf_op jit(solution)/shard_map/all_to_all | solution.py:477
  105.3 0.7 copy.51
  106.1 2.8 %shard_map.208.flow_ref = f32[11,32,256]{2,1,0:T(8,128)} custom-call(bf16[256,512]{1,0:T(8,128)(2,1)} %bitcast.34, bf16[256,1024]{1,0:T(8,128)(2,1)} %constant.114.clone.high_ref, bf16[256,1024]{1,0:T(8,128)(2,1)} %constant.115.clone.low_ref), custom_call_target="tpu_custom_call" | custom-call | flops 536870912 | bytes 2097152 | tf_op jit(solution)/shard_map/pallas_call | solution.py:362
  108.9 7.1 %shard_map.209.inner_ref = f32[128,4096]{1,0:T(8,128)} custom-call(bf16[128,8704]{1,0:T(8,128)(2,1)} %get-tuple-element.52.center_ref, f32[11,32,256]{2,1,0:T(8,128)} %shard_map.208.flow_ref, bf16[128,1664]{1,0:T(8,128)(2,1)} %shard_map.205.weight_ref, f32[128,1]{1,0:T(8,128)} %broadcast_in_dim_reshape.4.damp_ref), custom_call_target="tpu_custom_call" | custom-call | flops 137438953472 | bytes 3670016 | tf_op jit(solution)/shard_map/pallas_call | solution.py:362
  116.0 1.1 copy-done.5
  117.0 1.0 copy-done.6
  118.0 5.8 %shard_map.210 = bf16[8,15,16,256]{3,2,1,0:T(8,128)(2,1)} custom-call(f32[128,4096]{1,0:T(8,128)} %shard_map.209.inner_ref, bf16[128,4096]{1,0:T(8,128)(2,1)} %copy-done.5, bf16[128,4096]{1,0:T(8,128)(2,1)} %copy-done.6, f32[11,32,256]{2,1,0:T(8,128)} %shard_map.208.flow_ref, bf16[128,1664]{1,0:T(8,128)(2,1)} %shard_map.205.weight_ref), custom_call_target="tpu_custom_call" | custom-call | flops 8589934592 | bytes 4718592 | tf_op jit(solution)/shard_map/pallas_call | solution.py:362
  123.8 6.9 %all-to-all-start.2 = ((bf16[8,15,16,256]{3,2,1,0:T(8,128)(2,1)}), bf16[8,15,16,256]{3,2,1,0:T(8,128)(2,1)}, u32[]{:S(2)}, u32[]{:S(2)}) async-start(bf16[8,15,16,256]{3,2,1,0:T(8,128)(2,1)} %shard_map.210), calls=%async_computation.2 | async-start | bytes 1966080 | tf_op jit(solution)/shard_map/all_to_all | solution.py:513
  130.8 7.1 %shard_map.211.inner_ref = f32[128,4096]{1,0:T(8,128)} custom-call(bf16[128,8704]{1,0:T(8,128)(2,1)} %get-tuple-element.52.center_ref, f32[11,32,256]{2,1,0:T(8,128)} %shard_map.208.flow_ref, bf16[128,1664]{1,0:T(8,128)(2,1)} %shard_map.205.weight_ref, f32[128,1]{1,0:T(8,128)} %broadcast_in_dim_reshape.4.damp_ref), custom_call_target="tpu_custom_call" | custom-call | flops 137438953472 | bytes 3670016 | tf_op jit(solution)/shard_map/pallas_call | solution.py:362
  137.8 5.8 %shard_map.212 = bf16[8,15,16,256]{3,2,1,0:T(8,128)(2,1)} custom-call(f32[128,4096]{1,0:T(8,128)} %shard_map.211.inner_ref, bf16[128,4096]{1,0:T(8,128)(2,1)} %collective-permute-done.9.zlow_ref, bf16[128,4096]{1,0:T(8,128)(2,1)} %collective-permute-done.10.zhigh_ref, f32[11,32,256]{2,1,0:T(8,128)} %shard_map.208.flow_ref, ...), custom_call_target="tpu_custom_call" | custom-call | flops 8589934592 | bytes 4718592 | tf_op jit(solution)/shard_map/pallas_call | solution.py:362
  143.6 14.4 %all-to-all-done.2.refs_0_ = bf16[8,15,16,256]{3,2,1,0:T(8,128)(2,1)} async-done(((bf16[8,15,16,256]{3,2,1,0:T(8,128)(2,1)}), bf16[8,15,16,256]{3,2,1,0:T(8,128)(2,1)}, u32[]{:S(2)}, u32[]{:S(2)}) %all-to-all-start.2) | async-done | bytes 983072 | tf_op jit(solution)/shard_map/all_to_all | solution.py:513
  158.0 4.9 %all-to-all-start.3 = ((bf16[8,15,16,256]{3,2,1,0:T(8,128)(2,1)}), bf16[8,15,16,256]{3,2,1,0:T(8,128)(2,1)S(1)}, u32[]{:S(2)}, u32[]{:S(2)}) async-start(bf16[8,15,16,256]{3,2,1,0:T(8,128)(2,1)} %shard_map.212), calls=%async_computation.3 | async-start | bytes 1966080 | tf_op jit(solution)/shard_map/all_to_all | solution.py:513
  162.9 0.9 slice.16
  163.8 7.3 %collective-permute-start.11 = (f32[3,32,256]{2,1,0:T(8,128)S(1)}, f32[3,32,256]{2,1,0:T(8,128)S(1)}, u32[]{:S(2)}, u32[]{:S(2)}) collective-permute-start(f32[3,32,256]{2,1,0:T(8,128)S(1)} %slice.16), channel_id=1, source_target_pairs={{0,0},{1,1},{2,2},{3,3},{4,4},{5,5},{6,6},{7,7},{8,8},{9,9},{10,10... | collective-permute-start | bytes 294920 | tf_op jit(solution)/shard_map/ppermute | solution.py:516
  171.1 18.3 %collective-permute-done.11 = f32[3,32,256]{2,1,0:T(8,128)S(1)} collective-permute-done((f32[3,32,256]{2,1,0:T(8,128)S(1)}, f32[3,32,256]{2,1,0:T(8,128)S(1)}, u32[]{:S(2)}, u32[]{:S(2)}) %collective-permute-start.11) | collective-permute-done | bytes 98336 | tf_op jit(solution)/shard_map/ppermute | solution.py:516
  189.4 1.0 copy-done
  190.4 2.9 %shard_map.213 = bf16[15,256,256]{2,1,0:T(8,128)(2,1)} custom-call(s32[1]{0:T(128)S(6)} %xor.11.swap_ref, bf16[8,15,16,256]{3,2,1,0:T(8,128)(2,1)} %all-to-all-done.2.refs_0_, bf16[8,15,16,256]{3,2,1,0:T(8,128)(2,1)} %copy-done), custom_call_target="tpu_custom_call" | custom-call | bytes 4194304 | tf_op jit(solution)/shard_map/pallas_call | solution.py:362
  193.3 0.6 copy.55
  (45 shorter events, 1.5 us)
Async XLA Ops:
  9.7 46.2 %copy-start.2 = (bf16[256,120]{0,1:T(8,128)(2,1)S(1)}, bf16[256,120]{0,1:T(8,128)(2,1)}, u32[]{:S(2)}) copy-start(bf16[256,120]{0,1:T(8,128)(2,1)} %param.21) | copy-start | bytes 184324
  10.7 46.0 %copy-start.3 = (bf16[120,256]{1,0:T(8,128)(2,1)S(1)}, bf16[120,256]{1,0:T(8,128)(2,1)}, u32[]{:S(2)}) copy-start(bf16[120,256]{1,0:T(8,128)(2,1)} %param.22) | copy-start | bytes 184324
  10.7 46.7 %copy-start.1 = (bf16[3,120,256]{2,1,0:T(8,128)(2,1)S(1)}, bf16[3,120,256]{2,1,0:T(8,128)(2,1)}, u32[]{:S(2)}) copy-start(bf16[3,120,256]{2,1,0:T(8,128)(2,1)} %param.23) | copy-start | bytes 552964
  10.7 49.9 %all-to-all-start = ((bf16[256,2,640]{2,1,0:T(2,128)(2,1)}), bf16[256,2,640]{2,1,0:T(2,128)(2,1)S(1)}, u32[]{:S(2)}, u32[]{:S(2)}) async-start(bf16[256,2,640]{2,1,0:T(2,128)(2,1)} %reshape.60), calls=%async_computation | async-start | bytes 1310720 | tf_op jit(solution)/shard_map/all_to_all | solution.py:445
  31.4 12.1 %collective-permute-start = (bf16[16,8704]{1,0:T(8,128)(2,1)}, bf16[16,8704]{1,0:T(8,128)(2,1)S(1)}, u32[]{:S(2)}, u32[]{:S(2)}) collective-permute-start(bf16[16,8704]{1,0:T(8,128)(2,1)} %get-tuple-element.32), channel_id=1, source_target_pairs={{0,1},{1,0},{2,3},{3,2},{4,5},{5,4},{6,7},{7,6},{8,9},{9,8},{10,11... | collective-permute-start | bytes 835592 | tf_op jit(solution)/shard_map/ppermute | solution.py:410
  32.2 17.3 %collective-permute-start.1 = (bf16[16,8704]{1,0:T(8,128)(2,1)}, bf16[16,8704]{1,0:T(8,128)(2,1)S(1)}, u32[]{:S(2)}, u32[]{:S(2)}) collective-permute-start(bf16[16,8704]{1,0:T(8,128)(2,1)} %get-tuple-element.33), channel_id=1, source_target_pairs={{0,2},{1,3},{2,0},{3,1},{4,6},{5,7},{6,4},{7,5},{8,10},{9,11},{10,... | collective-permute-start | bytes 835592 | tf_op jit(solution)/shard_map/ppermute | solution.py:410
  33.4 60.5 %collective-permute-start.2 = (bf16[16,8704]{1,0:T(8,128)(2,1)}, bf16[16,8704]{1,0:T(8,128)(2,1)S(1)}, u32[]{:S(2)}, u32[]{:S(2)}) collective-permute-start(bf16[16,8704]{1,0:T(8,128)(2,1)} %get-tuple-element.34), channel_id=1, source_target_pairs={{0,3},{1,2},{2,1},{3,0},{4,7},{5,6},{6,5},{7,4},{8,11},{9,10},{10,... | collective-permute-start | bytes 835592 | tf_op jit(solution)/shard_map/ppermute | solution.py:410
  36.1 57.8 %collective-permute-start.3 = (bf16[16,8704]{1,0:T(8,128)(2,1)}, bf16[16,8704]{1,0:T(8,128)(2,1)S(1)}, u32[]{:S(2)}, u32[]{:S(2)}) collective-permute-start(bf16[16,8704]{1,0:T(8,128)(2,1)} %get-tuple-element.35), channel_id=1, source_target_pairs={{0,4},{1,5},{2,6},{3,7},{4,0},{5,1},{6,2},{7,3},{8,12},{9,13},{10,... | collective-permute-start | bytes 835592 | tf_op jit(solution)/shard_map/ppermute | solution.py:410
  41.6 52.3 %collective-permute-start.4 = (bf16[16,8704]{1,0:T(8,128)(2,1)}, bf16[16,8704]{1,0:T(8,128)(2,1)S(1)}, u32[]{:S(2)}, u32[]{:S(2)}) collective-permute-start(bf16[16,8704]{1,0:T(8,128)(2,1)} %get-tuple-element.36), channel_id=1, source_target_pairs={{0,5},{1,4},{2,7},{3,6},{4,1},{5,0},{6,3},{7,2},{8,13},{9,12},{10,... | collective-permute-start | bytes 835592 | tf_op jit(solution)/shard_map/ppermute | solution.py:410
  43.5 17.7 %copy-start.7 = (bf16[16,8704]{1,0:T(8,128)(2,1)}, bf16[16,8704]{1,0:T(8,128)(2,1)S(1)}, u32[]{:S(2)}) copy-start(bf16[16,8704]{1,0:T(8,128)(2,1)S(1)} %collective-permute-done.refs_1_) | copy-start | bytes 835588
  43.5 50.4 %collective-permute-start.5 = (bf16[16,8704]{1,0:T(8,128)(2,1)}, bf16[16,8704]{1,0:T(8,128)(2,1)}, u32[]{:S(2)}, u32[]{:S(2)}) collective-permute-start(bf16[16,8704]{1,0:T(8,128)(2,1)} %get-tuple-element.37), channel_id=1, source_target_pairs={{0,6},{1,7},{2,4},{3,5},{4,2},{5,3},{6,0},{7,1},{8,14},{9,15},{10,... | collective-permute-start | bytes 835592 | tf_op jit(solution)/shard_map/ppermute | solution.py:410
  49.5 11.7 %copy-start.8 = (bf16[16,8704]{1,0:T(8,128)(2,1)}, bf16[16,8704]{1,0:T(8,128)(2,1)S(1)}, u32[]{:S(2)}) copy-start(bf16[16,8704]{1,0:T(8,128)(2,1)S(1)} %collective-permute-done.1.refs_2_) | copy-start | bytes 835588
  49.5 44.4 %collective-permute-start.6 = (bf16[16,8704]{1,0:T(8,128)(2,1)}, bf16[16,8704]{1,0:T(8,128)(2,1)}, u32[]{:S(2)}, u32[]{:S(2)}) collective-permute-start(bf16[16,8704]{1,0:T(8,128)(2,1)} %get-tuple-element.38), channel_id=1, source_target_pairs={{0,7},{1,6},{2,5},{3,4},{4,3},{5,2},{6,1},{7,0},{8,15},{9,14},{10,... | collective-permute-start | bytes 835592 | tf_op jit(solution)/shard_map/ppermute | solution.py:410
  62.1 30.9 %copy-start.4 = (f32[120]{0:T(128)S(1)}, f32[120]{0:T(128)}, u32[]{:S(2)}) copy-start(f32[120]{0:T(128)} %param.24) | copy-start | bytes 1444
  68.7 36.4 %all-to-all-start.1 = ((bf16[256,2,256]{2,1,0:T(2,128)(2,1)}), bf16[256,2,256]{2,1,0:T(2,128)(2,1)S(1)}, u32[]{:S(2)}, u32[]{:S(2)}) async-start(bf16[256,2,256]{2,1,0:T(2,128)(2,1)} %reshape.62), calls=%async_computation.1 | async-start | bytes 524288 | tf_op jit(solution)/shard_map/all_to_all | solution.py:477
  93.9 0.7 copy-start.9
  93.9 0.8 copy-start.10
  93.9 0.9 copy-start.11
  98.7 17.3 %collective-permute-start.7 = (bf16[128,4096]{1,0:T(8,128)(2,1)}, bf16[128,4096]{1,0:T(8,128)(2,1)S(1)}, u32[]{:S(2)}, u32[]{:S(2)}) collective-permute-start(bf16[128,4096]{1,0:T(8,128)(2,1)} %get-tuple-element.50), channel_id=1, source_target_pairs={{0,8},{1,9},{2,10},{3,11},{4,12},{5,13},{6,14},{7,15},{8,16},{9,17... | collective-permute-start | bytes 3145736 | tf_op jit(solution)/shard_map/ppermute | solution.py:485
  98.8 17.1 %collective-permute-start.8 = (bf16[128,4096]{1,0:T(8,128)(2,1)}, bf16[128,4096]{1,0:T(8,128)(2,1)S(1)}, u32[]{:S(2)}, u32[]{:S(2)}) collective-permute-start(bf16[128,4096]{1,0:T(8,128)(2,1)} %get-tuple-element.50), channel_id=1, source_target_pairs={{0,252},{1,253},{2,254},{3,255},{4,248},{5,249},{6,250},{7,251},{8... | collective-permute-start | bytes 3145736 | tf_op jit(solution)/shard_map/ppermute | solution.py:485
  100.4 37.4 %collective-permute-start.9 = (bf16[128,4096]{1,0:T(8,128)(2,1)}, bf16[128,4096]{1,0:T(8,128)(2,1)}, u32[]{:S(2)}, u32[]{:S(2)}) collective-permute-start(bf16[128,4096]{1,0:T(8,128)(2,1)} %get-tuple-element.53), channel_id=1, source_target_pairs={{0,8},{1,9},{2,10},{3,11},{4,12},{5,13},{6,14},{7,15},{8,16},{9,17... | collective-permute-start | bytes 3145736 | tf_op jit(solution)/shard_map/ppermute | solution.py:485
  100.5 37.3 %collective-permute-start.10 = (bf16[128,4096]{1,0:T(8,128)(2,1)}, bf16[128,4096]{1,0:T(8,128)(2,1)}, u32[]{:S(2)}, u32[]{:S(2)}) collective-permute-start(bf16[128,4096]{1,0:T(8,128)(2,1)} %get-tuple-element.53), channel_id=1, source_target_pairs={{0,252},{1,253},{2,254},{3,255},{4,248},{5,249},{6,250},{7,251},{8... | collective-permute-start | bytes 3145736 | tf_op jit(solution)/shard_map/ppermute | solution.py:485
  116.0 1.1 copy-start.5
  117.0 1.0 copy-start.6
  123.8 34.2 %all-to-all-start.2 = ((bf16[8,15,16,256]{3,2,1,0:T(8,128)(2,1)}), bf16[8,15,16,256]{3,2,1,0:T(8,128)(2,1)}, u32[]{:S(2)}, u32[]{:S(2)}) async-start(bf16[8,15,16,256]{3,2,1,0:T(8,128)(2,1)} %shard_map.210), calls=%async_computation.2 | async-start | bytes 1966080 | tf_op jit(solution)/shard_map/all_to_all | solution.py:513
  158.0 31.4 %all-to-all-start.3 = ((bf16[8,15,16,256]{3,2,1,0:T(8,128)(2,1)}), bf16[8,15,16,256]{3,2,1,0:T(8,128)(2,1)S(1)}, u32[]{:S(2)}, u32[]{:S(2)}) async-start(bf16[8,15,16,256]{3,2,1,0:T(8,128)(2,1)} %shard_map.212), calls=%async_computation.3 | async-start | bytes 1966080 | tf_op jit(solution)/shard_map/all_to_all | solution.py:513
  163.8 25.6 %collective-permute-start.11 = (f32[3,32,256]{2,1,0:T(8,128)S(1)}, f32[3,32,256]{2,1,0:T(8,128)S(1)}, u32[]{:S(2)}, u32[]{:S(2)}) collective-permute-start(f32[3,32,256]{2,1,0:T(8,128)S(1)} %slice.16), channel_id=1, source_target_pairs={{0,0},{1,1},{2,2},{3,3},{4,4},{5,5},{6,6},{7,7},{8,8},{9,9},{10,10... | collective-permute-start | bytes 294920 | tf_op jit(solution)/shard_map/ppermute | solution.py:516
  189.4 1.0 copy-start

commit v9 on v8

--- a/solution.py
+++ b/solution.py
@@ -31,7 +31,7 @@
 FLIP = GROUPS // 2
 PARTS = 2
 CHUNK = ROWS // PARTS
-BLOCKS = 13
+BLOCKS = 12
 bf16, f32 = jnp.bfloat16, jnp.float32
 VMEM = pl.BlockSpec(memory_space=pltpu.VMEM)
 SMEM = pl.BlockSpec(memory_space=pltpu.SMEM)
@@ -259,12 +259,11 @@
     def strain(i, j):
         return same * plain(i, j) + swap * plain(j, i)
 
-    left = [-0.5 * swim_speed * proj * p[j] for j in range(2)] + [-0.5 * proj]
+    left = [-0.5 * swim_speed * proj * p[j] for j in range(3)] + [-0.5 * proj]
     trace = strain(2, 2)
     left += [strain(0, 0) - trace, strain(1, 0), strain(2, 0)]
     left += [strain(0, 1), strain(1, 1) - trace, strain(2, 1)]
     left += [strain(0, 2), strain(1, 2)]
-    left += [-0.5 * swim_speed * proj * p[2], -0.5 * proj]
     for n, value in enumerate(left):
         high, low = halves(value)
         out_ref[:, n * ALL_PAD : (n + 1) * ALL_PAD] = (dot(high, synth) + dot(low, synth)).astype(bf16)
@@ -280,9 +279,10 @@
             part[where, :] = refs[j][:, (n * CHUNK + 1) * NX : ((n + 1) * CHUNK + 1) * NX]
 
 
-def inner_kernel(center_ref, flow_ref, weight_ref, damp_ref, out_ref, operands, locals_):
-    blocks = BLOCKS - 2
-
+def rate_kernel(
+    center_ref, zlow_ref, zhigh_ref, flow_ref, weight_ref, damp_ref,
+    out_ref, operands, locals_, *stages,
+):
     def build(r, operand, local_terms):
         here = pl.multiple_of(r * NX, NX)
         flow = [flow_ref[f, pl.ds(r, 1), :] for f in range(11)]
@@ -291,13 +291,15 @@
             value = center_ref[rows, pl.ds(here + NX, NX)].astype(f32)
             y_low = center_ref[rows, pl.ds(here, NX)].astype(f32)
             y_high = center_ref[rows, pl.ds(here + 2 * NX, NX)].astype(f32)
+            z_low = zlow_ref[rows, pl.ds(here, NX)].astype(f32)
+            z_high = zhigh_ref[rows, pl.ds(here, NX)].astype(f32)
             x_low = pltpu.roll(value, 1, 1)
             x_high = pltpu.roll(value, NX - 1, 1)
-            diff_x, diff_y = x_high - x_low, y_high - y_low
-            lap = x_high + x_low + y_high + y_low - 6.0 * value
+            diffs = (x_high - x_low, y_high - y_low, z_high - z_low)
+            drift = flow[0] * diffs[0] + flow[1] * diffs[1] + flow[2] * diffs[2]
+            lap = x_high + x_low + y_high + y_low + z_high + z_low - 6.0 * value
             local_terms[rows, :] = transl_diff * lap - damp_ref[rows, :] * value
-            terms = [diff_x, diff_y, flow[0] * diff_x + flow[1] * diff_y]
-            terms += [flow[3 + n] * value for n in range(8)]
+            terms = list(diffs) + [drift] + [flow[3 + n] * value for n in range(8)]
             for n, term in enumerate(terms):
                 operand[n * ALL_PAD + g * PAD : n * ALL_PAD + (g + 1) * PAD, :] = term.astype(bf16)
 
@@ -305,35 +307,7 @@
         for n in range(2):
             build(2 * i + n, operands.at[n], locals_.at[n])
         for n in range(2):
-            where = pl.ds(pl.multiple_of((2 * i + n) * NX, NX), NX)
-            out_ref[:, where] = locals_[n] + dot(weight_ref[:, : blocks * ALL_PAD], operands[n])
-        return carry
-
-    lax.fori_loop(0, CHUNK // 2, rows, 0)
-
-
-def rate_kernel(
-    inner_ref, zlow_ref, zhigh_ref, flow_ref, weight_ref, out_ref, operands, locals_, *stages
-):
-    skip = (BLOCKS - 2) * ALL_PAD
-
-    def build(r, operand, local_terms):
-        here = pl.multiple_of(r * NX, NX)
-        drift = flow_ref[2, pl.ds(r, 1), :]
-        for g in range(GROUPS):
-            rows = slice(g * PAD, (g + 1) * PAD)
-            z_low = zlow_ref[rows, pl.ds(here, NX)].astype(f32)
-            z_high = zhigh_ref[rows, pl.ds(here, NX)].astype(f32)
-            diff_z = z_high - z_low
-            local_terms[rows, :] = transl_diff * (z_high + z_low) + inner_ref[rows, pl.ds(here, NX)]
-            operand[rows, :] = diff_z.astype(bf16)
-            operand[ALL_PAD + g * PAD : ALL_PAD + (g + 1) * PAD, :] = (drift * diff_z).astype(bf16)
-
-    def rows(i, carry):
-        for n in range(2):
-            build(2 * i + n, operands.at[n], locals_.at[n])
-        for n in range(2):
-            result = dot(weight_ref[:, skip:], operands[n]) + locals_[n]
+            result = dot(weight_ref[...], operands[n]) + locals_[n]
             for side, stage in enumerate(stages):
                 stage[pl.ds(2 * i + n, ALL_PAD, stride=CHUNK), :] = result[
                     :, side * LANES : (side + 1) * LANES
@@ -484,29 +458,22 @@
     below = pairs(lambda s, b: ((s - 1) % SPACES, b))
     halo = [(lax.ppermute(rows, both, above), lax.ppermute(rows, both, below)) for rows in own_parts]
 
-    flow = call(fields_kernel, shape(11, ROWS, NX, dtype=f32), [mixed, *split_table(back_x)], (), 0, 1 << 29, 2 << 20)
+    flow = call(fields_kernel, shape(11, ROWS, NX, dtype=f32), [mixed, *split_table(back_x)], (), 0, 1 << 37, 2 << 20)
     damp = pad_groups(damping, 0)[:, None]
     returned = []
     for part in range(PARTS):
         size = (pl.Element(ALL_PAD), pl.Element((CHUNK + 2) * NX))
         here = pl.BlockSpec(size, lambda i, part=part: (0, part * CHUNK * NX))
         flow_here = pl.BlockSpec((11, CHUNK, NX), lambda i, part=part: (0, part, 0))
-        inner = call(
-            inner_kernel, shape(ALL_PAD, CHUNK * NX, dtype=f32), [center, flow, weights, damp],
-            [pltpu.VMEM((2, (BLOCKS - 2) * ALL_PAD, NX), bf16), pltpu.VMEM((2, ALL_PAD, NX), f32)],
-            0, 1 << 37, 7 << 19, [here, flow_here, VMEM, VMEM],
-        )
         rates = call(
-            rate_kernel, shape(GROUPS, OWN, CHUNK, NX),
-            [inner, *halo[part], flow, weights],
+            rate_kernel, shape(GROUPS, OWN, CHUNK, NX), [center, *halo[part], flow, weights, damp],
             [
-                pltpu.VMEM((2, 2 * ALL_PAD, NX), bf16),
+                pltpu.VMEM((2, BLOCKS * ALL_PAD, NX), bf16),
                 pltpu.VMEM((2, ALL_PAD, NX), f32),
                 pltpu.VMEM((ALL_PAD * CHUNK, LANES), f32),
                 pltpu.VMEM((ALL_PAD * CHUNK, LANES), f32),
             ],
-            0, 1 << 33, 9 << 19,
-            [VMEM, VMEM, VMEM, flow_here, VMEM],
+            0, 1 << 33, 9 << 19, [here, VMEM, VMEM, flow_here, VMEM, VMEM],
         )
         center, rates = lax.optimization_barrier((center, rates))
         returned, rates = lax.optimization_barrier((returned, rates))

time: 198 us -> 196 us (0.990); the launches traced: 194 us -> 195 us
  waiting for transfers between devices: 38.1 us -> 47.1 us
  Pallas kernels: 53 us -> 44.5 us
    pallas_call x11 -> x9, Pallas kernels: 53 us -> 44.5 us  [call(): pl.pallas_call(kernel, out_shape=out_shape, grid=(1,) if specs else (), i...]
    all_to_all x2, waiting for transfers between devices: 14.4 us -> 19.7 us  [local(): returned.append(lax.all_to_all(rates, 'harm', 0, 0, tiled=True))]
    ppermute x2, waiting for transfers between devices: 0.01 us -> 4.44 us  [local(): lax.ppermute(rows, both, above)]
    all_to_all x2, starting transfers between devices: 11.8 us -> 14.2 us  [local(): returned.append(lax.all_to_all(rates, 'harm', 0, 0, tiled=True))]
    unnamed x31 -> x33, local copies, waits for them, and re-layouts: 8.7 us -> 7.97 us
  transfers between devices with their start and end apart: 16 -> 16, of which waited for: 5 -> 6; matrix products, arithmetic and copies ran while one was open for 5% -> 5% of each run, Pallas kernels for 23% -> 19%
where the time goes in v9:
time: 196 us; the launch traced here: 195 us
  starting transfers between devices  84.4 us (43%)
  waiting for transfers between devices  47.1 us (24%)
  Pallas kernels  44.5 us (23%)
  local copies, waits for them, and re-layouts  12.5 us (6%)
  other arithmetic  4.47 us (2%)
    pallas_call x9, Pallas kernels, call(): pl.pallas_call(kernel, out_shape=out_shape, grid=(1,) if specs else (), i...  44.5 us
    all_to_all x1, starting transfers between devices, local(): mixed = lax.all_to_all(sent, everyone, 0, 0, tiled=True)  24.3 us
    ppermute x7, starting transfers between devices, exchanged(): lax.ppermute(c, 'harm', partner(j + 1))  22.2 us
    all_to_all x2, waiting for transfers between devices, local(): returned.append(lax.all_to_all(rates, 'harm', 0, 0, tiled=True))  19.7 us
    ppermute x1, waiting for transfers between devices, local(): velocity = lax.ppermute(late, both, swap)  16.4 us
    all_to_all x1, starting transfers between devices, local(): columns = lax.all_to_all(sent, everyone, 0, 0, tiled=True)  14.2 us
    all_to_all x2, starting transfers between devices, local(): returned.append(lax.all_to_all(rates, 'harm', 0, 0, tiled=True))  14.2 us
    unnamed x33, local copies, waits for them, and re-layouts  7.97 us
  transfers between devices with their start and end apart: 16, of which 6 were waited for; matrix products, arithmetic and copies ran while one was open for 5% of the time, Pallas kernels for 19%

profile of v9, /device:TPU:62, one launch (start us, length us, event | category | flops | bytes accessed | tf_op | source)
XLA Modules:
  0.0 194.6 jit_solution(8857176075113892073)
XLA Ops:
  0.6 0.8 fusion.2
  1.5 0.6 pad_maximum_fusion.table_ref
  2.1 4.8 %shard_map.203 = bf16[256,1280]{1,0:T(8,128)(2,1)} custom-call(f32[5,15]{1,0:T(8,128)} %pad_maximum_fusion.table_ref, bf16[15,256,256]{2,1,0:T(8,128)(2,1)} %bitcast.29, bf16[256,256]{1,0:T(8,128)(2,1)} %constant.102.clone.high_ref, bf16[256,256]{1,0:T(8,128)(2,1)} %constant.103.clone.low_ref), custom_call_target="tpu_custom_call" | custom-call | flops 1073741824 | bytes 3145728 | tf_op jit(solution)/shard_map/pallas_call | solution.py:336
  6.9 0.6 broadcast.14
  7.5 2.2 %reduce = bf16[256,1280]{1,0:T(8,128)(2,1)S(1)} reduce(bf16[256,1,1280]{2,0,1:T(8,128)(2,1)} %bitcast.32, bf16[]{:T(256)} %broadcast.14), dimensions={1}, to_apply=%copy.39.reduce_sub_computation | reduce | bytes 1310722 | tf_op jit(solution)/shard_map/all_to_all | solution.py:419
  9.7 1.0 reshape.60
  10.7 14.2 %all-to-all-start = ((bf16[256,2,640]{2,1,0:T(2,128)(2,1)}), bf16[256,2,640]{2,1,0:T(2,128)(2,1)S(1)}, u32[]{:S(2)}, u32[]{:S(2)}) async-start(bf16[256,2,640]{2,1,0:T(2,128)(2,1)} %reshape.60), calls=%async_computation | async-start | bytes 1310720 | tf_op jit(solution)/shard_map/all_to_all | solution.py:419
  24.9 6.4 %shard_map.204 = (bf16[16,8704]{1,0:T(8,128)(2,1)}, bf16[16,8704]{1,0:T(8,128)(2,1)}, bf16[16,8704]{1,0:T(8,128)(2,1)}, bf16[16,8704]{1,0:T(8,128)(2,1)}, bf16[1...) custom-call(s32[1]{0:T(128)S(6)} %xor.10.block_ref, ...), custom_call_target="tpu_custom_call" | custom-call | bytes 4194304 | tf_op jit(solution)/shard_map/pallas_call | solution.py:336
  31.3 0.8 collective-permute-start
  32.1 1.1 collective-permute-start.1
  33.3 2.7 %collective-permute-start.2 = (bf16[16,8704]{1,0:T(8,128)(2,1)}, bf16[16,8704]{1,0:T(8,128)(2,1)S(1)}, u32[]{:S(2)}, u32[]{:S(2)}) collective-permute-start(bf16[16,8704]{1,0:T(8,128)(2,1)} %get-tuple-element.34), channel_id=1, source_target_pairs={{0,3},{1,2},{2,1},{3,0},{4,7},{5,6},{6,5},{7,4},{8,11},{9,10},{10,... | collective-permute-start | bytes 835592 | tf_op jit(solution)/shard_map/ppermute | solution.py:384
  36.0 5.5 %collective-permute-start.3 = (bf16[16,8704]{1,0:T(8,128)(2,1)}, bf16[16,8704]{1,0:T(8,128)(2,1)S(1)}, u32[]{:S(2)}, u32[]{:S(2)}) collective-permute-start(bf16[16,8704]{1,0:T(8,128)(2,1)} %get-tuple-element.35), channel_id=1, source_target_pairs={{0,4},{1,5},{2,6},{3,7},{4,0},{5,1},{6,2},{7,3},{8,12},{9,13},{10,... | collective-permute-start | bytes 835592 | tf_op jit(solution)/shard_map/ppermute | solution.py:384
  41.6 1.9 collective-permute-done.refs_1_
  43.4 5.5 %collective-permute-start.5 = (bf16[16,8704]{1,0:T(8,128)(2,1)}, bf16[16,8704]{1,0:T(8,128)(2,1)}, u32[]{:S(2)}, u32[]{:S(2)}) collective-permute-start(bf16[16,8704]{1,0:T(8,128)(2,1)} %get-tuple-element.37), channel_id=1, source_target_pairs={{0,6},{1,7},{2,4},{3,5},{4,2},{5,3},{6,0},{7,1},{8,14},{9,15},{10,... | collective-permute-start | bytes 835592 | tf_op jit(solution)/shard_map/ppermute | solution.py:384
  49.0 0.5 collective-permute-done.1.refs_2_
  49.5 6.4 %collective-permute-start.6 = (bf16[16,8704]{1,0:T(8,128)(2,1)}, bf16[16,8704]{1,0:T(8,128)(2,1)}, u32[]{:S(2)}, u32[]{:S(2)}) collective-permute-start(bf16[16,8704]{1,0:T(8,128)(2,1)} %get-tuple-element.38), channel_id=1, source_target_pairs={{0,7},{1,6},{2,5},{3,4},{4,3},{5,2},{6,1},{7,0},{8,15},{9,14},{10,... | collective-permute-start | bytes 835592 | tf_op jit(solution)/shard_map/ppermute | solution.py:384
  56.0 0.7 pad.18
  56.7 0.7 copy.40.synth_ref
  57.5 0.6 pad.17
  58.1 2.5 %shard_map.205.weight_ref = bf16[128,1536]{1,0:T(8,128)(2,1)} custom-call(f32[3,256]{1,0:T(4,128)} %constant.104.clone.dir_ref, bf16[256,128]{1,0:T(8,128)(2,1)} %copy.40.synth_ref, bf16[128,256]{1,0:T(8,128)(2,1)} %bitcast.39, bf16[3,128,256]{2,1,0:T(8,128)(2,1)} %bitcast.37), custom_call_target="tpu_custom_call" | custom-call | flops 268435456 | bytes 1048576 | tf_op jit(solution)/shard_map/pallas_call | solution.py:336
  60.6 0.5 reshape.61
  61.2 0.9 copy.50
  62.1 4.0 %shard_map.206 = bf16[256,512]{1,0:T(8,128)(2,1)} custom-call(f32[1]{0:T(128)} %bitcast.5.wave_ref, s32[1]{0:T(128)} %bitcast.6.half_ref, f32[1,256]{1,0:T(1,128)} %constant.105.clone.ky_ref, f32[32,1]{1,0:T(8,128)} %constant.106.clone.kz_ref, bf16[256,1280]{1,0:T(8,128)(2,1)} %bitcast.33, bf16[64,256]{1,0:T(8,128)(2,1)} %constant.107.clone.fz_high, ...), custom_call_target="tpu_custom_call" | custom-call | flops 1073741824 | bytes 3145728 | tf_op jit(solution)/shard_map/pallas_call | solution.py:336
  66.1 1.7 reduce.1
  67.8 0.8 reshape.62
  68.6 24.3 %all-to-all-start.1 = ((bf16[256,2,256]{2,1,0:T(2,128)(2,1)}), bf16[256,2,256]{2,1,0:T(2,128)(2,1)S(1)}, u32[]{:S(2)}, u32[]{:S(2)}) async-start(bf16[256,2,256]{2,1,0:T(2,128)(2,1)} %reshape.62), calls=%async_computation.1 | async-start | bytes 524288 | tf_op jit(solution)/shard_map/all_to_all | solution.py:451
  93.0 0.7 broadcast_in_dim_reshape.4.damp_ref
  93.8 0.6 copy-done.10
  94.7 3.9 %shard_map.207 = (bf16[128,8704]{1,0:T(8,128)(2,1)}, bf16[128,4096]{1,0:T(8,128)(2,1)}, bf16[128,4096]{1,0:T(8,128)(2,1)}) custom-call(s32[1]{0:T(128)} %bitcast.group_ref, bf16[16,8704]{1,0:T(8,128)(2,1)} %get-tuple-element.40.refs_0_, bf16[16,8704]{1,0:T(8,128)(2,1)} %copy-done.8, bf16[16,8704]{1,0:T(8,128)(2,1)} %copy-done.9, ...), custom_call_target="tpu_custom_call" | custom-call | flops 4294967296 | bytes 4194304 | tf_op jit(solution)/shard_map/pallas_call | solution.py:336
  98.7 1.6 collective-permute-start.8
  100.4 0.5 collective-permute-start.9
  100.8 4.1 %all-to-all-done.1 = bf16[256,2,256]{2,1,0:T(2,128)(2,1)S(1)} async-done(((bf16[256,2,256]{2,1,0:T(2,128)(2,1)}), bf16[256,2,256]{2,1,0:T(2,128)(2,1)S(1)}, u32[]{:S(2)}, u32[]{:S(2)}) %all-to-all-start.1) | async-done | bytes 262176 | tf_op jit(solution)/shard_map/all_to_all | solution.py:451
  105.2 0.7 copy.51
  105.9 2.8 %shard_map.208.flow_ref = f32[11,32,256]{2,1,0:T(8,128)} custom-call(bf16[256,512]{1,0:T(8,128)(2,1)} %bitcast.34, bf16[256,1024]{1,0:T(8,128)(2,1)} %constant.114.clone.high_ref, bf16[256,1024]{1,0:T(8,128)(2,1)} %constant.115.clone.low_ref), custom_call_target="tpu_custom_call" | custom-call | flops 137438953472 | bytes 2097152 | tf_op jit(solution)/shard_map/pallas_call | solution.py:336
  108.7 4.4 %collective-permute-done.7.zlow_ref = bf16[128,4096]{1,0:T(8,128)(2,1)S(1)} collective-permute-done((bf16[128,4096]{1,0:T(8,128)(2,1)}, bf16[128,4096]{1,0:T(8,128)(2,1)S(1)}, u32[]{:S(2)}, u32[]{:S(2)}) %collective-permute-start.7) | collective-permute-done | bytes 1048608 | tf_op jit(solution)/shard_map/ppermute | solution.py:459
  113.2 1.0 copy-done.6
  114.2 0.3 copy-done.7
  114.5 8.6 %shard_map.209 = bf16[8,15,16,256]{3,2,1,0:T(8,128)(2,1)} custom-call(bf16[128,8704]{1,0:T(8,128)(2,1)} %get-tuple-element.52.center_ref, bf16[128,4096]{1,0:T(8,128)(2,1)} %copy-done.6, bf16[128,4096]{1,0:T(8,128)(2,1)} %copy-done.7, f32[11,32,256]{2,1,0:T(8,128)} %shard_map.208.flow_ref, bf16[128,1536]{1,0:T(8,128)(2,1)} %shard_map.205.weight_ref, ...), custom_call_target="tpu_custom_call" | custom-call | flops 8589934592 | bytes 4718592 | tf_op jit(solution)/shard_map/pallas_call | solution.py:336
  123.1 9.6 %all-to-all-start.2 = ((bf16[8,15,16,256]{3,2,1,0:T(8,128)(2,1)}), bf16[8,15,16,256]{3,2,1,0:T(8,128)(2,1)S(1)}, u32[]{:S(2)}, u32[]{:S(2)}) async-start(bf16[8,15,16,256]{3,2,1,0:T(8,128)(2,1)} %shard_map.209), calls=%async_computation.2 | async-start | bytes 1966080 | tf_op jit(solution)/shard_map/all_to_all | solution.py:480
  132.7 8.6 %shard_map.210 = bf16[8,15,16,256]{3,2,1,0:T(8,128)(2,1)} custom-call(bf16[128,8704]{1,0:T(8,128)(2,1)} %get-tuple-element.52.center_ref, bf16[128,4096]{1,0:T(8,128)(2,1)} %collective-permute-done.9.zlow_ref, bf16[128,4096]{1,0:T(8,128)(2,1)} %collective-permute-done.10.zhigh_ref, f32[11,32,256]{2,1,0:T(8,128)} %shard_map.208.flow_ref, ...), custom_call_target="tpu_custom_call" | custom-call | flops 8589934592 | bytes 4718592 | tf_op jit(solution)/shard_map/pallas_call | solution.py:336
  141.2 19.7 %all-to-all-done.2.refs_0_ = bf16[8,15,16,256]{3,2,1,0:T(8,128)(2,1)S(1)} async-done(((bf16[8,15,16,256]{3,2,1,0:T(8,128)(2,1)}), bf16[8,15,16,256]{3,2,1,0:T(8,128)(2,1)S(1)}, u32[]{:S(2)}, u32[]{:S(2)}) %all-to-all-start.2) | async-done | bytes 983072 | tf_op jit(solution)/shard_map/all_to_all | solution.py:480
  160.9 4.6 %all-to-all-start.3 = ((bf16[8,15,16,256]{3,2,1,0:T(8,128)(2,1)}), bf16[8,15,16,256]{3,2,1,0:T(8,128)(2,1)S(1)}, u32[]{:S(2)}, u32[]{:S(2)}) async-start(bf16[8,15,16,256]{3,2,1,0:T(8,128)(2,1)} %shard_map.210), calls=%async_computation.3 | async-start | bytes 1966080 | tf_op jit(solution)/shard_map/all_to_all | solution.py:480
  165.5 0.9 slice.16
  166.4 7.3 %collective-permute-start.11 = (f32[3,32,256]{2,1,0:T(8,128)S(1)}, f32[3,32,256]{2,1,0:T(8,128)S(1)}, u32[]{:S(2)}, u32[]{:S(2)}) collective-permute-start(f32[3,32,256]{2,1,0:T(8,128)S(1)} %slice.16), channel_id=1, source_target_pairs={{0,0},{1,1},{2,2},{3,3},{4,4},{5,5},{6,6},{7,7},{8,8},{9,9},{10,10... | collective-permute-start | bytes 294920 | tf_op jit(solution)/shard_map/ppermute | solution.py:483
  173.7 16.4 %collective-permute-done.11 = f32[3,32,256]{2,1,0:T(8,128)S(1)} collective-permute-done((f32[3,32,256]{2,1,0:T(8,128)S(1)}, f32[3,32,256]{2,1,0:T(8,128)S(1)}, u32[]{:S(2)}, u32[]{:S(2)}) %collective-permute-start.11) | collective-permute-done | bytes 98336 | tf_op jit(solution)/shard_map/ppermute | solution.py:483
  190.1 1.0 copy-done.1
  191.1 2.9 %shard_map.211 = bf16[15,256,256]{2,1,0:T(8,128)(2,1)} custom-call(s32[1]{0:T(128)S(6)} %xor.11.swap_ref, bf16[8,15,16,256]{3,2,1,0:T(8,128)(2,1)} %copy-done, bf16[8,15,16,256]{3,2,1,0:T(8,128)(2,1)} %copy-done.1), custom_call_target="tpu_custom_call" | custom-call | bytes 4194304 | tf_op jit(solution)/shard_map/pallas_call | solution.py:336
  194.0 0.6 copy.55
  (45 shorter events, 0.9 us)
Async XLA Ops:
  10.7 45.2 %copy-start.3 = (bf16[256,120]{0,1:T(8,128)(2,1)S(1)}, bf16[256,120]{0,1:T(8,128)(2,1)}, u32[]{:S(2)}) copy-start(bf16[256,120]{0,1:T(8,128)(2,1)} %param.21) | copy-start | bytes 184324
  10.7 45.3 %copy-start.2 = (bf16[3,120,256]{2,1,0:T(8,128)(2,1)S(1)}, bf16[3,120,256]{2,1,0:T(8,128)(2,1)}, u32[]{:S(2)}) copy-start(bf16[3,120,256]{2,1,0:T(8,128)(2,1)} %param.23) | copy-start | bytes 552964
  10.7 46.8 %copy-start.4 = (bf16[120,256]{1,0:T(8,128)(2,1)S(1)}, bf16[120,256]{1,0:T(8,128)(2,1)}, u32[]{:S(2)}) copy-start(bf16[120,256]{1,0:T(8,128)(2,1)} %param.22) | copy-start | bytes 184324
  10.7 49.9 %all-to-all-start = ((bf16[256,2,640]{2,1,0:T(2,128)(2,1)}), bf16[256,2,640]{2,1,0:T(2,128)(2,1)S(1)}, u32[]{:S(2)}, u32[]{:S(2)}) async-start(bf16[256,2,640]{2,1,0:T(2,128)(2,1)} %reshape.60), calls=%async_computation | async-start | bytes 1310720 | tf_op jit(solution)/shard_map/all_to_all | solution.py:419
  31.3 12.1 %collective-permute-start = (bf16[16,8704]{1,0:T(8,128)(2,1)}, bf16[16,8704]{1,0:T(8,128)(2,1)S(1)}, u32[]{:S(2)}, u32[]{:S(2)}) collective-permute-start(bf16[16,8704]{1,0:T(8,128)(2,1)} %get-tuple-element.32), channel_id=1, source_target_pairs={{0,1},{1,0},{2,3},{3,2},{4,5},{5,4},{6,7},{7,6},{8,9},{9,8},{10,11... | collective-permute-start | bytes 835592 | tf_op jit(solution)/shard_map/ppermute | solution.py:384
  32.1 17.3 %collective-permute-start.1 = (bf16[16,8704]{1,0:T(8,128)(2,1)}, bf16[16,8704]{1,0:T(8,128)(2,1)S(1)}, u32[]{:S(2)}, u32[]{:S(2)}) collective-permute-start(bf16[16,8704]{1,0:T(8,128)(2,1)} %get-tuple-element.33), channel_id=1, source_target_pairs={{0,2},{1,3},{2,0},{3,1},{4,6},{5,7},{6,4},{7,5},{8,10},{9,11},{10,... | collective-permute-start | bytes 835592 | tf_op jit(solution)/shard_map/ppermute | solution.py:384
  33.3 60.5 %collective-permute-start.2 = (bf16[16,8704]{1,0:T(8,128)(2,1)}, bf16[16,8704]{1,0:T(8,128)(2,1)S(1)}, u32[]{:S(2)}, u32[]{:S(2)}) collective-permute-start(bf16[16,8704]{1,0:T(8,128)(2,1)} %get-tuple-element.34), channel_id=1, source_target_pairs={{0,3},{1,2},{2,1},{3,0},{4,7},{5,6},{6,5},{7,4},{8,11},{9,10},{10,... | collective-permute-start | bytes 835592 | tf_op jit(solution)/shard_map/ppermute | solution.py:384
  36.0 57.8 %collective-permute-start.3 = (bf16[16,8704]{1,0:T(8,128)(2,1)}, bf16[16,8704]{1,0:T(8,128)(2,1)S(1)}, u32[]{:S(2)}, u32[]{:S(2)}) collective-permute-start(bf16[16,8704]{1,0:T(8,128)(2,1)} %get-tuple-element.35), channel_id=1, source_target_pairs={{0,4},{1,5},{2,6},{3,7},{4,0},{5,1},{6,2},{7,3},{8,12},{9,13},{10,... | collective-permute-start | bytes 835592 | tf_op jit(solution)/shard_map/ppermute | solution.py:384
  41.5 52.2 %collective-permute-start.4 = (bf16[16,8704]{1,0:T(8,128)(2,1)}, bf16[16,8704]{1,0:T(8,128)(2,1)S(1)}, u32[]{:S(2)}, u32[]{:S(2)}) collective-permute-start(bf16[16,8704]{1,0:T(8,128)(2,1)} %get-tuple-element.36), channel_id=1, source_target_pairs={{0,5},{1,4},{2,7},{3,6},{4,1},{5,0},{6,3},{7,2},{8,13},{9,12},{10,... | collective-permute-start | bytes 835592 | tf_op jit(solution)/shard_map/ppermute | solution.py:384
  43.4 17.7 %copy-start.8 = (bf16[16,8704]{1,0:T(8,128)(2,1)}, bf16[16,8704]{1,0:T(8,128)(2,1)S(1)}, u32[]{:S(2)}) copy-start(bf16[16,8704]{1,0:T(8,128)(2,1)S(1)} %collective-permute-done.refs_1_) | copy-start | bytes 835588
  43.4 50.4 %collective-permute-start.5 = (bf16[16,8704]{1,0:T(8,128)(2,1)}, bf16[16,8704]{1,0:T(8,128)(2,1)}, u32[]{:S(2)}, u32[]{:S(2)}) collective-permute-start(bf16[16,8704]{1,0:T(8,128)(2,1)} %get-tuple-element.37), channel_id=1, source_target_pairs={{0,6},{1,7},{2,4},{3,5},{4,2},{5,3},{6,0},{7,1},{8,14},{9,15},{10,... | collective-permute-start | bytes 835592 | tf_op jit(solution)/shard_map/ppermute | solution.py:384
  49.5 11.7 %copy-start.9 = (bf16[16,8704]{1,0:T(8,128)(2,1)}, bf16[16,8704]{1,0:T(8,128)(2,1)S(1)}, u32[]{:S(2)}) copy-start(bf16[16,8704]{1,0:T(8,128)(2,1)S(1)} %collective-permute-done.1.refs_2_) | copy-start | bytes 835588
  49.5 44.3 %collective-permute-start.6 = (bf16[16,8704]{1,0:T(8,128)(2,1)}, bf16[16,8704]{1,0:T(8,128)(2,1)}, u32[]{:S(2)}, u32[]{:S(2)}) collective-permute-start(bf16[16,8704]{1,0:T(8,128)(2,1)} %get-tuple-element.38), channel_id=1, source_target_pairs={{0,7},{1,6},{2,5},{3,4},{4,3},{5,2},{6,1},{7,0},{8,15},{9,14},{10,... | collective-permute-start | bytes 835592 | tf_op jit(solution)/shard_map/ppermute | solution.py:384
  62.1 30.9 %copy-start.5 = (f32[120]{0:T(128)S(1)}, f32[120]{0:T(128)}, u32[]{:S(2)}) copy-start(f32[120]{0:T(128)} %param.24) | copy-start | bytes 1444
  68.6 36.4 %all-to-all-start.1 = ((bf16[256,2,256]{2,1,0:T(2,128)(2,1)}), bf16[256,2,256]{2,1,0:T(2,128)(2,1)S(1)}, u32[]{:S(2)}, u32[]{:S(2)}) async-start(bf16[256,2,256]{2,1,0:T(2,128)(2,1)} %reshape.62), calls=%async_computation.1 | async-start | bytes 524288 | tf_op jit(solution)/shard_map/all_to_all | solution.py:451
  93.7 0.7 copy-start.10
  93.8 0.8 copy-start.11
  93.8 0.9 copy-start.12
  98.6 14.6 %collective-permute-start.7 = (bf16[128,4096]{1,0:T(8,128)(2,1)}, bf16[128,4096]{1,0:T(8,128)(2,1)S(1)}, u32[]{:S(2)}, u32[]{:S(2)}) collective-permute-start(bf16[128,4096]{1,0:T(8,128)(2,1)} %get-tuple-element.49), channel_id=1, source_target_pairs={{0,8},{1,9},{2,10},{3,11},{4,12},{5,13},{6,14},{7,15},{8,16},{9,17... | collective-permute-start | bytes 3145736 | tf_op jit(solution)/shard_map/ppermute | solution.py:459
  98.7 14.5 %collective-permute-start.8 = (bf16[128,4096]{1,0:T(8,128)(2,1)}, bf16[128,4096]{1,0:T(8,128)(2,1)S(1)}, u32[]{:S(2)}, u32[]{:S(2)}) collective-permute-start(bf16[128,4096]{1,0:T(8,128)(2,1)} %get-tuple-element.49), channel_id=1, source_target_pairs={{0,252},{1,253},{2,254},{3,255},{4,248},{5,249},{6,250},{7,251},{8... | collective-permute-start | bytes 3145736 | tf_op jit(solution)/shard_map/ppermute | solution.py:459
  100.3 32.3 %collective-permute-start.10 = (bf16[128,4096]{1,0:T(8,128)(2,1)}, bf16[128,4096]{1,0:T(8,128)(2,1)}, u32[]{:S(2)}, u32[]{:S(2)}) collective-permute-start(bf16[128,4096]{1,0:T(8,128)(2,1)} %get-tuple-element.53), channel_id=1, source_target_pairs={{0,252},{1,253},{2,254},{3,255},{4,248},{5,249},{6,250},{7,251},{8... | collective-permute-start | bytes 3145736 | tf_op jit(solution)/shard_map/ppermute | solution.py:459
  100.4 32.3 %collective-permute-start.9 = (bf16[128,4096]{1,0:T(8,128)(2,1)}, bf16[128,4096]{1,0:T(8,128)(2,1)}, u32[]{:S(2)}, u32[]{:S(2)}) collective-permute-start(bf16[128,4096]{1,0:T(8,128)(2,1)} %get-tuple-element.53), channel_id=1, source_target_pairs={{0,8},{1,9},{2,10},{3,11},{4,12},{5,13},{6,14},{7,15},{8,16},{9,17... | collective-permute-start | bytes 3145736 | tf_op jit(solution)/shard_map/ppermute | solution.py:459
  113.2 1.0 copy-start.6
  113.2 1.3 copy-start.7
  123.1 37.9 %all-to-all-start.2 = ((bf16[8,15,16,256]{3,2,1,0:T(8,128)(2,1)}), bf16[8,15,16,256]{3,2,1,0:T(8,128)(2,1)S(1)}, u32[]{:S(2)}, u32[]{:S(2)}) async-start(bf16[8,15,16,256]{3,2,1,0:T(8,128)(2,1)} %shard_map.209), calls=%async_computation.2 | async-start | bytes 1966080 | tf_op jit(solution)/shard_map/all_to_all | solution.py:480
  160.9 29.2 %copy-start = (bf16[8,15,16,256]{3,2,1,0:T(8,128)(2,1)}, bf16[8,15,16,256]{3,2,1,0:T(8,128)(2,1)S(1)}, u32[]{:S(2)}) copy-start(bf16[8,15,16,256]{3,2,1,0:T(8,128)(2,1)S(1)} %all-to-all-done.2.refs_0_) | copy-start | bytes 2949124
  160.9 29.2 %all-to-all-start.3 = ((bf16[8,15,16,256]{3,2,1,0:T(8,128)(2,1)}), bf16[8,15,16,256]{3,2,1,0:T(8,128)(2,1)S(1)}, u32[]{:S(2)}, u32[]{:S(2)}) async-start(bf16[8,15,16,256]{3,2,1,0:T(8,128)(2,1)} %shard_map.210), calls=%async_computation.3 | async-start | bytes 1966080 | tf_op jit(solution)/shard_map/all_to_all | solution.py:480
  166.4 23.7 %collective-permute-start.11 = (f32[3,32,256]{2,1,0:T(8,128)S(1)}, f32[3,32,256]{2,1,0:T(8,128)S(1)}, u32[]{:S(2)}, u32[]{:S(2)}) collective-permute-start(f32[3,32,256]{2,1,0:T(8,128)S(1)} %slice.16), channel_id=1, source_target_pairs={{0,0},{1,1},{2,2},{3,3},{4,4},{5,5},{6,6},{7,7},{8,8},{9,9},{10,10... | collective-permute-start | bytes 294920 | tf_op jit(solution)/shard_map/ppermute | solution.py:483
  190.1 1.0 copy-start.1

commit v10 on v9

--- a/solution.py
+++ b/solution.py
@@ -304,17 +304,17 @@
                 operand[n * ALL_PAD + g * PAD : n * ALL_PAD + (g + 1) * PAD, :] = term.astype(bf16)
 
     def rows(i, carry):
-        for n in range(2):
-            build(2 * i + n, operands.at[n], locals_.at[n])
-        for n in range(2):
+        for n in range(4):
+            build(4 * i + n, operands.at[n], locals_.at[n])
+        for n in range(4):
             result = dot(weight_ref[...], operands[n]) + locals_[n]
             for side, stage in enumerate(stages):
-                stage[pl.ds(2 * i + n, ALL_PAD, stride=CHUNK), :] = result[
+                stage[pl.ds(4 * i + n, ALL_PAD, stride=CHUNK), :] = result[
                     :, side * LANES : (side + 1) * LANES
                 ]
         return carry
 
-    lax.fori_loop(0, CHUNK // 2, rows, 0)
+    lax.fori_loop(0, CHUNK // 4, rows, 0)
     for g in range(GROUPS):
         for c in range(OWN):
             first = (g * PAD + c) * CHUNK
@@ -468,8 +468,8 @@
         rates = call(
             rate_kernel, shape(GROUPS, OWN, CHUNK, NX), [center, *halo[part], flow, weights, damp],
             [
-                pltpu.VMEM((2, BLOCKS * ALL_PAD, NX), bf16),
-                pltpu.VMEM((2, ALL_PAD, NX), f32),
+                pltpu.VMEM((4, BLOCKS * ALL_PAD, NX), bf16),
+                pltpu.VMEM((4, ALL_PAD, NX), f32),
                 pltpu.VMEM((ALL_PAD * CHUNK, LANES), f32),
                 pltpu.VMEM((ALL_PAD * CHUNK, LANES), f32),
             ],

time: 196 us -> 195 us (level)
  transfers between devices with their start and end apart: 16 -> 16, of which waited for: 6 -> 6; matrix products, arithmetic and copies ran while one was open for 5% -> 5% of each run, Pallas kernels for 19% -> 18%
where the time goes in v10:
time: 195 us; the launch traced here: 194 us
  starting transfers between devices  84.4 us (43%)
  waiting for transfers between devices  47.9 us (25%)
  Pallas kernels  42.8 us (22%)
  local copies, waits for them, and re-layouts  12.5 us (6%)
  other arithmetic  4.47 us (2%)
    pallas_call x9, Pallas kernels, call(): pl.pallas_call(kernel, out_shape=out_shape, grid=(1,) if specs else (), i...  42.8 us
    all_to_all x1, starting transfers between devices, local(): mixed = lax.all_to_all(sent, everyone, 0, 0, tiled=True)  24.3 us
    ppermute x7, starting transfers between devices, exchanged(): lax.ppermute(c, 'harm', partner(j + 1))  22.2 us
    all_to_all x2, waiting for transfers between devices, local(): returned.append(lax.all_to_all(rates, 'harm', 0, 0, tiled=True))  20.5 us
    ppermute x1, waiting for transfers between devices, local(): velocity = lax.ppermute(late, both, swap)  16.4 us
    all_to_all x1, starting transfers between devices, local(): columns = lax.all_to_all(sent, everyone, 0, 0, tiled=True)  14.2 us
    all_to_all x2, starting transfers between devices, local(): returned.append(lax.all_to_all(rates, 'harm', 0, 0, tiled=True))  14.2 us
    unnamed x33, local copies, waits for them, and re-layouts  7.97 us
  transfers between devices with their start and end apart: 16, of which 6 were waited for; matrix products, arithmetic and copies ran while one was open for 5% of the time, Pallas kernels for 18%

profile of v10, /device:TPU:62, one launch (start us, length us, event | category | flops | bytes accessed | tf_op | source)
XLA Modules:
  0.0 193.8 jit_solution(15752872205765450544)
XLA Ops:
  0.6 0.8 fusion.2
  1.5 0.6 pad_maximum_fusion.table_ref
  2.1 4.8 %shard_map.203 = bf16[256,1280]{1,0:T(8,128)(2,1)} custom-call(f32[5,15]{1,0:T(8,128)} %pad_maximum_fusion.table_ref, bf16[15,256,256]{2,1,0:T(8,128)(2,1)} %bitcast.29, bf16[256,256]{1,0:T(8,128)(2,1)} %constant.102.clone.high_ref, bf16[256,256]{1,0:T(8,128)(2,1)} %constant.103.clone.low_ref), custom_call_target="tpu_custom_call" | custom-call | flops 1073741824 | bytes 3145728 | tf_op jit(solution)/shard_map/pallas_call | solution.py:336
  6.9 0.6 broadcast.14
  7.5 2.2 %reduce = bf16[256,1280]{1,0:T(8,128)(2,1)S(1)} reduce(bf16[256,1,1280]{2,0,1:T(8,128)(2,1)} %bitcast.32, bf16[]{:T(256)} %broadcast.14), dimensions={1}, to_apply=%copy.39.reduce_sub_computation | reduce | bytes 1310722 | tf_op jit(solution)/shard_map/all_to_all | solution.py:419
  9.7 1.0 reshape.60
  10.7 14.2 %all-to-all-start = ((bf16[256,2,640]{2,1,0:T(2,128)(2,1)}), bf16[256,2,640]{2,1,0:T(2,128)(2,1)S(1)}, u32[]{:S(2)}, u32[]{:S(2)}) async-start(bf16[256,2,640]{2,1,0:T(2,128)(2,1)} %reshape.60), calls=%async_computation | async-start | bytes 1310720 | tf_op jit(solution)/shard_map/all_to_all | solution.py:419
  24.9 6.4 %shard_map.204 = (bf16[16,8704]{1,0:T(8,128)(2,1)}, bf16[16,8704]{1,0:T(8,128)(2,1)}, bf16[16,8704]{1,0:T(8,128)(2,1)}, bf16[16,8704]{1,0:T(8,128)(2,1)}, bf16[1...) custom-call(s32[1]{0:T(128)S(6)} %xor.10.block_ref, ...), custom_call_target="tpu_custom_call" | custom-call | bytes 4194304 | tf_op jit(solution)/shard_map/pallas_call | solution.py:336
  31.3 0.8 collective-permute-start
  32.1 1.1 collective-permute-start.1
  33.3 2.7 %collective-permute-start.2 = (bf16[16,8704]{1,0:T(8,128)(2,1)}, bf16[16,8704]{1,0:T(8,128)(2,1)S(1)}, u32[]{:S(2)}, u32[]{:S(2)}) collective-permute-start(bf16[16,8704]{1,0:T(8,128)(2,1)} %get-tuple-element.34), channel_id=1, source_target_pairs={{0,3},{1,2},{2,1},{3,0},{4,7},{5,6},{6,5},{7,4},{8,11},{9,10},{10,... | collective-permute-start | bytes 835592 | tf_op jit(solution)/shard_map/ppermute | solution.py:384
  36.0 5.5 %collective-permute-start.3 = (bf16[16,8704]{1,0:T(8,128)(2,1)}, bf16[16,8704]{1,0:T(8,128)(2,1)S(1)}, u32[]{:S(2)}, u32[]{:S(2)}) collective-permute-start(bf16[16,8704]{1,0:T(8,128)(2,1)} %get-tuple-element.35), channel_id=1, source_target_pairs={{0,4},{1,5},{2,6},{3,7},{4,0},{5,1},{6,2},{7,3},{8,12},{9,13},{10,... | collective-permute-start | bytes 835592 | tf_op jit(solution)/shard_map/ppermute | solution.py:384
  41.6 1.9 collective-permute-done.refs_1_
  43.4 5.5 %collective-permute-start.5 = (bf16[16,8704]{1,0:T(8,128)(2,1)}, bf16[16,8704]{1,0:T(8,128)(2,1)}, u32[]{:S(2)}, u32[]{:S(2)}) collective-permute-start(bf16[16,8704]{1,0:T(8,128)(2,1)} %get-tuple-element.37), channel_id=1, source_target_pairs={{0,6},{1,7},{2,4},{3,5},{4,2},{5,3},{6,0},{7,1},{8,14},{9,15},{10,... | collective-permute-start | bytes 835592 | tf_op jit(solution)/shard_map/ppermute | solution.py:384
  49.0 0.5 collective-permute-done.1.refs_2_
  49.5 6.4 %collective-permute-start.6 = (bf16[16,8704]{1,0:T(8,128)(2,1)}, bf16[16,8704]{1,0:T(8,128)(2,1)}, u32[]{:S(2)}, u32[]{:S(2)}) collective-permute-start(bf16[16,8704]{1,0:T(8,128)(2,1)} %get-tuple-element.38), channel_id=1, source_target_pairs={{0,7},{1,6},{2,5},{3,4},{4,3},{5,2},{6,1},{7,0},{8,15},{9,14},{10,... | collective-permute-start | bytes 835592 | tf_op jit(solution)/shard_map/ppermute | solution.py:384
  56.0 0.7 pad.18
  56.7 0.7 copy.40.synth_ref
  57.5 0.6 pad.17
  58.1 2.5 %shard_map.205.weight_ref = bf16[128,1536]{1,0:T(8,128)(2,1)} custom-call(f32[3,256]{1,0:T(4,128)} %constant.104.clone.dir_ref, bf16[256,128]{1,0:T(8,128)(2,1)} %copy.40.synth_ref, bf16[128,256]{1,0:T(8,128)(2,1)} %bitcast.39, bf16[3,128,256]{2,1,0:T(8,128)(2,1)} %bitcast.37), custom_call_target="tpu_custom_call" | custom-call | flops 268435456 | bytes 1048576 | tf_op jit(solution)/shard_map/pallas_call | solution.py:336
  60.6 0.5 reshape.61
  61.2 0.9 copy.50
  62.1 4.0 %shard_map.206 = bf16[256,512]{1,0:T(8,128)(2,1)} custom-call(f32[1]{0:T(128)} %bitcast.5.wave_ref, s32[1]{0:T(128)} %bitcast.6.half_ref, f32[1,256]{1,0:T(1,128)} %constant.105.clone.ky_ref, f32[32,1]{1,0:T(8,128)} %constant.106.clone.kz_ref, bf16[256,1280]{1,0:T(8,128)(2,1)} %bitcast.33, bf16[64,256]{1,0:T(8,128)(2,1)} %constant.107.clone.fz_high, ...), custom_call_target="tpu_custom_call" | custom-call | flops 1073741824 | bytes 3145728 | tf_op jit(solution)/shard_map/pallas_call | solution.py:336
  66.1 1.7 reduce.1
  67.8 0.8 reshape.62
  68.6 24.3 %all-to-all-start.1 = ((bf16[256,2,256]{2,1,0:T(2,128)(2,1)}), bf16[256,2,256]{2,1,0:T(2,128)(2,1)S(1)}, u32[]{:S(2)}, u32[]{:S(2)}) async-start(bf16[256,2,256]{2,1,0:T(2,128)(2,1)} %reshape.62), calls=%async_computation.1 | async-start | bytes 524288 | tf_op jit(solution)/shard_map/all_to_all | solution.py:451
  93.0 0.7 broadcast_in_dim_reshape.4.damp_ref
  93.8 0.6 copy-done.10
  94.7 3.9 %shard_map.207 = (bf16[128,8704]{1,0:T(8,128)(2,1)}, bf16[128,4096]{1,0:T(8,128)(2,1)}, bf16[128,4096]{1,0:T(8,128)(2,1)}) custom-call(s32[1]{0:T(128)} %bitcast.group_ref, bf16[16,8704]{1,0:T(8,128)(2,1)} %get-tuple-element.40.refs_0_, bf16[16,8704]{1,0:T(8,128)(2,1)} %copy-done.8, bf16[16,8704]{1,0:T(8,128)(2,1)} %copy-done.9, ...), custom_call_target="tpu_custom_call" | custom-call | flops 4294967296 | bytes 4194304 | tf_op jit(solution)/shard_map/pallas_call | solution.py:336
  98.7 1.6 collective-permute-start.8
  100.4 0.5 collective-permute-start.9
  100.8 4.1 %all-to-all-done.1 = bf16[256,2,256]{2,1,0:T(2,128)(2,1)S(1)} async-done(((bf16[256,2,256]{2,1,0:T(2,128)(2,1)}), bf16[256,2,256]{2,1,0:T(2,128)(2,1)S(1)}, u32[]{:S(2)}, u32[]{:S(2)}) %all-to-all-start.1) | async-done | bytes 262176 | tf_op jit(solution)/shard_map/all_to_all | solution.py:451
  105.2 0.7 copy.51
  105.9 2.8 %shard_map.208.flow_ref = f32[11,32,256]{2,1,0:T(8,128)} custom-call(bf16[256,512]{1,0:T(8,128)(2,1)} %bitcast.34, bf16[256,1024]{1,0:T(8,128)(2,1)} %constant.114.clone.high_ref, bf16[256,1024]{1,0:T(8,128)(2,1)} %constant.115.clone.low_ref), custom_call_target="tpu_custom_call" | custom-call | flops 137438953472 | bytes 2097152 | tf_op jit(solution)/shard_map/pallas_call | solution.py:336
  108.7 4.4 %collective-permute-done.7.zlow_ref = bf16[128,4096]{1,0:T(8,128)(2,1)S(1)} collective-permute-done((bf16[128,4096]{1,0:T(8,128)(2,1)}, bf16[128,4096]{1,0:T(8,128)(2,1)S(1)}, u32[]{:S(2)}, u32[]{:S(2)}) %collective-permute-start.7) | collective-permute-done | bytes 1048608 | tf_op jit(solution)/shard_map/ppermute | solution.py:459
  113.2 1.0 copy-done.6
  114.2 0.3 copy-done.7
  114.5 7.7 %shard_map.209 = bf16[8,15,16,256]{3,2,1,0:T(8,128)(2,1)} custom-call(bf16[128,8704]{1,0:T(8,128)(2,1)} %get-tuple-element.52.center_ref, bf16[128,4096]{1,0:T(8,128)(2,1)} %copy-done.6, bf16[128,4096]{1,0:T(8,128)(2,1)} %copy-done.7, f32[11,32,256]{2,1,0:T(8,128)} %shard_map.208.flow_ref, bf16[128,1536]{1,0:T(8,128)(2,1)} %shard_map.205.weight_ref, ...), custom_call_target="tpu_custom_call" | custom-call | flops 8589934592 | bytes 4718592 | tf_op jit(solution)/shard_map/pallas_call | solution.py:336
  122.2 9.6 %all-to-all-start.2 = ((bf16[8,15,16,256]{3,2,1,0:T(8,128)(2,1)}), bf16[8,15,16,256]{3,2,1,0:T(8,128)(2,1)S(1)}, u32[]{:S(2)}, u32[]{:S(2)}) async-start(bf16[8,15,16,256]{3,2,1,0:T(8,128)(2,1)} %shard_map.209), calls=%async_computation.2 | async-start | bytes 1966080 | tf_op jit(solution)/shard_map/all_to_all | solution.py:480
  131.8 7.7 %shard_map.210 = bf16[8,15,16,256]{3,2,1,0:T(8,128)(2,1)} custom-call(bf16[128,8704]{1,0:T(8,128)(2,1)} %get-tuple-element.52.center_ref, bf16[128,4096]{1,0:T(8,128)(2,1)} %collective-permute-done.9.zlow_ref, bf16[128,4096]{1,0:T(8,128)(2,1)} %collective-permute-done.10.zhigh_ref, f32[11,32,256]{2,1,0:T(8,128)} %shard_map.208.flow_ref, ...), custom_call_target="tpu_custom_call" | custom-call | flops 8589934592 | bytes 4718592 | tf_op jit(solution)/shard_map/pallas_call | solution.py:336
  139.6 20.5 %all-to-all-done.2.refs_0_ = bf16[8,15,16,256]{3,2,1,0:T(8,128)(2,1)S(1)} async-done(((bf16[8,15,16,256]{3,2,1,0:T(8,128)(2,1)}), bf16[8,15,16,256]{3,2,1,0:T(8,128)(2,1)S(1)}, u32[]{:S(2)}, u32[]{:S(2)}) %all-to-all-start.2) | async-done | bytes 983072 | tf_op jit(solution)/shard_map/all_to_all | solution.py:480
  160.1 4.6 %all-to-all-start.3 = ((bf16[8,15,16,256]{3,2,1,0:T(8,128)(2,1)}), bf16[8,15,16,256]{3,2,1,0:T(8,128)(2,1)S(1)}, u32[]{:S(2)}, u32[]{:S(2)}) async-start(bf16[8,15,16,256]{3,2,1,0:T(8,128)(2,1)} %shard_map.210), calls=%async_computation.3 | async-start | bytes 1966080 | tf_op jit(solution)/shard_map/all_to_all | solution.py:480
  164.7 0.9 slice.16
  165.6 7.3 %collective-permute-start.11 = (f32[3,32,256]{2,1,0:T(8,128)S(1)}, f32[3,32,256]{2,1,0:T(8,128)S(1)}, u32[]{:S(2)}, u32[]{:S(2)}) collective-permute-start(f32[3,32,256]{2,1,0:T(8,128)S(1)} %slice.16), channel_id=1, source_target_pairs={{0,0},{1,1},{2,2},{3,3},{4,4},{5,5},{6,6},{7,7},{8,8},{9,9},{10,10... | collective-permute-start | bytes 294920 | tf_op jit(solution)/shard_map/ppermute | solution.py:483
  172.9 16.4 %collective-permute-done.11 = f32[3,32,256]{2,1,0:T(8,128)S(1)} collective-permute-done((f32[3,32,256]{2,1,0:T(8,128)S(1)}, f32[3,32,256]{2,1,0:T(8,128)S(1)}, u32[]{:S(2)}, u32[]{:S(2)}) %collective-permute-start.11) | collective-permute-done | bytes 98336 | tf_op jit(solution)/shard_map/ppermute | solution.py:483
  189.3 1.0 copy-done.1
  190.2 2.9 %shard_map.211 = bf16[15,256,256]{2,1,0:T(8,128)(2,1)} custom-call(s32[1]{0:T(128)S(6)} %xor.11.swap_ref, bf16[8,15,16,256]{3,2,1,0:T(8,128)(2,1)} %copy-done, bf16[8,15,16,256]{3,2,1,0:T(8,128)(2,1)} %copy-done.1), custom_call_target="tpu_custom_call" | custom-call | bytes 4194304 | tf_op jit(solution)/shard_map/pallas_call | solution.py:336
  193.2 0.6 copy.55
  (45 shorter events, 0.9 us)
Async XLA Ops:
  10.7 45.2 %copy-start.3 = (bf16[256,120]{0,1:T(8,128)(2,1)S(1)}, bf16[256,120]{0,1:T(8,128)(2,1)}, u32[]{:S(2)}) copy-start(bf16[256,120]{0,1:T(8,128)(2,1)} %param.21) | copy-start | bytes 184324
  10.7 45.3 %copy-start.2 = (bf16[3,120,256]{2,1,0:T(8,128)(2,1)S(1)}, bf16[3,120,256]{2,1,0:T(8,128)(2,1)}, u32[]{:S(2)}) copy-start(bf16[3,120,256]{2,1,0:T(8,128)(2,1)} %param.23) | copy-start | bytes 552964
  10.7 46.8 %copy-start.4 = (bf16[120,256]{1,0:T(8,128)(2,1)S(1)}, bf16[120,256]{1,0:T(8,128)(2,1)}, u32[]{:S(2)}) copy-start(bf16[120,256]{1,0:T(8,128)(2,1)} %param.22) | copy-start | bytes 184324
  10.7 49.9 %all-to-all-start = ((bf16[256,2,640]{2,1,0:T(2,128)(2,1)}), bf16[256,2,640]{2,1,0:T(2,128)(2,1)S(1)}, u32[]{:S(2)}, u32[]{:S(2)}) async-start(bf16[256,2,640]{2,1,0:T(2,128)(2,1)} %reshape.60), calls=%async_computation | async-start | bytes 1310720 | tf_op jit(solution)/shard_map/all_to_all | solution.py:419
  31.3 12.1 %collective-permute-start = (bf16[16,8704]{1,0:T(8,128)(2,1)}, bf16[16,8704]{1,0:T(8,128)(2,1)S(1)}, u32[]{:S(2)}, u32[]{:S(2)}) collective-permute-start(bf16[16,8704]{1,0:T(8,128)(2,1)} %get-tuple-element.32), channel_id=1, source_target_pairs={{0,1},{1,0},{2,3},{3,2},{4,5},{5,4},{6,7},{7,6},{8,9},{9,8},{10,11... | collective-permute-start | bytes 835592 | tf_op jit(solution)/shard_map/ppermute | solution.py:384
  32.1 17.3 %collective-permute-start.1 = (bf16[16,8704]{1,0:T(8,128)(2,1)}, bf16[16,8704]{1,0:T(8,128)(2,1)S(1)}, u32[]{:S(2)}, u32[]{:S(2)}) collective-permute-start(bf16[16,8704]{1,0:T(8,128)(2,1)} %get-tuple-element.33), channel_id=1, source_target_pairs={{0,2},{1,3},{2,0},{3,1},{4,6},{5,7},{6,4},{7,5},{8,10},{9,11},{10,... | collective-permute-start | bytes 835592 | tf_op jit(solution)/shard_map/ppermute | solution.py:384
  33.3 60.5 %collective-permute-start.2 = (bf16[16,8704]{1,0:T(8,128)(2,1)}, bf16[16,8704]{1,0:T(8,128)(2,1)S(1)}, u32[]{:S(2)}, u32[]{:S(2)}) collective-permute-start(bf16[16,8704]{1,0:T(8,128)(2,1)} %get-tuple-element.34), channel_id=1, source_target_pairs={{0,3},{1,2},{2,1},{3,0},{4,7},{5,6},{6,5},{7,4},{8,11},{9,10},{10,... | collective-permute-start | bytes 835592 | tf_op jit(solution)/shard_map/ppermute | solution.py:384
  36.0 57.8 %collective-permute-start.3 = (bf16[16,8704]{1,0:T(8,128)(2,1)}, bf16[16,8704]{1,0:T(8,128)(2,1)S(1)}, u32[]{:S(2)}, u32[]{:S(2)}) collective-permute-start(bf16[16,8704]{1,0:T(8,128)(2,1)} %get-tuple-element.35), channel_id=1, source_target_pairs={{0,4},{1,5},{2,6},{3,7},{4,0},{5,1},{6,2},{7,3},{8,12},{9,13},{10,... | collective-permute-start | bytes 835592 | tf_op jit(solution)/shard_map/ppermute | solution.py:384
  41.5 52.2 %collective-permute-start.4 = (bf16[16,8704]{1,0:T(8,128)(2,1)}, bf16[16,8704]{1,0:T(8,128)(2,1)S(1)}, u32[]{:S(2)}, u32[]{:S(2)}) collective-permute-start(bf16[16,8704]{1,0:T(8,128)(2,1)} %get-tuple-element.36), channel_id=1, source_target_pairs={{0,5},{1,4},{2,7},{3,6},{4,1},{5,0},{6,3},{7,2},{8,13},{9,12},{10,... | collective-permute-start | bytes 835592 | tf_op jit(solution)/shard_map/ppermute | solution.py:384
  43.4 17.7 %copy-start.8 = (bf16[16,8704]{1,0:T(8,128)(2,1)}, bf16[16,8704]{1,0:T(8,128)(2,1)S(1)}, u32[]{:S(2)}) copy-start(bf16[16,8704]{1,0:T(8,128)(2,1)S(1)} %collective-permute-done.refs_1_) | copy-start | bytes 835588
  43.4 50.4 %collective-permute-start.5 = (bf16[16,8704]{1,0:T(8,128)(2,1)}, bf16[16,8704]{1,0:T(8,128)(2,1)}, u32[]{:S(2)}, u32[]{:S(2)}) collective-permute-start(bf16[16,8704]{1,0:T(8,128)(2,1)} %get-tuple-element.37), channel_id=1, source_target_pairs={{0,6},{1,7},{2,4},{3,5},{4,2},{5,3},{6,0},{7,1},{8,14},{9,15},{10,... | collective-permute-start | bytes 835592 | tf_op jit(solution)/shard_map/ppermute | solution.py:384
  49.5 11.7 %copy-start.9 = (bf16[16,8704]{1,0:T(8,128)(2,1)}, bf16[16,8704]{1,0:T(8,128)(2,1)S(1)}, u32[]{:S(2)}) copy-start(bf16[16,8704]{1,0:T(8,128)(2,1)S(1)} %collective-permute-done.1.refs_2_) | copy-start | bytes 835588
  49.5 44.3 %collective-permute-start.6 = (bf16[16,8704]{1,0:T(8,128)(2,1)}, bf16[16,8704]{1,0:T(8,128)(2,1)}, u32[]{:S(2)}, u32[]{:S(2)}) collective-permute-start(bf16[16,8704]{1,0:T(8,128)(2,1)} %get-tuple-element.38), channel_id=1, source_target_pairs={{0,7},{1,6},{2,5},{3,4},{4,3},{5,2},{6,1},{7,0},{8,15},{9,14},{10,... | collective-permute-start | bytes 835592 | tf_op jit(solution)/shard_map/ppermute | solution.py:384
  62.1 30.9 %copy-start.5 = (f32[120]{0:T(128)S(1)}, f32[120]{0:T(128)}, u32[]{:S(2)}) copy-start(f32[120]{0:T(128)} %param.24) | copy-start | bytes 1444
  68.6 36.4 %all-to-all-start.1 = ((bf16[256,2,256]{2,1,0:T(2,128)(2,1)}), bf16[256,2,256]{2,1,0:T(2,128)(2,1)S(1)}, u32[]{:S(2)}, u32[]{:S(2)}) async-start(bf16[256,2,256]{2,1,0:T(2,128)(2,1)} %reshape.62), calls=%async_computation.1 | async-start | bytes 524288 | tf_op jit(solution)/shard_map/all_to_all | solution.py:451
  93.7 0.7 copy-start.10
  93.8 0.8 copy-start.11
  93.8 0.9 copy-start.12
  98.6 14.6 %collective-permute-start.7 = (bf16[128,4096]{1,0:T(8,128)(2,1)}, bf16[128,4096]{1,0:T(8,128)(2,1)S(1)}, u32[]{:S(2)}, u32[]{:S(2)}) collective-permute-start(bf16[128,4096]{1,0:T(8,128)(2,1)} %get-tuple-element.49), channel_id=1, source_target_pairs={{0,8},{1,9},{2,10},{3,11},{4,12},{5,13},{6,14},{7,15},{8,16},{9,17... | collective-permute-start | bytes 3145736 | tf_op jit(solution)/shard_map/ppermute | solution.py:459
  98.7 14.5 %collective-permute-start.8 = (bf16[128,4096]{1,0:T(8,128)(2,1)}, bf16[128,4096]{1,0:T(8,128)(2,1)S(1)}, u32[]{:S(2)}, u32[]{:S(2)}) collective-permute-start(bf16[128,4096]{1,0:T(8,128)(2,1)} %get-tuple-element.49), channel_id=1, source_target_pairs={{0,252},{1,253},{2,254},{3,255},{4,248},{5,249},{6,250},{7,251},{8... | collective-permute-start | bytes 3145736 | tf_op jit(solution)/shard_map/ppermute | solution.py:459
  100.3 31.5 %collective-permute-start.10 = (bf16[128,4096]{1,0:T(8,128)(2,1)}, bf16[128,4096]{1,0:T(8,128)(2,1)}, u32[]{:S(2)}, u32[]{:S(2)}) collective-permute-start(bf16[128,4096]{1,0:T(8,128)(2,1)} %get-tuple-element.53), channel_id=1, source_target_pairs={{0,252},{1,253},{2,254},{3,255},{4,248},{5,249},{6,250},{7,251},{8... | collective-permute-start | bytes 3145736 | tf_op jit(solution)/shard_map/ppermute | solution.py:459
  100.4 31.5 %collective-permute-start.9 = (bf16[128,4096]{1,0:T(8,128)(2,1)}, bf16[128,4096]{1,0:T(8,128)(2,1)}, u32[]{:S(2)}, u32[]{:S(2)}) collective-permute-start(bf16[128,4096]{1,0:T(8,128)(2,1)} %get-tuple-element.53), channel_id=1, source_target_pairs={{0,8},{1,9},{2,10},{3,11},{4,12},{5,13},{6,14},{7,15},{8,16},{9,17... | collective-permute-start | bytes 3145736 | tf_op jit(solution)/shard_map/ppermute | solution.py:459
  113.2 1.0 copy-start.6
  113.2 1.3 copy-start.7
  122.2 37.9 %all-to-all-start.2 = ((bf16[8,15,16,256]{3,2,1,0:T(8,128)(2,1)}), bf16[8,15,16,256]{3,2,1,0:T(8,128)(2,1)S(1)}, u32[]{:S(2)}, u32[]{:S(2)}) async-start(bf16[8,15,16,256]{3,2,1,0:T(8,128)(2,1)} %shard_map.209), calls=%async_computation.2 | async-start | bytes 1966080 | tf_op jit(solution)/shard_map/all_to_all | solution.py:480
  160.1 29.2 %copy-start = (bf16[8,15,16,256]{3,2,1,0:T(8,128)(2,1)}, bf16[8,15,16,256]{3,2,1,0:T(8,128)(2,1)S(1)}, u32[]{:S(2)}) copy-start(bf16[8,15,16,256]{3,2,1,0:T(8,128)(2,1)S(1)} %all-to-all-done.2.refs_0_) | copy-start | bytes 2949124
  160.1 29.2 %all-to-all-start.3 = ((bf16[8,15,16,256]{3,2,1,0:T(8,128)(2,1)}), bf16[8,15,16,256]{3,2,1,0:T(8,128)(2,1)S(1)}, u32[]{:S(2)}, u32[]{:S(2)}) async-start(bf16[8,15,16,256]{3,2,1,0:T(8,128)(2,1)} %shard_map.210), calls=%async_computation.3 | async-start | bytes 1966080 | tf_op jit(solution)/shard_map/all_to_all | solution.py:480
  165.6 23.7 %collective-permute-start.11 = (f32[3,32,256]{2,1,0:T(8,128)S(1)}, f32[3,32,256]{2,1,0:T(8,128)S(1)}, u32[]{:S(2)}, u32[]{:S(2)}) collective-permute-start(f32[3,32,256]{2,1,0:T(8,128)S(1)} %slice.16), channel_id=1, source_target_pairs={{0,0},{1,1},{2,2},{3,3},{4,4},{5,5},{6,6},{7,7},{8,8},{9,9},{10,10... | collective-permute-start | bytes 294920 | tf_op jit(solution)/shard_map/ppermute | solution.py:483
  189.3 1.0 copy-start.1
